TPU v7x, 32 devices: a whole 2x2x4 slice. The times are simulated.
32 devices in a mesh: dp: 4 (over x, core), fsdp: 8 (over z, y).
Axes of the slice: x: 2, y: 2, z: 4, core: 2. Of those that a mesh axis runs over, the one named last changes fastest.
Arguments:
- features: bfloat16 [24576, 512], P(('dp', 'fsdp')), may hold values from -8 to 8
- row_valid: int32 [24576], P(('dp', 'fsdp')), may hold values 0 or 1
- micro_batch: int32 [24576], P(('dp', 'fsdp')), may hold values from 0 to 3
- gains: float32 [2, 512], replicated, may hold values from 0.25 to 1.75
- shifts: float32 [2, 512], replicated, may hold values from -4 to 4
- mask_logits: float32 [2, 6, 512], replicated, may hold values from -6 to 6
- thresholds: float32 [2, 6], replicated, may hold values from 0.5 to 2.5
- gate_in: bfloat16 [2, 6, 1024, 1024], P(None, None, 'fsdp'), may hold values from -0.1875 to 0.1875
- bias_in: float32 [2, 6, 1024], replicated, may hold values from -4 to 4
- gate_out: bfloat16 [2, 6, 1024, 512], P(None, None, 'fsdp'), may hold values from -0.1875 to 0.1875
- bias_out: float32 [2, 6, 512], replicated, may hold values from -4 to 4
- cotangent: bfloat16 [24576, 512], P(('dp', 'fsdp')), may hold values from -6 to 6
Outputs:
- mixed_out: bfloat16 [24576, 512], P(('dp', 'fsdp'))
- grad_features: float32 [24576, 512], P(('dp', 'fsdp'))
- grad_gains: float32 [2, 512], replicated
- grad_shifts: float32 [2, 512], replicated
- grad_logits: float32 [2, 6, 512], replicated
- grad_thresholds: float32 [2, 6], replicated
- grad_gate_in: float32 [2, 6, 1024, 1024], P(None, None, 'fsdp')
- grad_bias_in: float32 [2, 6, 1024], replicated
- grad_gate_out: float32 [2, 6, 1024, 512], P(None, None, 'fsdp')
- grad_bias_out: float32 [2, 6, 512], replicated
Inputs may be any that keep to these rules, and one draw needn't show every extreme that they name: `row_valid`: 1 marks a real row, 0 a padded one.
All inputs are finite; a program needn't handle non-finite values. No bound on the sum of `row_valid` on one device may be relied on, other than what follows from the above.
Results may differ from a plain program's by a relative error of at most 0.015.
Values may be sent and summed in bfloat16 or wider, within the bound.
No kernel may reach another device: no remote copies, remote signals or barrier semaphores. Data moves between devices by JAX's collectives and lax.ppermute only.
A program may use at most 320 MiB of HBM per device.

v0:
```python
import jax
import jax.numpy as jnp
from jax import lax
from jax.sharding import PartitionSpec as P

SECTIONS = 6
LAYERS = 2
MB = 4


epsilon = 1e-05


def highest(left_side, right_side):
    return jnp.dot(left_side, right_side, precision=lax.Precision.HIGHEST)


def pool_rows(weights, values):
    return lax.dot_general(
        weights, values, (((0,), (0,)), ((), ())), precision=lax.Precision.HIGHEST
    )


def feature_mask(logits, thresh):
    centred = logits - jnp.max(logits)
    weights = jnp.exp(centred) * jax.nn.softplus(centred + thresh)
    return weights / jnp.sum(weights)


def add_rows(operand, shard_rows):
    return jnp.dot(operand, shard_rows, preferred_element_type=jnp.float32)


def back_rows(grad_rows, shard_rows):
    return lax.dot_general(
        grad_rows, shard_rows, (((1,), (1,)), ((), ())), preferred_element_type=jnp.float32
    )


def weight_rows(operand, grad_rows):
    return lax.dot_general(
        operand, grad_rows, (((0,), (0,)), ((), ())), preferred_element_type=jnp.float32
    )


def norm_forward(current, onehot, member):
    counts, totals = lax.psum((jnp.sum(member, axis=0), pool_rows(member, current)), ("dp", "fsdp"))
    average = totals / counts[:, None]
    centred = current - highest(onehot, average)
    spread = lax.psum(pool_rows(member, centred * centred), ("dp", "fsdp")) / counts[:, None]
    scaling = lax.rsqrt(spread + epsilon)
    row_scale = highest(onehot, scaling)
    standard = (current - highest(onehot, average)) * row_scale
    return (standard, row_scale, counts)


def local(
    features,
    row_valid,
    micro_batch,
    gains,
    shifts,
    mask_logits,
    thresholds,
    gate_in,
    bias_in,
    gate_out,
    bias_out,
    cotangent,
):
    columns = features.shape[1]
    valid_rows = row_valid.astype(jnp.float32)
    onehot = (micro_batch[:, None] == jnp.arange(MB, dtype=jnp.int32)[None, :]).astype(jnp.float32)
    member = onehot * valid_rows[:, None]
    current = features.astype(jnp.float32)
    records = []
    for layer_no in range(LAYERS):
        standard, row_scale, counts = norm_forward(current, onehot, member)
        normed = standard * gains[layer_no] + shifts[layer_no]
        hidden = normed
        stored = []
        for section_no in range(SECTIONS):
            feat_mask = feature_mask(
                mask_logits[layer_no, section_no], thresholds[layer_no, section_no]
            )
            scaled_mask = columns * feat_mask
            first_in = jnp.concatenate([scaled_mask * normed, hidden], axis=1).astype(jnp.bfloat16)
            whole_in, whole_out = (None, None)
            gate_pre = add_rows(
                first_in, lax.all_gather(gate_in[layer_no, section_no], "fsdp", axis=0, tiled=True)
            )
            gate_pre = gate_pre + bias_in[layer_no, section_no]
            update = jax.nn.sigmoid(gate_pre[:, :columns])
            reset_gate = jax.nn.sigmoid(gate_pre[:, columns:])
            second_in = jnp.concatenate([reset_gate * hidden, normed], axis=1).astype(jnp.bfloat16)
            raw_out = add_rows(
                second_in,
                lax.all_gather(gate_out[layer_no, section_no], "fsdp", axis=0, tiled=True),
            )
            candidate = jnp.tanh(raw_out + bias_out[layer_no, section_no])
            stored.append((hidden, update, reset_gate, candidate, scaled_mask, whole_in, whole_out))
            hidden = (1.0 - update) * hidden + update * candidate
        records.append((standard, row_scale, counts, normed, stored))
        current = current + hidden
    mixed_out = current.astype(jnp.bfloat16)
    carried = cotangent.astype(jnp.float32) * valid_rows[:, None]
    mask_parts = [[None] * SECTIONS for layer_no in range(LAYERS)]
    bias_in_parts = [[None] * SECTIONS for layer_no in range(LAYERS)]
    bias_out_parts = [[None] * SECTIONS for layer_no in range(LAYERS)]
    in_parts = [[None] * SECTIONS for layer_no in range(LAYERS)]
    out_parts = [[None] * SECTIONS for layer_no in range(LAYERS)]
    gain_grads = [None] * LAYERS
    shift_grads = [None] * LAYERS
    for layer_no in reversed(range(LAYERS)):
        standard, row_scale, counts, normed, stored = records[layer_no]
        grad_hidden = carried
        grad_normed = jnp.zeros_like(normed)
        for section_no in reversed(range(SECTIONS)):
            hidden, update, reset_gate, candidate, scaled_mask, whole_in, whole_out = stored[
                section_no
            ]
            grad_update = grad_hidden * (candidate - hidden)
            grad_raw = (grad_hidden * update * (1.0 - candidate * candidate)).astype(jnp.bfloat16)
            second_in = jnp.concatenate([reset_gate * hidden, normed], axis=1).astype(jnp.bfloat16)
            out_parts[layer_no][section_no] = lax.psum_scatter(
                weight_rows(second_in, grad_raw).astype(jnp.bfloat16),
                "fsdp",
                scatter_dimension=0,
                tiled=True,
            ).astype(jnp.float32)
            grad_second = back_rows(
                grad_raw, lax.all_gather(gate_out[layer_no, section_no], "fsdp", axis=0, tiled=True)
            )
            grad_reset = grad_second[:, :columns] * hidden
            grad_gates = jnp.concatenate(
                [
                    grad_update * update * (1.0 - update),
                    grad_reset * reset_gate * (1.0 - reset_gate),
                ],
                axis=1,
            ).astype(jnp.bfloat16)
            first_in = jnp.concatenate([scaled_mask * normed, hidden], axis=1).astype(jnp.bfloat16)
            in_parts[layer_no][section_no] = lax.psum_scatter(
                weight_rows(first_in, grad_gates).astype(jnp.bfloat16),
                "fsdp",
                scatter_dimension=0,
                tiled=True,
            ).astype(jnp.float32)
            grad_first = back_rows(
                grad_gates,
                lax.all_gather(gate_in[layer_no, section_no], "fsdp", axis=0, tiled=True),
            )
            grad_masked = grad_first[:, :columns]
            mask_parts[layer_no][section_no] = columns * jnp.sum(grad_masked * normed, axis=0)
            bias_in_parts[layer_no][section_no] = jnp.sum(grad_gates, axis=0, dtype=jnp.float32)
            bias_out_parts[layer_no][section_no] = jnp.sum(grad_raw, axis=0, dtype=jnp.float32)
            grad_normed = grad_normed + grad_second[:, columns:] + grad_masked * scaled_mask
            grad_hidden = (
                grad_hidden * (1.0 - update)
                + grad_second[:, :columns] * reset_gate
                + grad_first[:, columns:]
            )
        grad_normed = grad_normed + grad_hidden
        gain = gains[layer_no]
        pooled_grad, pooled_prod = lax.psum(
            (pool_rows(onehot, grad_normed), pool_rows(onehot, grad_normed * standard)),
            ("dp", "fsdp"),
        )
        gain_grads[layer_no] = jnp.sum(pooled_prod, axis=0)
        shift_grads[layer_no] = jnp.sum(pooled_grad, axis=0)
        shift_term = highest(onehot, gain * pooled_grad / counts[:, None])
        scale_term = highest(onehot, gain * pooled_prod / counts[:, None])
        carried = carried + row_scale * (
            grad_normed * gain - valid_rows[:, None] * (shift_term + standard * scale_term)
        )
    mask_sum, bias_in_sum, bias_out_sum = lax.psum(
        (
            jnp.stack([jnp.stack(layer_list, 0) for layer_list in mask_parts], 0),
            jnp.stack([jnp.stack(layer_list, 0) for layer_list in bias_in_parts], 0),
            jnp.stack([jnp.stack(layer_list, 0) for layer_list in bias_out_parts], 0),
        ),
        ("dp", "fsdp"),
    )
    stacked_in = jnp.stack([jnp.stack(layer_list, 0) for layer_list in in_parts], 0)
    stacked_out = jnp.stack([jnp.stack(layer_list, 0) for layer_list in out_parts], 0)
    grad_gate_in, grad_gate_out = (
        lax.psum(stacked_in.astype(jnp.bfloat16), "dp").astype(jnp.float32),
        lax.psum(stacked_out.astype(jnp.bfloat16), "dp").astype(jnp.float32),
    )
    mask_value, mask_pull = jax.vjp(jax.vmap(jax.vmap(feature_mask)), mask_logits, thresholds)
    grad_logits, grad_thresholds = mask_pull(mask_sum)
    return (
        mixed_out,
        carried,
        jnp.stack(gain_grads, 0),
        jnp.stack(shift_grads, 0),
        grad_logits,
        grad_thresholds,
        grad_gate_in,
        bias_in_sum,
        grad_gate_out,
        bias_out_sum,
    )


def solution(mesh):
    in_specs = (
        P(("dp", "fsdp"), None),
        P(("dp", "fsdp")),
        P(("dp", "fsdp")),
        P(),
        P(),
        P(),
        P(),
        P(None, None, "fsdp", None),
        P(),
        P(None, None, "fsdp", None),
        P(),
        P(("dp", "fsdp"), None),
    )
    out_specs = (
        P(("dp", "fsdp"), None),
        P(("dp", "fsdp"), None),
        P(),
        P(),
        P(),
        P(),
        P(None, None, "fsdp", None),
        P(),
        P(None, None, "fsdp", None),
        P(),
    )
    return jax.shard_map(local, mesh=mesh, in_specs=in_specs, out_specs=out_specs, check_vma=False)
```

profile of v0, /device:TPU:0, one launch (start us, length us, event | category | flops | bytes accessed | tf_op | source)
XLA Modules:
  0.0 3078.6 jit_solution(207808555481785867)
XLA Ops:
  37.0 6.4 subtract_add_fusion.4
  48.6 5.9 subtract_exponential_fusion.4
  61.0 42.5 %all-reduce.2 = (f32[4,512]{1,0:T(4,128)S(1)}, f32[4]{0:T(128)}) all-reduce(f32[4,512]{1,0:T(4,128)S(1)} %fusion.222, f32[4]{0:T(128)S(1)} %select_reduce_fusion), channel_id=1, replica_groups=mesh['dp'=4,'fsdp'=8] {'dp','fsdp'}, use_global_device_ids=true, to_apply=%region_2.0 | all-reduce | flops 2052 | bytes 16416 | tf_op jit(solution)/shard_map/psum | solution.py:47
  107.0 41.2 %psum.103 = f32[4,512]{1,0:T(4,128)S(1)} all-reduce(f32[4,512]{1,0:T(4,128)S(1)} %fusion.174), channel_id=1, replica_groups=mesh['dp'=4,'fsdp'=8] {'dp','fsdp'}, use_global_device_ids=true, to_apply=%region_5.6 | all-reduce | flops 2048 | bytes 16384 | tf_op jit(solution)/shard_map/psum | solution.py:50
  160.9 5.3 fusion.388
  172.0 23.7 all-gather.55.cloned.1.call-done
  195.8 5.4 fusion.387
  201.2 44.6 %all-gather.57.cloned.1.call-done = bf16[1,1,1024,1024]{3,2,1,0:T(8,128)(2,1)} async-done(((bf16[1,1,128,1024]{3,2,1,0:T(8,128)(2,1)}), bf16[1,1,1024,1024]{3,2,1,0:T(8,128)(2,1)}) %all-gather.57.cloned.1.call-update) | async-done | bytes 2097168 | tf_op jit(solution)/shard_map/all_gather | solution.py:90
  251.5 35.0 %all-gather.59.cloned.1.call-done = bf16[1,1,1024,512]{3,2,1,0:T(8,128)(2,1)} async-done(((bf16[1,1,128,512]{3,2,1,0:T(8,128)(2,1)}), bf16[1,1,1024,512]{3,2,1,0:T(8,128)(2,1)}) %all-gather.59.cloned.1.call-update) | async-done | bytes 1048592 | tf_op jit(solution)/shard_map/all_gather | solution.py:98
  286.5 5.5 fusion.386
  292.0 44.7 %all-gather.61.cloned.1.call-done = bf16[1,1,1024,1024]{3,2,1,0:T(8,128)(2,1)} async-done(((bf16[1,1,128,1024]{3,2,1,0:T(8,128)(2,1)}), bf16[1,1,1024,1024]{3,2,1,0:T(8,128)(2,1)}) %all-gather.61.cloned.1.call-update) | async-done | bytes 2097168 | tf_op jit(solution)/shard_map/all_gather | solution.py:90
  342.9 34.6 %all-gather.63.cloned.1.call-done = bf16[1,1,1024,512]{3,2,1,0:T(8,128)(2,1)} async-done(((bf16[1,1,128,512]{3,2,1,0:T(8,128)(2,1)}), bf16[1,1,1024,512]{3,2,1,0:T(8,128)(2,1)}) %all-gather.63.cloned.1.call-update) | async-done | bytes 1048592 | tf_op jit(solution)/shard_map/all_gather | solution.py:98
  377.5 5.4 fusion.385
  382.9 44.8 %all-gather.65.cloned.1.call-done = bf16[1,1,1024,1024]{3,2,1,0:T(8,128)(2,1)} async-done(((bf16[1,1,128,1024]{3,2,1,0:T(8,128)(2,1)}), bf16[1,1,1024,1024]{3,2,1,0:T(8,128)(2,1)}) %all-gather.65.cloned.1.call-update) | async-done | bytes 2097168 | tf_op jit(solution)/shard_map/all_gather | solution.py:90
  433.5 34.8 %all-gather.67.cloned.1.call-done = bf16[1,1,1024,512]{3,2,1,0:T(8,128)(2,1)} async-done(((bf16[1,1,128,512]{3,2,1,0:T(8,128)(2,1)}), bf16[1,1,1024,512]{3,2,1,0:T(8,128)(2,1)}) %all-gather.67.cloned.1.call-update) | async-done | bytes 1048592 | tf_op jit(solution)/shard_map/all_gather | solution.py:98
  468.3 5.4 fusion.384
  473.8 44.8 %all-gather.69.cloned.1.call-done = bf16[1,1,1024,1024]{3,2,1,0:T(8,128)(2,1)} async-done(((bf16[1,1,128,1024]{3,2,1,0:T(8,128)(2,1)}), bf16[1,1,1024,1024]{3,2,1,0:T(8,128)(2,1)}) %all-gather.69.cloned.1.call-update) | async-done | bytes 2097168 | tf_op jit(solution)/shard_map/all_gather | solution.py:90
  524.3 34.9 %all-gather.71.cloned.1.call-done = bf16[1,1,1024,512]{3,2,1,0:T(8,128)(2,1)} async-done(((bf16[1,1,128,512]{3,2,1,0:T(8,128)(2,1)}), bf16[1,1,1024,512]{3,2,1,0:T(8,128)(2,1)}) %all-gather.71.cloned.1.call-update) | async-done | bytes 1048592 | tf_op jit(solution)/shard_map/all_gather | solution.py:98
  559.2 5.0 convert_add_fusion
  567.5 39.2 %psum.104 = f32[4,512]{1,0:T(4,128)S(1)} all-reduce(f32[4,512]{1,0:T(4,128)S(1)} %fusion.219), channel_id=1, replica_groups=mesh['dp'=4,'fsdp'=8] {'dp','fsdp'}, use_global_device_ids=true, to_apply=%region_18.19 | all-reduce | flops 2048 | bytes 16384 | tf_op jit(solution)/shard_map/psum | solution.py:47
  611.0 41.1 %psum.105 = f32[4,512]{1,0:T(4,128)S(1)} all-reduce(f32[4,512]{1,0:T(4,128)S(1)} %fusion.172), channel_id=1, replica_groups=mesh['dp'=4,'fsdp'=8] {'dp','fsdp'}, use_global_device_ids=true, to_apply=%region_19.20 | all-reduce | flops 2048 | bytes 16384 | tf_op jit(solution)/shard_map/psum | solution.py:50
  665.9 5.1 fusion.383
  671.0 30.3 all-gather.77.cloned.1.call-done
  708.3 33.7 %all-gather.79.cloned.1.call-done = bf16[1,1,1024,512]{3,2,1,0:T(8,128)(2,1)} async-done(((bf16[1,1,128,512]{3,2,1,0:T(8,128)(2,1)}), bf16[1,1,1024,512]{3,2,1,0:T(8,128)(2,1)}) %all-gather.79.cloned.1.call-update) | async-done | bytes 1048592 | tf_op jit(solution)/shard_map/all_gather | solution.py:98
  742.0 5.5 fusion.382
  747.4 44.6 %all-gather.81.cloned.1.call-done = bf16[1,1,1024,1024]{3,2,1,0:T(8,128)(2,1)} async-done(((bf16[1,1,128,1024]{3,2,1,0:T(8,128)(2,1)}), bf16[1,1,1024,1024]{3,2,1,0:T(8,128)(2,1)}) %all-gather.81.cloned.1.call-update) | async-done | bytes 2097168 | tf_op jit(solution)/shard_map/all_gather | solution.py:90
  799.2 33.4 %all-gather.83.cloned.1.call-done = bf16[1,1,1024,512]{3,2,1,0:T(8,128)(2,1)} async-done(((bf16[1,1,128,512]{3,2,1,0:T(8,128)(2,1)}), bf16[1,1,1024,512]{3,2,1,0:T(8,128)(2,1)}) %all-gather.83.cloned.1.call-update) | async-done | bytes 1048592 | tf_op jit(solution)/shard_map/all_gather | solution.py:98
  832.7 5.5 fusion.381
  838.2 44.7 %all-gather.85.cloned.1.call-done = bf16[1,1,1024,1024]{3,2,1,0:T(8,128)(2,1)} async-done(((bf16[1,1,128,1024]{3,2,1,0:T(8,128)(2,1)}), bf16[1,1,1024,1024]{3,2,1,0:T(8,128)(2,1)}) %all-gather.85.cloned.1.call-update) | async-done | bytes 2097168 | tf_op jit(solution)/shard_map/all_gather | solution.py:90
  890.5 33.0 %all-gather.87.cloned.1.call-done = bf16[1,1,1024,512]{3,2,1,0:T(8,128)(2,1)} async-done(((bf16[1,1,128,512]{3,2,1,0:T(8,128)(2,1)}), bf16[1,1,1024,512]{3,2,1,0:T(8,128)(2,1)}) %all-gather.87.cloned.1.call-update) | async-done | bytes 1048592 | tf_op jit(solution)/shard_map/all_gather | solution.py:98
  923.5 5.5 fusion.380
  929.0 44.7 %all-gather.89.cloned.1.call-done = bf16[1,1,1024,1024]{3,2,1,0:T(8,128)(2,1)} async-done(((bf16[1,1,128,1024]{3,2,1,0:T(8,128)(2,1)}), bf16[1,1,1024,1024]{3,2,1,0:T(8,128)(2,1)}) %all-gather.89.cloned.1.call-update) | async-done | bytes 2097168 | tf_op jit(solution)/shard_map/all_gather | solution.py:90
  980.8 33.7 %all-gather.91.cloned.1.call-done = bf16[1,1,1024,512]{3,2,1,0:T(8,128)(2,1)} async-done(((bf16[1,1,128,512]{3,2,1,0:T(8,128)(2,1)}), bf16[1,1,1024,512]{3,2,1,0:T(8,128)(2,1)}) %all-gather.91.cloned.1.call-update) | async-done | bytes 1048592 | tf_op jit(solution)/shard_map/all_gather | solution.py:98
  1014.5 5.4 fusion.379
  1019.9 44.8 %all-gather.93.cloned.1.call-done = bf16[1,1,1024,1024]{3,2,1,0:T(8,128)(2,1)} async-done(((bf16[1,1,128,1024]{3,2,1,0:T(8,128)(2,1)}), bf16[1,1,1024,1024]{3,2,1,0:T(8,128)(2,1)}) %all-gather.93.cloned.1.call-update) | async-done | bytes 2097168 | tf_op jit(solution)/shard_map/all_gather | solution.py:90
  1071.8 33.5 %all-gather.95.cloned.1.call-done = bf16[1,1,1024,512]{3,2,1,0:T(8,128)(2,1)} async-done(((bf16[1,1,128,512]{3,2,1,0:T(8,128)(2,1)}), bf16[1,1,1024,512]{3,2,1,0:T(8,128)(2,1)}) %all-gather.95.cloned.1.call-update) | async-done | bytes 1048592 | tf_op jit(solution)/shard_map/all_gather | solution.py:98
  1105.4 6.5 multiply_convert_fusion.34
  1170.6 5.5 fusion.90
  1177.9 38.7 %all-reduce.1 = (f32[4,512]{1,0:T(4,128)S(1)}, f32[4,512]{1,0:T(4,128)S(1)}) all-reduce(f32[4,512]{1,0:T(4,128)S(1)} %fusion.228, f32[4,512]{1,0:T(4,128)S(1)} %fusion.170), channel_id=1, replica_groups=mesh['dp'=4,'fsdp'=8] {'dp','fsdp'}, use_global_device_ids=true, to_apply=%region_30.31 | all-reduce | flops 4096 | bytes 32768 | tf_op jit(solution)/shard_map/psum | solution.py:165
  1404.9 9.7 fusion.84
  1422.6 42.5 %reduce-scatter.65.cloned.1.call-done = bf16[128,512]{1,0:T(8,128)(2,1)} async-done(((bf16[1024,512]{1,0:T(8,128)(2,1)}), bf16[128,512]{1,0:T(8,128)(2,1)}) %reduce-scatter.65.cloned.1.call-update) | async-done | bytes 131088 | tf_op jit(solution)/shard_map/reduce_scatter | solution.py:125
  1466.7 64.4 %reduce-scatter.67.cloned.1.call-done = bf16[128,512]{1,0:T(8,128)(2,1)} async-done(((bf16[1024,512]{1,0:T(8,128)(2,1)}), bf16[128,512]{1,0:T(8,128)(2,1)}) %reduce-scatter.67.cloned.1.call-update) | async-done | bytes 131088 | tf_op jit(solution)/shard_map/reduce_scatter | solution.py:125
  1532.6 64.6 %reduce-scatter.69.cloned.1.call-done = bf16[128,512]{1,0:T(8,128)(2,1)} async-done(((bf16[1024,512]{1,0:T(8,128)(2,1)}), bf16[128,512]{1,0:T(8,128)(2,1)}) %reduce-scatter.69.cloned.1.call-update) | async-done | bytes 131088 | tf_op jit(solution)/shard_map/reduce_scatter | solution.py:125
  1598.8 64.3 %reduce-scatter.71.cloned.1.call-done = bf16[128,512]{1,0:T(8,128)(2,1)} async-done(((bf16[1024,512]{1,0:T(8,128)(2,1)}), bf16[128,512]{1,0:T(8,128)(2,1)}) %reduce-scatter.71.cloned.1.call-update) | async-done | bytes 131088 | tf_op jit(solution)/shard_map/reduce_scatter | solution.py:125
  1664.7 64.8 %reduce-scatter.51.cloned.1.call-done = bf16[128,512]{1,0:T(8,128)(2,1)} async-done(((bf16[1024,512]{1,0:T(8,128)(2,1)}), bf16[128,512]{1,0:T(8,128)(2,1)}) %reduce-scatter.51.cloned.1.call-update) | async-done | bytes 131088 | tf_op jit(solution)/shard_map/reduce_scatter | solution.py:125
  1731.0 64.2 %reduce-scatter.53.cloned.1.call-done = bf16[128,512]{1,0:T(8,128)(2,1)} async-done(((bf16[1024,512]{1,0:T(8,128)(2,1)}), bf16[128,512]{1,0:T(8,128)(2,1)}) %reduce-scatter.53.cloned.1.call-update) | async-done | bytes 131088 | tf_op jit(solution)/shard_map/reduce_scatter | solution.py:125
  1796.8 64.8 %reduce-scatter.55.cloned.1.call-done = bf16[128,512]{1,0:T(8,128)(2,1)} async-done(((bf16[1024,512]{1,0:T(8,128)(2,1)}), bf16[128,512]{1,0:T(8,128)(2,1)}) %reduce-scatter.55.cloned.1.call-update) | async-done | bytes 131088 | tf_op jit(solution)/shard_map/reduce_scatter | solution.py:125
  1863.1 64.2 %reduce-scatter.57.cloned.1.call-done = bf16[128,512]{1,0:T(8,128)(2,1)} async-done(((bf16[1024,512]{1,0:T(8,128)(2,1)}), bf16[128,512]{1,0:T(8,128)(2,1)}) %reduce-scatter.57.cloned.1.call-update) | async-done | bytes 131088 | tf_op jit(solution)/shard_map/reduce_scatter | solution.py:125
  1928.9 64.7 %reduce-scatter.59.cloned.1.call-done = bf16[128,512]{1,0:T(8,128)(2,1)} async-done(((bf16[1024,512]{1,0:T(8,128)(2,1)}), bf16[128,512]{1,0:T(8,128)(2,1)}) %reduce-scatter.59.cloned.1.call-update) | async-done | bytes 131088 | tf_op jit(solution)/shard_map/reduce_scatter | solution.py:125
  1997.8 65.8 %reduce-scatter.37.cloned.1.call-done = bf16[128,1024]{1,0:T(8,128)(2,1)} async-done(((bf16[1024,1024]{1,0:T(8,128)(2,1)}), bf16[128,1024]{1,0:T(8,128)(2,1)}) %reduce-scatter.37.cloned.1.call-update) | async-done | bytes 262160 | tf_op jit(solution)/shard_map/reduce_scatter | solution.py:143
  2065.3 68.4 %reduce-scatter.25.cloned.1.call-done = bf16[128,1024]{1,0:T(8,128)(2,1)} async-done(((bf16[1024,1024]{1,0:T(8,128)(2,1)}), bf16[128,1024]{1,0:T(8,128)(2,1)}) %reduce-scatter.25.cloned.1.call-update) | async-done | bytes 262160 | tf_op jit(solution)/shard_map/reduce_scatter | solution.py:143
  2135.4 68.4 %reduce-scatter.39.cloned.1.call-done = bf16[128,1024]{1,0:T(8,128)(2,1)} async-done(((bf16[1024,1024]{1,0:T(8,128)(2,1)}), bf16[128,1024]{1,0:T(8,128)(2,1)}) %reduce-scatter.39.cloned.1.call-update) | async-done | bytes 262160 | tf_op jit(solution)/shard_map/reduce_scatter | solution.py:143
  2205.4 68.5 %reduce-scatter.41.cloned.1.call-done = bf16[128,1024]{1,0:T(8,128)(2,1)} async-done(((bf16[1024,1024]{1,0:T(8,128)(2,1)}), bf16[128,1024]{1,0:T(8,128)(2,1)}) %reduce-scatter.41.cloned.1.call-update) | async-done | bytes 262160 | tf_op jit(solution)/shard_map/reduce_scatter | solution.py:143
  2275.6 68.6 %reduce-scatter.43.cloned.1.call-done = bf16[128,1024]{1,0:T(8,128)(2,1)} async-done(((bf16[1024,1024]{1,0:T(8,128)(2,1)}), bf16[128,1024]{1,0:T(8,128)(2,1)}) %reduce-scatter.43.cloned.1.call-update) | async-done | bytes 262160 | tf_op jit(solution)/shard_map/reduce_scatter | solution.py:143
  2345.8 68.7 %reduce-scatter.45.cloned.1.call-done = bf16[128,1024]{1,0:T(8,128)(2,1)} async-done(((bf16[1024,1024]{1,0:T(8,128)(2,1)}), bf16[128,1024]{1,0:T(8,128)(2,1)}) %reduce-scatter.45.cloned.1.call-update) | async-done | bytes 262160 | tf_op jit(solution)/shard_map/reduce_scatter | solution.py:143
  2416.2 68.2 %reduce-scatter.47.cloned.1.call-done = bf16[128,1024]{1,0:T(8,128)(2,1)} async-done(((bf16[1024,1024]{1,0:T(8,128)(2,1)}), bf16[128,1024]{1,0:T(8,128)(2,1)}) %reduce-scatter.47.cloned.1.call-update) | async-done | bytes 262160 | tf_op jit(solution)/shard_map/reduce_scatter | solution.py:143
  2486.0 68.6 %reduce-scatter.27.cloned.1.call-done = bf16[128,1024]{1,0:T(8,128)(2,1)} async-done(((bf16[1024,1024]{1,0:T(8,128)(2,1)}), bf16[128,1024]{1,0:T(8,128)(2,1)}) %reduce-scatter.27.cloned.1.call-update) | async-done | bytes 262160 | tf_op jit(solution)/shard_map/reduce_scatter | solution.py:143
  2556.3 68.4 %reduce-scatter.29.cloned.1.call-done = bf16[128,1024]{1,0:T(8,128)(2,1)} async-done(((bf16[1024,1024]{1,0:T(8,128)(2,1)}), bf16[128,1024]{1,0:T(8,128)(2,1)}) %reduce-scatter.29.cloned.1.call-update) | async-done | bytes 262160 | tf_op jit(solution)/shard_map/reduce_scatter | solution.py:143
  2626.4 68.4 %reduce-scatter.31.cloned.1.call-done = bf16[128,1024]{1,0:T(8,128)(2,1)} async-done(((bf16[1024,1024]{1,0:T(8,128)(2,1)}), bf16[128,1024]{1,0:T(8,128)(2,1)}) %reduce-scatter.31.cloned.1.call-update) | async-done | bytes 262160 | tf_op jit(solution)/shard_map/reduce_scatter | solution.py:143
  2696.4 68.2 %reduce-scatter.33.cloned.1.call-done = bf16[128,1024]{1,0:T(8,128)(2,1)} async-done(((bf16[1024,1024]{1,0:T(8,128)(2,1)}), bf16[128,1024]{1,0:T(8,128)(2,1)}) %reduce-scatter.33.cloned.1.call-update) | async-done | bytes 262160 | tf_op jit(solution)/shard_map/reduce_scatter | solution.py:143
  2766.3 68.4 %reduce-scatter.35.cloned.1.call-done = bf16[128,1024]{1,0:T(8,128)(2,1)} async-done(((bf16[1024,1024]{1,0:T(8,128)(2,1)}), bf16[128,1024]{1,0:T(8,128)(2,1)}) %reduce-scatter.35.cloned.1.call-update) | async-done | bytes 262160 | tf_op jit(solution)/shard_map/reduce_scatter | solution.py:143
  2843.7 120.2 %all-reduce.7.cloned.1.call-done = (f32[4,512]{1,0:T(4,128)}, f32[4,512]{1,0:T(4,128)}, f32[2,6,512]{2,1,0:T(8,128)}, f32[2,6,1024]{2,1,0:T(8,128)}, f32[2,6,512]{2,1,0:T(8,128)}) async-done(((f32[4,512]{1,0:T(4,128)}, f32[4,512]{1,0:T(4,128)}, f32[2,6,512]{2,1,0:T(8,128)}, f32[2,6,1024]{2,1,0:T(8,128)}, f32[2,6,512]{2,1,0:T(8,128)}), (f32[4,512]{1,0:T(4,128)}, f32[4,512]{1,0:T(4,128)}, ...) | async-done | bytes 114704 | tf_op jit(solution)/shard_map/psum | solution.py:165
  2981.3 83.0 %all-reduce.9.cloned.1.call-done = (bf16[2,6,128,1024]{3,2,1,0:T(8,128)(2,1)}, bf16[2,6,128,512]{3,2,1,0:T(8,128)(2,1)}) async-done(((bf16[2,6,128,1024]{3,2,1,0:T(8,128)(2,1)}, bf16[2,6,128,512]{3,2,1,0:T(8,128)(2,1)}), (bf16[2,6,128,1024]{3,2,1,0:T(8,128)(2,1)}, bf16[2,6,128,512]{3,2,1,0:T(8,128)(2,1)})) %all-reduce.9.cloned.1.call-update) | async-done | bytes 4718608 | tf_op jit(solution)/shard_map/psum | solution.py:187
  3064.3 5.5 convert_element_type.317
  (796 shorter events, 461.6 us)
Async XLA Ops:
  7.2 146.5 %all-gather.49.cloned.1.call-start = ((), (), s32[]{:S(2)}) async-start(), calls=%async_computation.48 | async-start | bytes 2359296 | tf_op jit(solution)/shard_map/all_gather | solution.py:90
  10.9 150.0 %all-gather.51.cloned.1.call-start = ((), (), s32[]{:S(2)}) async-start(), calls=%async_computation.49 | async-start | bytes 1179648 | tf_op jit(solution)/shard_map/all_gather | solution.py:98
  12.1 154.2 %all-gather.53.cloned.1.call-start = ((), (), s32[]{:S(2)}) async-start(), calls=%async_computation.50 | async-start | bytes 2359296 | tf_op jit(solution)/shard_map/all_gather | solution.py:90
  12.8 183.0 %all-gather.55.cloned.1.call-start = ((), (), s32[]{:S(2)}) async-start(), calls=%async_computation.51 | async-start | bytes 1179648 | tf_op jit(solution)/shard_map/all_gather | solution.py:98
  13.4 232.4 %all-gather.57.cloned.1.call-start = ((), (), s32[]{:S(2)}) async-start(), calls=%async_computation.52 | async-start | bytes 2359296 | tf_op jit(solution)/shard_map/all_gather | solution.py:90
  14.0 272.5 %all-gather.59.cloned.1.call-start = ((), (), s32[]{:S(2)}) async-start(), calls=%async_computation.53 | async-start | bytes 1179648 | tf_op jit(solution)/shard_map/all_gather | solution.py:98
  14.6 322.1 %all-gather.61.cloned.1.call-start = ((), (), s32[]{:S(2)}) async-start(), calls=%async_computation.54 | async-start | bytes 2359296 | tf_op jit(solution)/shard_map/all_gather | solution.py:90
  15.3 362.2 %all-gather.63.cloned.1.call-start = ((), (), s32[]{:S(2)}) async-start(), calls=%async_computation.55 | async-start | bytes 1179648 | tf_op jit(solution)/shard_map/all_gather | solution.py:98
  16.1 411.6 %all-gather.65.cloned.1.call-start = ((), (), s32[]{:S(2)}) async-start(), calls=%async_computation.56 | async-start | bytes 2359296 | tf_op jit(solution)/shard_map/all_gather | solution.py:90
  16.8 451.5 %all-gather.67.cloned.1.call-start = ((), (), s32[]{:S(2)}) async-start(), calls=%async_computation.57 | async-start | bytes 1179648 | tf_op jit(solution)/shard_map/all_gather | solution.py:98
  17.4 501.1 %all-gather.69.cloned.1.call-start = ((), (), s32[]{:S(2)}) async-start(), calls=%async_computation.58 | async-start | bytes 2359296 | tf_op jit(solution)/shard_map/all_gather | solution.py:90
  18.1 541.1 %all-gather.71.cloned.1.call-start = ((), (), s32[]{:S(2)}) async-start(), calls=%async_computation.59 | async-start | bytes 1179648 | tf_op jit(solution)/shard_map/all_gather | solution.py:98
  18.7 639.3 %all-gather.73.cloned.1.call-start = ((), (), s32[]{:S(2)}) async-start(), calls=%async_computation.60 | async-start | bytes 2359296 | tf_op jit(solution)/shard_map/all_gather | solution.py:90
  19.4 646.5 %all-gather.75.cloned.1.call-start = ((), (), s32[]{:S(2)}) async-start(), calls=%async_computation.61 | async-start | bytes 1179648 | tf_op jit(solution)/shard_map/all_gather | solution.py:98
  20.0 681.3 %all-gather.77.cloned.1.call-start = ((), (), s32[]{:S(2)}) async-start(), calls=%async_computation.62 | async-start | bytes 2359296 | tf_op jit(solution)/shard_map/all_gather | solution.py:90
  20.6 721.3 %all-gather.79.cloned.1.call-start = ((), (), s32[]{:S(2)}) async-start(), calls=%async_computation.63 | async-start | bytes 1179648 | tf_op jit(solution)/shard_map/all_gather | solution.py:98
  21.2 770.8 %all-gather.81.cloned.1.call-start = ((), (), s32[]{:S(2)}) async-start(), calls=%async_computation.64 | async-start | bytes 2359296 | tf_op jit(solution)/shard_map/all_gather | solution.py:90
  21.8 810.9 %all-gather.83.cloned.1.call-start = ((), (), s32[]{:S(2)}) async-start(), calls=%async_computation.65 | async-start | bytes 1179648 | tf_op jit(solution)/shard_map/all_gather | solution.py:98
  22.4 860.5 %all-gather.85.cloned.1.call-start = ((), (), s32[]{:S(2)}) async-start(), calls=%async_computation.66 | async-start | bytes 2359296 | tf_op jit(solution)/shard_map/all_gather | solution.py:90
  23.1 900.4 %all-gather.87.cloned.1.call-start = ((), (), s32[]{:S(2)}) async-start(), calls=%async_computation.67 | async-start | bytes 1179648 | tf_op jit(solution)/shard_map/all_gather | solution.py:98
  23.7 950.0 %all-gather.89.cloned.1.call-start = ((), (), s32[]{:S(2)}) async-start(), calls=%async_computation.68 | async-start | bytes 2359296 | tf_op jit(solution)/shard_map/all_gather | solution.py:90
  24.4 990.1 %all-gather.91.cloned.1.call-start = ((), (), s32[]{:S(2)}) async-start(), calls=%async_computation.69 | async-start | bytes 1179648 | tf_op jit(solution)/shard_map/all_gather | solution.py:98
  25.2 1039.5 %all-gather.93.cloned.1.call-start = ((), (), s32[]{:S(2)}) async-start(), calls=%async_computation.70 | async-start | bytes 2359296 | tf_op jit(solution)/shard_map/all_gather | solution.py:90
  25.9 1079.4 %all-gather.95.cloned.1.call-start = ((), (), s32[]{:S(2)}) async-start(), calls=%async_computation.71 | async-start | bytes 1179648 | tf_op jit(solution)/shard_map/all_gather | solution.py:98
  26.5 1391.4 %reduce-scatter.61.cloned.1.call-start = ((), (), s32[]{:S(2)}) async-start(), calls=%async_computation.42 | async-start | bytes 1179648 | tf_op jit(solution)/shard_map/reduce_scatter | solution.py:125
  29.4 75.6 %copy-start.125 = (bf16[768,512]{0,1:T(8,128)(2,1)}, bf16[768,512]{0,1:T(8,128)(2,1)S(1)}, u32[]{:S(2)}) copy-start(bf16[768,512]{0,1:T(8,128)(2,1)S(1)} %copy.241) | copy-start | bytes 2359300
  29.4 131.5 %copy-start.185 = (f32[1,512]{1,0:T(1,128)}, f32[1,512]{1,0:T(1,128)S(1)}, u32[]{:S(2)}) copy-start(f32[1,512]{1,0:T(1,128)S(1)} %get-tuple-element.259) | copy-start | bytes 6148
  30.1 130.8 %copy-start.187 = (f32[1,512]{1,0:T(1,128)}, f32[1,512]{1,0:T(1,128)S(1)}, u32[]{:S(2)}) copy-start(f32[1,512]{1,0:T(1,128)S(1)} %get-tuple-element.261) | copy-start | bytes 6148
  36.3 115.0 %copy-start.198 = (f32[512]{0:T(512)}, f32[512]{0:T(512)S(1)}, u32[]{:S(2)}) copy-start(f32[512]{0:T(512)S(1)} %divide_multiply_fusion.8) | copy-start | bytes 6148
  37.0 114.4 %copy-start.200 = (f32[512]{0:T(512)}, f32[512]{0:T(512)S(1)}, u32[]{:S(2)}) copy-start(f32[512]{0:T(512)S(1)} %divide_multiply_fusion.9) | copy-start | bytes 6148
  44.7 106.7 %copy-start.202 = (f32[512]{0:T(512)}, f32[512]{0:T(512)S(1)}, u32[]{:S(2)}) copy-start(f32[512]{0:T(512)S(1)} %divide_multiply_fusion.6) | copy-start | bytes 6148
  45.4 106.0 %copy-start.204 = (f32[512]{0:T(512)}, f32[512]{0:T(512)S(1)}, u32[]{:S(2)}) copy-start(f32[512]{0:T(512)S(1)} %divide_multiply_fusion.7) | copy-start | bytes 6148
  59.0 92.4 %copy-start.206 = (f32[512]{0:T(512)}, f32[512]{0:T(512)S(1)}, u32[]{:S(2)}) copy-start(f32[512]{0:T(512)S(1)} %divide_multiply_fusion.10) | copy-start | bytes 6148
  59.7 88.5 %copy-start.208 = (f32[512]{0:T(512)}, f32[512]{0:T(512)S(1)}, u32[]{:S(2)}) copy-start(f32[512]{0:T(512)S(1)} %divide_multiply_fusion.11) | copy-start | bytes 6148
  249.9 36.6 %copy-start.25 = (f32[768,1024]{0,1:T(8,128)}, f32[768,1024]{0,1:T(8,128)S(1)}, u32[]{:S(2)}) copy-start(f32[768,1024]{0,1:T(8,128)S(1)} %fusion.54) | copy-start | bytes 9437188
  341.1 36.3 %copy-start.27 = (f32[768,1024]{0,1:T(8,128)}, f32[768,1024]{0,1:T(8,128)S(1)}, u32[]{:S(2)}) copy-start(f32[768,1024]{0,1:T(8,128)S(1)} %fusion.57) | copy-start | bytes 9437188
  431.7 36.6 %copy-start.29 = (f32[768,1024]{0,1:T(8,128)}, f32[768,1024]{0,1:T(8,128)S(1)}, u32[]{:S(2)}) copy-start(f32[768,1024]{0,1:T(8,128)S(1)} %fusion.60) | copy-start | bytes 9437188
  522.6 36.6 %copy-start.40 = (f32[768,1024]{0,1:T(8,128)}, f32[768,1024]{0,1:T(8,128)S(1)}, u32[]{:S(2)}) copy-start(f32[768,1024]{0,1:T(8,128)S(1)} %fusion.63) | copy-start | bytes 9437188
  671.0 70.9 %copy-start.88 = (f32[768,512]{0,1:T(8,128)}, f32[768,512]{0,1:T(8,128)S(1)}, u32[]{:S(2)}) copy-start(f32[768,512]{0,1:T(8,128)S(1)} %get-tuple-element.134) | copy-start | bytes 4718596
  1177.8 241.7 %reduce-scatter.49.cloned.1.call-start = ((), (), s32[]{:S(2)}) async-start(), calls=%async_computation.36 | async-start | bytes 1179648 | tf_op jit(solution)/shard_map/reduce_scatter | solution.py:125
  1269.5 151.6 %reduce-scatter.63.cloned.1.call-start = ((), (), s32[]{:S(2)}) async-start(), calls=%async_computation.43 | async-start | bytes 1179648 | tf_op jit(solution)/shard_map/reduce_scatter | solution.py:125
  1273.0 192.1 %reduce-scatter.65.cloned.1.call-start = ((), (), s32[]{:S(2)}) async-start(), calls=%async_computation.44 | async-start | bytes 1179648 | tf_op jit(solution)/shard_map/reduce_scatter | solution.py:125
  1276.5 254.5 %reduce-scatter.67.cloned.1.call-start = ((), (), s32[]{:S(2)}) async-start(), calls=%async_computation.45 | async-start | bytes 1179648 | tf_op jit(solution)/shard_map/reduce_scatter | solution.py:125
  1280.0 317.2 %reduce-scatter.69.cloned.1.call-start = ((), (), s32[]{:S(2)}) async-start(), calls=%async_computation.46 | async-start | bytes 1179648 | tf_op jit(solution)/shard_map/reduce_scatter | solution.py:125
  1283.6 379.5 %reduce-scatter.71.cloned.1.call-start = ((), (), s32[]{:S(2)}) async-start(), calls=%async_computation.47 | async-start | bytes 1179648 | tf_op jit(solution)/shard_map/reduce_scatter | solution.py:125
  1287.1 442.3 %reduce-scatter.51.cloned.1.call-start = ((), (), s32[]{:S(2)}) async-start(), calls=%async_computation.37 | async-start | bytes 1179648 | tf_op jit(solution)/shard_map/reduce_scatter | solution.py:125
  1290.6 504.6 %reduce-scatter.53.cloned.1.call-start = ((), (), s32[]{:S(2)}) async-start(), calls=%async_computation.38 | async-start | bytes 1179648 | tf_op jit(solution)/shard_map/reduce_scatter | solution.py:125
  1294.2 567.4 %reduce-scatter.55.cloned.1.call-start = ((), (), s32[]{:S(2)}) async-start(), calls=%async_computation.39 | async-start | bytes 1179648 | tf_op jit(solution)/shard_map/reduce_scatter | solution.py:125
  1297.7 629.6 %reduce-scatter.57.cloned.1.call-start = ((), (), s32[]{:S(2)}) async-start(), calls=%async_computation.40 | async-start | bytes 1179648 | tf_op jit(solution)/shard_map/reduce_scatter | solution.py:125
  1301.3 692.3 %reduce-scatter.59.cloned.1.call-start = ((), (), s32[]{:S(2)}) async-start(), calls=%async_computation.41 | async-start | bytes 1179648 | tf_op jit(solution)/shard_map/reduce_scatter | solution.py:125
  1304.8 758.8 %reduce-scatter.37.cloned.1.call-start = ((), (), s32[]{:S(2)}) async-start(), calls=%async_computation.30 | async-start | bytes 2359296 | tf_op jit(solution)/shard_map/reduce_scatter | solution.py:143
  1309.7 824.0 %reduce-scatter.25.cloned.1.call-start = ((), (), s32[]{:S(2)}) async-start(), calls=%async_computation.24 | async-start | bytes 2359296 | tf_op jit(solution)/shard_map/reduce_scatter | solution.py:143
  1319.8 883.9 %reduce-scatter.39.cloned.1.call-start = ((), (), s32[]{:S(2)}) async-start(), calls=%async_computation.31 | async-start | bytes 2359296 | tf_op jit(solution)/shard_map/reduce_scatter | solution.py:143
  1325.3 948.6 %reduce-scatter.41.cloned.1.call-start = ((), (), s32[]{:S(2)}) async-start(), calls=%async_computation.32 | async-start | bytes 2359296 | tf_op jit(solution)/shard_map/reduce_scatter | solution.py:143
  1330.4 1013.8 %reduce-scatter.43.cloned.1.call-start = ((), (), s32[]{:S(2)}) async-start(), calls=%async_computation.33 | async-start | bytes 2359296 | tf_op jit(solution)/shard_map/reduce_scatter | solution.py:143
  1335.5 1079.0 %reduce-scatter.45.cloned.1.call-start = ((), (), s32[]{:S(2)}) async-start(), calls=%async_computation.34 | async-start | bytes 2359296 | tf_op jit(solution)/shard_map/reduce_scatter | solution.py:143
  1340.5 1143.8 %reduce-scatter.47.cloned.1.call-start = ((), (), s32[]{:S(2)}) async-start(), calls=%async_computation.35 | async-start | bytes 2359296 | tf_op jit(solution)/shard_map/reduce_scatter | solution.py:143
  1345.6 1209.0 %reduce-scatter.27.cloned.1.call-start = ((), (), s32[]{:S(2)}) async-start(), calls=%async_computation.25 | async-start | bytes 2359296 | tf_op jit(solution)/shard_map/reduce_scatter | solution.py:143
  1350.7 1274.0 %reduce-scatter.29.cloned.1.call-start = ((), (), s32[]{:S(2)}) async-start(), calls=%async_computation.26 | async-start | bytes 2359296 | tf_op jit(solution)/shard_map/reduce_scatter | solution.py:143
  1355.8 1338.9 %reduce-scatter.31.cloned.1.call-start = ((), (), s32[]{:S(2)}) async-start(), calls=%async_computation.27 | async-start | bytes 2359296 | tf_op jit(solution)/shard_map/reduce_scatter | solution.py:143
  1360.9 1403.7 %reduce-scatter.33.cloned.1.call-start = ((), (), s32[]{:S(2)}) async-start(), calls=%async_computation.28 | async-start | bytes 2359296 | tf_op jit(solution)/shard_map/reduce_scatter | solution.py:143
  1366.0 1468.7 %reduce-scatter.35.cloned.1.call-start = ((), (), s32[]{:S(2)}) async-start(), calls=%async_computation.29 | async-start | bytes 2359296 | tf_op jit(solution)/shard_map/reduce_scatter | solution.py:143
  1393.1 1570.8 %all-reduce.7.cloned.1.call-start = ((), (), s32[]{:S(2)}) async-start(), calls=%async_computation.72 | async-start | bytes 294912 | tf_op jit(solution)/shard_map/psum | solution.py:165
  1417.6 1646.6 %all-reduce.9.cloned.1.call-start = ((), (), s32[]{:S(2)}) async-start(), calls=%async_computation.73 | async-start | bytes 9437184 | tf_op jit(solution)/shard_map/psum | solution.py:187
  (217 other events, 941.3 us)
Sparse Core Ops, SparseCore 0:
  11.0 52.1 all-gather.48
  65.3 38.6 all-gather.50
  106.1 48.1 all-gather.52
  156.3 39.4 all-gather.54
  197.8 48.0 all-gather.56
  247.8 38.6 all-gather.58
  288.6 48.0 all-gather.60
  338.8 38.6 all-gather.62
  379.6 48.0 all-gather.64
  429.7 38.6 all-gather.66
  470.5 48.0 all-gather.68
  520.5 38.6 all-gather.70
  561.9 47.8 all-gather.72
  611.8 39.2 all-gather.74
  653.1 48.2 all-gather.76
  703.3 38.6 all-gather.78
  743.9 48.0 all-gather.80
  794.0 38.6 all-gather.82
  834.8 48.0 all-gather.84
  884.8 38.6 all-gather.86
  925.6 48.0 all-gather.88
  975.8 38.6 all-gather.90
  1016.6 48.0 all-gather.92
  1066.7 38.6 all-gather.94
  1177.9 62.1 reduce-scatter.60
  1269.6 63.6 reduce-scatter.48
  1336.5 62.3 reduce-scatter.62
  1402.7 62.3 reduce-scatter.64
  1468.5 62.4 reduce-scatter.66
  1534.7 62.4 reduce-scatter.68
  1600.6 62.4 reduce-scatter.70
  1666.9 62.5 reduce-scatter.50
  1732.7 62.4 reduce-scatter.52
  1799.0 62.5 reduce-scatter.54
  1865.0 62.2 reduce-scatter.56
  1930.9 62.5 reduce-scatter.58
  1996.9 66.6 reduce-scatter.36
  2067.1 66.4 reduce-scatter.24
  2137.1 66.6 reduce-scatter.38
  2207.3 66.5 reduce-scatter.40
  2277.4 66.6 reduce-scatter.42
  2347.7 66.7 reduce-scatter.44
  2417.9 66.4 reduce-scatter.46
  2487.9 66.7 reduce-scatter.26
  2558.0 66.6 reduce-scatter.28
  2628.1 66.6 reduce-scatter.30
  2698.1 66.4 reduce-scatter.32
  2768.0 66.6 reduce-scatter.34
  2842.1 121.6 all-reduce.6
  2966.9 97.2 all-reduce.8
where the time goes:
time: 3090 us; the launch traced here: 3080 us
  waiting for transfers between devices  2310 us (75%)
  matrix products  284 us (9%)
  blocking collectives  203 us (7%)
  other arithmetic  151 us (5%)
  local copies, waits for them, and re-layouts  109 us (4%)
    reduce_scatter x12, waiting for transfers between devices, local(): lax.psum_scatter(weight_rows(first_in, grad_gates).astype(jnp.bfloat16),...  818 us
    reduce_scatter x12, waiting for transfers between devices, local(): lax.psum_scatter(weight_rows(second_in, grad_raw).astype(jnp.bfloat16), '...  558 us
    all_gather x12, waiting for transfers between devices, local(): lax.all_gather(gate_in[layer_no, section_no], 'fsdp', axis=0, tiled=True)  388 us
    all_gather x12, waiting for transfers between devices, local(): lax.all_gather(gate_out[layer_no, section_no], 'fsdp', axis=0, tiled=True)  330 us
    psum x1, waiting for transfers between devices, local(): lax.psum((pool_rows(onehot, grad_normed), pool_rows(onehot, grad_normed *...  120 us
    dot_general x24, matrix products, add_rows(): return jnp.dot(operand, shard_rows, preferred_element_type=jnp.float32)  115 us
    unnamed x489, local copies, waits for them, and re-layouts  95.6 us
    dot_general x24, matrix products, weight_rows(): lax.dot_general(operand, grad_rows, (((0,), (0,)), ((), ())), preferred_e...  94.6 us
  transfers between devices with their start and end apart: 50, of which 42 were waited for; matrix products, arithmetic and copies ran while one was open for 14% of the time, Pallas kernels for 0%

commit v1 on v0

v1 whole, which is shorter than its diff:
```python
import functools

import jax
import jax.numpy as jnp
from jax import lax
from jax.experimental import pallas as pl
from jax.experimental.pallas import tpu as pltpu
from jax.sharding import PartitionSpec as P

SECTIONS = 6
LAYERS = 2
MB = 4
BF16 = jnp.bfloat16
F32 = jnp.float32
EPSILON = 1e-05
TILE = 256
VMEM_LIMIT = 60 * 1024 * 1024
GROUPS = (((0, 1), (1, 3), (3, 6)), ((0, 3), (3, 5), (5, 6)))


def gate(x):
    return 0.5 * jnp.tanh(0.5 * x) + 0.5


def load_weights(table, arrays, wbuf, sems, n, pr):
    for part, lo, hi in ((0, 0, 1), (1, 1, n)):
        if lo == hi:
            continue
        at = 0
        for array in arrays:
            for slot in range(array.shape[0]):
                row = pl.multiple_of(table[at], pr)
                pltpu.make_async_copy(
                    array.at[slot, pl.ds(lo, hi - lo)],
                    wbuf.at[pl.ds(lo, hi - lo), pl.ds(row, pr)],
                    sems.at[part],
                ).start()
                at += 1


def wait_weights(wbuf, sems, n, part):
    lo, hi = (0, 1) if part == 0 else (1, n)
    whole = wbuf.at[pl.ds(lo, hi - lo)]
    pltpu.make_async_copy(whole, whole, sems.at[part]).wait()


def forward_kernel(n, n_arrays, pr, tile, table, *refs):
    hidden_in, normed, mask, bias_in, bias_out = refs[:5]
    arrays = refs[5 : 5 + n_arrays]
    hidden_out, s_hidden, s_update, s_reset, s_cand = refs[5 + n_arrays : 10 + n_arrays]
    wbuf, hid, sems = refs[10 + n_arrays :]
    step = pl.program_id(0)
    rows, cols = hid.shape

    @pl.when(step == 0)
    def _():
        load_weights(table, arrays, wbuf, sems, n, pr)
        hid[...] = hidden_in[...]
        wait_weights(wbuf, sems, n, 0)

    if n > 1:
        @pl.when(step == 1)
        def _():
            wait_weights(wbuf, sems, n, 1)

    w = wbuf.at[step]
    mask_row = mask[0]
    b_in = bias_in[0]
    b_out = bias_out[0]

    def body(t, _):
        at = pl.ds(pl.multiple_of(t * tile, tile), tile)
        h = hid[at, :]
        x = normed[at, :]
        first_in = jnp.concatenate([(mask_row * x).astype(BF16), h.astype(BF16)], axis=1)
        pre = jnp.dot(first_in, w[:, : 2 * cols], preferred_element_type=F32) + b_in
        update = gate(pre[:, :cols])
        reset = gate(pre[:, cols:])
        second_in = jnp.concatenate([(reset * h).astype(BF16), x.astype(BF16)], axis=1)
        raw = jnp.dot(second_in, w[:, 2 * cols :], preferred_element_type=F32) + b_out
        cand = jnp.tanh(raw)
        s_hidden[0, at, :] = h.astype(s_hidden.dtype)
        s_update[0, at, :] = update.astype(s_update.dtype)
        s_reset[0, at, :] = reset.astype(s_reset.dtype)
        s_cand[0, at, :] = cand.astype(s_cand.dtype)
        hid[at, :] = h + update * (cand - h)
        return 0

    lax.fori_loop(0, rows // tile, body, 0)

    @pl.when(step == n - 1)
    def _():
        hidden_out[...] = hid[...]


def forward_chunk(table, hidden, normed, masks, bias_in, bias_out, arrays, tile=256, sdt=F32):
    n = masks.shape[0]
    rows, cols = hidden.shape
    pr = arrays[0].shape[2]
    depth = 2 * cols
    whole = pl.BlockSpec((rows, cols), lambda i, *_: (0, 0))
    row = lambda width: pl.BlockSpec((1, 1, width), lambda i, *_: (i, 0, 0))
    per = pl.BlockSpec((1, rows, cols), lambda i, *_: (i, 0, 0))
    saved = jax.ShapeDtypeStruct((n, rows, cols), sdt)
    return pl.pallas_call(
        functools.partial(forward_kernel, n, len(arrays), pr, tile),
        grid_spec=pltpu.PrefetchScalarGridSpec(
            num_scalar_prefetch=1,
            grid=(n,),
            in_specs=[whole, whole, row(cols), row(2 * cols), row(cols)] + [pl.BlockSpec(memory_space=pl.ANY)] * len(arrays),
            out_specs=[whole, per, per, per, per],
            scratch_shapes=[
                pltpu.VMEM((n, depth, 3 * cols), BF16),
                pltpu.VMEM((rows, cols), F32),
                pltpu.SemaphoreType.DMA((2,)),
            ],
        ),
        out_shape=[jax.ShapeDtypeStruct((rows, cols), F32)] + [saved] * 4,
        compiler_params=pltpu.CompilerParams(vmem_limit_bytes=VMEM_LIMIT),
        cost_estimate=pl.CostEstimate(
            flops=n * 2 * rows * depth * 3 * cols, bytes_accessed=n * (depth * 3 * cols * 2 + 16 * rows * cols), transcendentals=n * 3 * rows * cols
        ),
        name="forward_sections",
    )(table, hidden, normed, masks[:, None], bias_in[:, None], bias_out[:, None], *arrays)


def backward_kernel(n, n_in, n_out, pr, tile, table, *refs):
    gh_in, gn_in, normed, mask, s_hidden, s_update, s_reset, s_cand = refs[:8]
    arrays = refs[8 : 8 + n_in]
    gh_out, gn_out, g_mask, g_bin, g_bout = refs[8 + n_in : 13 + n_in]
    outs = refs[13 + n_in : 13 + n_in + n_out]
    wbuf, gh, gn, fi, si, gg, gr, stage, sems, out_sems = refs[13 + n_in + n_out :]
    step = pl.program_id(0)
    sec = n - 1 - step
    rows, cols = gh.shape
    wide = 2 * cols

    def wait_out(slot):
        whole = stage.at[slot]
        pltpu.make_async_copy(whole, whole, out_sems.at[slot]).wait()

    @pl.when(step == 0)
    def _():
        for part, lo, hi in ((0, n - 1, n), (1, 0, n - 1)):
            if lo == hi:
                continue
            at = 0
            for array in arrays:
                for slot in range(array.shape[0]):
                    row = pl.multiple_of(table[at], pr)
                    pltpu.make_async_copy(
                        array.at[slot, pl.ds(lo, hi - lo)],
                        wbuf.at[pl.ds(lo, hi - lo), pl.ds(row, pr)],
                        sems.at[part],
                    ).start()
                    at += 1
        gh[...] = gh_in[...]
        gn[...] = gn_in[...]
        whole = wbuf.at[pl.ds(n - 1, 1)]
        pltpu.make_async_copy(whole, whole, sems.at[0]).wait()

    if n > 1:
        @pl.when(step == 1)
        def _():
            whole = wbuf.at[pl.ds(0, n - 1)]
            pltpu.make_async_copy(whole, whole, sems.at[1]).wait()

    w = wbuf.at[sec]
    mask_row = mask[0]
    nt = (((1,), (1,)), ((), ()))
    tn = (((0,), (0,)), ((), ()))

    def body(t, sums):
        m_sum, bi_sum, bo_sum = sums
        at = pl.ds(pl.multiple_of(t * tile, tile), tile)
        g = gh[at, :]
        h = s_hidden[0, at, :].astype(F32)
        u = s_update[0, at, :].astype(F32)
        r = s_reset[0, at, :].astype(F32)
        c = s_cand[0, at, :].astype(F32)
        x = normed[at, :]
        grad_update = g * (c - h)
        grad_raw = (g * u * (1.0 - c * c)).astype(BF16)
        gr[at, :] = grad_raw
        si[at, :cols] = (r * h).astype(BF16)
        si[at, cols:] = x.astype(BF16)
        fi[at, :cols] = (mask_row * x).astype(BF16)
        fi[at, cols:] = h.astype(BF16)
        second = lax.dot_general(grad_raw, w[:, wide:], nt, preferred_element_type=F32)
        g2 = second[:, :cols]
        gates_u = (grad_update * u * (1.0 - u)).astype(BF16)
        gates_r = (g2 * h * r * (1.0 - r)).astype(BF16)
        gates = jnp.concatenate([gates_u, gates_r], axis=1)
        gg[at, :] = gates
        first = lax.dot_general(gates, w[:, :wide], nt, preferred_element_type=F32)
        gm = first[:, :cols]
        gn[at, :] = gn[at, :] + second[:, cols:] + gm * mask_row
        gh[at, :] = g * (1.0 - u) + g2 * r + first[:, cols:]
        m_sum = m_sum + jnp.sum(gm * x, axis=0, keepdims=True)
        bi_sum = bi_sum + jnp.sum(gates.astype(F32), axis=0, keepdims=True)
        bo_sum = bo_sum + jnp.sum(grad_raw.astype(F32), axis=0, keepdims=True)
        return m_sum, bi_sum, bo_sum

    zero = lambda width: jnp.zeros((1, width), F32)
    m_sum, bi_sum, bo_sum = lax.fori_loop(0, rows // tile, body, (zero(cols), zero(wide), zero(cols)))
    g_mask[0] = m_sum * float(cols)
    g_bin[0] = bi_sum
    g_bout[0] = bo_sum

    slot = lax.rem(step, 2)
    if n > 2:
        @pl.when(step >= 2)
        def _():
            wait_out(slot)

    mt = 256
    for m in range(0, wide, mt):
        stage[slot, m : m + mt, wide:] = lax.dot_general(si[:, m : m + mt], gr[...], tn, preferred_element_type=F32).astype(BF16)
        stage[slot, m : m + mt, :wide] = lax.dot_general(fi[:, m : m + mt], gg[...], tn, preferred_element_type=F32).astype(BF16)

    at = 0
    for out in outs:
        for s in range(out.shape[0]):
            row = pl.multiple_of(table[at], pr)
            pltpu.make_async_copy(stage.at[slot, pl.ds(row, pr)], out.at[s, sec], out_sems.at[slot]).start()
            at += 1

    @pl.when(step == n - 1)
    def _():
        gh_out[...] = gh[...]
        gn_out[...] = gn[...]
        if n > 1:
            wait_out(1 - slot)
        wait_out(slot)


def backward_chunk(table, gh, gn, normed, masks, saved, arrays, out_slots, tile=256):
    n = masks.shape[0]
    rows, cols = gh.shape
    pr = arrays[0].shape[2]
    depth = 2 * cols
    whole = pl.BlockSpec((rows, cols), lambda i, *_: (0, 0))
    row = lambda width: pl.BlockSpec((1, 1, width), lambda i, *_: (n - 1 - i, 0, 0))
    per = pl.BlockSpec((1, rows, cols), lambda i, *_: (n - 1 - i, 0, 0))
    any_spec = pl.BlockSpec(memory_space=pl.ANY)
    state = jax.ShapeDtypeStruct((rows, cols), F32)
    vec = lambda width: jax.ShapeDtypeStruct((n, 1, width), F32)
    results = pl.pallas_call(
        functools.partial(backward_kernel, n, len(arrays), len(out_slots), pr, tile),
        grid_spec=pltpu.PrefetchScalarGridSpec(
            num_scalar_prefetch=1,
            grid=(n,),
            in_specs=[whole, whole, whole, row(cols), per, per, per, per] + [any_spec] * len(arrays),
            out_specs=[whole, whole, row(cols), row(depth), row(cols)] + [any_spec] * len(out_slots),
            scratch_shapes=[
                pltpu.VMEM((n, depth, 3 * cols), BF16),
                pltpu.VMEM((rows, cols), F32),
                pltpu.VMEM((rows, cols), F32),
                pltpu.VMEM((rows, depth), BF16),
                pltpu.VMEM((rows, depth), BF16),
                pltpu.VMEM((rows, depth), BF16),
                pltpu.VMEM((rows, cols), BF16),
                pltpu.VMEM((2, depth, 3 * cols), BF16),
                pltpu.SemaphoreType.DMA((2,)),
                pltpu.SemaphoreType.DMA((2,)),
            ],
        ),
        out_shape=[state, state, vec(cols), vec(depth), vec(cols)]
        + [jax.ShapeDtypeStruct((s, n, pr, 3 * cols), BF16) for s in out_slots],
        compiler_params=pltpu.CompilerParams(vmem_limit_bytes=VMEM_LIMIT),
        cost_estimate=pl.CostEstimate(
            flops=n * 4 * rows * depth * 3 * cols, bytes_accessed=n * (depth * 3 * cols * 4 + 16 * rows * cols), transcendentals=0
        ),
        name="backward_sections",
    )(table, gh, gn, normed, masks[:, None], *saved, *arrays)
    gh, gn, g_mask, g_bin, g_bout = results[:5]
    return gh, gn, g_mask[:, 0], g_bin[:, 0], g_bout[:, 0], results[5:]


def pick(micro, table):
    out = table[MB - 1 : MB, :]
    for b in range(MB - 2, -1, -1):
        out = jnp.where(micro == b, table[b : b + 1, :], out)
    return out


def stats_kernel(with_hidden, *refs):
    if with_hidden:
        u_ref, hidden_ref, micro_ref, valid_ref, out_ref, stats_ref = refs
        u = u_ref[...] + hidden_ref[...]
        out_ref[...] = u
    else:
        u_ref, micro_ref, valid_ref, stats_ref = refs
        u = u_ref[...].astype(F32)
    micro = micro_ref[...]
    valid = valid_ref[...]
    width = u.shape[1]
    counts, means = [], []
    for b in range(MB):
        member = jnp.where(micro == b, valid, 0.0)
        count = jnp.sum(member)
        total = jnp.sum(u * member, axis=0, keepdims=True)
        counts.append(jnp.full((1, width), count, F32))
        means.append(total / jnp.maximum(count, 1.0))
    centred = u - pick(micro, jnp.concatenate(means, axis=0))
    squares = centred * centred * valid
    for b in range(MB):
        stats_ref[b : b + 1, :] = counts[b]
        stats_ref[MB + b : MB + b + 1, :] = means[b]
        stats_ref[2 * MB + b : 2 * MB + b + 1, :] = jnp.sum(jnp.where(micro == b, squares, 0.0), axis=0, keepdims=True)


def local_stats(u, hidden, micro, valid):
    rows, cols = u.shape
    stats = jax.ShapeDtypeStruct((3 * MB, cols), F32)
    args = (u, micro, valid) if hidden is None else (u, hidden, micro, valid)
    out = [stats] if hidden is None else [jax.ShapeDtypeStruct((rows, cols), F32), stats]
    res = pl.pallas_call(
        functools.partial(stats_kernel, hidden is not None),
        out_shape=out,
        compiler_params=pltpu.CompilerParams(vmem_limit_bytes=VMEM_LIMIT),
        cost_estimate=pl.CostEstimate(flops=20 * rows * cols, bytes_accessed=8 * rows * cols, transcendentals=0),
        name="local_stats",
    )(*args)
    return (None, res[0]) if hidden is None else res


def merge_stats(a, b):
    na, ma, qa = a[:MB], a[MB : 2 * MB], a[2 * MB :]
    nb, mb, qb = b[:MB], b[MB : 2 * MB], b[2 * MB :]
    n = na + nb
    inverse = 1.0 / jnp.maximum(n, 1.0)
    apart = ma - mb
    return jnp.concatenate([n, (na * ma + nb * mb) * inverse, qa + qb + apart * apart * (na * nb * inverse)], axis=0)


def norm_kernel(u_ref, micro_ref, stats_ref, gain_ref, shift_ref, normed_ref):
    stats = stats_ref[...]
    scale = lax.rsqrt(stats[2 * MB :] / stats[:MB] + EPSILON)
    micro = micro_ref[...]
    standard = (u_ref[...].astype(F32) - pick(micro, stats[MB : 2 * MB])) * pick(micro, scale)
    normed_ref[...] = standard * gain_ref[...] + shift_ref[...]


def norm_rows(u, micro, stats, gain, shift):
    rows, cols = u.shape
    return pl.pallas_call(
        norm_kernel,
        out_shape=jax.ShapeDtypeStruct((rows, cols), F32),
        compiler_params=pltpu.CompilerParams(vmem_limit_bytes=VMEM_LIMIT),
        cost_estimate=pl.CostEstimate(flops=20 * rows * cols, bytes_accessed=8 * rows * cols, transcendentals=0),
        name="norm_rows",
    )(u, micro, stats, gain[None], shift[None])


def pool_kernel(u_ref, micro_ref, stats_ref, gn_ref, gh_ref, total_ref, pooled_ref):
    stats = stats_ref[...]
    scale = lax.rsqrt(stats[2 * MB :] / stats[:MB] + EPSILON)
    micro = micro_ref[...]
    standard = (u_ref[...].astype(F32) - pick(micro, stats[MB : 2 * MB])) * pick(micro, scale)
    total = gn_ref[...] + gh_ref[...]
    total_ref[...] = total
    product = total * standard
    for b in range(MB):
        pooled_ref[b : b + 1, :] = jnp.sum(jnp.where(micro == b, total, 0.0), axis=0, keepdims=True)
        pooled_ref[MB + b : MB + b + 1, :] = jnp.sum(jnp.where(micro == b, product, 0.0), axis=0, keepdims=True)


def pool_grads(u, micro, stats, gn, gh):
    rows, cols = u.shape
    return pl.pallas_call(
        pool_kernel,
        out_shape=[jax.ShapeDtypeStruct((rows, cols), F32), jax.ShapeDtypeStruct((2 * MB, cols), F32)],
        compiler_params=pltpu.CompilerParams(vmem_limit_bytes=VMEM_LIMIT),
        cost_estimate=pl.CostEstimate(flops=20 * rows * cols, bytes_accessed=16 * rows * cols, transcendentals=0),
        name="pool_grads",
    )(u, micro, stats, gn, gh)


def carry_kernel(u_ref, micro_ref, valid_ref, stats_ref, gain_ref, total_ref, pooled_ref, carried_ref, out_ref):
    stats = stats_ref[...]
    gain = gain_ref[...]
    counts = stats[:MB]
    scale = lax.rsqrt(stats[2 * MB :] / counts + EPSILON)
    pooled = pooled_ref[...]
    micro = micro_ref[...]
    row_scale = pick(micro, scale)
    standard = (u_ref[...].astype(F32) - pick(micro, stats[MB : 2 * MB])) * row_scale
    shift_term = pick(micro, gain * pooled[:MB] / counts)
    scale_term = pick(micro, gain * pooled[MB:] / counts)
    out_ref[...] = carried_ref[...] + row_scale * (
        total_ref[...] * gain - valid_ref[...] * (shift_term + standard * scale_term)
    )


def carry_grads(u, micro, valid, stats, gain, total, pooled, carried):
    rows, cols = u.shape
    return pl.pallas_call(
        carry_kernel,
        out_shape=jax.ShapeDtypeStruct((rows, cols), F32),
        compiler_params=pltpu.CompilerParams(vmem_limit_bytes=VMEM_LIMIT),
        cost_estimate=pl.CostEstimate(flops=30 * rows * cols, bytes_accessed=16 * rows * cols, transcendentals=0),
        name="carry_grads",
    )(u, micro, valid, stats, gain[None], total, pooled, carried)


def feature_mask(logits, thresh):
    centred = logits - jnp.max(logits)
    weights = jnp.exp(centred) * jax.nn.softplus(centred + thresh)
    return weights / jnp.sum(weights)


def along(axis, size, flip):
    return [(i, i ^ flip) for i in range(size)]


class CubeTransfers:
    def __init__(self, dp_size, fsdp_size):
        self.dp_size, self.fsdp_size = dp_size, fsdp_size
        self.slots = [4, 4, 4, 2, 2, 16]

    def core(self, v):
        return lax.ppermute(v, "dp", along("dp", self.dp_size, 1))

    def x(self, v):
        return lax.ppermute(v, "dp", along("dp", self.dp_size, 2))

    def y(self, v):
        return lax.ppermute(v, "fsdp", along("fsdp", self.fsdp_size, 1))

    def z(self, v, flip):
        return lax.ppermute(v, "fsdp", along("fsdp", self.fsdp_size, 2 * flip))

    def all_reduce(self, v, merge):
        for step in (self.core, self.x, self.y, lambda a: self.z(a, 1), lambda a: self.z(a, 2)):
            v = merge(v, step(v))
        return v

    def table(self, shard_rows):
        q = lax.axis_index("dp").astype(jnp.int32)
        f = lax.axis_index("fsdp").astype(jnp.int32)
        rows = []
        for core in (0, 1):
            for flip_q, flip_y, slots in ((0, 0, range(4)), (0, 1, range(4)), (2, 0, range(4)), (2, 1, range(4))):
                for j in slots:
                    place = f ^ (2 * j + flip_y)
                    rows.append(place * shard_rows + (q ^ (flip_q + core)) * (shard_rows // self.dp_size))
        return jnp.stack(rows)

    def gather(self, shard):
        rows = shard.shape[1] // self.dp_size
        own = lax.dynamic_slice_in_dim(shard, lax.axis_index("dp") * rows, rows, axis=1)
        held = jnp.stack([own] + [self.z(own, j) for j in (1, 2, 3)])
        by_y, by_x = self.y(held), self.x(held)
        far_x, far_y = self.x(by_y[:2]), self.y(by_x[2:])
        mine = [held, by_y, by_x, far_x, far_y]
        return mine + [self.core(v) for v in mine]

    def scatter(self, parts):
        held, by_y, by_x, far_x, far_y, other = parts
        other = self.core(other)
        add = lambda *vs: sum(v.astype(F32) for v in vs)
        low = lambda v: v.astype(BF16)
        far_x = low(add(far_x, other[12:14]))
        far_y = low(add(far_y, other[14:16]))
        got_x, got_y = self.x(far_x), self.y(far_y)
        by_y = low(jnp.concatenate([add(by_y[:2], other[4:6], got_x), add(by_y[2:], other[6:8])]))
        by_x = low(jnp.concatenate([add(by_x[:2], other[8:10]), add(by_x[2:], other[10:12], got_y)]))
        got_y, got_x = self.y(by_y), self.x(by_x)
        sums = [low(add(held[j], other[j], got_y[j], got_x[j])) for j in range(4)]
        got = [self.z(sums[j], j) for j in (1, 2, 3)]
        own = low(add(sums[0], *got))
        by_x = self.x(own)
        return [own, self.core(own), by_x, self.core(by_x)]

    def pieces_table(self, shard_rows):
        q = lax.axis_index("dp").astype(jnp.int32)
        return jnp.stack([(q ^ j) * (shard_rows // self.dp_size) for j in range(4)])


class PlainTransfers:
    def __init__(self, dp_size, fsdp_size):
        self.fsdp_size = fsdp_size
        self.slots = [fsdp_size]

    def all_reduce(self, v, merge):
        every = lax.all_gather(v, ("dp", "fsdp"))
        while every.shape[0] > 1:
            half = every.shape[0] // 2
            every = jax.vmap(merge)(every[:half], every[half:])
        return every[0]

    def table(self, shard_rows):
        return jnp.arange(self.fsdp_size, dtype=jnp.int32) * shard_rows

    def gather(self, shard):
        return [lax.all_gather(shard, "fsdp")]

    def scatter(self, parts):
        own = lax.psum_scatter(parts[0], "fsdp", scatter_dimension=0)
        return [lax.psum(own, "dp")]

    def pieces_table(self, shard_rows):
        return jnp.zeros((1,), jnp.int32)


def place_kernel(n_pieces, first, table, *refs):
    pieces = refs[:n_pieces]
    g_in, g_out = refs[-2:]
    pr = pieces[0].shape[1]
    wide = g_in.shape[-1]
    for piece, j in zip(pieces, range(n_pieces)):
        row = pl.multiple_of(table[j], pr)
        value = piece[0].astype(F32)
        g_in[0, 0, pl.ds(row, pr), :] = value[:, :wide]
        g_out[0, 0, pl.ds(row, pr), :] = value[:, wide:]


def place_grads(table, pieces, layer, start, shard_rows, previous):
    n, pr, width = pieces[0].shape
    wide = 2 * width // 3
    shapes = [
        jax.ShapeDtypeStruct((LAYERS, SECTIONS, shard_rows, wide), F32),
        jax.ShapeDtypeStruct((LAYERS, SECTIONS, shard_rows, width - wide), F32),
    ]
    block = lambda w: pl.BlockSpec((1, 1, shard_rows, w), lambda i, *_: (layer, start + i, 0, 0))
    n_pieces = len(pieces)
    extra = [] if previous is None else list(previous)
    return pl.pallas_call(
        functools.partial(place_kernel, n_pieces, previous is None),
        grid_spec=pltpu.PrefetchScalarGridSpec(
            num_scalar_prefetch=1,
            grid=(n,),
            in_specs=[pl.BlockSpec((1, pr, width), lambda i, *_: (i, 0, 0))] * n_pieces
            + [pl.BlockSpec(memory_space=pl.ANY)] * len(extra),
            out_specs=[block(wide), block(width - wide)],
        ),
        out_shape=shapes,
        input_output_aliases={} if previous is None else {1 + n_pieces: 0, 2 + n_pieces: 1},
        cost_estimate=pl.CostEstimate(flops=0, bytes_accessed=n * shard_rows * width * 6, transcendentals=0),
        name="place_grads",
    )(table, *pieces, *extra)


def local(
    moves,
    features,
    row_valid,
    micro_batch,
    gains,
    shifts,
    mask_logits,
    thresholds,
    gate_in,
    bias_in,
    gate_out,
    bias_out,
    cotangent,
):
    columns = features.shape[1]
    shard_rows = gate_in.shape[2]
    valid = row_valid.astype(F32)[:, None]
    micro = micro_batch[:, None]
    table = moves.table(shard_rows)
    weights = [
        [
            moves.gather(jnp.concatenate([gate_in[layer, lo:hi], gate_out[layer, lo:hi]], axis=-1))
            for lo, hi in GROUPS[layer]
        ]
        for layer in range(LAYERS)
    ]
    masks = columns * jax.vmap(jax.vmap(feature_mask))(mask_logits, thresholds)
    add = lambda a, b: a + b

    current = features
    hidden = None
    records = []
    for layer in range(LAYERS):
        summed, stats = local_stats(current, hidden, micro, valid)
        current = current if summed is None else summed
        stats = moves.all_reduce(stats, merge_stats)
        normed = norm_rows(current, micro, stats, gains[layer], shifts[layer])
        hidden = normed
        stored = []
        for (lo, hi), arrays in zip(GROUPS[layer], weights[layer]):
            hidden, *saved = forward_chunk(
                table, hidden, normed, masks[layer, lo:hi], bias_in[layer, lo:hi], bias_out[layer, lo:hi], arrays
            )
            stored.append(saved)
        records.append((current, stats, normed, stored))
    mixed_out = (current + hidden).astype(BF16)

    carried = cotangent.astype(F32) * valid
    pieces_table = moves.pieces_table(shard_rows)
    grads = None
    sums = [None] * LAYERS
    pooled_of = [None] * LAYERS
    for layer in reversed(range(LAYERS)):
        current, stats, normed, stored = records[layer]
        gh = carried
        gn = jnp.zeros_like(carried)
        parts = []
        for (lo, hi), arrays, saved in reversed(list(zip(GROUPS[layer], weights[layer], stored))):
            gh, gn, g_mask, g_bin, g_bout, out = backward_chunk(
                table, gh, gn, normed, masks[layer, lo:hi], saved, arrays, moves.slots
            )
            parts.append((g_mask, g_bin, g_bout))
            grads = place_grads(pieces_table, moves.scatter(out), layer, lo, shard_rows, grads)
        total, pooled = pool_grads(current, micro, stats, gn, gh)
        vectors = jnp.concatenate([jnp.concatenate(p, axis=1) for p in reversed(parts)], axis=0)
        if layer == 0:
            both = moves.all_reduce(jnp.concatenate([pooled, vectors.reshape(-1, columns)]), add)
            pooled = both[: 2 * MB]
            vectors = both[2 * MB :].reshape(vectors.shape)
        else:
            pooled = moves.all_reduce(pooled, add)
            vectors = moves.all_reduce(vectors, add)
        sums[layer] = vectors
        pooled_of[layer] = pooled
        carried = carry_grads(current, micro, valid, stats, gains[layer], total, pooled, carried)
    stacked = jnp.stack(sums)
    pooled = jnp.stack(pooled_of)
    _, mask_pull = jax.vjp(jax.vmap(jax.vmap(feature_mask)), mask_logits, thresholds)
    grad_logits, grad_thresholds = mask_pull(stacked[..., :columns])
    return (
        mixed_out,
        carried,
        jnp.sum(pooled[:, MB:], axis=1),
        jnp.sum(pooled[:, :MB], axis=1),
        grad_logits,
        grad_thresholds,
        grads[0],
        stacked[..., columns : 3 * columns],
        grads[1],
        stacked[..., 3 * columns :],
    )


def solution(mesh):
    rows = P(("dp", "fsdp"), None)
    row = P(("dp", "fsdp"))
    shard = P(None, None, "fsdp", None)
    in_specs = (rows, row, row, P(), P(), P(), P(), shard, P(), shard, P(), rows)
    out_specs = (rows, rows, P(), P(), P(), P(), shard, P(), shard, P())
    dp_size, fsdp_size = mesh.shape["dp"], mesh.shape["fsdp"]
    kind = CubeTransfers if (dp_size, fsdp_size) == (4, 8) else PlainTransfers
    return jax.shard_map(
        functools.partial(local, kind(dp_size, fsdp_size)),
        mesh=mesh,
        in_specs=in_specs,
        out_specs=out_specs,
        check_vma=False,
    )
```

time: 3090 us -> 929 us (0.30)
  waiting for transfers between devices: 2310 us -> 374 us
  Pallas kernels: 0 us -> 290 us
  matrix products: 284 us -> 0 us
  blocking collectives: 203 us -> 0 us
  starting transfers between devices: 2.79 us -> 175 us
  other arithmetic: 151 us -> 41.9 us
  local copies, waits for them, and re-layouts: 109 us -> 36.3 us
    reduce_scatter x24 -> x0, waiting for transfers between devices: 1380 us -> none  [the longest x12 818 us: local(): lax.psum_scatter(weight_rows(first_in, grad_gates).astype(jnp.bfloat16),...]
    all_gather x24 -> x0, waiting for transfers between devices: 718 us -> none  [the longest x12 388 us: local(): lax.all_gather(gate_in[layer_no, section_no], 'fsdp', axis=0, tiled=True)]
    ppermute x0 -> x163, waiting for transfers between devices: none -> 374 us  [the longest x29 181 us: y(): return lax.ppermute(v, 'fsdp', along('fsdp', self.fsdp_size, 1))]
    pallas_call x0 -> x26, Pallas kernels: none -> 290 us  [the longest x6 147 us: backward_chunk(): pl.pallas_call(functools.partial(backward_kernel, n, len(arrays), len(out...]
    dot_general x88 -> x0, matrix products: 284 us -> none  [the longest x24 115 us: add_rows(): return jnp.dot(operand, shard_rows, preferred_element_type=jnp.float32)]
    psum x2 -> x0, waiting for transfers between devices: 203 us -> none  [the longest x1 120 us: local(): lax.psum((pool_rows(onehot, grad_normed), pool_rows(onehot, grad_normed *...]
    psum x5 -> x0, blocking collectives: 203 us -> none  [the longest x2 82.3 us: norm_forward(): lax.psum(pool_rows(member, centred * centred), ('dp', 'fsdp'))]
    ppermute x0 -> x163, starting transfers between devices: none -> 175 us  [the longest x46 86.9 us: z(): return lax.ppermute(v, 'fsdp', along('fsdp', self.fsdp_size, 2 * flip))]
  transfers between devices with their start and end apart: 50 -> 163, of which waited for: 42 -> 56; matrix products, arithmetic and copies ran while one was open for 14% -> 8% of each run, Pallas kernels for 0% -> 22%
where the time goes in v1:
time: 929 us; the launch traced here: 920 us
  waiting for transfers between devices  374 us (40%)
  Pallas kernels  290 us (31%)
  starting transfers between devices  175 us (19%)
  other arithmetic  41.9 us (5%)
  local copies, waits for them, and re-layouts  36.3 us (4%)
    ppermute x29, waiting for transfers between devices, y(): return lax.ppermute(v, 'fsdp', along('fsdp', self.fsdp_size, 1))  181 us
    pallas_call x6, Pallas kernels, backward_chunk(): pl.pallas_call(functools.partial(backward_kernel, n, len(arrays), len(out...  147 us
    ppermute x46, waiting for transfers between devices, z(): return lax.ppermute(v, 'fsdp', along('fsdp', self.fsdp_size, 2 * flip))  110 us
    pallas_call x6, Pallas kernels, forward_chunk(): pl.pallas_call(functools.partial(forward_kernel, n, len(arrays), pr, tile...  87.6 us
    ppermute x46, starting transfers between devices, z(): return lax.ppermute(v, 'fsdp', along('fsdp', self.fsdp_size, 2 * flip))  86.9 us
    ppermute x35, waiting for transfers between devices, x(): return lax.ppermute(v, 'dp', along('dp', self.dp_size, 2))  80.8 us
    ppermute x35, starting transfers between devices, x(): return lax.ppermute(v, 'dp', along('dp', self.dp_size, 2))  45.8 us
    ppermute x29, starting transfers between devices, y(): return lax.ppermute(v, 'fsdp', along('fsdp', self.fsdp_size, 1))  31.8 us
  transfers between devices with their start and end apart: 163, of which 56 were waited for; matrix products, arithmetic and copies ran while one was open for 8% of the time, Pallas kernels for 22%

profile of v1, /device:TPU:0, one launch (start us, length us, event | category | flops | bytes accessed | tf_op | source)
XLA Modules:
  0.0 920.0 jit_solution(5191989884942977308)
XLA Ops:
  2.8 4.1 collective-permute-start.71
  10.3 4.0 local_stats.2
  38.0 2.9 collective-permute-start.17
  45.0 25.2 %collective-permute-done.4 = f32[12,512]{1,0:T(8,128)S(1)} collective-permute-done((f32[12,512]{1,0:T(8,128)S(1)}, f32[12,512]{1,0:T(8,128)S(1)}, u32[]{:S(2)}, u32[]{:S(2)}) %collective-permute-start.4) | collective-permute-done | bytes 24608 | tf_op jit(solution)/shard_map/ppermute | solution.py:432
  76.9 7.9 collective-permute-done.46
  88.5 18.4 %collective-permute-done.30 = bf16[3,32,1536]{2,1,0:T(8,128)(2,1)S(1)} collective-permute-done((bf16[3,32,1536]{2,1,0:T(8,128)(2,1)S(1)}, bf16[3,32,1536]{2,1,0:T(8,128)(2,1)S(1)}, u32[]{:S(2)}, u32[]{:S(2)}) %collective-permute-start.30) | collective-permute-done | bytes 294944 | tf_op jit(solution)/shard_map/ppermute | solution.py:432
  113.6 14.7 %collective-permute-done.11.refs_9_.refs_12_ = bf16[2,1,32,1536]{3,2,1,0:T(8,128)(2,1)S(1)} collective-permute-done((bf16[2,1,32,1536]{3,2,1,0:T(8,128)(2,1)S(1)}, bf16[2,1,32,1536]{3,2,1,0:T(8,128)(2,1)S(1)}, u32[]{:S(2)}, u32[]{:S(2)}) %collective-permute-start.11) | collective-permute-done | bytes 196640 | tf_op jit(solution)/shard_map/ppermute | solution.py:429
  137.6 20.8 %collective-permute-done.23.refs_9_.refs_12_ = bf16[2,2,32,1536]{3,2,1,0:T(8,128)(2,1)S(1)} collective-permute-done((bf16[2,2,32,1536]{3,2,1,0:T(8,128)(2,1)S(1)}, bf16[2,2,32,1536]{3,2,1,0:T(8,128)(2,1)S(1)}, u32[]{:S(2)}, u32[]{:S(2)}) %collective-permute-start.23) | collective-permute-done | bytes 393248 | tf_op jit(solution)/shard_map/ppermute | solution.py:429
  172.2 3.3 norm_rows.2.refs_0_.refs_1_.refs_2_
  176.6 8.0 collective-permute-done.35.refs_9_.refs_12_
  185.6 10.5 %forward_sections.6 = (f32[768,512]{1,0:T(8,128)}, f32[1,768,512]{2,1,0:T(8,128)}, f32[1,768,512]{2,1,0:T(8,128)}, f32[1,768,512]{2,1,0:T(8,128)}, f32[1,768,512]{2,1,0:T(8,128)}) custom-call(s32[32]{0:T(128)} %stack.251.table, f32[768,512]{1,0:T(8,128)} %norm_rows.2.refs_0_.refs_1_.refs_2_, f32[768,512]{1,0:T(8,128)} %norm_rows.2.refs_0_.refs_1_.refs_2_, ...), custom_call_target="tpu_custom_call" | custom-call | flops 2415919104 | bytes 9437184 | tf_op jit(solution)/shard_map/forward_sections/pallas_call | solution.py:105
  196.1 14.8 %forward_sections.7 = (f32[768,512]{1,0:T(8,128)}, f32[2,768,512]{2,1,0:T(8,128)}, f32[2,768,512]{2,1,0:T(8,128)}, f32[2,768,512]{2,1,0:T(8,128)}, f32[2,768,512]{2,1,0:T(8,128)}) custom-call(s32[32]{0:T(128)} %stack.251.table, f32[768,512]{1,0:T(8,128)} %get-tuple-element.124.refs_0_, f32[768,512]{1,0:T(8,128)} %norm_rows.2.refs_0_.refs_1_.refs_2_, ...), custom_call_target="tpu_custom_call" | custom-call | flops 4831838208 | bytes 18874368 | tf_op jit(solution)/shard_map/forward_sections/pallas_call | solution.py:105
  211.1 5.3 collective-permute-start.58
  218.5 18.3 %forward_sections.8 = (f32[768,512]{1,0:T(8,128)}, f32[3,768,512]{2,1,0:T(8,128)}, f32[3,768,512]{2,1,0:T(8,128)}, f32[3,768,512]{2,1,0:T(8,128)}, f32[3,768,512]{2,1,0:T(8,128)}) custom-call(s32[32]{0:T(128)} %stack.251.table, f32[768,512]{1,0:T(8,128)} %get-tuple-element.125.refs_0_, f32[768,512]{1,0:T(8,128)} %norm_rows.2.refs_0_.refs_1_.refs_2_, ...), custom_call_target="tpu_custom_call" | custom-call | flops 7247757312 | bytes 28311552 | tf_op jit(solution)/shard_map/forward_sections/pallas_call | solution.py:105
  236.9 4.4 local_stats.3
  245.7 24.9 %collective-permute-done.42 = f32[12,512]{1,0:T(8,128)S(1)} collective-permute-done((f32[12,512]{1,0:T(8,128)S(1)}, f32[12,512]{1,0:T(8,128)S(1)}, u32[]{:S(2)}, u32[]{:S(2)}) %collective-permute-start.42) | collective-permute-done | bytes 24608 | tf_op jit(solution)/shard_map/ppermute | solution.py:426
  271.1 24.3 %collective-permute-done.73.refs_6_.refs_9_ = bf16[4,1,32,1536]{3,2,1,0:T(8,128)(2,1)S(1)} collective-permute-done((bf16[4,1,32,1536]{3,2,1,0:T(8,128)(2,1)}, bf16[4,1,32,1536]{3,2,1,0:T(8,128)(2,1)S(1)}, u32[]{:S(2)}, u32[]{:S(2)}) %collective-permute-start.73) | collective-permute-done | bytes 393248 | tf_op jit(solution)/shard_map/ppermute | solution.py:429
  304.9 6.2 collective-permute-done.64.refs_9_.refs_12_
  316.6 8.9 collective-permute-done.52.refs_9_.refs_12_
  325.5 3.1 collective-permute-start.45
  333.9 3.7 norm_rows.3.refs_0_.refs_1_.refs_2_
  338.1 18.6 %forward_sections.9 = (f32[768,512]{1,0:T(8,128)}, f32[3,768,512]{2,1,0:T(8,128)}, f32[3,768,512]{2,1,0:T(8,128)}, f32[3,768,512]{2,1,0:T(8,128)}, f32[3,768,512]{2,1,0:T(8,128)}) custom-call(s32[32]{0:T(128)} %stack.251.table, f32[768,512]{1,0:T(8,128)} %norm_rows.3.refs_0_.refs_1_.refs_2_, f32[768,512]{1,0:T(8,128)} %norm_rows.3.refs_0_.refs_1_.refs_2_, ...), custom_call_target="tpu_custom_call" | custom-call | flops 7247757312 | bytes 28311552 | tf_op jit(solution)/shard_map/forward_sections/pallas_call | solution.py:105
  358.2 15.2 %forward_sections.10 = (f32[768,512]{1,0:T(8,128)}, f32[2,768,512]{2,1,0:T(8,128)}, f32[2,768,512]{2,1,0:T(8,128)}, f32[2,768,512]{2,1,0:T(8,128)}, f32[2,768,512]{2,1,0:T(8,128)}) custom-call(s32[32]{0:T(128)} %stack.251.table, f32[768,512]{1,0:T(8,128)} %get-tuple-element.129.refs_0_, f32[768,512]{1,0:T(8,128)} %norm_rows.3.refs_0_.refs_1_.refs_2_, ...), custom_call_target="tpu_custom_call" | custom-call | flops 4831838208 | bytes 18874368 | tf_op jit(solution)/shard_map/forward_sections/pallas_call | solution.py:105
  374.5 10.2 %forward_sections.11 = (f32[768,512]{1,0:T(8,128)}, f32[1,768,512]{2,1,0:T(8,128)}, f32[1,768,512]{2,1,0:T(8,128)}, f32[1,768,512]{2,1,0:T(8,128)}, f32[1,768,512]{2,1,0:T(8,128)}) custom-call(s32[32]{0:T(128)} %stack.251.table, f32[768,512]{1,0:T(8,128)} %get-tuple-element.130.refs_0_, f32[768,512]{1,0:T(8,128)} %norm_rows.3.refs_0_.refs_1_.refs_2_, ...), custom_call_target="tpu_custom_call" | custom-call | flops 2415919104 | bytes 9437184 | tf_op jit(solution)/shard_map/forward_sections/pallas_call | solution.py:105
  386.1 16.8 %backward_sections.6 = (f32[768,512]{1,0:T(8,128)}, f32[768,512]{1,0:T(8,128)}, f32[1,1,512]{2,1,0:T(1,128)}, f32[1,1,1024]{2,1,0:T(1,128)}, f32[1,1,512]{2,1,0:...) custom-call(s32[32]{0:T(128)} %stack.251.table, ...), custom_call_target="tpu_custom_call" | custom-call | flops 4831838208 | bytes 12582912 | tf_op jit(solution)/shard_map/backward_sections/pallas_call | solution.py:248
  402.9 24.8 %backward_sections.7 = (f32[768,512]{1,0:T(8,128)}, f32[768,512]{1,0:T(8,128)}, f32[2,1,512]{2,1,0:T(1,128)}, f32[2,1,1024]{2,1,0:T(1,128)}, f32[2,1,512]{2,1,0:...) custom-call(s32[32]{0:T(128)} %stack.251.table, ...), custom_call_target="tpu_custom_call" | custom-call | flops 9663676416 | bytes 25165824 | tf_op jit(solution)/shard_map/backward_sections/pallas_call | solution.py:248
  427.7 31.9 %backward_sections.8 = (f32[768,512]{1,0:T(8,128)}, f32[768,512]{1,0:T(8,128)}, f32[3,1,512]{2,1,0:T(1,128)}, f32[3,1,1024]{2,1,0:T(1,128)}, f32[3,1,512]{2,1,0:...) custom-call(s32[32]{0:T(128)} %stack.251.table, ...), custom_call_target="tpu_custom_call" | custom-call | flops 14495514624 | bytes 37748736 | tf_op jit(solution)/shard_map/backward_sections/pallas_call | solution.py:248
  459.7 5.4 pool_grads.2
  478.8 3.0 collective-permute-start.86
  484.1 5.3 carry_grads.2.refs_0_.carried_ref
  489.5 31.4 %backward_sections.9 = (f32[768,512]{1,0:T(8,128)}, f32[768,512]{1,0:T(8,128)}, f32[3,1,512]{2,1,0:T(1,128)}, f32[3,1,1024]{2,1,0:T(1,128)}, f32[3,1,512]{2,1,0:...) custom-call(s32[32]{0:T(128)} %stack.251.table, ...), custom_call_target="tpu_custom_call" | custom-call | flops 14495514624 | bytes 37748736 | tf_op jit(solution)/shard_map/backward_sections/pallas_call | solution.py:248
  521.0 24.7 %backward_sections.10 = (f32[768,512]{1,0:T(8,128)}, f32[768,512]{1,0:T(8,128)}, f32[2,1,512]{2,1,0:T(1,128)}, f32[2,1,1024]{2,1,0:T(1,128)}, f32[2,1,512]{2,1,0...) custom-call(s32[32]{0:T(128)} %stack.251.table, ...), custom_call_target="tpu_custom_call" | custom-call | flops 9663676416 | bytes 25165824 | tf_op jit(solution)/shard_map/backward_sections/pallas_call | solution.py:248
  547.8 17.1 %backward_sections.11 = (f32[768,512]{1,0:T(8,128)}, f32[768,512]{1,0:T(8,128)}, f32[1,1,512]{2,1,0:T(1,128)}, f32[1,1,1024]{2,1,0:T(1,128)}, f32[1,1,512]{2,1,0...) custom-call(s32[32]{0:T(128)} %stack.251.table, ...), custom_call_target="tpu_custom_call" | custom-call | flops 4831838208 | bytes 12582912 | tf_op jit(solution)/shard_map/backward_sections/pallas_call | solution.py:248
  565.8 5.4 pool_grads.3
  585.5 3.0 collective-permute-start.96
  594.6 5.1 collective-permute-done.91
  607.2 4.5 collective-permute-done.153
  617.6 3.3 collective-permute-done.155
  623.1 8.7 collective-permute-done.100
  635.3 4.3 collective-permute-done.156
  643.3 4.1 collective-permute-start.159
  649.1 3.0 collective-permute-start.102
  658.9 3.9 collective-permute-done.103
  667.9 9.4 %collective-permute-done.142 = bf16[2,2,32,1536]{3,2,1,0:T(8,128)(2,1)S(1)} collective-permute-done((bf16[2,2,32,1536]{3,2,1,0:T(8,128)(2,1)S(1)}, bf16[2,2,32,1536]{3,2,1,0:T(8,128)(2,1)S(1)}, u32[]{:S(2)}, u32[]{:S(2)}) %collective-permute-start.142) | collective-permute-done | bytes 393248 | tf_op jit(solution)/shard_map/ppermute | solution.py:426
  682.9 8.1 collective-permute-done.144
  694.3 19.1 %collective-permute-done.111 = bf16[2,2,32,1536]{3,2,1,0:T(8,128)(2,1)S(1)} collective-permute-done((bf16[2,2,32,1536]{3,2,1,0:T(8,128)(2,1)S(1)}, bf16[2,2,32,1536]{3,2,1,0:T(8,128)(2,1)S(1)}, u32[]{:S(2)}, u32[]{:S(2)}) %collective-permute-start.111) | collective-permute-done | bytes 393248 | tf_op jit(solution)/shard_map/ppermute | solution.py:429
  720.8 4.7 collective-permute-done.110
  734.0 8.7 collective-permute-done.131
  745.3 7.3 collective-permute-done.120
  754.5 13.5 %collective-permute-done.133 = bf16[2,3,32,1536]{3,2,1,0:T(8,128)(2,1)S(1)} collective-permute-done((bf16[2,3,32,1536]{3,2,1,0:T(8,128)(2,1)S(1)}, bf16[2,3,32,1536]{3,2,1,0:T(8,128)(2,1)S(1)}, u32[]{:S(2)}, u32[]{:S(2)}) %collective-permute-start.133) | collective-permute-done | bytes 589856 | tf_op jit(solution)/shard_map/ppermute | solution.py:429
  769.7 10.4 %collective-permute-done.122 = bf16[2,3,32,1536]{3,2,1,0:T(8,128)(2,1)S(1)} collective-permute-done((bf16[2,3,32,1536]{3,2,1,0:T(8,128)(2,1)S(1)}, bf16[2,3,32,1536]{3,2,1,0:T(8,128)(2,1)S(1)}, u32[]{:S(2)}, u32[]{:S(2)}) %collective-permute-start.122) | collective-permute-done | bytes 589856 | tf_op jit(solution)/shard_map/ppermute | solution.py:429
  780.1 9.7 %collective-permute-start.115 = (bf16[2,32,1536]{2,1,0:T(8,128)(2,1)S(1)}, bf16[2,32,1536]{2,1,0:T(8,128)(2,1)S(1)}, u32[]{:S(2)}, u32[]{:S(2)}) collective-permute-start(bf16[2,32,1536]{2,1,0:T(8,128)(2,1)S(1)} %get-tuple-element.310), channel_id=1, source_target_pairs={{0,6},{1,7},{2,4},{3,5},{4,2},{5,3},{6,0},{7,1},{8,14},{9,15},{10,... | collective-permute-start | bytes 589832 | tf_op jit(solution)/shard_map/ppermute | solution.py:432
  796.4 3.5 collective-permute-done.114
  801.6 14.2 %collective-permute-done.132 = bf16[4,3,32,1536]{3,2,1,0:T(8,128)(2,1)S(1)} collective-permute-done((bf16[4,3,32,1536]{3,2,1,0:T(8,128)(2,1)S(1)}, bf16[4,3,32,1536]{3,2,1,0:T(8,128)(2,1)S(1)}, u32[]{:S(2)}, u32[]{:S(2)}) %collective-permute-start.132) | collective-permute-done | bytes 1179680 | tf_op jit(solution)/shard_map/ppermute | solution.py:429
  818.2 10.2 %collective-permute-done.121 = bf16[4,3,32,1536]{3,2,1,0:T(8,128)(2,1)S(1)} collective-permute-done((bf16[4,3,32,1536]{3,2,1,0:T(8,128)(2,1)S(1)}, bf16[4,3,32,1536]{3,2,1,0:T(8,128)(2,1)S(1)}, u32[]{:S(2)}, u32[]{:S(2)}) %collective-permute-start.121) | collective-permute-done | bytes 1179680 | tf_op jit(solution)/shard_map/ppermute | solution.py:429
  828.4 4.3 collective-permute-start.137
  833.9 6.4 collective-permute-done.137
  840.3 4.4 collective-permute-start.126
  844.7 17.4 %collective-permute-done.136 = bf16[3,32,1536]{2,1,0:T(8,128)(2,1)S(1)} collective-permute-done((bf16[3,32,1536]{2,1,0:T(8,128)(2,1)S(1)}, bf16[3,32,1536]{2,1,0:T(8,128)(2,1)S(1)}, u32[]{:S(2)}, u32[]{:S(2)}) %collective-permute-start.136) | collective-permute-done | bytes 294944 | tf_op jit(solution)/shard_map/ppermute | solution.py:432
  864.5 7.5 collective-permute-done.125
  876.6 8.5 collective-permute-done.117.refs_2_
  893.1 5.1 carry_grads.3
  904.5 4.2 place_grads.8
  909.4 4.2 place_grads.9
  (724 shorter events, 252.4 us)
Async XLA Ops:
  2.8 33.6 %collective-permute-start.71 = (bf16[1,32,1536]{2,1,0:T(8,128)(2,1)S(1)}, bf16[1,32,1536]{2,1,0:T(8,128)(2,1)}, u32[]{:S(2)}, u32[]{:S(2)}) collective-permute-start(bf16[1,32,1536]{2,1,0:T(8,128)(2,1)S(1)} %fusion.46), channel_id=1, source_target_pairs={{0,4},{1,5},{2,6},{3,7},{4,0},{5,1},{6,2},{7,3},{8,12},{9,13},{10,... | collective-permute-start | bytes 294920 | tf_op jit(solution)/shard_map/ppermute | solution.py:432
  6.9 29.6 %collective-permute-start.70 = (bf16[1,32,1536]{2,1,0:T(8,128)(2,1)S(1)}, bf16[1,32,1536]{2,1,0:T(8,128)(2,1)}, u32[]{:S(2)}, u32[]{:S(2)}) collective-permute-start(bf16[1,32,1536]{2,1,0:T(8,128)(2,1)S(1)} %fusion.46), channel_id=1, source_target_pairs={{0,2},{1,3},{2,0},{3,1},{4,6},{5,7},{6,4},{7,5},{8,10},{9,11},{10,... | collective-permute-start | bytes 294920 | tf_op jit(solution)/shard_map/ppermute | solution.py:432
  8.4 29.5 %collective-permute-start.72 = (bf16[1,32,1536]{2,1,0:T(8,128)(2,1)S(1)}, bf16[1,32,1536]{2,1,0:T(8,128)(2,1)}, u32[]{:S(2)}, u32[]{:S(2)}) collective-permute-start(bf16[1,32,1536]{2,1,0:T(8,128)(2,1)S(1)} %fusion.46), channel_id=1, source_target_pairs={{0,6},{1,7},{2,4},{3,5},{4,2},{5,3},{6,0},{7,1},{8,14},{9,15},{10,... | collective-permute-start | bytes 294920 | tf_op jit(solution)/shard_map/ppermute | solution.py:432
  14.3 26.6 %collective-permute-start.6 = (bf16[1,32,1536]{2,1,0:T(8,128)(2,1)S(1)}, bf16[1,32,1536]{2,1,0:T(8,128)(2,1)}, u32[]{:S(2)}, u32[]{:S(2)}) collective-permute-start(bf16[1,32,1536]{2,1,0:T(8,128)(2,1)S(1)} %fusion.47), channel_id=1, source_target_pairs={{0,4},{1,5},{2,6},{3,7},{4,0},{5,1},{6,2},{7,3},{8,12},{9,13},{10,... | collective-permute-start | bytes 294920 | tf_op jit(solution)/shard_map/ppermute | solution.py:432
  36.4 33.8 %collective-permute-start.18 = (bf16[2,32,1536]{2,1,0:T(8,128)(2,1)S(1)}, bf16[2,32,1536]{2,1,0:T(8,128)(2,1)S(1)}, u32[]{:S(2)}, u32[]{:S(2)}) collective-permute-start(bf16[2,32,1536]{2,1,0:T(8,128)(2,1)S(1)} %fusion.31), channel_id=1, source_target_pairs={{0,4},{1,5},{2,6},{3,7},{4,0},{5,1},{6,2},{7,3},{8,12},{9,13},{10,... | collective-permute-start | bytes 589832 | tf_op jit(solution)/shard_map/ppermute | solution.py:432
  38.0 34.7 %collective-permute-start.17 = (bf16[2,32,1536]{2,1,0:T(8,128)(2,1)S(1)}, bf16[2,32,1536]{2,1,0:T(8,128)(2,1)S(1)}, u32[]{:S(2)}, u32[]{:S(2)}) collective-permute-start(bf16[2,32,1536]{2,1,0:T(8,128)(2,1)S(1)} %fusion.31), channel_id=1, source_target_pairs={{0,2},{1,3},{2,0},{3,1},{4,6},{5,7},{6,4},{7,5},{8,10},{9,11},{10,... | collective-permute-start | bytes 589832 | tf_op jit(solution)/shard_map/ppermute | solution.py:432
  40.9 32.8 %collective-permute-start.19 = (bf16[2,32,1536]{2,1,0:T(8,128)(2,1)S(1)}, bf16[2,32,1536]{2,1,0:T(8,128)(2,1)S(1)}, u32[]{:S(2)}, u32[]{:S(2)}) collective-permute-start(bf16[2,32,1536]{2,1,0:T(8,128)(2,1)S(1)} %fusion.31), channel_id=1, source_target_pairs={{0,6},{1,7},{2,4},{3,5},{4,2},{5,3},{6,0},{7,1},{8,14},{9,15},{10,... | collective-permute-start | bytes 589832 | tf_op jit(solution)/shard_map/ppermute | solution.py:432
  41.1 34.1 %collective-permute-start.47 = (bf16[3,32,1536]{2,1,0:T(8,128)(2,1)S(1)}, bf16[3,32,1536]{2,1,0:T(8,128)(2,1)S(1)}, u32[]{:S(2)}, u32[]{:S(2)}) collective-permute-start(bf16[3,32,1536]{2,1,0:T(8,128)(2,1)S(1)} %fusion.20), channel_id=1, source_target_pairs={{0,4},{1,5},{2,6},{3,7},{4,0},{5,1},{6,2},{7,3},{8,12},{9,13},{10,... | collective-permute-start | bytes 884744 | tf_op jit(solution)/shard_map/ppermute | solution.py:432
  43.9 26.3 %collective-permute-start.4 = (f32[12,512]{1,0:T(8,128)S(1)}, f32[12,512]{1,0:T(8,128)S(1)}, u32[]{:S(2)}, u32[]{:S(2)}) collective-permute-start(f32[12,512]{1,0:T(8,128)S(1)} %pad_maximum_fusion.23), channel_id=1, source_target_pairs={{0,4},{1,5},{2,6},{3,7},{4,0},{5,1},{6,2},{7,3},{8,12},{9,13},{10,... | collective-permute-start | bytes 73736 | tf_op jit(solution)/shard_map/ppermute | solution.py:432
  72.6 34.3 %collective-permute-start.30 = (bf16[3,32,1536]{2,1,0:T(8,128)(2,1)S(1)}, bf16[3,32,1536]{2,1,0:T(8,128)(2,1)S(1)}, u32[]{:S(2)}, u32[]{:S(2)}) collective-permute-start(bf16[3,32,1536]{2,1,0:T(8,128)(2,1)S(1)} %fusion.21), channel_id=1, source_target_pairs={{0,4},{1,5},{2,6},{3,7},{4,0},{5,1},{6,2},{7,3},{8,12},{9,13},{10,... | collective-permute-start | bytes 884744 | tf_op jit(solution)/shard_map/ppermute | solution.py:432
  73.7 34.7 %collective-permute-start.9 = (bf16[4,1,32,1536]{3,2,1,0:T(8,128)(2,1)S(1)}, bf16[4,1,32,1536]{3,2,1,0:T(8,128)(2,1)S(1)}, u32[]{:S(2)}, u32[]{:S(2)}) collective-permute-start(bf16[4,1,32,1536]{3,2,1,0:T(8,128)(2,1)S(1)} %pad_maximum_fusion.12.refs_5_.refs_8_), channel_id=1, source_target_pairs={{0,16},{8,24},{16,0},{24,8},{1,17},{9,25},{17,1},{25,9},{2,18},{10... | collective-permute-start | bytes 1179656 | tf_op jit(solution)/shard_map/ppermute | solution.py:426
  75.2 34.7 %collective-permute-start.8 = (bf16[4,1,32,1536]{3,2,1,0:T(8,128)(2,1)S(1)}, bf16[4,1,32,1536]{3,2,1,0:T(8,128)(2,1)S(1)}, u32[]{:S(2)}, u32[]{:S(2)}) collective-permute-start(bf16[4,1,32,1536]{3,2,1,0:T(8,128)(2,1)S(1)} %pad_maximum_fusion.12.refs_5_.refs_8_), channel_id=1, source_target_pairs={{0,1},{1,0},{2,3},{3,2},{4,5},{5,4},{6,7},{7,6},{8,9},{9,8},{10,11... | collective-permute-start | bytes 1179656 | tf_op jit(solution)/shard_map/ppermute | solution.py:429
  84.8 25.9 %collective-permute-start.29 = (bf16[3,32,1536]{2,1,0:T(8,128)(2,1)S(1)}, bf16[3,32,1536]{2,1,0:T(8,128)(2,1)S(1)}, u32[]{:S(2)}, u32[]{:S(2)}) collective-permute-start(bf16[3,32,1536]{2,1,0:T(8,128)(2,1)S(1)} %fusion.21), channel_id=1, source_target_pairs={{0,2},{1,3},{2,0},{3,1},{4,6},{5,7},{6,4},{7,5},{8,10},{9,11},{10,... | collective-permute-start | bytes 884744 | tf_op jit(solution)/shard_map/ppermute | solution.py:432
  87.0 24.3 %collective-permute-start.31 = (bf16[3,32,1536]{2,1,0:T(8,128)(2,1)S(1)}, bf16[3,32,1536]{2,1,0:T(8,128)(2,1)S(1)}, u32[]{:S(2)}, u32[]{:S(2)}) collective-permute-start(bf16[3,32,1536]{2,1,0:T(8,128)(2,1)S(1)} %fusion.21), channel_id=1, source_target_pairs={{0,6},{1,7},{2,4},{3,5},{4,2},{5,3},{6,0},{7,1},{8,14},{9,15},{10,... | collective-permute-start | bytes 884744 | tf_op jit(solution)/shard_map/ppermute | solution.py:432
  106.9 24.6 %collective-permute-start.21 = (bf16[4,2,32,1536]{3,2,1,0:T(8,128)(2,1)S(1)}, bf16[4,2,32,1536]{3,2,1,0:T(8,128)(2,1)}, u32[]{:S(2)}, u32[]{:S(2)}) collective-permute-start(bf16[4,2,32,1536]{3,2,1,0:T(8,128)(2,1)S(1)} %pad_maximum_fusion.6.refs_5_.refs_8_), channel_id=1, source_target_pairs={{0,16},{8,24},{16,0},{24,8},{1,17},{9,25},{17,1},{25,9},{2,18},{10... | collective-permute-start | bytes 2359304 | tf_op jit(solution)/shard_map/ppermute | solution.py:426
  112.0 49.6 %collective-permute-start.33 = (bf16[4,3,32,1536]{3,2,1,0:T(8,128)(2,1)S(1)}, bf16[4,3,32,1536]{3,2,1,0:T(8,128)(2,1)}, u32[]{:S(2)}, u32[]{:S(2)}) collective-permute-start(bf16[4,3,32,1536]{3,2,1,0:T(8,128)(2,1)S(1)} %pad_maximum_fusion.refs_5_.refs_8_), channel_id=1, source_target_pairs={{0,16},{8,24},{16,0},{24,8},{1,17},{9,25},{17,1},{25,9},{2,18},{10... | collective-permute-start | bytes 3538952 | tf_op jit(solution)/shard_map/ppermute | solution.py:426
  128.3 33.8 %collective-permute-start.32 = (bf16[4,3,32,1536]{3,2,1,0:T(8,128)(2,1)S(1)}, bf16[4,3,32,1536]{3,2,1,0:T(8,128)(2,1)}, u32[]{:S(2)}, u32[]{:S(2)}) collective-permute-start(bf16[4,3,32,1536]{3,2,1,0:T(8,128)(2,1)S(1)} %pad_maximum_fusion.refs_5_.refs_8_), channel_id=1, source_target_pairs={{0,1},{1,0},{2,3},{3,2},{4,5},{5,4},{6,7},{7,6},{8,9},{9,8},{10,11... | collective-permute-start | bytes 3538952 | tf_op jit(solution)/shard_map/ppermute | solution.py:429
  137.5 31.0 %collective-permute-start.24 = (bf16[4,2,32,1536]{3,2,1,0:T(8,128)(2,1)S(1)}, bf16[4,2,32,1536]{3,2,1,0:T(8,128)(2,1)}, u32[]{:S(2)}, u32[]{:S(2)}) collective-permute-start(bf16[4,2,32,1536]{3,2,1,0:T(8,128)(2,1)S(1)} %pad_maximum_fusion.6.refs_5_.refs_8_), channel_id=1, source_target_pairs={{0,8},{8,0},{16,24},{24,16},{1,9},{9,1},{17,25},{25,17},{2,10},{10... | collective-permute-start | bytes 2359304 | tf_op jit(solution)/shard_map/ppermute | solution.py:423
  168.5 42.5 %collective-permute-start.36 = (bf16[4,3,32,1536]{3,2,1,0:T(8,128)(2,1)S(1)}, bf16[4,3,32,1536]{3,2,1,0:T(8,128)(2,1)}, u32[]{:S(2)}, u32[]{:S(2)}) collective-permute-start(bf16[4,3,32,1536]{3,2,1,0:T(8,128)(2,1)S(1)} %pad_maximum_fusion.refs_5_.refs_8_), channel_id=1, source_target_pairs={{0,8},{8,0},{16,24},{24,16},{1,9},{9,1},{17,25},{25,17},{2,10},{10... | collective-permute-start | bytes 3538952 | tf_op jit(solution)/shard_map/ppermute | solution.py:423
  171.0 40.1 %collective-permute-start.38 = (bf16[4,3,32,1536]{3,2,1,0:T(8,128)(2,1)}, bf16[4,3,32,1536]{3,2,1,0:T(8,128)(2,1)}, u32[]{:S(2)}, u32[]{:S(2)}) collective-permute-start(bf16[4,3,32,1536]{3,2,1,0:T(8,128)(2,1)} %collective-permute-done.33.refs_7_.refs_10_), channel_id=1, source_target_pairs={{0,8},{8,0},{16,24},{24,16},{1,9},{9,1},{17,25},{25,17},{2,10},{10... | collective-permute-start | bytes 3538952 | tf_op jit(solution)/shard_map/ppermute | solution.py:423
  171.0 45.4 %collective-permute-start.37 = (bf16[4,3,32,1536]{3,2,1,0:T(8,128)(2,1)}, bf16[4,3,32,1536]{3,2,1,0:T(8,128)(2,1)}, u32[]{:S(2)}, u32[]{:S(2)}) collective-permute-start(bf16[4,3,32,1536]{3,2,1,0:T(8,128)(2,1)} %collective-permute-done.32.refs_6_.refs_9_), channel_id=1, source_target_pairs={{0,8},{8,0},{16,24},{24,16},{1,9},{9,1},{17,25},{25,17},{2,10},{10... | collective-permute-start | bytes 3538952 | tf_op jit(solution)/shard_map/ppermute | solution.py:423
  184.6 31.8 %collective-permute-start.40 = (bf16[2,3,32,1536]{3,2,1,0:T(8,128)(2,1)}, bf16[2,3,32,1536]{3,2,1,0:T(8,128)(2,1)S(1)}, u32[]{:S(2)}, u32[]{:S(2)}) collective-permute-start(bf16[2,3,32,1536]{3,2,1,0:T(8,128)(2,1)} %collective-permute-done.35.refs_9_.refs_12_), channel_id=1, source_target_pairs={{0,8},{8,0},{16,24},{24,16},{1,9},{9,1},{17,25},{25,17},{2,10},{10... | collective-permute-start | bytes 1769480 | tf_op jit(solution)/shard_map/ppermute | solution.py:423
  185.6 31.4 %collective-permute-start.39 = (bf16[2,3,32,1536]{3,2,1,0:T(8,128)(2,1)}, bf16[2,3,32,1536]{3,2,1,0:T(8,128)(2,1)}, u32[]{:S(2)}, u32[]{:S(2)}) collective-permute-start(bf16[2,3,32,1536]{3,2,1,0:T(8,128)(2,1)} %collective-permute-done.34.refs_8_.refs_11_), channel_id=1, source_target_pairs={{0,8},{8,0},{16,24},{24,16},{1,9},{9,1},{17,25},{25,17},{2,10},{10... | collective-permute-start | bytes 1769480 | tf_op jit(solution)/shard_map/ppermute | solution.py:423
  211.0 30.3 %collective-permute-start.59 = (bf16[2,32,1536]{2,1,0:T(8,128)(2,1)S(1)}, bf16[2,32,1536]{2,1,0:T(8,128)(2,1)S(1)}, u32[]{:S(2)}, u32[]{:S(2)}) collective-permute-start(bf16[2,32,1536]{2,1,0:T(8,128)(2,1)S(1)} %fusion.30), channel_id=1, source_target_pairs={{0,4},{1,5},{2,6},{3,7},{4,0},{5,1},{6,2},{7,3},{8,12},{9,13},{10,... | collective-permute-start | bytes 589832 | tf_op jit(solution)/shard_map/ppermute | solution.py:432
  211.1 30.2 %collective-permute-start.58 = (bf16[2,32,1536]{2,1,0:T(8,128)(2,1)S(1)}, bf16[2,32,1536]{2,1,0:T(8,128)(2,1)S(1)}, u32[]{:S(2)}, u32[]{:S(2)}) collective-permute-start(bf16[2,32,1536]{2,1,0:T(8,128)(2,1)S(1)} %fusion.30), channel_id=1, source_target_pairs={{0,2},{1,3},{2,0},{3,1},{4,6},{5,7},{6,4},{7,5},{8,10},{9,11},{10,... | collective-permute-start | bytes 589832 | tf_op jit(solution)/shard_map/ppermute | solution.py:432
  216.4 24.8 %collective-permute-start.60 = (bf16[2,32,1536]{2,1,0:T(8,128)(2,1)S(1)}, bf16[2,32,1536]{2,1,0:T(8,128)(2,1)S(1)}, u32[]{:S(2)}, u32[]{:S(2)}) collective-permute-start(bf16[2,32,1536]{2,1,0:T(8,128)(2,1)S(1)} %fusion.30), channel_id=1, source_target_pairs={{0,6},{1,7},{2,4},{3,5},{4,2},{5,3},{6,0},{7,1},{8,14},{9,15},{10,... | collective-permute-start | bytes 589832 | tf_op jit(solution)/shard_map/ppermute | solution.py:432
  216.4 27.7 %collective-permute-start.74 = (bf16[4,1,32,1536]{3,2,1,0:T(8,128)(2,1)}, bf16[4,1,32,1536]{3,2,1,0:T(8,128)(2,1)S(1)}, u32[]{:S(2)}, u32[]{:S(2)}) collective-permute-start(bf16[4,1,32,1536]{3,2,1,0:T(8,128)(2,1)} %pad_maximum_fusion.13.refs_5_.refs_8_), channel_id=1, source_target_pairs={{0,16},{8,24},{16,0},{24,8},{1,17},{9,25},{17,1},{25,9},{2,18},{10... | collective-permute-start | bytes 1179656 | tf_op jit(solution)/shard_map/ppermute | solution.py:426
  217.0 84.1 %collective-permute-start.50 = (bf16[4,3,32,1536]{3,2,1,0:T(8,128)(2,1)S(1)}, bf16[4,3,32,1536]{3,2,1,0:T(8,128)(2,1)}, u32[]{:S(2)}, u32[]{:S(2)}) collective-permute-start(bf16[4,3,32,1536]{3,2,1,0:T(8,128)(2,1)S(1)} %pad_maximum_fusion.1.refs_5_.refs_8_), channel_id=1, source_target_pairs={{0,16},{8,24},{16,0},{24,8},{1,17},{9,25},{17,1},{25,9},{2,18},{10... | collective-permute-start | bytes 3538952 | tf_op jit(solution)/shard_map/ppermute | solution.py:426
  241.4 55.0 %collective-permute-start.62 = (bf16[4,2,32,1536]{3,2,1,0:T(8,128)(2,1)S(1)}, bf16[4,2,32,1536]{3,2,1,0:T(8,128)(2,1)}, u32[]{:S(2)}, u32[]{:S(2)}) collective-permute-start(bf16[4,2,32,1536]{3,2,1,0:T(8,128)(2,1)S(1)} %pad_maximum_fusion.7.refs_5_.refs_8_), channel_id=1, source_target_pairs={{0,16},{8,24},{16,0},{24,8},{1,17},{9,25},{17,1},{25,9},{2,18},{10... | collective-permute-start | bytes 2359304 | tf_op jit(solution)/shard_map/ppermute | solution.py:426
  242.0 56.5 %collective-permute-start.61 = (bf16[4,2,32,1536]{3,2,1,0:T(8,128)(2,1)S(1)}, bf16[4,2,32,1536]{3,2,1,0:T(8,128)(2,1)}, u32[]{:S(2)}, u32[]{:S(2)}) collective-permute-start(bf16[4,2,32,1536]{3,2,1,0:T(8,128)(2,1)S(1)} %pad_maximum_fusion.7.refs_5_.refs_8_), channel_id=1, source_target_pairs={{0,1},{1,0},{2,3},{3,2},{4,5},{5,4},{6,7},{7,6},{8,9},{9,8},{10,11... | collective-permute-start | bytes 2359304 | tf_op jit(solution)/shard_map/ppermute | solution.py:429
  243.0 61.6 %collective-permute-start.49 = (bf16[4,3,32,1536]{3,2,1,0:T(8,128)(2,1)S(1)}, bf16[4,3,32,1536]{3,2,1,0:T(8,128)(2,1)S(1)}, u32[]{:S(2)}, u32[]{:S(2)}) collective-permute-start(bf16[4,3,32,1536]{3,2,1,0:T(8,128)(2,1)S(1)} %pad_maximum_fusion.1.refs_5_.refs_8_), channel_id=1, source_target_pairs={{0,1},{1,0},{2,3},{3,2},{4,5},{5,4},{6,7},{7,6},{8,9},{9,8},{10,11... | collective-permute-start | bytes 3538952 | tf_op jit(solution)/shard_map/ppermute | solution.py:429
  244.1 26.4 %collective-permute-start.42 = (f32[12,512]{1,0:T(8,128)S(1)}, f32[12,512]{1,0:T(8,128)S(1)}, u32[]{:S(2)}, u32[]{:S(2)}) collective-permute-start(f32[12,512]{1,0:T(8,128)S(1)} %pad_maximum_fusion.25), channel_id=1, source_target_pairs={{0,16},{8,24},{16,0},{24,8},{1,17},{9,25},{17,1},{25,9},{2,18},{10... | collective-permute-start | bytes 73736 | tf_op jit(solution)/shard_map/ppermute | solution.py:426
  270.5 24.8 %collective-permute-start.73 = (bf16[4,1,32,1536]{3,2,1,0:T(8,128)(2,1)}, bf16[4,1,32,1536]{3,2,1,0:T(8,128)(2,1)S(1)}, u32[]{:S(2)}, u32[]{:S(2)}) collective-permute-start(bf16[4,1,32,1536]{3,2,1,0:T(8,128)(2,1)} %pad_maximum_fusion.13.refs_5_.refs_8_), channel_id=1, source_target_pairs={{0,1},{1,0},{2,3},{3,2},{4,5},{5,4},{6,7},{7,6},{8,9},{9,8},{10,11... | collective-permute-start | bytes 1179656 | tf_op jit(solution)/shard_map/ppermute | solution.py:429
  304.0 27.9 %collective-permute-start.53 = (bf16[4,3,32,1536]{3,2,1,0:T(8,128)(2,1)S(1)}, bf16[4,3,32,1536]{3,2,1,0:T(8,128)(2,1)S(1)}, u32[]{:S(2)}, u32[]{:S(2)}) collective-permute-start(bf16[4,3,32,1536]{3,2,1,0:T(8,128)(2,1)S(1)} %pad_maximum_fusion.1.refs_5_.refs_8_), channel_id=1, source_target_pairs={{0,8},{8,0},{16,24},{24,16},{1,9},{9,1},{17,25},{25,17},{2,10},{10... | collective-permute-start | bytes 3538952 | tf_op jit(solution)/shard_map/ppermute | solution.py:423
  304.4 28.1 %collective-permute-start.55 = (bf16[4,3,32,1536]{3,2,1,0:T(8,128)(2,1)}, bf16[4,3,32,1536]{3,2,1,0:T(8,128)(2,1)S(1)}, u32[]{:S(2)}, u32[]{:S(2)}) collective-permute-start(bf16[4,3,32,1536]{3,2,1,0:T(8,128)(2,1)} %collective-permute-done.50.refs_7_.refs_10_), channel_id=1, source_target_pairs={{0,8},{8,0},{16,24},{24,16},{1,9},{9,1},{17,25},{25,17},{2,10},{10... | collective-permute-start | bytes 3538952 | tf_op jit(solution)/shard_map/ppermute | solution.py:423
  304.6 28.0 %collective-permute-start.54 = (bf16[4,3,32,1536]{3,2,1,0:T(8,128)(2,1)S(1)}, bf16[4,3,32,1536]{3,2,1,0:T(8,128)(2,1)S(1)}, u32[]{:S(2)}, u32[]{:S(2)}) collective-permute-start(bf16[4,3,32,1536]{3,2,1,0:T(8,128)(2,1)S(1)} %collective-permute-done.49.refs_6_.refs_9_), channel_id=1, source_target_pairs={{0,8},{8,0},{16,24},{24,16},{1,9},{9,1},{17,25},{25,17},{2,10},{10... | collective-permute-start | bytes 3538952 | tf_op jit(solution)/shard_map/ppermute | solution.py:423
  331.9 24.8 %collective-permute-start.65 = (bf16[4,2,32,1536]{3,2,1,0:T(8,128)(2,1)S(1)}, bf16[4,2,32,1536]{3,2,1,0:T(8,128)(2,1)S(1)}, u32[]{:S(2)}, u32[]{:S(2)}) collective-permute-start(bf16[4,2,32,1536]{3,2,1,0:T(8,128)(2,1)S(1)} %pad_maximum_fusion.7.refs_5_.refs_8_), channel_id=1, source_target_pairs={{0,8},{8,0},{16,24},{24,16},{1,9},{9,1},{17,25},{25,17},{2,10},{10... | collective-permute-start | bytes 2359304 | tf_op jit(solution)/shard_map/ppermute | solution.py:423
  332.5 24.8 %collective-permute-start.67 = (bf16[4,2,32,1536]{3,2,1,0:T(8,128)(2,1)}, bf16[4,2,32,1536]{3,2,1,0:T(8,128)(2,1)S(1)}, u32[]{:S(2)}, u32[]{:S(2)}) collective-permute-start(bf16[4,2,32,1536]{3,2,1,0:T(8,128)(2,1)} %collective-permute-done.62.refs_7_.refs_10_), channel_id=1, source_target_pairs={{0,8},{8,0},{16,24},{24,16},{1,9},{9,1},{17,25},{25,17},{2,10},{10... | collective-permute-start | bytes 2359304 | tf_op jit(solution)/shard_map/ppermute | solution.py:423
  332.6 25.3 %collective-permute-start.66 = (bf16[4,2,32,1536]{3,2,1,0:T(8,128)(2,1)}, bf16[4,2,32,1536]{3,2,1,0:T(8,128)(2,1)}, u32[]{:S(2)}, u32[]{:S(2)}) collective-permute-start(bf16[4,2,32,1536]{3,2,1,0:T(8,128)(2,1)} %collective-permute-done.61.refs_6_.refs_9_), channel_id=1, source_target_pairs={{0,8},{8,0},{16,24},{24,16},{1,9},{9,1},{17,25},{25,17},{2,10},{10... | collective-permute-start | bytes 2359304 | tf_op jit(solution)/shard_map/ppermute | solution.py:423
  481.9 90.1 %collective-permute-start.92 = (f32[6,2048]{1,0:T(8,128)S(1)}, f32[6,2048]{1,0:T(8,128)S(1)}, u32[]{:S(2)}, u32[]{:S(2)}) collective-permute-start(f32[6,2048]{1,0:T(8,128)S(1)} %maximum_maximum_fusion.1), channel_id=1, source_target_pairs={{0,8},{8,0},{16,24},{24,16},{1,9},{9,1},{17,25},{25,17},{2,10},{10... | collective-permute-start | bytes 147464 | tf_op jit(solution)/shard_map/ppermute | solution.py:423
  574.1 28.8 %collective-permute-start.152 = (bf16[16,1,32,1536]{3,2,1,0:T(8,128)(2,1)}, bf16[16,1,32,1536]{3,2,1,0:T(8,128)(2,1)}, u32[]{:S(2)}, u32[]{:S(2)}) collective-permute-start(bf16[16,1,32,1536]{3,2,1,0:T(8,128)(2,1)} %get-tuple-element.221), channel_id=1, source_target_pairs={{0,8},{8,0},{16,24},{24,16},{1,9},{9,1},{17,25},{25,17},{2,10},{10... | collective-permute-start | bytes 4718600 | tf_op jit(solution)/shard_map/ppermute | solution.py:423
  591.4 73.1 %collective-permute-start.141 = (bf16[16,2,32,1536]{3,2,1,0:T(8,128)(2,1)}, bf16[16,2,32,1536]{3,2,1,0:T(8,128)(2,1)}, u32[]{:S(2)}, u32[]{:S(2)}) collective-permute-start(bf16[16,2,32,1536]{3,2,1,0:T(8,128)(2,1)} %get-tuple-element.215), channel_id=1, source_target_pairs={{0,8},{8,0},{16,24},{24,16},{1,9},{9,1},{17,25},{25,17},{2,10},{10... | collective-permute-start | bytes 9437192 | tf_op jit(solution)/shard_map/ppermute | solution.py:423
  592.9 74.5 %collective-permute-start.108 = (bf16[16,2,32,1536]{3,2,1,0:T(8,128)(2,1)}, bf16[16,2,32,1536]{3,2,1,0:T(8,128)(2,1)S(1)}, u32[]{:S(2)}, u32[]{:S(2)}) collective-permute-start(bf16[16,2,32,1536]{3,2,1,0:T(8,128)(2,1)} %get-tuple-element.197), channel_id=1, source_target_pairs={{0,8},{8,0},{16,24},{24,16},{1,9},{9,1},{17,25},{25,17},{2,10},{10... | collective-permute-start | bytes 9437192 | tf_op jit(solution)/shard_map/ppermute | solution.py:423
  658.3 60.2 %collective-permute-start.130 = (bf16[16,3,32,1536]{3,2,1,0:T(8,128)(2,1)}, bf16[16,3,32,1536]{3,2,1,0:T(8,128)(2,1)S(1)}, u32[]{:S(2)}, u32[]{:S(2)}) collective-permute-start(bf16[16,3,32,1536]{3,2,1,0:T(8,128)(2,1)} %get-tuple-element.209), channel_id=1, source_target_pairs={{0,8},{8,0},{16,24},{24,16},{1,9},{9,1},{17,25},{25,17},{2,10},{10... | collective-permute-start | bytes 14155784 | tf_op jit(solution)/shard_map/ppermute | solution.py:423
  658.6 72.7 %collective-permute-start.119 = (bf16[16,3,32,1536]{3,2,1,0:T(8,128)(2,1)S(1)}, bf16[16,3,32,1536]{3,2,1,0:T(8,128)(2,1)S(1)}, u32[]{:S(2)}, u32[]{:S(2)}) collective-permute-start(bf16[16,3,32,1536]{3,2,1,0:T(8,128)(2,1)S(1)} %copy-done.107), channel_id=1, source_target_pairs={{0,8},{8,0},{16,24},{24,16},{1,9},{9,1},{17,25},{25,17},{2,10},{10... | collective-permute-start | bytes 14155784 | tf_op jit(solution)/shard_map/ppermute | solution.py:423
  680.0 34.8 %collective-permute-start.143 = (bf16[4,2,32,1536]{3,2,1,0:T(8,128)(2,1)S(1)}, bf16[4,2,32,1536]{3,2,1,0:T(8,128)(2,1)S(1)}, u32[]{:S(2)}, u32[]{:S(2)}) collective-permute-start(bf16[4,2,32,1536]{3,2,1,0:T(8,128)(2,1)S(1)} %pad_maximum_fusion.10), channel_id=1, source_target_pairs={{0,1},{1,0},{2,3},{3,2},{4,5},{5,4},{6,7},{7,6},{8,9},{9,8},{10,11... | collective-permute-start | bytes 2359304 | tf_op jit(solution)/shard_map/ppermute | solution.py:429
  681.8 31.7 %collective-permute-start.111 = (bf16[2,2,32,1536]{3,2,1,0:T(8,128)(2,1)S(1)}, bf16[2,2,32,1536]{3,2,1,0:T(8,128)(2,1)S(1)}, u32[]{:S(2)}, u32[]{:S(2)}) collective-permute-start(bf16[2,2,32,1536]{3,2,1,0:T(8,128)(2,1)S(1)} %get-tuple-element.323), channel_id=1, source_target_pairs={{0,1},{1,0},{2,3},{3,2},{4,5},{5,4},{6,7},{7,6},{8,9},{9,8},{10,11... | collective-permute-start | bytes 1179656 | tf_op jit(solution)/shard_map/ppermute | solution.py:429
  692.5 24.2 %collective-permute-start.145 = (bf16[4,2,32,1536]{3,2,1,0:T(8,128)(2,1)S(1)}, bf16[4,2,32,1536]{3,2,1,0:T(8,128)(2,1)S(1)}, u32[]{:S(2)}, u32[]{:S(2)}) collective-permute-start(bf16[4,2,32,1536]{3,2,1,0:T(8,128)(2,1)S(1)} %pad_maximum_fusion.11), channel_id=1, source_target_pairs={{0,16},{8,24},{16,0},{24,8},{1,17},{9,25},{17,1},{25,9},{2,18},{10... | collective-permute-start | bytes 2359304 | tf_op jit(solution)/shard_map/ppermute | solution.py:426
  718.1 72.1 %collective-permute-start.146 = (bf16[2,32,1536]{2,1,0:T(8,128)(2,1)S(1)}, bf16[2,32,1536]{2,1,0:T(8,128)(2,1)S(1)}, u32[]{:S(2)}, u32[]{:S(2)}) collective-permute-start(bf16[2,32,1536]{2,1,0:T(8,128)(2,1)S(1)} %get-tuple-element.306), channel_id=1, source_target_pairs={{0,2},{1,3},{2,0},{3,1},{4,6},{5,7},{6,4},{7,5},{8,10},{9,11},{10,... | collective-permute-start | bytes 589832 | tf_op jit(solution)/shard_map/ppermute | solution.py:432
  718.5 72.9 %collective-permute-start.148 = (bf16[2,32,1536]{2,1,0:T(8,128)(2,1)S(1)}, bf16[2,32,1536]{2,1,0:T(8,128)(2,1)S(1)}, u32[]{:S(2)}, u32[]{:S(2)}) collective-permute-start(bf16[2,32,1536]{2,1,0:T(8,128)(2,1)S(1)} %get-tuple-element.307), channel_id=1, source_target_pairs={{0,6},{1,7},{2,4},{3,5},{4,2},{5,3},{6,0},{7,1},{8,14},{9,15},{10,... | collective-permute-start | bytes 589832 | tf_op jit(solution)/shard_map/ppermute | solution.py:432
  725.5 67.8 %collective-permute-start.147 = (bf16[2,32,1536]{2,1,0:T(8,128)(2,1)S(1)}, bf16[2,32,1536]{2,1,0:T(8,128)(2,1)S(1)}, u32[]{:S(2)}, u32[]{:S(2)}) collective-permute-start(bf16[2,32,1536]{2,1,0:T(8,128)(2,1)S(1)} %get-tuple-element.308), channel_id=1, source_target_pairs={{0,4},{1,5},{2,6},{3,7},{4,0},{5,1},{6,2},{7,3},{8,12},{9,13},{10,... | collective-permute-start | bytes 589832 | tf_op jit(solution)/shard_map/ppermute | solution.py:432
  731.3 62.1 %collective-permute-start.113 = (bf16[2,32,1536]{2,1,0:T(8,128)(2,1)S(1)}, bf16[2,32,1536]{2,1,0:T(8,128)(2,1)S(1)}, u32[]{:S(2)}, u32[]{:S(2)}) collective-permute-start(bf16[2,32,1536]{2,1,0:T(8,128)(2,1)S(1)} %get-tuple-element.309), channel_id=1, source_target_pairs={{0,2},{1,3},{2,0},{3,1},{4,6},{5,7},{6,4},{7,5},{8,10},{9,11},{10,... | collective-permute-start | bytes 589832 | tf_op jit(solution)/shard_map/ppermute | solution.py:432
  790.2 25.6 %collective-permute-start.132 = (bf16[4,3,32,1536]{3,2,1,0:T(8,128)(2,1)S(1)}, bf16[4,3,32,1536]{3,2,1,0:T(8,128)(2,1)S(1)}, u32[]{:S(2)}, u32[]{:S(2)}) collective-permute-start(bf16[4,3,32,1536]{3,2,1,0:T(8,128)(2,1)S(1)} %pad_maximum_fusion.4), channel_id=1, source_target_pairs={{0,1},{1,0},{2,3},{3,2},{4,5},{5,4},{6,7},{7,6},{8,9},{9,8},{10,11... | collective-permute-start | bytes 3538952 | tf_op jit(solution)/shard_map/ppermute | solution.py:429
  791.4 24.4 %collective-permute-start.134 = (bf16[4,3,32,1536]{3,2,1,0:T(8,128)(2,1)S(1)}, bf16[4,3,32,1536]{3,2,1,0:T(8,128)(2,1)S(1)}, u32[]{:S(2)}, u32[]{:S(2)}) collective-permute-start(bf16[4,3,32,1536]{3,2,1,0:T(8,128)(2,1)S(1)} %pad_maximum_fusion.5), channel_id=1, source_target_pairs={{0,16},{8,24},{16,0},{24,8},{1,17},{9,25},{17,1},{25,9},{2,18},{10... | collective-permute-start | bytes 3538952 | tf_op jit(solution)/shard_map/ppermute | solution.py:426
  793.3 35.1 %collective-permute-start.121 = (bf16[4,3,32,1536]{3,2,1,0:T(8,128)(2,1)S(1)}, bf16[4,3,32,1536]{3,2,1,0:T(8,128)(2,1)S(1)}, u32[]{:S(2)}, u32[]{:S(2)}) collective-permute-start(bf16[4,3,32,1536]{3,2,1,0:T(8,128)(2,1)S(1)} %pad_maximum_fusion.2), channel_id=1, source_target_pairs={{0,1},{1,0},{2,3},{3,2},{4,5},{5,4},{6,7},{7,6},{8,9},{9,8},{10,11... | collective-permute-start | bytes 3538952 | tf_op jit(solution)/shard_map/ppermute | solution.py:429
  794.3 38.5 %collective-permute-start.123 = (bf16[4,3,32,1536]{3,2,1,0:T(8,128)(2,1)S(1)}, bf16[4,3,32,1536]{3,2,1,0:T(8,128)(2,1)S(1)}, u32[]{:S(2)}, u32[]{:S(2)}) collective-permute-start(bf16[4,3,32,1536]{3,2,1,0:T(8,128)(2,1)S(1)} %pad_maximum_fusion.3), channel_id=1, source_target_pairs={{0,16},{8,24},{16,0},{24,8},{1,17},{9,25},{17,1},{25,9},{2,18},{10... | collective-permute-start | bytes 3538952 | tf_op jit(solution)/shard_map/ppermute | solution.py:426
  799.9 62.5 %collective-permute-start.161 = (bf16[1,32,1536]{2,1,0:T(8,128)(2,1)S(1)}, bf16[1,32,1536]{2,1,0:T(8,128)(2,1)S(1)}, u32[]{:S(2)}, u32[]{:S(2)}) collective-permute-start(bf16[1,32,1536]{2,1,0:T(8,128)(2,1)S(1)} %fusion.34.refs_0_), channel_id=1, source_target_pairs={{0,16},{8,24},{16,0},{24,8},{1,17},{9,25},{17,1},{25,9},{2,18},{10... | collective-permute-start | bytes 294920 | tf_op jit(solution)/shard_map/ppermute | solution.py:426
  815.8 58.3 %collective-permute-start.160 = (bf16[1,32,1536]{2,1,0:T(8,128)(2,1)S(1)}, bf16[1,32,1536]{2,1,0:T(8,128)(2,1)S(1)}, u32[]{:S(2)}, u32[]{:S(2)}) collective-permute-start(bf16[1,32,1536]{2,1,0:T(8,128)(2,1)S(1)} %fusion.34.refs_0_), channel_id=1, source_target_pairs={{0,8},{8,0},{16,24},{24,16},{1,9},{9,1},{17,25},{25,17},{2,10},{10... | collective-permute-start | bytes 294920 | tf_op jit(solution)/shard_map/ppermute | solution.py:423
  832.8 29.2 %collective-permute-start.136 = (bf16[3,32,1536]{2,1,0:T(8,128)(2,1)S(1)}, bf16[3,32,1536]{2,1,0:T(8,128)(2,1)S(1)}, u32[]{:S(2)}, u32[]{:S(2)}) collective-permute-start(bf16[3,32,1536]{2,1,0:T(8,128)(2,1)S(1)} %get-tuple-element.294), channel_id=1, source_target_pairs={{0,4},{1,5},{2,6},{3,7},{4,0},{5,1},{6,2},{7,3},{8,12},{9,13},{10,... | collective-permute-start | bytes 884744 | tf_op jit(solution)/shard_map/ppermute | solution.py:432
  833.3 30.9 %collective-permute-start.124 = (bf16[3,32,1536]{2,1,0:T(8,128)(2,1)S(1)}, bf16[3,32,1536]{2,1,0:T(8,128)(2,1)S(1)}, u32[]{:S(2)}, u32[]{:S(2)}) collective-permute-start(bf16[3,32,1536]{2,1,0:T(8,128)(2,1)S(1)} %get-tuple-element.295), channel_id=1, source_target_pairs={{0,2},{1,3},{2,0},{3,1},{4,6},{5,7},{6,4},{7,5},{8,10},{9,11},{10,... | collective-permute-start | bytes 884744 | tf_op jit(solution)/shard_map/ppermute | solution.py:432
  885.7 27.9 %collective-permute-start.116 = (bf16[2,32,1536]{2,1,0:T(8,128)(2,1)S(1)}, bf16[2,32,1536]{2,1,0:T(8,128)(2,1)S(1)}, u32[]{:S(2)}, u32[]{:S(2)}) collective-permute-start(bf16[2,32,1536]{2,1,0:T(8,128)(2,1)S(1)} %fusion.11.refs_0_), channel_id=1, source_target_pairs={{0,8},{8,0},{16,24},{24,16},{1,9},{9,1},{17,25},{25,17},{2,10},{10... | collective-permute-start | bytes 589832 | tf_op jit(solution)/shard_map/ppermute | solution.py:423
  885.9 27.7 %collective-permute-start.118 = (bf16[2,32,1536]{2,1,0:T(8,128)(2,1)S(1)}, bf16[2,32,1536]{2,1,0:T(8,128)(2,1)}, u32[]{:S(2)}, u32[]{:S(2)}) collective-permute-start(bf16[2,32,1536]{2,1,0:T(8,128)(2,1)S(1)} %collective-permute-done.117.refs_2_), channel_id=1, source_target_pairs={{0,8},{8,0},{16,24},{24,16},{1,9},{9,1},{17,25},{25,17},{2,10},{10... | collective-permute-start | bytes 589832 | tf_op jit(solution)/shard_map/ppermute | solution.py:423
  890.6 26.6 %collective-permute-start.105 = (bf16[1,32,1536]{2,1,0:T(8,128)(2,1)}, bf16[1,32,1536]{2,1,0:T(8,128)(2,1)}, u32[]{:S(2)}, u32[]{:S(2)}) collective-permute-start(bf16[1,32,1536]{2,1,0:T(8,128)(2,1)} %fusion.37.refs_0_), channel_id=1, source_target_pairs={{0,8},{8,0},{16,24},{24,16},{1,9},{9,1},{17,25},{25,17},{2,10},{10... | collective-permute-start | bytes 294920 | tf_op jit(solution)/shard_map/ppermute | solution.py:423
  891.1 26.1 %collective-permute-start.107 = (bf16[1,32,1536]{2,1,0:T(8,128)(2,1)}, bf16[1,32,1536]{2,1,0:T(8,128)(2,1)}, u32[]{:S(2)}, u32[]{:S(2)}) collective-permute-start(bf16[1,32,1536]{2,1,0:T(8,128)(2,1)} %collective-permute-done.106.refs_2_), channel_id=1, source_target_pairs={{0,8},{8,0},{16,24},{24,16},{1,9},{9,1},{17,25},{25,17},{2,10},{10... | collective-permute-start | bytes 294920 | tf_op jit(solution)/shard_map/ppermute | solution.py:423
  (231 other events, 3865.4 us)

commit v2 on v1

v2 whole, which is shorter than its diff:
```python
import functools

import jax
import jax.numpy as jnp
from jax import lax
from jax.experimental import pallas as pl
from jax.experimental.pallas import tpu as pltpu
from jax.sharding import PartitionSpec as P

SECTIONS = 6
LAYERS = 2
MB = 4
BF16 = jnp.bfloat16
F32 = jnp.float32
EPSILON = 1e-05
TILE = 256
COST = pl.CostEstimate(flops=1, bytes_accessed=1, transcendentals=0)
LONG = pl.CostEstimate(flops=2 * 10**10, bytes_accessed=1, transcendentals=0)
VMEM_LIMIT = 60 * 1024 * 1024
GATHERS = ((0, 3), (3, 6), (6, 12))
GROUPS = ((0, 3), (3, 6), (6, 9), (9, 12))
RING_SUM = (6, 12)


def gate(x):
    return 0.5 * jnp.tanh(0.5 * x) + 0.5


def load_weights(table, arrays, wbuf, sems, n, pr, first):
    for part, lo, hi in ((0, 0, 1), (1, 1, n)):
        if lo == hi:
            continue
        at = 0
        for array in arrays:
            for slot in range(array.shape[0]):
                row = pl.multiple_of(table[at], pr)
                pltpu.make_async_copy(
                    array.at[slot, pl.ds(first + lo, hi - lo)],
                    wbuf.at[pl.ds(lo, hi - lo), pl.ds(row, pr)],
                    sems.at[part],
                ).start()
                at += 1


def wait_weights(wbuf, sems, n, part):
    lo, hi = (0, 1) if part == 0 else (1, n)
    whole = wbuf.at[pl.ds(lo, hi - lo)]
    pltpu.make_async_copy(whole, whole, sems.at[part]).wait()


def forward_kernel(n, first, n_arrays, n_tokens, pr, tile, table, *refs):
    hidden_in, normed, mask, bias_in, bias_out = refs[:5]
    arrays = refs[5 : 5 + n_arrays]
    refs = refs[n_tokens:]
    hidden_out = refs[5 + n_arrays]
    factors = refs[6 + n_arrays : 11 + n_arrays]
    h_turned, rh_turned = refs[11 + n_arrays : 13 + n_arrays]
    wbuf, hid, sems = refs[13 + n_arrays :]
    step = pl.program_id(0)
    rows, cols = hid.shape

    @pl.when(step == 0)
    def _():
        load_weights(table, arrays, wbuf, sems, n, pr, first)
        hid[...] = hidden_in[...]
        wait_weights(wbuf, sems, n, 0)

    if n > 1:
        @pl.when(step == 1)
        def _():
            wait_weights(wbuf, sems, n, 1)

    w = wbuf.at[step]
    mask_row = mask[0]
    b_in = bias_in[0]
    b_out = bias_out[0]

    for t in range(rows // tile):
        at = slice(t * tile, (t + 1) * tile)
        h = hid[at, :]
        x = normed[at, :]
        low_h = h.astype(BF16)
        first_in = jnp.concatenate([(mask_row * x).astype(BF16), low_h], axis=1)
        pre = jnp.dot(first_in, w[:, : 2 * cols], preferred_element_type=F32) + b_in
        update = gate(pre[:, :cols])
        reset = gate(pre[:, cols:])
        low_rh = (reset * h).astype(BF16)
        second_in = jnp.concatenate([low_rh, x.astype(BF16)], axis=1)
        raw = jnp.dot(second_in, w[:, 2 * cols :], preferred_element_type=F32) + b_out
        cand = jnp.tanh(raw)
        keep = 1.0 - update
        apart = cand - h
        hid[at, :] = h + update * apart
        values = (update * (1.0 - cand * cand), apart * update * keep, h * reset * (1.0 - reset), keep, reset)
        for ref, value in zip(factors, values):
            ref[0, at, :] = value.astype(ref.dtype)
        h_turned[0, :, at] = low_h.T
        rh_turned[0, :, at] = low_rh.T

    @pl.when(step == n - 1)
    def _():
        hidden_out[...] = hid[...]


def forward_chunk(table, hidden, normed, masks, bias_in, bias_out, arrays, first, tokens=(), tile=TILE):
    n = masks.shape[0]
    rows, cols = hidden.shape
    pr = arrays[0].shape[2]
    depth = 2 * cols
    whole = pl.BlockSpec((rows, cols), lambda i, *_: (0, 0))
    row = lambda width: pl.BlockSpec((1, 1, width), lambda i, *_: (i, 0, 0))
    per = pl.BlockSpec((1, rows, cols), lambda i, *_: (i, 0, 0))
    turned = pl.BlockSpec((1, cols, rows), lambda i, *_: (i, 0, 0))
    saved = [jax.ShapeDtypeStruct((n, rows, cols), t) for t in (F32,) * 5] + [jax.ShapeDtypeStruct((n, cols, rows), BF16)] * 2
    return pl.pallas_call(
        functools.partial(forward_kernel, n, first, len(arrays), len(tokens), pr, tile),
        grid_spec=pltpu.PrefetchScalarGridSpec(
            num_scalar_prefetch=1,
            grid=(n,),
            in_specs=[whole, whole, row(cols), row(2 * cols), row(cols)] + [pl.BlockSpec(memory_space=pl.ANY)] * (len(arrays) + len(tokens)),
            out_specs=[whole] + [per] * 5 + [turned] * 2,
            scratch_shapes=[
                pltpu.VMEM((n, depth, 3 * cols), BF16),
                pltpu.VMEM((rows, cols), F32),
                pltpu.SemaphoreType.DMA((2,)),
            ],
        ),
        out_shape=[jax.ShapeDtypeStruct((rows, cols), F32)] + saved,
        compiler_params=pltpu.CompilerParams(vmem_limit_bytes=VMEM_LIMIT),
        cost_estimate=LONG,
        name="forward_sections",
    )(table, hidden, normed, masks[:, None], bias_in[:, None], bias_out[:, None], *arrays, *tokens)


def backward_kernel(n, first, n_in, n_out, n_tokens, pr, tile, table, *refs):
    gh_in, normed, x_turned, mask, mask_column = refs[:5]
    factors = refs[5:10]
    h_turned, rh_turned = refs[10:12]
    arrays = refs[12 : 12 + n_in]
    refs = refs[12 + n_in + n_tokens :]
    gh_out, gn_out, g_mask, g_bin, g_bout = refs[:5]
    outs = refs[5 : 5 + n_out]
    wbuf, gh, gn, gg, gr, stage, sems, out_sems = refs[5 + n_out :]
    step = pl.program_id(0)
    sec = n - 1 - step
    rows, cols = gh.shape
    wide = 2 * cols

    def wait_out(slot):
        whole = stage.at[slot]
        pltpu.make_async_copy(whole, whole, out_sems.at[slot]).wait()

    @pl.when(step == 0)
    def _():
        for part, lo, hi in ((0, n - 1, n), (1, 0, n - 1)):
            if lo == hi:
                continue
            at = 0
            for array in arrays:
                for slot in range(array.shape[0]):
                    row = pl.multiple_of(table[at], pr)
                    pltpu.make_async_copy(
                        array.at[slot, pl.ds(first + lo, hi - lo)],
                        wbuf.at[pl.ds(lo, hi - lo), pl.ds(row, pr)],
                        sems.at[part],
                    ).start()
                    at += 1
        gh[...] = gh_in[...]
        gn[...] = jnp.zeros_like(gn)
        whole = wbuf.at[pl.ds(n - 1, 1)]
        pltpu.make_async_copy(whole, whole, sems.at[0]).wait()

    if n > 1:
        @pl.when(step == 1)
        def _():
            whole = wbuf.at[pl.ds(0, n - 1)]
            pltpu.make_async_copy(whole, whole, sems.at[1]).wait()

    w = wbuf.at[sec]
    mask_row = mask[0]
    nt = (((1,), (1,)), ((), ()))

    m_sum = jnp.zeros((1, cols), F32)
    bi_sum = jnp.zeros((1, wide), F32)
    bo_sum = jnp.zeros((1, cols), F32)
    for t in range(rows // tile):
        at = slice(t * tile, (t + 1) * tile)
        g = gh[at, :]
        by_raw, by_update, by_reset, keep, reset = (ref[0, at, :].astype(F32) for ref in factors)
        grad_raw = (g * by_raw).astype(BF16)
        gr[at, :] = grad_raw
        second = lax.dot_general(grad_raw, w[:, wide:], nt, preferred_element_type=F32)
        g2 = second[:, :cols]
        gates = jnp.concatenate([(g * by_update).astype(BF16), (g2 * by_reset).astype(BF16)], axis=1)
        gg[at, :] = gates
        first = lax.dot_general(gates, w[:, :wide], nt, preferred_element_type=F32)
        gm = first[:, :cols]
        gn[at, :] = gn[at, :] + second[:, cols:] + gm * mask_row
        gh[at, :] = g * keep + g2 * reset + first[:, cols:]
        m_sum = m_sum + jnp.sum(gm * normed[at, :], axis=0, keepdims=True)
        bi_sum = bi_sum + jnp.sum(gates.astype(F32), axis=0, keepdims=True)
        bo_sum = bo_sum + jnp.sum(grad_raw.astype(F32), axis=0, keepdims=True)
    g_mask[0] = m_sum * float(cols)
    g_bin[0] = bi_sum
    g_bout[0] = bo_sum

    slot = lax.rem(step, 2)
    if n > 2:
        @pl.when(step >= 2)
        def _():
            wait_out(slot)

    stage[slot, :cols, wide:] = jnp.dot(rh_turned[0], gr[...], preferred_element_type=F32).astype(BF16)
    stage[slot, cols:, wide:] = jnp.dot(x_turned[...], gr[...], preferred_element_type=F32).astype(BF16)
    masked = jnp.dot(x_turned[...], gg[...], preferred_element_type=F32)
    stage[slot, :cols, :wide] = (masked * mask_column[0]).astype(BF16)
    stage[slot, cols:, :wide] = jnp.dot(h_turned[0], gg[...], preferred_element_type=F32).astype(BF16)

    at = sum(array.shape[0] for array in arrays)
    for out in outs:
        for s in range(out.shape[0]):
            row = pl.multiple_of(table[at], pr)
            pltpu.make_async_copy(stage.at[slot, pl.ds(row, pr)], out.at[s, sec], out_sems.at[slot]).start()
            at += 1

    @pl.when(step == n - 1)
    def _():
        gh_out[...] = gh[...]
        gn_out[...] = gn[...]
        if n > 1:
            wait_out(1 - slot)
        wait_out(slot)


def backward_chunk(table, gh, normed, x_turned, masks, saved, first_saved, arrays, first, out_slots, tokens=(), tile=TILE):
    n = masks.shape[0]
    rows, cols = gh.shape
    pr = arrays[0].shape[2]
    depth = 2 * cols
    whole = pl.BlockSpec((rows, cols), lambda i, *_: (0, 0))
    row = lambda width: pl.BlockSpec((1, 1, width), lambda i, *_: (n - 1 - i, 0, 0))
    turned = pl.BlockSpec((1, cols, rows), lambda i, *_: (first_saved + n - 1 - i, 0, 0))
    per = pl.BlockSpec((1, rows, cols), lambda i, *_: (first_saved + n - 1 - i, 0, 0))
    column = pl.BlockSpec((1, cols, 1), lambda i, *_: (n - 1 - i, 0, 0))
    any_spec = pl.BlockSpec(memory_space=pl.ANY)
    state = jax.ShapeDtypeStruct((rows, cols), F32)
    vec = lambda width: jax.ShapeDtypeStruct((n, 1, width), F32)
    results = pl.pallas_call(
        functools.partial(backward_kernel, n, first, len(arrays), len(out_slots), len(tokens), pr, tile),
        grid_spec=pltpu.PrefetchScalarGridSpec(
            num_scalar_prefetch=1,
            grid=(n,),
            in_specs=[whole, whole, pl.BlockSpec((cols, rows), lambda i, *_: (0, 0)), row(cols), column]
            + [per] * 5
            + [turned] * 2
            + [any_spec] * (len(arrays) + len(tokens)),
            out_specs=[whole, whole, row(cols), row(depth), row(cols)] + [any_spec] * len(out_slots),
            scratch_shapes=[
                pltpu.VMEM((n, depth, 3 * cols), BF16),
                pltpu.VMEM((rows, cols), F32),
                pltpu.VMEM((rows, cols), F32),
                pltpu.VMEM((rows, depth), BF16),
                pltpu.VMEM((rows, cols), BF16),
                pltpu.VMEM((2, depth, 3 * cols), BF16),
                pltpu.SemaphoreType.DMA((2,)),
                pltpu.SemaphoreType.DMA((2,)),
            ],
        ),
        out_shape=[state, state, vec(cols), vec(depth), vec(cols)]
        + [jax.ShapeDtypeStruct((s, n, pr, 3 * cols), BF16) for s in out_slots],
        compiler_params=pltpu.CompilerParams(vmem_limit_bytes=VMEM_LIMIT),
        cost_estimate=LONG,
        name="backward_sections",
    )(table, gh, normed, x_turned, masks[:, None], masks[:, :, None], *saved, *arrays, *tokens)
    gh, gn, g_mask, g_bin, g_bout = results[:5]
    return gh, gn, g_mask[:, 0], g_bin[:, 0], g_bout[:, 0], results[5:]


def pick(micro, table):
    out = table[MB - 1 : MB, :]
    for b in range(MB - 2, -1, -1):
        out = jnp.where(micro == b, table[b : b + 1, :], out)
    return out


def stats_kernel(with_hidden, n_tokens, *refs):
    if with_hidden:
        refs = refs[:4] + refs[4 + n_tokens :]
        u_ref, hidden_ref, micro_ref, valid_ref, out_ref, stats_ref = refs
        u = u_ref[...] + hidden_ref[...]
        out_ref[...] = u
    else:
        u_ref, micro_ref, valid_ref, stats_ref = refs
        u = u_ref[...].astype(F32)
    micro = micro_ref[...]
    valid = valid_ref[...]
    width = u.shape[1]
    counts, means = [], []
    for b in range(MB):
        member = jnp.where(micro == b, valid, 0.0)
        count = jnp.sum(member)
        total = jnp.sum(u * member, axis=0, keepdims=True)
        counts.append(jnp.full((1, width), count, F32))
        means.append(total / jnp.maximum(count, 1.0))
    centred = u - pick(micro, jnp.concatenate(means, axis=0))
    squares = centred * centred * valid
    for b in range(MB):
        stats_ref[b : b + 1, :] = counts[b]
        stats_ref[MB + b : MB + b + 1, :] = means[b]
        stats_ref[2 * MB + b : 2 * MB + b + 1, :] = jnp.sum(jnp.where(micro == b, squares, 0.0), axis=0, keepdims=True)


def local_stats(u, hidden, micro, valid, tokens=()):
    rows, cols = u.shape
    stats = jax.ShapeDtypeStruct((3 * MB, cols), F32)
    args = (u, micro, valid) if hidden is None else (u, hidden, micro, valid)
    out = [stats] if hidden is None else [jax.ShapeDtypeStruct((rows, cols), F32), stats]
    res = pl.pallas_call(
        functools.partial(stats_kernel, hidden is not None, len(tokens)),
        in_specs=[pl.BlockSpec(memory_space=pltpu.VMEM)] * len(args) + [pl.BlockSpec(memory_space=pl.ANY)] * len(tokens),
        out_shape=out,
        compiler_params=pltpu.CompilerParams(vmem_limit_bytes=VMEM_LIMIT),
        cost_estimate=COST,
        name="local_stats",
    )(*args, *tokens)
    return (None, res[0]) if hidden is None else res


def merge_stats(a, b):
    na, ma, qa = a[:MB], a[MB : 2 * MB], a[2 * MB :]
    nb, mb, qb = b[:MB], b[MB : 2 * MB], b[2 * MB :]
    n = na + nb
    inverse = 1.0 / jnp.maximum(n, 1.0)
    apart = ma - mb
    return jnp.concatenate([n, (na * ma + nb * mb) * inverse, qa + qb + apart * apart * (na * nb * inverse)], axis=0)


def norm_kernel(u_ref, micro_ref, stats_ref, gain_ref, shift_ref, normed_ref, turned_ref):
    stats = stats_ref[...]
    scale = lax.rsqrt(stats[2 * MB :] / stats[:MB] + EPSILON)
    micro = micro_ref[...]
    standard = (u_ref[...].astype(F32) - pick(micro, stats[MB : 2 * MB])) * pick(micro, scale)
    normed = standard * gain_ref[...] + shift_ref[...]
    normed_ref[...] = normed
    turned_ref[...] = normed.astype(BF16).T


def norm_rows(u, micro, stats, gain, shift):
    rows, cols = u.shape
    return pl.pallas_call(
        norm_kernel,
        out_shape=[jax.ShapeDtypeStruct((rows, cols), F32), jax.ShapeDtypeStruct((cols, rows), BF16)],
        compiler_params=pltpu.CompilerParams(vmem_limit_bytes=VMEM_LIMIT),
        cost_estimate=COST,
        name="norm_rows",
    )(u, micro, stats, gain[None], shift[None])


def pool_kernel(u_ref, micro_ref, stats_ref, *refs):
    parts, (total_ref, pooled_ref) = refs[:-2], refs[-2:]
    stats = stats_ref[...]
    scale = lax.rsqrt(stats[2 * MB :] / stats[:MB] + EPSILON)
    micro = micro_ref[...]
    standard = (u_ref[...].astype(F32) - pick(micro, stats[MB : 2 * MB])) * pick(micro, scale)
    total = sum(ref[...] for ref in parts)
    total_ref[...] = total
    product = total * standard
    for b in range(MB):
        pooled_ref[b : b + 1, :] = jnp.sum(jnp.where(micro == b, total, 0.0), axis=0, keepdims=True)
        pooled_ref[MB + b : MB + b + 1, :] = jnp.sum(jnp.where(micro == b, product, 0.0), axis=0, keepdims=True)


def pool_grads(u, micro, stats, parts):
    rows, cols = u.shape
    return pl.pallas_call(
        pool_kernel,
        out_shape=[jax.ShapeDtypeStruct((rows, cols), F32), jax.ShapeDtypeStruct((2 * MB, cols), F32)],
        compiler_params=pltpu.CompilerParams(vmem_limit_bytes=VMEM_LIMIT),
        cost_estimate=COST,
        name="pool_grads",
    )(u, micro, stats, *parts)


def carry_kernel(u_ref, micro_ref, valid_ref, stats_ref, gain_ref, total_ref, pooled_ref, carried_ref, out_ref):
    stats = stats_ref[...]
    gain = gain_ref[...]
    counts = stats[:MB]
    scale = lax.rsqrt(stats[2 * MB :] / counts + EPSILON)
    pooled = pooled_ref[...]
    micro = micro_ref[...]
    row_scale = pick(micro, scale)
    standard = (u_ref[...].astype(F32) - pick(micro, stats[MB : 2 * MB])) * row_scale
    shift_term = pick(micro, gain * pooled[:MB] / counts)
    scale_term = pick(micro, gain * pooled[MB:] / counts)
    out_ref[...] = carried_ref[...] + row_scale * (
        total_ref[...] * gain - valid_ref[...] * (shift_term + standard * scale_term)
    )


def carry_grads(u, micro, valid, stats, gain, total, pooled, carried):
    rows, cols = u.shape
    return pl.pallas_call(
        carry_kernel,
        out_shape=jax.ShapeDtypeStruct((rows, cols), F32),
        compiler_params=pltpu.CompilerParams(vmem_limit_bytes=VMEM_LIMIT),
        cost_estimate=COST,
        name="carry_grads",
    )(u, micro, valid, stats, gain[None], total, pooled, carried)


def feature_mask(logits, thresh):
    centred = logits - jnp.max(logits)
    weights = jnp.exp(centred) * jax.nn.softplus(centred + thresh)
    return weights / jnp.sum(weights)


def combine_kernel(plan, n_in, n_tokens, *refs):
    ins, outs = refs[:n_in], refs[n_in + n_tokens :]
    for out, slots in zip(outs, plan):
        for s, terms in enumerate(slots):
            if len(terms) == 1:
                out[s, 0] = ins[terms[0][0]][terms[0][1], 0]
            else:
                out[s, 0] = sum(ins[k][j, 0].astype(F32) for k, j in terms).astype(out.dtype)


def combine(plan, parts, tokens=()):
    parts = [p if isinstance(p, tuple) else (p, p.shape[0], 0) for p in parts]
    out_n = [{p[0].shape[1] for p, used in zip(parts, uses) if used} for uses in uses_of(plan, len(parts))]
    pr, width = parts[0][0].shape[2:]
    n = max(max(v) for v in out_n)
    step = pr

    def block(slots, at, size):
        if size == n:
            return pl.BlockSpec((slots, 1, step, width), lambda i, r: (at, i, r, 0))
        return pl.BlockSpec((slots, 1, step, width), lambda i, r: (at, jnp.minimum(i, size - 1), r, 0))

    return pl.pallas_call(
        functools.partial(combine_kernel, plan, len(parts), len(tokens)),
        grid=(n, pr // step),
        in_specs=[block(slots, at, a.shape[1]) for a, slots, at in parts]
        + [pl.BlockSpec(memory_space=pl.ANY)] * len(tokens),
        out_specs=[block(len(slots), 0, min(v)) for slots, v in zip(plan, out_n)],
        out_shape=[jax.ShapeDtypeStruct((len(slots), min(v), pr, width), BF16) for slots, v in zip(plan, out_n)],
        compiler_params=pltpu.CompilerParams(vmem_limit_bytes=VMEM_LIMIT),
        cost_estimate=LONG,
        name="combine",
    )(*[p[0] for p in parts], *tokens)


def uses_of(plan, n_parts):
    return [[any(k == part for terms in slots for k, _ in terms) for part in range(n_parts)] for slots in plan]


def pack_kernel(place, g_in, g_out, *refs):
    out = refs[-1]
    wide = g_in.shape[-1]
    out[0, 0, :, :wide] = g_in[0]
    out[0, 0, :, wide:] = g_out[0]


def pack(place, gate_in, gate_out, lo, hi, rows, tokens):
    wide, cols = gate_in.shape[-1], gate_out.shape[-1]
    block = lambda w: pl.BlockSpec((1, rows, w), lambda i, place: (lo + i, place[0], 0))
    return pl.pallas_call(
        pack_kernel,
        grid_spec=pltpu.PrefetchScalarGridSpec(
            num_scalar_prefetch=1,
            grid=(hi - lo,),
            in_specs=[block(wide), block(cols)] + [pl.BlockSpec(memory_space=pl.ANY)] * len(tokens),
            out_specs=pl.BlockSpec((1, 1, rows, wide + cols), lambda i, place: (0, i, 0, 0)),
        ),
        out_shape=jax.ShapeDtypeStruct((1, hi - lo, rows, wide + cols), BF16),
        cost_estimate=COST,
        name="pack",
    )(place, gate_in, gate_out, *tokens)


def along(axis, size, flip):
    return [(i, i ^ flip) for i in range(size)]


def tie_kernel(*refs):
    pass


def tie(arrays, tokens):
    if not tokens:
        return list(arrays)
    any_spec = pl.BlockSpec(memory_space=pl.ANY)
    return pl.pallas_call(
        tie_kernel,
        in_specs=[any_spec] * (len(arrays) + len(tokens)),
        out_specs=[any_spec] * len(arrays),
        out_shape=[jax.ShapeDtypeStruct(a.shape, a.dtype) for a in arrays],
        input_output_aliases={i: i for i in range(len(arrays))},
        cost_estimate=COST,
        name="tie",
    )(*arrays, *tokens)


def low_sum(*terms):
    return sum(v.astype(F32) for v in terms).astype(BF16)


class CubeTransfers:
    def __init__(self, dp_size, fsdp_size):
        self.dp_size, self.fsdp_size = dp_size, fsdp_size
        self.slots = [4, 4, 4, 2, 2, 16]
        self.ring_slots = [dp_size * fsdp_size // 2] * 2

    def core(self, v):
        return lax.ppermute(v, "dp", along("dp", self.dp_size, 1))

    def x(self, v):
        return lax.ppermute(v, "dp", along("dp", self.dp_size, 2))

    def y(self, v):
        return lax.ppermute(v, "fsdp", along("fsdp", self.fsdp_size, 1))

    def z(self, v, flip):
        return lax.ppermute(v, "fsdp", along("fsdp", self.fsdp_size, 2 * flip))

    def far(self, v):
        size = self.dp_size * self.fsdp_size
        return lax.ppermute(v, ("dp", "fsdp"), along(("dp", "fsdp"), size, 2 * self.fsdp_size + 1))

    def all_reduce(self, v, merge):
        v = merge(v, self.core(v))
        v = merge(merge(v, self.x(v)), merge(self.y(v), self.far(v)))
        return merge(merge(v, self.z(v, 1)), merge(self.z(v, 2), self.z(v, 3)))

    def table(self, shard_rows):
        q = lax.axis_index("dp").astype(jnp.int32)
        f = lax.axis_index("fsdp").astype(jnp.int32)
        rows = []
        for core in (0, 1):
            for flip_q, flip_y, slots in ((0, 0, range(4)), (0, 1, range(4)), (2, 0, range(4)), (2, 1, range(4))):
                for j in slots:
                    place = f ^ (2 * j + flip_y)
                    rows.append(place * shard_rows + (q ^ (flip_q + core)) * (shard_rows // self.dp_size))
        return jnp.stack(rows)


    def ring_table(self, shard_rows):
        rows = shard_rows // self.dp_size
        core = lax.axis_index("dp").astype(jnp.int32) % 2
        order = [(f, x) for x in range(self.dp_size // 2) for f in range(self.fsdp_size)]
        halves = [jnp.array([f * shard_rows + 2 * x * rows for f, x in order], jnp.int32) + c * rows for c in (core, 1 - core)]
        return jnp.concatenate(halves)

    def ring_core(self, parts):
        return parts[0], self.core(parts[1])

    def ring_sums(self, parts):
        halves = jnp.concatenate([low_sum(*part) for part in parts], axis=1)
        same = [[d * self.fsdp_size + f for d in range(c, self.dp_size, 2) for f in range(self.fsdp_size)] for c in (0, 1)]
        own = lax.psum_scatter(halves, ("dp", "fsdp"), scatter_dimension=0, axis_index_groups=same)[None]
        return self.dp_pieces(own)
        yield


    def begin(self, gate_in, gate_out, lo, hi, tokens=()):
        place = lax.axis_index("dp").astype(jnp.int32)[None]
        own = pack(place, gate_in, gate_out, lo, hi, gate_in.shape[1] // self.dp_size, tokens)
        return [own] + [self.z(own, j) for j in (1, 2, 3)]

    def spread(self, pieces, tokens=()):
        (held,) = combine([[[(k, 0)] for k in range(4)]], pieces, tokens)
        return held, self.y(held), self.x(held)

    def relay(self, arrays, tokens=()):
        held, by_y, by_x = arrays
        half_y, half_x = combine([[[(0, 0)], [(0, 1)]], [[(1, 0)], [(1, 1)]]], [(by_y, 2, 0), (by_x, 2, 1)], tokens)
        return [held, by_y, by_x, self.x(half_y), self.y(half_x)], half_y

    def finish(self, mine):
        return mine + [self.core(v) for v in mine]


    def sums(self, parts):
        held, by_y, by_x, far_x, far_y, other = parts
        other = self.core(other)
        far_x, far_y = yield [low_sum(far_x, other[12:14]), low_sum(far_y, other[14:16])]
        got_x, got_y = self.x(far_x), self.y(far_y)
        by_y = jnp.concatenate([low_sum(by_y[:2], other[4:6], got_x), low_sum(by_y[2:], other[6:8])])
        by_x = jnp.concatenate([low_sum(by_x[:2], other[8:10]), low_sum(by_x[2:], other[10:12], got_y)])
        by_y, by_x = yield [by_y, by_x]
        got_y, got_x = self.y(by_y), self.x(by_x)
        held = [low_sum(*(v[k : k + 1] for v in (held, other, got_y, got_x))) for k in range(4)]
        sent = yield held[1:]
        own = low_sum(held[0], *(self.z(v, k + 1) for k, v in enumerate(sent)))
        (own,) = yield [own]
        return self.dp_pieces(own)

    def dp_pieces(self, own):
        by_x = self.x(own)
        return [own, self.core(own), by_x, self.core(by_x)]

    def pieces_table(self, shard_rows):
        q = lax.axis_index("dp").astype(jnp.int32)
        return jnp.stack([(q ^ j) * (shard_rows // self.dp_size) for j in range(4)])


class PlainTransfers:
    def __init__(self, dp_size, fsdp_size):
        self.fsdp_size = fsdp_size
        self.slots = self.ring_slots = [fsdp_size]

    def all_reduce(self, v, merge):
        every = lax.all_gather(v, ("dp", "fsdp"))
        while every.shape[0] > 1:
            half = every.shape[0] // 2
            every = jax.vmap(merge)(every[:half], every[half:])
        return every[0]

    def table(self, shard_rows):
        return jnp.arange(self.fsdp_size, dtype=jnp.int32) * shard_rows

    ring_table = table

    def ring_core(self, parts):
        return parts

    def begin(self, gate_in, gate_out, lo, hi, tokens=()):
        return jnp.concatenate([gate_in[lo:hi], gate_out[lo:hi]], axis=-1)

    def spread(self, shard, tokens=()):
        return [lax.all_gather(shard, "fsdp")]

    def relay(self, arrays, tokens=()):
        return arrays, arrays[0]

    def finish(self, mine):
        return mine

    def sums(self, parts):
        own = lax.psum_scatter(parts[0], "fsdp", scatter_dimension=0)
        return [lax.psum(own, "dp")[None]]
        yield

    def ring_sums(self, parts):
        return (yield from self.sums([jnp.concatenate([part[0] for part in parts], axis=1)]))

    def pieces_table(self, shard_rows):
        return jnp.zeros((1,), jnp.int32)


def place_kernel(n_pieces, table, *refs):
    pieces = refs[:n_pieces]
    g_in, g_out = refs[-2:]
    pr = pieces[0].shape[2]
    wide = g_in.shape[-1]
    for j, piece in enumerate(pieces):
        row = pl.multiple_of(table[j], pr)
        value = piece[0, 0].astype(F32)
        g_in[0, pl.ds(row, pr), :] = value[:, :wide]
        g_out[0, pl.ds(row, pr), :] = value[:, wide:]


def place_grads(table, pieces, start, shard_rows, previous):
    _, n, pr, width = pieces[0].shape
    wide = 2 * width // 3
    shapes = [
        jax.ShapeDtypeStruct((LAYERS * SECTIONS, shard_rows, wide), F32),
        jax.ShapeDtypeStruct((LAYERS * SECTIONS, shard_rows, width - wide), F32),
    ]
    block = lambda w: pl.BlockSpec((1, shard_rows, w), lambda i, *_: (start + i, 0, 0))
    n_pieces = len(pieces)
    extra = [] if previous is None else list(previous)
    return pl.pallas_call(
        functools.partial(place_kernel, n_pieces),
        grid_spec=pltpu.PrefetchScalarGridSpec(
            num_scalar_prefetch=1,
            grid=(n,),
            in_specs=[pl.BlockSpec((1, 1, pr, width), lambda i, *_: (0, i, 0, 0))] * n_pieces
            + [pl.BlockSpec(memory_space=pl.ANY)] * len(extra),
            out_specs=[block(wide), block(width - wide)],
        ),
        out_shape=shapes,
        input_output_aliases={} if previous is None else {1 + n_pieces: 0, 2 + n_pieces: 1},
        cost_estimate=COST,
        name="place_grads",
    )(table, *pieces, *extra)


def local(
    moves,
    features,
    row_valid,
    micro_batch,
    gains,
    shifts,
    mask_logits,
    thresholds,
    gate_in,
    bias_in,
    gate_out,
    bias_out,
    cotangent,
):
    columns = features.shape[1]
    shard_rows = gate_in.shape[2]
    valid = row_valid.astype(F32)[:, None]
    micro = micro_batch[:, None]
    tables = (moves.table(shard_rows), moves.ring_table(shard_rows))
    flat = lambda v: v.reshape((LAYERS * SECTIONS,) + v.shape[2:])
    gate_in, gate_out, bias_in, bias_out = flat(gate_in), flat(gate_out), flat(bias_in), flat(bias_out)
    masks = columns * flat(jax.vmap(jax.vmap(feature_mask))(mask_logits, thresholds))
    add = lambda a, b: a + b
    begin = lambda j, tokens=(): moves.begin(gate_in, gate_out, *GATHERS[j], tokens)

    gathered, records, stored = [], [], []
    current, hidden = features, None
    _, stats = local_stats(current, None, micro, valid)
    begun = {0: begin(0)}
    spreads = {0: moves.spread(begun[0], (stats,))}
    begun[1] = begin(1, (spreads[0][0],))
    stats = moves.all_reduce(stats, merge_stats)
    before = ()
    for k, (lo, hi) in enumerate(GATHERS):
        layer = lo // SECTIONS
        if lo % SECTIONS == 0:
            if k > 0:
                current, stats = local_stats(current, hidden, micro, valid)
                stats = moves.all_reduce(stats, merge_stats)
                before = (stats,)
            normed, x_turned = norm_rows(current, micro, stats, gains[layer], shifts[layer])
            hidden = normed
            records.append((current, stats, normed, x_turned))
        arrays, token = moves.relay(spreads[k], before)
        tokens = [token]
        if k + 1 < len(GATHERS):
            spreads[k + 1] = moves.spread(begun[k + 1], tokens)
            tokens = [spreads[k + 1][0]]
        if k + 2 < len(GATHERS):
            begun[k + 2] = begin(k + 2, tokens)
            tokens = [begun[k + 2][0]]
        arrays = moves.finish(arrays)
        hidden, *saved = forward_chunk(
            tables[0], hidden, normed, masks[lo:hi], bias_in[lo:hi], bias_out[lo:hi], arrays, 0, tokens
        )
        before = (hidden,)
        stored.append((lo, hi, arrays, saved))
    mixed_out = (current + hidden).astype(BF16)

    carried = cotangent.astype(F32) * valid
    pieces_table = moves.pieces_table(shard_rows)
    grads = None
    results = [None] * LAYERS
    under_way = []
    tokens = []

    def advance(item, sent):
        try:
            item[1] = item[0].send(sent)
            return True
        except StopIteration as stop:
            item[2](stop.value)
            return False

    def start(generator, at_end):
        item = [generator, None, at_end]
        if advance(item, None):
            under_way.append(item)

    def send_all(after=None):
        ready = [item[1] for item in under_way]
        if after is not None:
            tied = iter(tie([v for sent in ready for v in sent], after))
            ready = [[next(tied) for _ in sent] for sent in ready]
        made = [v for sent in ready for v in sent]
        under_way[:] = [item for item, sent in zip(list(under_way), ready) if advance(item, sent)]
        return made

    def placed(lo):
        def at_end(pieces):
            nonlocal grads
            grads = place_grads(pieces_table, pieces, lo, shard_rows, grads)

        return at_end

    ring_parts = []
    for k, (lo, hi) in reversed(list(enumerate(GROUPS))):
        layer = lo // SECTIONS
        current, stats, normed, x_turned = records[layer]
        if hi % SECTIONS == 0:
            gh = carried
            normed_parts, vectors = [], []
        ((start_at, _, arrays, saved),) = [g for g in stored if g[0] <= lo and hi <= g[1]]
        ring = RING_SUM[0] <= lo < RING_SUM[1]
        gh, gn, g_mask, g_bin, g_bout, out = backward_chunk(
            jnp.concatenate([tables[0], tables[1 if ring else 0]]),
            gh,
            normed,
            x_turned,
            masks[lo:hi],
            saved,
            lo - start_at,
            arrays,
            lo - start_at,
            moves.ring_slots if ring else moves.slots,
            tokens,
        )
        normed_parts.append(gn)
        vectors.insert(0, jnp.concatenate([g_mask, g_bin, g_bout], axis=1))
        tokens = []
        if ring:
            ring_parts.insert(0, moves.ring_core(out))
        else:
            start(moves.sums(out), placed(lo))
            if k > 0:
                tokens = send_all()
        if lo % SECTIONS == 0:
            total, pooled = pool_grads(current, micro, stats, normed_parts + [gh])
            vectors = jnp.concatenate(vectors, axis=0)
            results[layer] = moves.all_reduce(jnp.concatenate([pooled, vectors.reshape(-1, columns)]), add)
            carried = carry_grads(current, micro, valid, stats, gains[layer], total, results[layer][: 2 * MB], carried)
    after = [carried]
    while under_way:
        after = send_all(after) + list(grads or ())
    start(moves.ring_sums(ring_parts), placed(RING_SUM[0]))
    pooled = jnp.stack([both[: 2 * MB] for both in results])
    stacked = jnp.stack([both[2 * MB :].reshape(SECTIONS, 4 * columns) for both in results])
    _, mask_pull = jax.vjp(jax.vmap(jax.vmap(feature_mask)), mask_logits, thresholds)
    grad_logits, grad_thresholds = mask_pull(stacked[..., :columns])
    unflat = lambda v: v.reshape((LAYERS, SECTIONS) + v.shape[1:])
    return (
        mixed_out,
        carried,
        jnp.sum(pooled[:, MB:], axis=1),
        jnp.sum(pooled[:, :MB], axis=1),
        grad_logits,
        grad_thresholds,
        unflat(grads[0]),
        stacked[..., columns : 3 * columns],
        unflat(grads[1]),
        stacked[..., 3 * columns :],
    )


def solution(mesh):
    rows = P(("dp", "fsdp"), None)
    row = P(("dp", "fsdp"))
    shard = P(None, None, "fsdp", None)
    in_specs = (rows, row, row, P(), P(), P(), P(), shard, P(), shard, P(), rows)
    out_specs = (rows, rows, P(), P(), P(), P(), shard, P(), shard, P())
    dp_size, fsdp_size = mesh.shape["dp"], mesh.shape["fsdp"]
    kind = CubeTransfers if (dp_size, fsdp_size) == (4, 8) else PlainTransfers
    return jax.shard_map(
        functools.partial(local, kind(dp_size, fsdp_size)),
        mesh=mesh,
        in_specs=in_specs,
        out_specs=out_specs,
        check_vma=False,
    )
```

time: 929 us -> 713 us (0.77)
  waiting for transfers between devices: 374 us -> 224 us
  starting transfers between devices: 175 us -> 102 us
  between operations: 3.15 us -> 15.6 us
  Pallas kernels: 290 us -> 280 us
    ppermute x29 -> x14, waiting for transfers between devices: 181 us -> 33.5 us  [y(): return lax.ppermute(v, 'fsdp', along('fsdp', self.fsdp_size, 1))]
    ppermute x0 -> x4, waiting for transfers between devices: none -> 45.3 us  [far(): lax.ppermute(v, ('dp', 'fsdp'), along(('dp', 'fsdp'), size, 2 * self.fsdp...]
    ppermute x35 -> x17, waiting for transfers between devices: 80.8 us -> 47.3 us  [x(): return lax.ppermute(v, 'dp', along('dp', self.dp_size, 2))]
    ppermute x46 -> x27, starting transfers between devices: 86.9 us -> 56.7 us  [z(): return lax.ppermute(v, 'fsdp', along('fsdp', self.fsdp_size, 2 * flip))]
    ppermute x35 -> x17, starting transfers between devices: 45.8 us -> 20.6 us  [x(): return lax.ppermute(v, 'dp', along('dp', self.dp_size, 2))]
    ppermute x46 -> x27, waiting for transfers between devices: 110 us -> 86.7 us  [z(): return lax.ppermute(v, 'fsdp', along('fsdp', self.fsdp_size, 2 * flip))]
    convert_element_type x12 -> x10, other arithmetic: 8.04 us -> 30.8 us  [low_sum(): return sum((v.astype(F32) for v in terms)).astype(BF16)]
    ppermute x29 -> x14, starting transfers between devices: 31.8 us -> 14.3 us  [y(): return lax.ppermute(v, 'fsdp', along('fsdp', self.fsdp_size, 1))]
  transfers between devices with their start and end apart: 163 -> 92, of which waited for: 56 -> 36; matrix products, arithmetic and copies ran while one was open for 8% -> 11% of each run, Pallas kernels for 22% -> 30%
where the time goes in v2:
time: 713 us; the launch traced here: 703 us
  Pallas kernels  280 us (39%)
  waiting for transfers between devices  224 us (31%)
  starting transfers between devices  102 us (14%)
  other arithmetic  50.5 us (7%)
  local copies, waits for them, and re-layouts  31.6 us (4%)
  between operations  15.6 us (2%)
    pallas_call x4, Pallas kernels, backward_chunk(): pl.pallas_call(functools.partial(backward_kernel, n, first, len(arrays),...  125 us
    ppermute x27, waiting for transfers between devices, z(): return lax.ppermute(v, 'fsdp', along('fsdp', self.fsdp_size, 2 * flip))  86.7 us
    pallas_call x3, Pallas kernels, forward_chunk(): pl.pallas_call(functools.partial(forward_kernel, n, first, len(arrays), l...  69.9 us
    ppermute x27, starting transfers between devices, z(): return lax.ppermute(v, 'fsdp', along('fsdp', self.fsdp_size, 2 * flip))  56.7 us
    ppermute x17, waiting for transfers between devices, x(): return lax.ppermute(v, 'dp', along('dp', self.dp_size, 2))  47.3 us
    ppermute x4, waiting for transfers between devices, far(): lax.ppermute(v, ('dp', 'fsdp'), along(('dp', 'fsdp'), size, 2 * self.fsdp...  45.3 us
    ppermute x14, waiting for transfers between devices, y(): return lax.ppermute(v, 'fsdp', along('fsdp', self.fsdp_size, 1))  33.5 us
    convert_element_type x10, other arithmetic, low_sum(): return sum((v.astype(F32) for v in terms)).astype(BF16)  30.8 us
  transfers between devices with their start and end apart: 92, of which 36 were waited for; matrix products, arithmetic and copies ran while one was open for 11% of the time, Pallas kernels for 30%

profile of v2, /device:TPU:0, one launch (start us, length us, event | category | flops | bytes accessed | tf_op | source)
XLA Modules:
  0.0 702.7 jit_solution(12438934263942720762)
XLA Ops:
  7.2 2.5 pack.3.refs_0_
  9.7 3.0 collective-permute-start.7
  12.7 2.6 collective-permute-start.8
  17.2 3.9 local_stats.2.refs_4_
  25.5 10.9 %collective-permute-done.8.refs_2_ = bf16[1,3,32,1536]{3,2,1,0:T(8,128)(2,1)S(1)} collective-permute-done((bf16[1,3,32,1536]{3,2,1,0:T(8,128)(2,1)}, bf16[1,3,32,1536]{3,2,1,0:T(8,128)(2,1)S(1)}, u32[]{:S(2)}, u32[]{:S(2)}) %collective-permute-start.8) | collective-permute-done | bytes 294944 | tf_op jit(solution)/shard_map/ppermute | solution.py:523
  37.8 3.2 combine.6.refs_0_.refs_5_.refs_12_
  47.7 20.3 %collective-permute-done.3 = f32[12,512]{1,0:T(8,128)S(1)} collective-permute-done((f32[12,512]{1,0:T(8,128)S(1)}, f32[12,512]{1,0:T(8,128)S(1)}, u32[]{:S(2)}, u32[]{:S(2)}) %collective-permute-start.3) | collective-permute-done | bytes 24608 | tf_op jit(solution)/shard_map/ppermute | solution.py:527
  70.0 6.9 collective-permute-start.5
  78.1 3.2 combine.7
  87.0 2.5 pack.4.refs_0_
  94.6 4.8 collective-permute-done.19.refs_1_
  99.4 13.3 %collective-permute-done.20.refs_2_ = bf16[1,3,32,1536]{3,2,1,0:T(8,128)(2,1)S(1)} collective-permute-done((bf16[1,3,32,1536]{3,2,1,0:T(8,128)(2,1)}, bf16[1,3,32,1536]{3,2,1,0:T(8,128)(2,1)S(1)}, u32[]{:S(2)}, u32[]{:S(2)}) %collective-permute-start.20) | collective-permute-done | bytes 294944 | tf_op jit(solution)/shard_map/ppermute | solution.py:523
  113.8 3.2 combine.8.refs_0_.refs_5_.refs_12_
  117.0 3.6 norm_rows.2
  120.6 4.0 pack.5.refs_15_.refs_0_
  126.8 3.4 collective-permute-start.31
  132.6 19.2 %forward_sections.3 = (f32[768,512]{1,0:T(8,128)}, f32[3,768,512]{2,1,0:T(8,128)}, f32[3,768,512]{2,1,0:T(8,128)}, f32[3,768,512]{2,1,0:T(8,128)}, f32[3,768,512...) custom-call(s32[32]{0:T(128)} %stack.158.table, ...), custom_call_target="tpu_custom_call" | custom-call | flops 20000000000 | bytes 1 | tf_op jit(solution)/shard_map/forward_sections/pallas_call | solution.py:115
  154.1 3.2 combine.9
  160.8 12.1 %collective-permute-done.32.refs_2_ = bf16[1,6,32,1536]{3,2,1,0:T(8,128)(2,1)} collective-permute-done((bf16[1,6,32,1536]{3,2,1,0:T(8,128)(2,1)}, bf16[1,6,32,1536]{3,2,1,0:T(8,128)(2,1)}, u32[]{:S(2)}, u32[]{:S(2)}) %collective-permute-start.32) | collective-permute-done | bytes 589856 | tf_op jit(solution)/shard_map/ppermute | solution.py:523
  173.9 5.1 combine.10.refs_15_.refs_5_.refs_12_
  181.1 19.3 %forward_sections.4 = (f32[768,512]{1,0:T(8,128)}, f32[3,768,512]{2,1,0:T(8,128)}, f32[3,768,512]{2,1,0:T(8,128)}, f32[3,768,512]{2,1,0:T(8,128)}, f32[3,768,512...) custom-call(s32[32]{0:T(128)} %stack.158.table, ...), custom_call_target="tpu_custom_call" | custom-call | flops 20000000000 | bytes 1 | tf_op jit(solution)/shard_map/forward_sections/pallas_call | solution.py:115
  200.5 4.5 local_stats.3
  211.6 23.2 %collective-permute-done.37 = f32[12,512]{1,0:T(8,128)S(1)} collective-permute-done((f32[12,512]{1,0:T(8,128)S(1)}, f32[12,512]{1,0:T(8,128)S(1)}, u32[]{:S(2)}, u32[]{:S(2)}) %collective-permute-start.37) | collective-permute-done | bytes 24608 | tf_op jit(solution)/shard_map/ppermute | solution.py:527
  234.8 2.5 collective-permute-start.40
  237.3 10.7 %collective-permute-start.39 = (f32[12,512]{1,0:T(8,128)S(1)}, f32[12,512]{1,0:T(8,128)S(1)}, u32[]{:S(2)}, u32[]{:S(2)}) collective-permute-start(f32[12,512]{1,0:T(8,128)S(1)} %pad_maximum_fusion.9), channel_id=1, source_target_pairs={{0,4},{1,5},{2,6},{3,7},{4,0},{5,1},{6,2},{7,3},{8,12},{9,13},{10,... | collective-permute-start | bytes 73736 | tf_op jit(solution)/shard_map/ppermute | solution.py:523
  248.1 2.5 collective-permute-done.39
  252.6 5.0 combine.11
  260.6 22.3 %collective-permute-done.43.refs_8_.refs_15_ = bf16[2,6,32,1536]{3,2,1,0:T(8,128)(2,1)S(1)} collective-permute-done((bf16[2,6,32,1536]{3,2,1,0:T(8,128)(2,1)}, bf16[2,6,32,1536]{3,2,1,0:T(8,128)(2,1)S(1)}, u32[]{:S(2)}, u32[]{:S(2)}) %collective-permute-start.43) | collective-permute-done | bytes 1179680 | tf_op jit(solution)/shard_map/ppermute | solution.py:517
  282.9 5.0 collective-permute-done.44.refs_9_.refs_16_
  299.5 3.8 norm_rows.3
  303.3 31.3 %forward_sections.5 = (f32[768,512]{1,0:T(8,128)}, f32[6,768,512]{2,1,0:T(8,128)}, f32[6,768,512]{2,1,0:T(8,128)}, f32[6,768,512]{2,1,0:T(8,128)}, f32[6,768,512...) custom-call(s32[32]{0:T(128)} %stack.158.table, ...), custom_call_target="tpu_custom_call" | custom-call | flops 20000000000 | bytes 1 | tf_op jit(solution)/shard_map/forward_sections/pallas_call | solution.py:115
  334.6 31.3 %backward_sections.4 = (f32[768,512]{1,0:T(8,128)}, f32[768,512]{1,0:T(8,128)}, f32[3,1,512]{2,1,0:T(1,128)}, f32[3,1,1024]{2,1,0:T(1,128)}, f32[3,1,512]{2,1,0:...) custom-call(s32[64]{0:T(128)} %concatenate.77.table, ...), custom_call_target="tpu_custom_call" | custom-call | flops 20000000000 | bytes 1 | tf_op jit(solution)/shard_map/backward_sections/pallas_call | solution.py:248
  366.6 31.0 %backward_sections.5 = (f32[768,512]{1,0:T(8,128)}, f32[768,512]{1,0:T(8,128)}, f32[3,1,512]{2,1,0:T(1,128)}, f32[3,1,1024]{2,1,0:T(1,128)}, f32[3,1,512]{2,1,0:...) custom-call(s32[64]{0:T(128)} %concatenate.77.table, ...), custom_call_target="tpu_custom_call" | custom-call | flops 20000000000 | bytes 1 | tf_op jit(solution)/shard_map/backward_sections/pallas_call | solution.py:248
  397.8 6.0 pool_grads.2
  416.6 5.6 add_convert_fusion
  422.3 4.1 add_convert_fusion.1
  426.4 4.0 pad_maximum_fusion
  431.8 5.3 carry_grads.2.refs_0_.carried_ref
  437.1 31.3 %backward_sections.6 = (f32[768,512]{1,0:T(8,128)}, f32[768,512]{1,0:T(8,128)}, f32[3,1,512]{2,1,0:T(1,128)}, f32[3,1,1024]{2,1,0:T(1,128)}, f32[3,1,512]{2,1,0:...) custom-call(s32[64]{0:T(128)} %concatenate.76.table, ...), custom_call_target="tpu_custom_call" | custom-call | flops 20000000000 | bytes 1 | tf_op jit(solution)/shard_map/backward_sections/pallas_call | solution.py:248
  469.7 7.0 collective-permute-done.57
  476.7 2.8 add_convert_fusion.13
  479.6 31.6 %backward_sections.7 = (f32[768,512]{1,0:T(8,128)}, f32[768,512]{1,0:T(8,128)}, f32[3,1,512]{2,1,0:T(1,128)}, f32[3,1,1024]{2,1,0:T(1,128)}, f32[3,1,512]{2,1,0:...) custom-call(s32[64]{0:T(128)} %concatenate.76.table, ...), custom_call_target="tpu_custom_call" | custom-call | flops 20000000000 | bytes 1 | tf_op jit(solution)/shard_map/backward_sections/pallas_call | solution.py:248
  511.6 5.9 pool_grads.3
  528.3 2.7 collective-permute-start.63
  539.3 5.2 carry_grads.3.refs_4_
  544.5 2.7 add_convert_fusion.10
  550.0 2.6 add_convert_fusion.7
  556.7 14.2 %collective-permute-done.76 = bf16[2,3,32,1536]{3,2,1,0:T(8,128)(2,1)S(1)} collective-permute-done((bf16[2,3,32,1536]{3,2,1,0:T(8,128)(2,1)}, bf16[2,3,32,1536]{3,2,1,0:T(8,128)(2,1)S(1)}, u32[]{:S(2)}, u32[]{:S(2)}) %collective-permute-start.76) | collective-permute-done | bytes 589856 | tf_op jit(solution)/shard_map/ppermute | solution.py:520
  570.9 2.7 add_convert_fusion.4
  575.9 14.9 %collective-permute-done.74 = bf16[4,3,32,1536]{3,2,1,0:T(8,128)(2,1)S(1)} collective-permute-done((bf16[4,3,32,1536]{3,2,1,0:T(8,128)(2,1)}, bf16[4,3,32,1536]{3,2,1,0:T(8,128)(2,1)S(1)}, u32[]{:S(2)}, u32[]{:S(2)}) %collective-permute-start.74) | collective-permute-done | bytes 1179680 | tf_op jit(solution)/shard_map/ppermute | solution.py:517
  590.8 12.7 %collective-permute-done.73 = bf16[4,3,32,1536]{3,2,1,0:T(8,128)(2,1)S(1)} collective-permute-done((bf16[4,3,32,1536]{3,2,1,0:T(8,128)(2,1)}, bf16[4,3,32,1536]{3,2,1,0:T(8,128)(2,1)S(1)}, u32[]{:S(2)}, u32[]{:S(2)}) %collective-permute-start.73) | collective-permute-done | bytes 1179680 | tf_op jit(solution)/shard_map/ppermute | solution.py:520
  603.4 2.8 add_convert_fusion.22
  609.7 2.8 collective-permute-start.81
  615.4 6.6 collective-permute-done.81
  622.0 14.8 %collective-permute-done.80 = bf16[1,3,32,1536]{3,2,1,0:T(8,128)(2,1)} collective-permute-done((bf16[1,3,32,1536]{3,2,1,0:T(8,128)(2,1)}, bf16[1,3,32,1536]{3,2,1,0:T(8,128)(2,1)}, u32[]{:S(2)}, u32[]{:S(2)}) %collective-permute-start.80) | collective-permute-done | bytes 294944 | tf_op jit(solution)/shard_map/ppermute | solution.py:523
  639.2 3.0 add_convert_fusion.16
  643.9 2.8 collective-permute-start.82
  649.7 4.6 collective-permute-done.84
  654.4 2.5 collective-permute-done.86.refs_2_
  656.9 10.3 %collective-permute-done.83 = bf16[1,3,32,1536]{3,2,1,0:T(8,128)(2,1)S(1)} collective-permute-done((bf16[1,3,32,1536]{3,2,1,0:T(8,128)(2,1)}, bf16[1,3,32,1536]{3,2,1,0:T(8,128)(2,1)S(1)}, u32[]{:S(2)}, u32[]{:S(2)}) %collective-permute-start.83) | collective-permute-done | bytes 294944 | tf_op jit(solution)/shard_map/ppermute | solution.py:523
  670.0 4.2 place_grads.3
  677.3 3.9 collective-permute-done.89.refs_2_
  684.0 4.2 place_grads.4
  689.3 6.2 place_grads.5
  (430 shorter events, 133.7 us)
Async XLA Ops:
  7.2 641.4 %reduce-scatter.2.cloned.1.call-start = ((), (), s32[]{:S(2)}) async-start(), calls=%async_computation.1 | async-start | bytes 10027008 | tf_op jit(solution)/shard_map/reduce_scatter | solution.py:559
  9.7 15.8 %collective-permute-start.7 = (bf16[1,3,32,1536]{3,2,1,0:T(8,128)(2,1)}, bf16[1,3,32,1536]{3,2,1,0:T(8,128)(2,1)S(1)}, u32[]{:S(2)}, u32[]{:S(2)}) collective-permute-start(bf16[1,3,32,1536]{3,2,1,0:T(8,128)(2,1)} %pack.3.refs_0_), channel_id=1, source_target_pairs={{0,2},{1,3},{2,0},{3,1},{4,6},{5,7},{6,4},{7,5},{8,10},{9,11},{10,... | collective-permute-start | bytes 884744 | tf_op jit(solution)/shard_map/ppermute | solution.py:523
  12.7 23.7 %collective-permute-start.8 = (bf16[1,3,32,1536]{3,2,1,0:T(8,128)(2,1)}, bf16[1,3,32,1536]{3,2,1,0:T(8,128)(2,1)S(1)}, u32[]{:S(2)}, u32[]{:S(2)}) collective-permute-start(bf16[1,3,32,1536]{3,2,1,0:T(8,128)(2,1)} %pack.3.refs_0_), channel_id=1, source_target_pairs={{0,4},{1,5},{2,6},{3,7},{4,0},{5,1},{6,2},{7,3},{8,12},{9,13},{10,... | collective-permute-start | bytes 884744 | tf_op jit(solution)/shard_map/ppermute | solution.py:523
  15.3 21.1 %collective-permute-start.9 = (bf16[1,3,32,1536]{3,2,1,0:T(8,128)(2,1)}, bf16[1,3,32,1536]{3,2,1,0:T(8,128)(2,1)S(1)}, u32[]{:S(2)}, u32[]{:S(2)}) collective-permute-start(bf16[1,3,32,1536]{3,2,1,0:T(8,128)(2,1)} %pack.3.refs_0_), channel_id=1, source_target_pairs={{0,6},{1,7},{2,4},{3,5},{4,2},{5,3},{6,0},{7,1},{8,14},{9,15},{10,... | collective-permute-start | bytes 884744 | tf_op jit(solution)/shard_map/ppermute | solution.py:523
  21.0 23.1 %collective-permute-start = (f32[12,512]{1,0:T(8,128)}, f32[12,512]{1,0:T(8,128)S(1)}, u32[]{:S(2)}, u32[]{:S(2)}) collective-permute-start(f32[12,512]{1,0:T(8,128)} %local_stats.2.refs_4_), channel_id=1, source_target_pairs={{0,8},{8,0},{16,24},{24,16},{1,9},{9,1},{17,25},{25,17},{2,10},{10... | collective-permute-start | bytes 73736 | tf_op jit(solution)/shard_map/ppermute | solution.py:514
  41.1 35.9 %collective-permute-start.10 = (bf16[4,3,32,1536]{3,2,1,0:T(8,128)(2,1)}, bf16[4,3,32,1536]{3,2,1,0:T(8,128)(2,1)S(1)}, u32[]{:S(2)}, u32[]{:S(2)}) collective-permute-start(bf16[4,3,32,1536]{3,2,1,0:T(8,128)(2,1)} %combine.6.refs_0_.refs_5_.refs_12_), channel_id=1, source_target_pairs={{0,1},{1,0},{2,3},{3,2},{4,5},{5,4},{6,7},{7,6},{8,9},{9,8},{10,11... | collective-permute-start | bytes 3538952 | tf_op jit(solution)/shard_map/ppermute | solution.py:520
  42.6 34.4 %collective-permute-start.11 = (bf16[4,3,32,1536]{3,2,1,0:T(8,128)(2,1)}, bf16[4,3,32,1536]{3,2,1,0:T(8,128)(2,1)}, u32[]{:S(2)}, u32[]{:S(2)}) collective-permute-start(bf16[4,3,32,1536]{3,2,1,0:T(8,128)(2,1)} %combine.6.refs_0_.refs_5_.refs_12_), channel_id=1, source_target_pairs={{0,16},{8,24},{16,0},{24,8},{1,17},{9,25},{17,1},{25,9},{2,18},{10... | collective-permute-start | bytes 3538952 | tf_op jit(solution)/shard_map/ppermute | solution.py:517
  44.2 23.9 %collective-permute-start.3 = (f32[12,512]{1,0:T(8,128)S(1)}, f32[12,512]{1,0:T(8,128)S(1)}, u32[]{:S(2)}, u32[]{:S(2)}) collective-permute-start(f32[12,512]{1,0:T(8,128)S(1)} %pad_maximum_fusion.5), channel_id=1, source_target_pairs={{0,17},{1,16},{2,19},{3,18},{4,21},{5,20},{6,23},{7,22},{8,25},{9,... | collective-permute-start | bytes 73736 | tf_op jit(solution)/shard_map/ppermute | solution.py:527
  44.7 23.4 %collective-permute-start.2 = (f32[12,512]{1,0:T(8,128)S(1)}, f32[12,512]{1,0:T(8,128)S(1)}, u32[]{:S(2)}, u32[]{:S(2)}) collective-permute-start(f32[12,512]{1,0:T(8,128)S(1)} %pad_maximum_fusion.5), channel_id=1, source_target_pairs={{0,1},{1,0},{2,3},{3,2},{4,5},{5,4},{6,7},{7,6},{8,9},{9,8},{10,11... | collective-permute-start | bytes 73736 | tf_op jit(solution)/shard_map/ppermute | solution.py:520
  46.2 22.3 %collective-permute-start.1 = (f32[12,512]{1,0:T(8,128)S(1)}, f32[12,512]{1,0:T(8,128)S(1)}, u32[]{:S(2)}, u32[]{:S(2)}) collective-permute-start(f32[12,512]{1,0:T(8,128)S(1)} %pad_maximum_fusion.5), channel_id=1, source_target_pairs={{0,16},{8,24},{16,0},{24,8},{1,17},{9,25},{17,1},{25,9},{2,18},{10... | collective-permute-start | bytes 73736 | tf_op jit(solution)/shard_map/ppermute | solution.py:517
  68.6 18.4 %collective-permute-start.6 = (f32[12,512]{1,0:T(8,128)S(1)}, f32[12,512]{1,0:T(8,128)S(1)}, u32[]{:S(2)}, u32[]{:S(2)}) collective-permute-start(f32[12,512]{1,0:T(8,128)S(1)} %pad_maximum_fusion.6), channel_id=1, source_target_pairs={{0,6},{1,7},{2,4},{3,5},{4,2},{5,3},{6,0},{7,1},{8,14},{9,15},{10,... | collective-permute-start | bytes 73736 | tf_op jit(solution)/shard_map/ppermute | solution.py:523
  70.0 17.0 %collective-permute-start.5 = (f32[12,512]{1,0:T(8,128)S(1)}, f32[12,512]{1,0:T(8,128)S(1)}, u32[]{:S(2)}, u32[]{:S(2)}) collective-permute-start(f32[12,512]{1,0:T(8,128)S(1)} %pad_maximum_fusion.6), channel_id=1, source_target_pairs={{0,4},{1,5},{2,6},{3,7},{4,0},{5,1},{6,2},{7,3},{8,12},{9,13},{10,... | collective-permute-start | bytes 73736 | tf_op jit(solution)/shard_map/ppermute | solution.py:523
  81.2 32.0 %collective-permute-start.12 = (bf16[2,3,32,1536]{3,2,1,0:T(8,128)(2,1)}, bf16[2,3,32,1536]{3,2,1,0:T(8,128)(2,1)S(1)}, u32[]{:S(2)}, u32[]{:S(2)}) collective-permute-start(bf16[2,3,32,1536]{3,2,1,0:T(8,128)(2,1)} %get-tuple-element.106.refs_4_), channel_id=1, source_target_pairs={{0,16},{8,24},{16,0},{24,8},{1,17},{9,25},{17,1},{25,9},{2,18},{10... | collective-permute-start | bytes 1769480 | tf_op jit(solution)/shard_map/ppermute | solution.py:517
  82.7 30.6 %collective-permute-start.13 = (bf16[2,3,32,1536]{3,2,1,0:T(8,128)(2,1)}, bf16[2,3,32,1536]{3,2,1,0:T(8,128)(2,1)}, u32[]{:S(2)}, u32[]{:S(2)}) collective-permute-start(bf16[2,3,32,1536]{3,2,1,0:T(8,128)(2,1)} %get-tuple-element.107), channel_id=1, source_target_pairs={{0,1},{1,0},{2,3},{3,2},{4,5},{5,4},{6,7},{7,6},{8,9},{9,8},{10,11... | collective-permute-start | bytes 1769480 | tf_op jit(solution)/shard_map/ppermute | solution.py:520
  91.5 21.2 %collective-permute-start.20 = (bf16[1,3,32,1536]{3,2,1,0:T(8,128)(2,1)}, bf16[1,3,32,1536]{3,2,1,0:T(8,128)(2,1)S(1)}, u32[]{:S(2)}, u32[]{:S(2)}) collective-permute-start(bf16[1,3,32,1536]{3,2,1,0:T(8,128)(2,1)} %pack.4.refs_0_), channel_id=1, source_target_pairs={{0,4},{1,5},{2,6},{3,7},{4,0},{5,1},{6,2},{7,3},{8,12},{9,13},{10,... | collective-permute-start | bytes 884744 | tf_op jit(solution)/shard_map/ppermute | solution.py:523
  92.5 20.2 %collective-permute-start.21 = (bf16[1,3,32,1536]{3,2,1,0:T(8,128)(2,1)}, bf16[1,3,32,1536]{3,2,1,0:T(8,128)(2,1)S(1)}, u32[]{:S(2)}, u32[]{:S(2)}) collective-permute-start(bf16[1,3,32,1536]{3,2,1,0:T(8,128)(2,1)} %pack.4.refs_0_), channel_id=1, source_target_pairs={{0,6},{1,7},{2,4},{3,5},{4,2},{5,3},{6,0},{7,1},{8,14},{9,15},{10,... | collective-permute-start | bytes 884744 | tf_op jit(solution)/shard_map/ppermute | solution.py:523
  99.4 25.3 %collective-permute-start.14 = (bf16[4,3,32,1536]{3,2,1,0:T(8,128)(2,1)S(1)}, bf16[4,3,32,1536]{3,2,1,0:T(8,128)(2,1)}, u32[]{:S(2)}, u32[]{:S(2)}) collective-permute-start(bf16[4,3,32,1536]{3,2,1,0:T(8,128)(2,1)S(1)} %copy-done.4), channel_id=1, source_target_pairs={{0,8},{8,0},{16,24},{24,16},{1,9},{9,1},{17,25},{25,17},{2,10},{10... | collective-permute-start | bytes 3538952 | tf_op jit(solution)/shard_map/ppermute | solution.py:514
  112.7 13.5 %collective-permute-start.15 = (bf16[4,3,32,1536]{3,2,1,0:T(8,128)(2,1)}, bf16[4,3,32,1536]{3,2,1,0:T(8,128)(2,1)}, u32[]{:S(2)}, u32[]{:S(2)}) collective-permute-start(bf16[4,3,32,1536]{3,2,1,0:T(8,128)(2,1)} %copy-done.68), channel_id=1, source_target_pairs={{0,8},{8,0},{16,24},{24,16},{1,9},{9,1},{17,25},{25,17},{2,10},{10... | collective-permute-start | bytes 3538952 | tf_op jit(solution)/shard_map/ppermute | solution.py:514
  112.7 14.0 %collective-permute-start.16 = (bf16[4,3,32,1536]{3,2,1,0:T(8,128)(2,1)}, bf16[4,3,32,1536]{3,2,1,0:T(8,128)(2,1)}, u32[]{:S(2)}, u32[]{:S(2)}) collective-permute-start(bf16[4,3,32,1536]{3,2,1,0:T(8,128)(2,1)} %collective-permute-done.11.refs_1_.refs_7_.refs_14_), channel_id=1, source_target_pairs={{0,8},{8,0},{16,24},{24,16},{1,9},{9,1},{17,25},{25,17},{2,10},{10... | collective-permute-start | bytes 3538952 | tf_op jit(solution)/shard_map/ppermute | solution.py:514
  113.2 16.9 %collective-permute-start.17 = (bf16[2,3,32,1536]{3,2,1,0:T(8,128)(2,1)S(1)}, bf16[2,3,32,1536]{3,2,1,0:T(8,128)(2,1)}, u32[]{:S(2)}, u32[]{:S(2)}) collective-permute-start(bf16[2,3,32,1536]{3,2,1,0:T(8,128)(2,1)S(1)} %collective-permute-done.12.refs_8_.refs_15_), channel_id=1, source_target_pairs={{0,8},{8,0},{16,24},{24,16},{1,9},{9,1},{17,25},{25,17},{2,10},{10... | collective-permute-start | bytes 1769480 | tf_op jit(solution)/shard_map/ppermute | solution.py:514
  113.3 17.9 %collective-permute-start.18 = (bf16[2,3,32,1536]{3,2,1,0:T(8,128)(2,1)}, bf16[2,3,32,1536]{3,2,1,0:T(8,128)(2,1)}, u32[]{:S(2)}, u32[]{:S(2)}) collective-permute-start(bf16[2,3,32,1536]{3,2,1,0:T(8,128)(2,1)} %collective-permute-done.13.refs_9_.refs_16_), channel_id=1, source_target_pairs={{0,8},{8,0},{16,24},{24,16},{1,9},{9,1},{17,25},{25,17},{2,10},{10... | collective-permute-start | bytes 1769480 | tf_op jit(solution)/shard_map/ppermute | solution.py:514
  124.6 28.1 %collective-permute-start.22 = (bf16[4,3,32,1536]{3,2,1,0:T(8,128)(2,1)S(1)}, bf16[4,3,32,1536]{3,2,1,0:T(8,128)(2,1)S(1)}, u32[]{:S(2)}, u32[]{:S(2)}) collective-permute-start(bf16[4,3,32,1536]{3,2,1,0:T(8,128)(2,1)S(1)} %copy-done.5), channel_id=1, source_target_pairs={{0,1},{1,0},{2,3},{3,2},{4,5},{5,4},{6,7},{7,6},{8,9},{9,8},{10,11... | collective-permute-start | bytes 3538952 | tf_op jit(solution)/shard_map/ppermute | solution.py:520
  126.2 27.9 %collective-permute-start.23 = (bf16[4,3,32,1536]{3,2,1,0:T(8,128)(2,1)S(1)}, bf16[4,3,32,1536]{3,2,1,0:T(8,128)(2,1)}, u32[]{:S(2)}, u32[]{:S(2)}) collective-permute-start(bf16[4,3,32,1536]{3,2,1,0:T(8,128)(2,1)S(1)} %copy-done.5), channel_id=1, source_target_pairs={{0,16},{8,24},{16,0},{24,8},{1,17},{9,25},{17,1},{25,9},{2,18},{10... | collective-permute-start | bytes 3538952 | tf_op jit(solution)/shard_map/ppermute | solution.py:517
  126.8 34.1 %collective-permute-start.31 = (bf16[1,6,32,1536]{3,2,1,0:T(8,128)(2,1)}, bf16[1,6,32,1536]{3,2,1,0:T(8,128)(2,1)}, u32[]{:S(2)}, u32[]{:S(2)}) collective-permute-start(bf16[1,6,32,1536]{3,2,1,0:T(8,128)(2,1)} %pack.5.refs_15_.refs_0_), channel_id=1, source_target_pairs={{0,2},{1,3},{2,0},{3,1},{4,6},{5,7},{6,4},{7,5},{8,10},{9,11},{10,... | collective-permute-start | bytes 1769480 | tf_op jit(solution)/shard_map/ppermute | solution.py:523
  130.1 42.8 %collective-permute-start.32 = (bf16[1,6,32,1536]{3,2,1,0:T(8,128)(2,1)}, bf16[1,6,32,1536]{3,2,1,0:T(8,128)(2,1)}, u32[]{:S(2)}, u32[]{:S(2)}) collective-permute-start(bf16[1,6,32,1536]{3,2,1,0:T(8,128)(2,1)} %pack.5.refs_15_.refs_0_), channel_id=1, source_target_pairs={{0,4},{1,5},{2,6},{3,7},{4,0},{5,1},{6,2},{7,3},{8,12},{9,13},{10,... | collective-permute-start | bytes 1769480 | tf_op jit(solution)/shard_map/ppermute | solution.py:523
  131.2 41.7 %collective-permute-start.33 = (bf16[1,6,32,1536]{3,2,1,0:T(8,128)(2,1)}, bf16[1,6,32,1536]{3,2,1,0:T(8,128)(2,1)}, u32[]{:S(2)}, u32[]{:S(2)}) collective-permute-start(bf16[1,6,32,1536]{3,2,1,0:T(8,128)(2,1)} %pack.5.refs_15_.refs_0_), channel_id=1, source_target_pairs={{0,6},{1,7},{2,4},{3,5},{4,2},{5,3},{6,0},{7,1},{8,14},{9,15},{10,... | collective-permute-start | bytes 1769480 | tf_op jit(solution)/shard_map/ppermute | solution.py:523
  157.3 16.1 %collective-permute-start.24 = (bf16[2,3,32,1536]{3,2,1,0:T(8,128)(2,1)}, bf16[2,3,32,1536]{3,2,1,0:T(8,128)(2,1)}, u32[]{:S(2)}, u32[]{:S(2)}) collective-permute-start(bf16[2,3,32,1536]{3,2,1,0:T(8,128)(2,1)} %get-tuple-element.109.refs_4_), channel_id=1, source_target_pairs={{0,16},{8,24},{16,0},{24,8},{1,17},{9,25},{17,1},{25,9},{2,18},{10... | collective-permute-start | bytes 1769480 | tf_op jit(solution)/shard_map/ppermute | solution.py:517
  157.8 15.7 %collective-permute-start.25 = (bf16[2,3,32,1536]{3,2,1,0:T(8,128)(2,1)}, bf16[2,3,32,1536]{3,2,1,0:T(8,128)(2,1)}, u32[]{:S(2)}, u32[]{:S(2)}) collective-permute-start(bf16[2,3,32,1536]{3,2,1,0:T(8,128)(2,1)} %get-tuple-element.110), channel_id=1, source_target_pairs={{0,1},{1,0},{2,3},{3,2},{4,5},{5,4},{6,7},{7,6},{8,9},{9,8},{10,11... | collective-permute-start | bytes 1769480 | tf_op jit(solution)/shard_map/ppermute | solution.py:520
  160.8 18.2 %collective-permute-start.26 = (bf16[4,3,32,1536]{3,2,1,0:T(8,128)(2,1)S(1)}, bf16[4,3,32,1536]{3,2,1,0:T(8,128)(2,1)S(1)}, u32[]{:S(2)}, u32[]{:S(2)}) collective-permute-start(bf16[4,3,32,1536]{3,2,1,0:T(8,128)(2,1)S(1)} %copy-done.5), channel_id=1, source_target_pairs={{0,8},{8,0},{16,24},{24,16},{1,9},{9,1},{17,25},{25,17},{2,10},{10... | collective-permute-start | bytes 3538952 | tf_op jit(solution)/shard_map/ppermute | solution.py:514
  179.0 73.6 %collective-permute-start.41 = (bf16[4,6,32,1536]{3,2,1,0:T(8,128)(2,1)}, bf16[4,6,32,1536]{3,2,1,0:T(8,128)(2,1)}, u32[]{:S(2)}, u32[]{:S(2)}) collective-permute-start(bf16[4,6,32,1536]{3,2,1,0:T(8,128)(2,1)} %combine.10.refs_15_.refs_5_.refs_12_), channel_id=1, source_target_pairs={{0,1},{1,0},{2,3},{3,2},{4,5},{5,4},{6,7},{7,6},{8,9},{9,8},{10,11... | collective-permute-start | bytes 7077896 | tf_op jit(solution)/shard_map/ppermute | solution.py:520
  179.6 73.0 %collective-permute-start.42 = (bf16[4,6,32,1536]{3,2,1,0:T(8,128)(2,1)}, bf16[4,6,32,1536]{3,2,1,0:T(8,128)(2,1)}, u32[]{:S(2)}, u32[]{:S(2)}) collective-permute-start(bf16[4,6,32,1536]{3,2,1,0:T(8,128)(2,1)} %combine.10.refs_15_.refs_5_.refs_12_), channel_id=1, source_target_pairs={{0,16},{8,24},{16,0},{24,8},{1,17},{9,25},{17,1},{25,9},{2,18},{10... | collective-permute-start | bytes 7077896 | tf_op jit(solution)/shard_map/ppermute | solution.py:517
  208.0 26.7 %collective-permute-start.37 = (f32[12,512]{1,0:T(8,128)S(1)}, f32[12,512]{1,0:T(8,128)S(1)}, u32[]{:S(2)}, u32[]{:S(2)}) collective-permute-start(f32[12,512]{1,0:T(8,128)S(1)} %pad_maximum_fusion.8), channel_id=1, source_target_pairs={{0,17},{1,16},{2,19},{3,18},{4,21},{5,20},{6,23},{7,22},{8,25},{9,... | collective-permute-start | bytes 73736 | tf_op jit(solution)/shard_map/ppermute | solution.py:527
  210.0 24.7 %collective-permute-start.36 = (f32[12,512]{1,0:T(8,128)S(1)}, f32[12,512]{1,0:T(8,128)S(1)}, u32[]{:S(2)}, u32[]{:S(2)}) collective-permute-start(f32[12,512]{1,0:T(8,128)S(1)} %pad_maximum_fusion.8), channel_id=1, source_target_pairs={{0,1},{1,0},{2,3},{3,2},{4,5},{5,4},{6,7},{7,6},{8,9},{9,8},{10,11... | collective-permute-start | bytes 73736 | tf_op jit(solution)/shard_map/ppermute | solution.py:520
  210.6 24.2 %collective-permute-start.35 = (f32[12,512]{1,0:T(8,128)S(1)}, f32[12,512]{1,0:T(8,128)S(1)}, u32[]{:S(2)}, u32[]{:S(2)}) collective-permute-start(f32[12,512]{1,0:T(8,128)S(1)} %pad_maximum_fusion.8), channel_id=1, source_target_pairs={{0,16},{8,24},{16,0},{24,8},{1,17},{9,25},{17,1},{25,9},{2,18},{10... | collective-permute-start | bytes 73736 | tf_op jit(solution)/shard_map/ppermute | solution.py:517
  234.8 13.2 %collective-permute-start.40 = (f32[12,512]{1,0:T(8,128)S(1)}, f32[12,512]{1,0:T(8,128)S(1)}, u32[]{:S(2)}, u32[]{:S(2)}) collective-permute-start(f32[12,512]{1,0:T(8,128)S(1)} %pad_maximum_fusion.9), channel_id=1, source_target_pairs={{0,6},{1,7},{2,4},{3,5},{4,2},{5,3},{6,0},{7,1},{8,14},{9,15},{10,... | collective-permute-start | bytes 73736 | tf_op jit(solution)/shard_map/ppermute | solution.py:523
  237.3 13.3 %collective-permute-start.39 = (f32[12,512]{1,0:T(8,128)S(1)}, f32[12,512]{1,0:T(8,128)S(1)}, u32[]{:S(2)}, u32[]{:S(2)}) collective-permute-start(f32[12,512]{1,0:T(8,128)S(1)} %pad_maximum_fusion.9), channel_id=1, source_target_pairs={{0,4},{1,5},{2,6},{3,7},{4,0},{5,1},{6,2},{7,3},{8,12},{9,13},{10,... | collective-permute-start | bytes 73736 | tf_op jit(solution)/shard_map/ppermute | solution.py:523
  248.1 55.2 %collective-permute-start.45 = (bf16[4,6,32,1536]{3,2,1,0:T(8,128)(2,1)S(1)}, bf16[4,6,32,1536]{3,2,1,0:T(8,128)(2,1)}, u32[]{:S(2)}, u32[]{:S(2)}) collective-permute-start(bf16[4,6,32,1536]{3,2,1,0:T(8,128)(2,1)S(1)} %copy-done.1), channel_id=1, source_target_pairs={{0,8},{8,0},{16,24},{24,16},{1,9},{9,1},{17,25},{25,17},{2,10},{10... | collective-permute-start | bytes 7077896 | tf_op jit(solution)/shard_map/ppermute | solution.py:514
  257.6 25.3 %collective-permute-start.43 = (bf16[2,6,32,1536]{3,2,1,0:T(8,128)(2,1)}, bf16[2,6,32,1536]{3,2,1,0:T(8,128)(2,1)S(1)}, u32[]{:S(2)}, u32[]{:S(2)}) collective-permute-start(bf16[2,6,32,1536]{3,2,1,0:T(8,128)(2,1)} %get-tuple-element.115.refs_15_), channel_id=1, source_target_pairs={{0,16},{8,24},{16,0},{24,8},{1,17},{9,25},{17,1},{25,9},{2,18},{10... | collective-permute-start | bytes 3538952 | tf_op jit(solution)/shard_map/ppermute | solution.py:517
  259.2 44.1 %collective-permute-start.46 = (bf16[4,6,32,1536]{3,2,1,0:T(8,128)(2,1)}, bf16[4,6,32,1536]{3,2,1,0:T(8,128)(2,1)}, u32[]{:S(2)}, u32[]{:S(2)}) collective-permute-start(bf16[4,6,32,1536]{3,2,1,0:T(8,128)(2,1)} %collective-permute-done.41.refs_0_.refs_6_.refs_13_), channel_id=1, source_target_pairs={{0,8},{8,0},{16,24},{24,16},{1,9},{9,1},{17,25},{25,17},{2,10},{10... | collective-permute-start | bytes 7077896 | tf_op jit(solution)/shard_map/ppermute | solution.py:514
  259.2 44.1 %collective-permute-start.47 = (bf16[4,6,32,1536]{3,2,1,0:T(8,128)(2,1)}, bf16[4,6,32,1536]{3,2,1,0:T(8,128)(2,1)}, u32[]{:S(2)}, u32[]{:S(2)}) collective-permute-start(bf16[4,6,32,1536]{3,2,1,0:T(8,128)(2,1)} %collective-permute-done.42.refs_1_.refs_7_.refs_14_), channel_id=1, source_target_pairs={{0,8},{8,0},{16,24},{24,16},{1,9},{9,1},{17,25},{25,17},{2,10},{10... | collective-permute-start | bytes 7077896 | tf_op jit(solution)/shard_map/ppermute | solution.py:514
  259.7 28.2 %collective-permute-start.44 = (bf16[2,6,32,1536]{3,2,1,0:T(8,128)(2,1)}, bf16[2,6,32,1536]{3,2,1,0:T(8,128)(2,1)}, u32[]{:S(2)}, u32[]{:S(2)}) collective-permute-start(bf16[2,6,32,1536]{3,2,1,0:T(8,128)(2,1)} %get-tuple-element.116), channel_id=1, source_target_pairs={{0,1},{1,0},{2,3},{3,2},{4,5},{5,4},{6,7},{7,6},{8,9},{9,8},{10,11... | collective-permute-start | bytes 3538952 | tf_op jit(solution)/shard_map/ppermute | solution.py:520
  282.9 20.4 %collective-permute-start.48 = (bf16[2,6,32,1536]{3,2,1,0:T(8,128)(2,1)S(1)}, bf16[2,6,32,1536]{3,2,1,0:T(8,128)(2,1)}, u32[]{:S(2)}, u32[]{:S(2)}) collective-permute-start(bf16[2,6,32,1536]{3,2,1,0:T(8,128)(2,1)S(1)} %collective-permute-done.43.refs_8_.refs_15_), channel_id=1, source_target_pairs={{0,8},{8,0},{16,24},{24,16},{1,9},{9,1},{17,25},{25,17},{2,10},{10... | collective-permute-start | bytes 3538952 | tf_op jit(solution)/shard_map/ppermute | solution.py:514
  287.9 15.4 %collective-permute-start.49 = (bf16[2,6,32,1536]{3,2,1,0:T(8,128)(2,1)}, bf16[2,6,32,1536]{3,2,1,0:T(8,128)(2,1)}, u32[]{:S(2)}, u32[]{:S(2)}) collective-permute-start(bf16[2,6,32,1536]{3,2,1,0:T(8,128)(2,1)} %collective-permute-done.44.refs_9_.refs_16_), channel_id=1, source_target_pairs={{0,8},{8,0},{16,24},{24,16},{1,9},{9,1},{17,25},{25,17},{2,10},{10... | collective-permute-start | bytes 3538952 | tf_op jit(solution)/shard_map/ppermute | solution.py:514
  366.0 50.6 %collective-permute-start.66 = (bf16[16,3,32,1536]{3,2,1,0:T(8,128)(2,1)}, bf16[16,3,32,1536]{3,2,1,0:T(8,128)(2,1)}, u32[]{:S(2)}, u32[]{:S(2)}) collective-permute-start(bf16[16,3,32,1536]{3,2,1,0:T(8,128)(2,1)} %get-tuple-element.171), channel_id=1, source_target_pairs={{0,8},{8,0},{16,24},{24,16},{1,9},{9,1},{17,25},{25,17},{2,10},{10... | collective-permute-start | bytes 14155784 | tf_op jit(solution)/shard_map/ppermute | solution.py:514
  397.6 24.7 %collective-permute-start.65 = (bf16[16,3,32,1536]{3,2,1,0:T(8,128)(2,1)}, bf16[16,3,32,1536]{3,2,1,0:T(8,128)(2,1)}, u32[]{:S(2)}, u32[]{:S(2)}) collective-permute-start(bf16[16,3,32,1536]{3,2,1,0:T(8,128)(2,1)} %get-tuple-element.169), channel_id=1, source_target_pairs={{0,8},{8,0},{16,24},{24,16},{1,9},{9,1},{17,25},{25,17},{2,10},{10... | collective-permute-start | bytes 14155784 | tf_op jit(solution)/shard_map/ppermute | solution.py:514
  413.1 17.4 %collective-permute-start.55 = (f32[32,512]{1,0:T(8,128)S(1)}, f32[32,512]{1,0:T(8,128)S(1)}, u32[]{:S(2)}, u32[]{:S(2)}) collective-permute-start(f32[32,512]{1,0:T(8,128)S(1)} %add_add_fusion.3), channel_id=1, source_target_pairs={{0,4},{1,5},{2,6},{3,7},{4,0},{5,1},{6,2},{7,3},{8,12},{9,13},{10,... | collective-permute-start | bytes 196616 | tf_op jit(solution)/shard_map/ppermute | solution.py:523
  414.4 16.0 %collective-permute-start.56 = (f32[32,512]{1,0:T(8,128)S(1)}, f32[32,512]{1,0:T(8,128)S(1)}, u32[]{:S(2)}, u32[]{:S(2)}) collective-permute-start(f32[32,512]{1,0:T(8,128)S(1)} %add_add_fusion.3), channel_id=1, source_target_pairs={{0,6},{1,7},{2,4},{3,5},{4,2},{5,3},{6,0},{7,1},{8,14},{9,15},{10,... | collective-permute-start | bytes 196616 | tf_op jit(solution)/shard_map/ppermute | solution.py:523
  416.4 14.0 %collective-permute-start.54 = (f32[32,512]{1,0:T(8,128)S(1)}, f32[32,512]{1,0:T(8,128)S(1)}, u32[]{:S(2)}, u32[]{:S(2)}) collective-permute-start(f32[32,512]{1,0:T(8,128)S(1)} %add_add_fusion.3), channel_id=1, source_target_pairs={{0,2},{1,3},{2,0},{3,1},{4,6},{5,7},{6,4},{7,5},{8,10},{9,11},{10,... | collective-permute-start | bytes 196616 | tf_op jit(solution)/shard_map/ppermute | solution.py:523
  511.2 38.3 %collective-permute-start.70 = (bf16[16,3,32,1536]{3,2,1,0:T(8,128)(2,1)}, bf16[16,3,32,1536]{3,2,1,0:T(8,128)(2,1)}, u32[]{:S(2)}, u32[]{:S(2)}) collective-permute-start(bf16[16,3,32,1536]{3,2,1,0:T(8,128)(2,1)} %get-tuple-element.173), channel_id=1, source_target_pairs={{0,8},{8,0},{16,24},{24,16},{1,9},{9,1},{17,25},{25,17},{2,10},{10... | collective-permute-start | bytes 14155784 | tf_op jit(solution)/shard_map/ppermute | solution.py:514
  523.1 21.4 %collective-permute-start.72 = (bf16[2,3,32,1536]{3,2,1,0:T(8,128)(2,1)}, bf16[2,3,32,1536]{3,2,1,0:T(8,128)(2,1)S(1)}, u32[]{:S(2)}, u32[]{:S(2)}) collective-permute-start(bf16[2,3,32,1536]{3,2,1,0:T(8,128)(2,1)} %get-tuple-element.248.refs_23_), channel_id=1, source_target_pairs={{0,1},{1,0},{2,3},{3,2},{4,5},{5,4},{6,7},{7,6},{8,9},{9,8},{10,11... | collective-permute-start | bytes 1769480 | tf_op jit(solution)/shard_map/ppermute | solution.py:520
  524.7 19.8 %collective-permute-start.71 = (bf16[2,3,32,1536]{3,2,1,0:T(8,128)(2,1)S(1)}, bf16[2,3,32,1536]{3,2,1,0:T(8,128)(2,1)S(1)}, u32[]{:S(2)}, u32[]{:S(2)}) collective-permute-start(bf16[2,3,32,1536]{3,2,1,0:T(8,128)(2,1)S(1)} %copy-done.22), channel_id=1, source_target_pairs={{0,16},{8,24},{16,0},{24,8},{1,17},{9,25},{17,1},{25,9},{2,18},{10... | collective-permute-start | bytes 1769480 | tf_op jit(solution)/shard_map/ppermute | solution.py:517
  552.6 18.3 %collective-permute-start.76 = (bf16[2,3,32,1536]{3,2,1,0:T(8,128)(2,1)}, bf16[2,3,32,1536]{3,2,1,0:T(8,128)(2,1)S(1)}, u32[]{:S(2)}, u32[]{:S(2)}) collective-permute-start(bf16[2,3,32,1536]{3,2,1,0:T(8,128)(2,1)} %get-tuple-element.184.refs_8_), channel_id=1, source_target_pairs={{0,1},{1,0},{2,3},{3,2},{4,5},{5,4},{6,7},{7,6},{8,9},{9,8},{10,11... | collective-permute-start | bytes 1769480 | tf_op jit(solution)/shard_map/ppermute | solution.py:520
  553.6 17.3 %collective-permute-start.75 = (bf16[2,3,32,1536]{3,2,1,0:T(8,128)(2,1)}, bf16[2,3,32,1536]{3,2,1,0:T(8,128)(2,1)S(1)}, u32[]{:S(2)}, u32[]{:S(2)}) collective-permute-start(bf16[2,3,32,1536]{3,2,1,0:T(8,128)(2,1)} %get-tuple-element.182.refs_7_), channel_id=1, source_target_pairs={{0,16},{8,24},{16,0},{24,8},{1,17},{9,25},{17,1},{25,9},{2,18},{10... | collective-permute-start | bytes 1769480 | tf_op jit(solution)/shard_map/ppermute | solution.py:517
  554.4 36.3 %collective-permute-start.74 = (bf16[4,3,32,1536]{3,2,1,0:T(8,128)(2,1)}, bf16[4,3,32,1536]{3,2,1,0:T(8,128)(2,1)S(1)}, u32[]{:S(2)}, u32[]{:S(2)}) collective-permute-start(bf16[4,3,32,1536]{3,2,1,0:T(8,128)(2,1)} %get-tuple-element.180.refs_6_), channel_id=1, source_target_pairs={{0,16},{8,24},{16,0},{24,8},{1,17},{9,25},{17,1},{25,9},{2,18},{10... | collective-permute-start | bytes 3538952 | tf_op jit(solution)/shard_map/ppermute | solution.py:517
  555.6 47.8 %collective-permute-start.73 = (bf16[4,3,32,1536]{3,2,1,0:T(8,128)(2,1)}, bf16[4,3,32,1536]{3,2,1,0:T(8,128)(2,1)S(1)}, u32[]{:S(2)}, u32[]{:S(2)}) collective-permute-start(bf16[4,3,32,1536]{3,2,1,0:T(8,128)(2,1)} %get-tuple-element.179.refs_5_), channel_id=1, source_target_pairs={{0,1},{1,0},{2,3},{3,2},{4,5},{5,4},{6,7},{7,6},{8,9},{9,8},{10,11... | collective-permute-start | bytes 3538952 | tf_op jit(solution)/shard_map/ppermute | solution.py:520
  606.3 32.9 %collective-permute-start.78 = (bf16[4,3,32,1536]{3,2,1,0:T(8,128)(2,1)}, bf16[4,3,32,1536]{3,2,1,0:T(8,128)(2,1)}, u32[]{:S(2)}, u32[]{:S(2)}) collective-permute-start(bf16[4,3,32,1536]{3,2,1,0:T(8,128)(2,1)} %get-tuple-element.186.refs_8_), channel_id=1, source_target_pairs={{0,16},{8,24},{16,0},{24,8},{1,17},{9,25},{17,1},{25,9},{2,18},{10... | collective-permute-start | bytes 3538952 | tf_op jit(solution)/shard_map/ppermute | solution.py:517
  608.4 30.8 %collective-permute-start.77 = (bf16[4,3,32,1536]{3,2,1,0:T(8,128)(2,1)}, bf16[4,3,32,1536]{3,2,1,0:T(8,128)(2,1)}, u32[]{:S(2)}, u32[]{:S(2)}) collective-permute-start(bf16[4,3,32,1536]{3,2,1,0:T(8,128)(2,1)} %get-tuple-element.185.refs_7_), channel_id=1, source_target_pairs={{0,1},{1,0},{2,3},{3,2},{4,5},{5,4},{6,7},{7,6},{8,9},{9,8},{10,11... | collective-permute-start | bytes 3538952 | tf_op jit(solution)/shard_map/ppermute | solution.py:520
  612.5 24.3 %collective-permute-start.80 = (bf16[1,3,32,1536]{3,2,1,0:T(8,128)(2,1)}, bf16[1,3,32,1536]{3,2,1,0:T(8,128)(2,1)}, u32[]{:S(2)}, u32[]{:S(2)}) collective-permute-start(bf16[1,3,32,1536]{3,2,1,0:T(8,128)(2,1)} %get-tuple-element.188.refs_5_), channel_id=1, source_target_pairs={{0,4},{1,5},{2,6},{3,7},{4,0},{5,1},{6,2},{7,3},{8,12},{9,13},{10,... | collective-permute-start | bytes 884744 | tf_op jit(solution)/shard_map/ppermute | solution.py:523
  612.7 24.1 %collective-permute-start.79 = (bf16[1,3,32,1536]{3,2,1,0:T(8,128)(2,1)}, bf16[1,3,32,1536]{3,2,1,0:T(8,128)(2,1)}, u32[]{:S(2)}, u32[]{:S(2)}) collective-permute-start(bf16[1,3,32,1536]{3,2,1,0:T(8,128)(2,1)} %get-tuple-element.187.refs_4_), channel_id=1, source_target_pairs={{0,2},{1,3},{2,0},{3,1},{4,6},{5,7},{6,4},{7,5},{8,10},{9,11},{10,... | collective-permute-start | bytes 884744 | tf_op jit(solution)/shard_map/ppermute | solution.py:523
  643.9 23.2 %collective-permute-start.83 = (bf16[1,3,32,1536]{3,2,1,0:T(8,128)(2,1)}, bf16[1,3,32,1536]{3,2,1,0:T(8,128)(2,1)S(1)}, u32[]{:S(2)}, u32[]{:S(2)}) collective-permute-start(bf16[1,3,32,1536]{3,2,1,0:T(8,128)(2,1)} %get-tuple-element.191.refs_3_), channel_id=1, source_target_pairs={{0,4},{1,5},{2,6},{3,7},{4,0},{5,1},{6,2},{7,3},{8,12},{9,13},{10,... | collective-permute-start | bytes 884744 | tf_op jit(solution)/shard_map/ppermute | solution.py:523
  643.9 23.2 %collective-permute-start.82 = (bf16[1,3,32,1536]{3,2,1,0:T(8,128)(2,1)}, bf16[1,3,32,1536]{3,2,1,0:T(8,128)(2,1)S(1)}, u32[]{:S(2)}, u32[]{:S(2)}) collective-permute-start(bf16[1,3,32,1536]{3,2,1,0:T(8,128)(2,1)} %get-tuple-element.190.refs_2_), channel_id=1, source_target_pairs={{0,2},{1,3},{2,0},{3,1},{4,6},{5,7},{6,4},{7,5},{8,10},{9,11},{10,... | collective-permute-start | bytes 884744 | tf_op jit(solution)/shard_map/ppermute | solution.py:523
  648.6 26.7 %collective-permute-start.68 = (bf16[1,6,32,1536]{3,2,1,0:T(8,128)(2,1)}, bf16[1,6,32,1536]{3,2,1,0:T(8,128)(2,1)S(1)}, u32[]{:S(2)}, u32[]{:S(2)}) collective-permute-start(bf16[1,6,32,1536]{3,2,1,0:T(8,128)(2,1)} %reduce-scatter.2.cloned.1.call-done.refs_0_), channel_id=1, source_target_pairs={{0,16},{8,24},{16,0},{24,8},{1,17},{9,25},{17,1},{25,9},{2,18},{10... | collective-permute-start | bytes 1769480 | tf_op jit(solution)/shard_map/ppermute | solution.py:517
  654.4 14.9 %collective-permute-start.85 = (bf16[1,3,32,1536]{3,2,1,0:T(8,128)(2,1)}, bf16[1,3,32,1536]{3,2,1,0:T(8,128)(2,1)S(1)}, u32[]{:S(2)}, u32[]{:S(2)}) collective-permute-start(bf16[1,3,32,1536]{3,2,1,0:T(8,128)(2,1)} %get-tuple-element.193.refs_0_.refs_1_), channel_id=1, source_target_pairs={{0,8},{8,0},{16,24},{24,16},{1,9},{9,1},{17,25},{25,17},{2,10},{10... | collective-permute-start | bytes 884744 | tf_op jit(solution)/shard_map/ppermute | solution.py:514
  675.2 13.0 %collective-permute-start.69 = (bf16[1,6,32,1536]{3,2,1,0:T(8,128)(2,1)S(1)}, bf16[1,6,32,1536]{3,2,1,0:T(8,128)(2,1)S(1)}, u32[]{:S(2)}, u32[]{:S(2)}) collective-permute-start(bf16[1,6,32,1536]{3,2,1,0:T(8,128)(2,1)S(1)} %collective-permute-done.68.refs_2_), channel_id=1, source_target_pairs={{0,8},{8,0},{16,24},{24,16},{1,9},{9,1},{17,25},{25,17},{2,10},{10... | collective-permute-start | bytes 1769480 | tf_op jit(solution)/shard_map/ppermute | solution.py:514
  (111 other events, 971.9 us)
Sparse Core Ops, SparseCore 0:
  430.6 195.6 reduce-scatter.1

commit v3 on v2

--- a/solution.py
+++ b/solution.py
@@ -19,7 +19,6 @@
 VMEM_LIMIT = 60 * 1024 * 1024
 GATHERS = ((0, 3), (3, 6), (6, 12))
 GROUPS = ((0, 3), (3, 6), (6, 9), (9, 12))
-RING_SUM = (6, 12)
 
 
 def gate(x):
@@ -48,7 +47,8 @@
     pltpu.make_async_copy(whole, whole, sems.at[part]).wait()
 
 
-def forward_kernel(n, first, n_arrays, n_tokens, pr, tile, table, *refs):
+def forward_kernel(n, first, n_arrays, n_tokens, final, pr, tile, table, *refs):
+    base, refs = (refs[0], refs[1:]) if final else (None, refs)
     hidden_in, normed, mask, bias_in, bias_out = refs[:5]
     arrays = refs[5 : 5 + n_arrays]
     refs = refs[n_tokens:]
@@ -99,25 +99,27 @@
 
     @pl.when(step == n - 1)
     def _():
-        hidden_out[...] = hid[...]
-
-
-def forward_chunk(table, hidden, normed, masks, bias_in, bias_out, arrays, first, tokens=(), tile=TILE):
-    n = masks.shape[0]
+        hidden_out[...] = (base[...] + hid[...]).astype(BF16) if final else hid[...]
+
+
+def forward_chunk(table, lo, hi, hidden, normed, masks, bias_in, bias_out, arrays, first, tokens=(), base=None, tile=TILE):
+    n = hi - lo
+    bases = () if base is None else (base,)
     rows, cols = hidden.shape
     pr = arrays[0].shape[2]
     depth = 2 * cols
     whole = pl.BlockSpec((rows, cols), lambda i, *_: (0, 0))
-    row = lambda width: pl.BlockSpec((1, 1, width), lambda i, *_: (i, 0, 0))
+    row = lambda width: pl.BlockSpec((1, 1, width), lambda i, *_: (lo + i, 0, 0))
     per = pl.BlockSpec((1, rows, cols), lambda i, *_: (i, 0, 0))
     turned = pl.BlockSpec((1, cols, rows), lambda i, *_: (i, 0, 0))
     saved = [jax.ShapeDtypeStruct((n, rows, cols), t) for t in (F32,) * 5] + [jax.ShapeDtypeStruct((n, cols, rows), BF16)] * 2
     return pl.pallas_call(
-        functools.partial(forward_kernel, n, first, len(arrays), len(tokens), pr, tile),
+        functools.partial(forward_kernel, n, first, len(arrays), len(tokens), base is not None, pr, tile),
         grid_spec=pltpu.PrefetchScalarGridSpec(
             num_scalar_prefetch=1,
             grid=(n,),
-            in_specs=[whole, whole, row(cols), row(2 * cols), row(cols)] + [pl.BlockSpec(memory_space=pl.ANY)] * (len(arrays) + len(tokens)),
+            in_specs=[whole] * len(bases) + [whole, whole, row(cols), row(2 * cols), row(cols)]
+            + [pl.BlockSpec(memory_space=pl.ANY)] * (len(arrays) + len(tokens)),
             out_specs=[whole] + [per] * 5 + [turned] * 2,
             scratch_shapes=[
                 pltpu.VMEM((n, depth, 3 * cols), BF16),
@@ -125,22 +127,22 @@
                 pltpu.SemaphoreType.DMA((2,)),
             ],
         ),
-        out_shape=[jax.ShapeDtypeStruct((rows, cols), F32)] + saved,
+        out_shape=[jax.ShapeDtypeStruct((rows, cols), F32 if base is None else BF16)] + saved,
         compiler_params=pltpu.CompilerParams(vmem_limit_bytes=VMEM_LIMIT),
         cost_estimate=LONG,
         name="forward_sections",
-    )(table, hidden, normed, masks[:, None], bias_in[:, None], bias_out[:, None], *arrays, *tokens)
+    )(table, *bases, hidden, normed, masks, bias_in, bias_out, *arrays, *tokens)
 
 
 def backward_kernel(n, first, n_in, n_out, n_tokens, pr, tile, table, *refs):
-    gh_in, normed, x_turned, mask, mask_column = refs[:5]
-    factors = refs[5:10]
-    h_turned, rh_turned = refs[10:12]
-    arrays = refs[12 : 12 + n_in]
-    refs = refs[12 + n_in + n_tokens :]
-    gh_out, gn_out, g_mask, g_bin, g_bout = refs[:5]
-    outs = refs[5 : 5 + n_out]
-    wbuf, gh, gn, gg, gr, stage, sems, out_sems = refs[5 + n_out :]
+    gh_in, normed, x_turned, mask = refs[:4]
+    factors = refs[4:9]
+    h_turned, rh_turned = refs[9:11]
+    arrays = refs[11 : 11 + n_in]
+    refs = refs[11 + n_in + n_tokens :]
+    gh_out, gn_out, vectors = refs[:3]
+    outs = refs[3 : 3 + n_out]
+    wbuf, gh, gn, gg, gr, stage, sems, out_sems = refs[3 + n_out :]
     step = pl.program_id(0)
     sec = n - 1 - step
     rows, cols = gh.shape
@@ -200,9 +202,9 @@
         m_sum = m_sum + jnp.sum(gm * normed[at, :], axis=0, keepdims=True)
         bi_sum = bi_sum + jnp.sum(gates.astype(F32), axis=0, keepdims=True)
         bo_sum = bo_sum + jnp.sum(grad_raw.astype(F32), axis=0, keepdims=True)
-    g_mask[0] = m_sum * float(cols)
-    g_bin[0] = bi_sum
-    g_bout[0] = bo_sum
+    vectors[0, :, :cols] = m_sum * float(cols)
+    vectors[0, :, cols : 3 * cols] = bi_sum
+    vectors[0, :, 3 * cols :] = bo_sum
 
     slot = lax.rem(step, 2)
     if n > 2:
@@ -213,7 +215,8 @@
     stage[slot, :cols, wide:] = jnp.dot(rh_turned[0], gr[...], preferred_element_type=F32).astype(BF16)
     stage[slot, cols:, wide:] = jnp.dot(x_turned[...], gr[...], preferred_element_type=F32).astype(BF16)
     masked = jnp.dot(x_turned[...], gg[...], preferred_element_type=F32)
-    stage[slot, :cols, :wide] = (masked * mask_column[0]).astype(BF16)
+    mask_column = jnp.broadcast_to(mask_row, (128, cols)).T[:, :1]
+    stage[slot, :cols, :wide] = (masked * mask_column).astype(BF16)
     stage[slot, cols:, :wide] = jnp.dot(h_turned[0], gg[...], preferred_element_type=F32).astype(BF16)
 
     at = sum(array.shape[0] for array in arrays)
@@ -232,29 +235,27 @@
         wait_out(slot)
 
 
-def backward_chunk(table, gh, normed, x_turned, masks, saved, first_saved, arrays, first, out_slots, tokens=(), tile=TILE):
-    n = masks.shape[0]
+def backward_chunk(table, lo, hi, gh, normed, x_turned, masks, saved, arrays, first, out_slots, tokens=(), tile=TILE):
+    n = hi - lo
     rows, cols = gh.shape
     pr = arrays[0].shape[2]
     depth = 2 * cols
     whole = pl.BlockSpec((rows, cols), lambda i, *_: (0, 0))
-    row = lambda width: pl.BlockSpec((1, 1, width), lambda i, *_: (n - 1 - i, 0, 0))
-    turned = pl.BlockSpec((1, cols, rows), lambda i, *_: (first_saved + n - 1 - i, 0, 0))
-    per = pl.BlockSpec((1, rows, cols), lambda i, *_: (first_saved + n - 1 - i, 0, 0))
-    column = pl.BlockSpec((1, cols, 1), lambda i, *_: (n - 1 - i, 0, 0))
+    row = lambda width: pl.BlockSpec((1, 1, width), lambda i, *_: (hi - 1 - i, 0, 0))
+    turned = pl.BlockSpec((1, cols, rows), lambda i, *_: (first + n - 1 - i, 0, 0))
+    per = pl.BlockSpec((1, rows, cols), lambda i, *_: (first + n - 1 - i, 0, 0))
     any_spec = pl.BlockSpec(memory_space=pl.ANY)
     state = jax.ShapeDtypeStruct((rows, cols), F32)
-    vec = lambda width: jax.ShapeDtypeStruct((n, 1, width), F32)
     results = pl.pallas_call(
         functools.partial(backward_kernel, n, first, len(arrays), len(out_slots), len(tokens), pr, tile),
         grid_spec=pltpu.PrefetchScalarGridSpec(
             num_scalar_prefetch=1,
             grid=(n,),
-            in_specs=[whole, whole, pl.BlockSpec((cols, rows), lambda i, *_: (0, 0)), row(cols), column]
+            in_specs=[whole, whole, pl.BlockSpec((cols, rows), lambda i, *_: (0, 0)), row(cols)]
             + [per] * 5
             + [turned] * 2
             + [any_spec] * (len(arrays) + len(tokens)),
-            out_specs=[whole, whole, row(cols), row(depth), row(cols)] + [any_spec] * len(out_slots),
+            out_specs=[whole, whole, pl.BlockSpec((1, 1, 2 * depth), lambda i, *_: (n - 1 - i, 0, 0))] + [any_spec] * len(out_slots),
             scratch_shapes=[
                 pltpu.VMEM((n, depth, 3 * cols), BF16),
                 pltpu.VMEM((rows, cols), F32),
@@ -266,14 +267,13 @@
                 pltpu.SemaphoreType.DMA((2,)),
             ],
         ),
-        out_shape=[state, state, vec(cols), vec(depth), vec(cols)]
+        out_shape=[state, state, jax.ShapeDtypeStruct((n, 1, 2 * depth), F32)]
         + [jax.ShapeDtypeStruct((s, n, pr, 3 * cols), BF16) for s in out_slots],
         compiler_params=pltpu.CompilerParams(vmem_limit_bytes=VMEM_LIMIT),
         cost_estimate=LONG,
         name="backward_sections",
-    )(table, gh, normed, x_turned, masks[:, None], masks[:, :, None], *saved, *arrays, *tokens)
-    gh, gn, g_mask, g_bin, g_bout = results[:5]
-    return gh, gn, g_mask[:, 0], g_bin[:, 0], g_bout[:, 0], results[5:]
+    )(table, gh, normed, x_turned, masks, *saved, *arrays, *tokens)
+    return *results[:3], results[3:]
 
 
 def pick(micro, table):
@@ -356,8 +356,8 @@
     )(u, micro, stats, gain[None], shift[None])
 
 
-def pool_kernel(u_ref, micro_ref, stats_ref, *refs):
-    parts, (total_ref, pooled_ref) = refs[:-2], refs[-2:]
+def pool_kernel(n_parts, u_ref, micro_ref, stats_ref, *refs):
+    parts, (total_ref, pooled_ref) = refs[:n_parts], refs[-2:]
     stats = stats_ref[...]
     scale = lax.rsqrt(stats[2 * MB :] / stats[:MB] + EPSILON)
     micro = micro_ref[...]
@@ -370,18 +370,26 @@
         pooled_ref[MB + b : MB + b + 1, :] = jnp.sum(jnp.where(micro == b, product, 0.0), axis=0, keepdims=True)
 
 
-def pool_grads(u, micro, stats, parts):
+def in_vmem(arrays, tokens):
+    vmem, any_spec = pl.BlockSpec(memory_space=pltpu.VMEM), pl.BlockSpec(memory_space=pl.ANY)
+    return [vmem] * len(arrays) + [any_spec] * len(tokens)
+
+
+def pool_grads(u, micro, stats, parts, tokens=()):
     rows, cols = u.shape
+    args = (u, micro, stats, *parts)
     return pl.pallas_call(
-        pool_kernel,
+        functools.partial(pool_kernel, len(parts)),
+        in_specs=in_vmem(args, tokens),
         out_shape=[jax.ShapeDtypeStruct((rows, cols), F32), jax.ShapeDtypeStruct((2 * MB, cols), F32)],
         compiler_params=pltpu.CompilerParams(vmem_limit_bytes=VMEM_LIMIT),
-        cost_estimate=COST,
+        cost_estimate=LONG,
         name="pool_grads",
-    )(u, micro, stats, *parts)
-
-
-def carry_kernel(u_ref, micro_ref, valid_ref, stats_ref, gain_ref, total_ref, pooled_ref, carried_ref, out_ref):
+    )(*args, *tokens)
+
+
+def carry_kernel(u_ref, micro_ref, valid_ref, stats_ref, gain_ref, total_ref, pooled_ref, carried_ref, *refs):
+    out_ref = refs[-1]
     stats = stats_ref[...]
     gain = gain_ref[...]
     counts = stats[:MB]
@@ -397,15 +405,17 @@
     )
 
 
-def carry_grads(u, micro, valid, stats, gain, total, pooled, carried):
+def carry_grads(u, micro, valid, stats, gain, total, pooled, carried, tokens=()):
     rows, cols = u.shape
+    args = (u, micro, valid, stats, gain[None], total, pooled, carried)
     return pl.pallas_call(
         carry_kernel,
+        in_specs=in_vmem(args, tokens),
         out_shape=jax.ShapeDtypeStruct((rows, cols), F32),
         compiler_params=pltpu.CompilerParams(vmem_limit_bytes=VMEM_LIMIT),
         cost_estimate=COST,
         name="carry_grads",
-    )(u, micro, valid, stats, gain[None], total, pooled, carried)
+    )(*args, *tokens)
 
 
 def feature_mask(logits, thresh):
@@ -504,31 +514,67 @@
     return sum(v.astype(F32) for v in terms).astype(BF16)
 
 
+class Sending:
+    def __init__(self, steps):
+        self.steps, self.ready, self.result = steps, None, None
+        self.resume(None)
+
+    def resume(self, sent):
+        try:
+            self.ready = self.steps.send(sent)
+        except StopIteration as stop:
+            self.ready, self.result = None, stop.value
+
+    def send(self, tokens):
+        if self.ready is None:
+            return list(tokens)
+        sent = tie(self.ready, list(tokens))
+        self.resume(sent)
+        return sent
+
+
 class CubeTransfers:
     def __init__(self, dp_size, fsdp_size):
         self.dp_size, self.fsdp_size = dp_size, fsdp_size
         self.slots = [4, 4, 4, 2, 2, 16]
-        self.ring_slots = [dp_size * fsdp_size // 2] * 2
+        self.arrived, self.before_core = [], []
+
+    def permute(self, v, axis, size, flip):
+        self.arrived.append(lax.ppermute(v, axis, along(axis, size, flip)))
+        return self.arrived[-1]
+
+    def take_arrived(self):
+        arrived, self.arrived = self.arrived, []
+        return arrived
 
     def core(self, v):
-        return lax.ppermute(v, "dp", along("dp", self.dp_size, 1))
+        return self.permute(v, "dp", self.dp_size, 1)
 
     def x(self, v):
-        return lax.ppermute(v, "dp", along("dp", self.dp_size, 2))
+        return self.permute(v, "dp", self.dp_size, 2)
 
     def y(self, v):
-        return lax.ppermute(v, "fsdp", along("fsdp", self.fsdp_size, 1))
+        return self.permute(v, "fsdp", self.fsdp_size, 1)
 
     def z(self, v, flip):
-        return lax.ppermute(v, "fsdp", along("fsdp", self.fsdp_size, 2 * flip))
+        return self.permute(v, "fsdp", self.fsdp_size, 2 * flip)
 
     def far(self, v):
         size = self.dp_size * self.fsdp_size
         return lax.ppermute(v, ("dp", "fsdp"), along(("dp", "fsdp"), size, 2 * self.fsdp_size + 1))
 
-    def all_reduce(self, v, merge):
+    def all_reduce(self, v, merge, beside=()):
         v = merge(v, self.core(v))
         v = merge(merge(v, self.x(v)), merge(self.y(v), self.far(v)))
+        (v,) = tie([v], beside)
+        return merge(merge(v, self.z(v, 1)), merge(self.z(v, 2), self.z(v, 3)))
+
+    def all_reduce_steps(self, v, merge):
+        (v,) = yield [v]
+        v = merge(v, self.core(v))
+        (v,) = yield [v]
+        v = merge(merge(v, self.x(v)), merge(self.y(v), self.far(v)))
+        (v,) = yield [v]
         return merge(merge(v, self.z(v, 1)), merge(self.z(v, 2), self.z(v, 3)))
 
     def table(self, shard_rows):
@@ -543,31 +589,26 @@
         return jnp.stack(rows)
 
 
-    def ring_table(self, shard_rows):
+    def whole_table(self, shard_rows):
         rows = shard_rows // self.dp_size
-        core = lax.axis_index("dp").astype(jnp.int32) % 2
-        order = [(f, x) for x in range(self.dp_size // 2) for f in range(self.fsdp_size)]
-        halves = [jnp.array([f * shard_rows + 2 * x * rows for f, x in order], jnp.int32) + c * rows for c in (core, 1 - core)]
-        return jnp.concatenate(halves)
-
-    def ring_core(self, parts):
-        return parts[0], self.core(parts[1])
-
-    def ring_sums(self, parts):
-        halves = jnp.concatenate([low_sum(*part) for part in parts], axis=1)
-        same = [[d * self.fsdp_size + f for d in range(c, self.dp_size, 2) for f in range(self.fsdp_size)] for c in (0, 1)]
-        own = lax.psum_scatter(halves, ("dp", "fsdp"), scatter_dimension=0, axis_index_groups=same)[None]
-        return self.dp_pieces(own)
-        yield
+        order = [f * shard_rows + q * rows for q in range(self.dp_size) for f in range(self.fsdp_size)]
+        return jnp.array(order, jnp.int32)
+
+    def whole_gather(self, gate_in, gate_out, lo, hi, tokens=()):
+        place = lax.axis_index("dp").astype(jnp.int32)[None]
+        own = pack(place, gate_in, gate_out, lo, hi, gate_in.shape[1] // self.dp_size, tokens)
+        return [lax.all_gather(own[0], ("dp", "fsdp"))]
 
 
     def begin(self, gate_in, gate_out, lo, hi, tokens=()):
         place = lax.axis_index("dp").astype(jnp.int32)[None]
         own = pack(place, gate_in, gate_out, lo, hi, gate_in.shape[1] // self.dp_size, tokens)
-        return [own] + [self.z(own, j) for j in (1, 2, 3)]
+        by_2 = self.z(own, 2)
+        by_1 = self.z(jnp.concatenate([own, by_2]), 1)
+        return [own, by_1, by_2]
 
     def spread(self, pieces, tokens=()):
-        (held,) = combine([[[(k, 0)] for k in range(4)]], pieces, tokens)
+        (held,) = combine([[[(0, 0)], [(1, 0)], [(2, 0)], [(1, 1)]]], pieces, tokens)
         return held, self.y(held), self.x(held)
 
     def relay(self, arrays, tokens=()):
@@ -581,6 +622,7 @@
 
     def sums(self, parts):
         held, by_y, by_x, far_x, far_y, other = parts
+        (other,) = yield [other]
         other = self.core(other)
         far_x, far_y = yield [low_sum(far_x, other[12:14]), low_sum(far_y, other[14:16])]
         got_x, got_y = self.x(far_x), self.y(far_y)
@@ -589,13 +631,15 @@
         by_y, by_x = yield [by_y, by_x]
         got_y, got_x = self.y(by_y), self.x(by_x)
         held = [low_sum(*(v[k : k + 1] for v in (held, other, got_y, got_x))) for k in range(4)]
-        sent = yield held[1:]
-        own = low_sum(held[0], *(self.z(v, k + 1) for k, v in enumerate(sent)))
+        (sent,) = yield [jnp.concatenate([held[1], held[3]])]
+        got = self.z(sent, 1)
+        (sent,) = yield [low_sum(held[2], got[1:])]
+        own = low_sum(held[0], got[:1], self.z(sent, 2))
         (own,) = yield [own]
         return self.dp_pieces(own)
 
     def dp_pieces(self, own):
-        by_x = self.x(own)
+        (by_x,) = tie([self.x(own)], self.before_core)
         return [own, self.core(own), by_x, self.core(by_x)]
 
     def pieces_table(self, shard_rows):
@@ -606,22 +650,29 @@
 class PlainTransfers:
     def __init__(self, dp_size, fsdp_size):
         self.fsdp_size = fsdp_size
-        self.slots = self.ring_slots = [fsdp_size]
-
-    def all_reduce(self, v, merge):
+        self.slots = [fsdp_size]
+
+    def all_reduce(self, v, merge, beside=()):
         every = lax.all_gather(v, ("dp", "fsdp"))
         while every.shape[0] > 1:
             half = every.shape[0] // 2
             every = jax.vmap(merge)(every[:half], every[half:])
         return every[0]
 
+    def all_reduce_steps(self, v, merge):
+        return self.all_reduce(v, merge)
+        yield
+
     def table(self, shard_rows):
         return jnp.arange(self.fsdp_size, dtype=jnp.int32) * shard_rows
 
-    ring_table = table
-
-    def ring_core(self, parts):
-        return parts
+    whole_table = table
+
+    def take_arrived(self):
+        return []
+
+    def whole_gather(self, gate_in, gate_out, lo, hi, tokens=()):
+        return list(self.spread(self.begin(gate_in, gate_out, lo, hi)))
 
     def begin(self, gate_in, gate_out, lo, hi, tokens=()):
         return jnp.concatenate([gate_in[lo:hi], gate_out[lo:hi]], axis=-1)
@@ -639,9 +690,6 @@
         own = lax.psum_scatter(parts[0], "fsdp", scatter_dimension=0)
         return [lax.psum(own, "dp")[None]]
         yield
-
-    def ring_sums(self, parts):
-        return (yield from self.sums([jnp.concatenate([part[0] for part in parts], axis=1)]))
 
     def pieces_table(self, shard_rows):
         return jnp.zeros((1,), jnp.int32)
@@ -704,123 +752,135 @@
     shard_rows = gate_in.shape[2]
     valid = row_valid.astype(F32)[:, None]
     micro = micro_batch[:, None]
-    tables = (moves.table(shard_rows), moves.ring_table(shard_rows))
     flat = lambda v: v.reshape((LAYERS * SECTIONS,) + v.shape[2:])
     gate_in, gate_out, bias_in, bias_out = flat(gate_in), flat(gate_out), flat(bias_in), flat(bias_out)
     masks = columns * flat(jax.vmap(jax.vmap(feature_mask))(mask_logits, thresholds))
+    masks, bias_in, bias_out = masks[:, None], bias_in[:, None], bias_out[:, None]
     add = lambda a, b: a + b
     begin = lambda j, tokens=(): moves.begin(gate_in, gate_out, *GATHERS[j], tokens)
 
     gathered, records, stored = [], [], []
     current, hidden = features, None
     _, stats = local_stats(current, None, micro, valid)
-    begun = {0: begin(0)}
-    spreads = {0: moves.spread(begun[0], (stats,))}
-    begun[1] = begin(1, (spreads[0][0],))
+    begun = [begin(0)]
+    spreads = [moves.spread(begun[0], (stats,))]
+    begun.append(begin(1, spreads[0][:1]))
+    relayed = [moves.relay(spreads[0], begun[1][1:])]
+    whole = moves.whole_gather(gate_in, gate_out, *GATHERS[2], relayed[0][1:])
+    spreads.append(moves.spread(begun[1], relayed[0][1:]))
+    relayed.append(moves.relay(spreads[1]))
+    (stats,) = tie([stats], spreads[1][:1])
     stats = moves.all_reduce(stats, merge_stats)
-    before = ()
     for k, (lo, hi) in enumerate(GATHERS):
         layer = lo // SECTIONS
         if lo % SECTIONS == 0:
             if k > 0:
                 current, stats = local_stats(current, hidden, micro, valid)
                 stats = moves.all_reduce(stats, merge_stats)
-                before = (stats,)
             normed, x_turned = norm_rows(current, micro, stats, gains[layer], shifts[layer])
             hidden = normed
             records.append((current, stats, normed, x_turned))
-        arrays, token = moves.relay(spreads[k], before)
-        tokens = [token]
-        if k + 1 < len(GATHERS):
-            spreads[k + 1] = moves.spread(begun[k + 1], tokens)
-            tokens = [spreads[k + 1][0]]
-        if k + 2 < len(GATHERS):
-            begun[k + 2] = begin(k + 2, tokens)
-            tokens = [begun[k + 2][0]]
-        arrays = moves.finish(arrays)
+        if k < 2:
+            arrays = relayed[k][0]
+            if k == 1:
+                arrays = [*arrays[:3], *tie(arrays[3:], [hidden])] if len(arrays) > 3 else arrays
+            arrays, table = moves.finish(arrays), moves.table(shard_rows)
+        else:
+            arrays, table = whole, moves.whole_table(shard_rows)
         hidden, *saved = forward_chunk(
-            tables[0], hidden, normed, masks[lo:hi], bias_in[lo:hi], bias_out[lo:hi], arrays, 0, tokens
+            table,
+            lo,
+            hi,
+            hidden,
+            normed,
+            masks,
+            bias_in,
+            bias_out,
+            arrays,
+            0,
+            relayed[1][1:] if k == 0 else (),
+            current if k == 2 else None,
         )
-        before = (hidden,)
-        stored.append((lo, hi, arrays, saved))
-    mixed_out = (current + hidden).astype(BF16)
+        stored.append((lo, hi, arrays, table, saved))
+    mixed_out = hidden
 
     carried = cotangent.astype(F32) * valid
     pieces_table = moves.pieces_table(shard_rows)
-    grads = None
-    results = [None] * LAYERS
-    under_way = []
-    tokens = []
-
-    def advance(item, sent):
-        try:
-            item[1] = item[0].send(sent)
-            return True
-        except StopIteration as stop:
-            item[2](stop.value)
-            return False
-
-    def start(generator, at_end):
-        item = [generator, None, at_end]
-        if advance(item, None):
-            under_way.append(item)
-
-    def send_all(after=None):
-        ready = [item[1] for item in under_way]
-        if after is not None:
-            tied = iter(tie([v for sent in ready for v in sent], after))
-            ready = [[next(tied) for _ in sent] for sent in ready]
-        made = [v for sent in ready for v in sent]
-        under_way[:] = [item for item, sent in zip(list(under_way), ready) if advance(item, sent)]
-        return made
-
-    def placed(lo):
-        def at_end(pieces):
-            nonlocal grads
-            grads = place_grads(pieces_table, pieces, lo, shard_rows, grads)
-
-        return at_end
-
-    ring_parts = []
-    for k, (lo, hi) in reversed(list(enumerate(GROUPS))):
-        layer = lo // SECTIONS
-        current, stats, normed, x_turned = records[layer]
-        if hi % SECTIONS == 0:
-            gh = carried
-            normed_parts, vectors = [], []
-        ((start_at, _, arrays, saved),) = [g for g in stored if g[0] <= lo and hi <= g[1]]
-        ring = RING_SUM[0] <= lo < RING_SUM[1]
-        gh, gn, g_mask, g_bin, g_bout, out = backward_chunk(
-            jnp.concatenate([tables[0], tables[1 if ring else 0]]),
+
+    def backward(k, gh, tokens):
+        lo, hi = GROUPS[k]
+        current, stats, normed, x_turned = records[lo // SECTIONS]
+        ((start_at, _, arrays, table, saved),) = [g for g in stored if g[0] <= lo and hi <= g[1]]
+        return backward_chunk(
+            jnp.concatenate([table, moves.table(shard_rows)]),
+            lo,
+            hi,
             gh,
             normed,
             x_turned,
-            masks[lo:hi],
+            masks,
             saved,
-            lo - start_at,
             arrays,
             lo - start_at,
-            moves.ring_slots if ring else moves.slots,
+            moves.slots,
             tokens,
         )
-        normed_parts.append(gn)
-        vectors.insert(0, jnp.concatenate([g_mask, g_bin, g_bout], axis=1))
-        tokens = []
-        if ring:
-            ring_parts.insert(0, moves.ring_core(out))
-        else:
-            start(moves.sums(out), placed(lo))
-            if k > 0:
-                tokens = send_all()
-        if lo % SECTIONS == 0:
-            total, pooled = pool_grads(current, micro, stats, normed_parts + [gh])
-            vectors = jnp.concatenate(vectors, axis=0)
-            results[layer] = moves.all_reduce(jnp.concatenate([pooled, vectors.reshape(-1, columns)]), add)
-            carried = carry_grads(current, micro, valid, stats, gains[layer], total, results[layer][: 2 * MB], carried)
-    after = [carried]
-    while under_way:
-        after = send_all(after) + list(grads or ())
-    start(moves.ring_sums(ring_parts), placed(RING_SUM[0]))
+
+    moves.take_arrived()
+    gh, gn_3, vectors_3, out_3 = backward(3, carried, ())
+    sums_3 = Sending(moves.sums(out_3))
+    sums_3.send(())
+    tokens = sums_3.send(())
+    moves.take_arrived()
+    gh, gn_2, vectors_2, out_2 = backward(2, gh, tokens)
+    sums_2 = Sending(moves.sums(out_2))
+    tokens = sums_2.send(())
+    current, stats, _, _ = records[1]
+    total, pooled = pool_grads(current, micro, stats, [gn_3, gn_2, gh], tokens)
+    vectors = jnp.concatenate([vectors_2, vectors_3])
+    both_1 = moves.all_reduce(jnp.concatenate([pooled, vectors.reshape(-1, columns)]), add, sums_3.ready or ())
+    moves.take_arrived()
+    tokens = sums_3.send((both_1,)) + sums_2.send((both_1,))
+    carried = carry_grads(current, micro, valid, stats, gains[1], total, both_1[: 2 * MB], carried, tokens)
+    gh, gn_1, vectors_1, out_1 = backward(1, carried, ())
+    sums_1 = Sending(moves.sums(out_1))
+    tokens = sums_1.send(moves.take_arrived())
+    moves.take_arrived()
+    tokens = sums_3.send(tokens)
+    tokens = sums_2.send(tokens)
+    tokens = sums_1.send(tokens)
+    gh, gn_0, vectors_0, out_0 = backward(0, gh, tokens)
+    sums_0 = Sending(moves.sums(out_0))
+    tokens = sums_0.send(moves.take_arrived())
+    tokens = sums_1.send(tokens)
+    tokens = sums_3.send(tokens)
+    current, stats, _, _ = records[0]
+    total, pooled = pool_grads(current, micro, stats, [gn_1, gn_0, gh], tokens)
+    vectors = jnp.concatenate([vectors_0, vectors_1])
+    both_0 = Sending(moves.all_reduce_steps(jnp.concatenate([pooled, vectors.reshape(-1, columns)]), add))
+    tokens = sums_0.send((total,))
+    tokens = sums_2.send(tokens)
+    tokens = both_0.send(tokens)
+    tokens = sums_0.send(tokens)
+    tokens = sums_1.send(tokens)
+    tokens = sums_2.send(tokens)
+    tokens = sums_0.send(tokens)
+    tokens = sums_3.send(tokens)
+    grads = place_grads(pieces_table, sums_3.result, 9, shard_rows, None)
+    tokens = sums_1.send(tokens)
+    tokens = both_0.send([*tokens, *grads])
+    tokens = sums_2.send(tokens)
+    tokens = sums_0.send(tokens)
+    tokens = both_0.send(tokens)
+    tokens = sums_1.send(tokens)
+    grads = place_grads(pieces_table, sums_2.result, 6, shard_rows, grads)
+    both_0 = both_0.result
+    carried = carry_grads(current, micro, valid, stats, gains[0], total, both_0[: 2 * MB], carried)
+    moves.before_core = [carried]
+    tokens = sums_0.send([*tokens, *grads])
+    grads = place_grads(pieces_table, sums_1.result, 3, shard_rows, grads)
+    grads = place_grads(pieces_table, sums_0.result, 0, shard_rows, grads)
+    results = [both_0, both_1]
     pooled = jnp.stack([both[: 2 * MB] for both in results])
     stacked = jnp.stack([both[2 * MB :].reshape(SECTIONS, 4 * columns) for both in results])
     _, mask_pull = jax.vjp(jax.vmap(jax.vmap(feature_mask)), mask_logits, thresholds)

time: 713 us -> 684 us (0.959)
  waiting for transfers between devices: 224 us -> 193 us
  other arithmetic: 50.5 us -> 79 us
  starting transfers between devices: 102 us -> 81.3 us
    ppermute x4, waiting for transfers between devices: 45.3 us -> 4.22 us  [far(): lax.ppermute(v, ('dp', 'fsdp'), along(('dp', 'fsdp'), size, 2 * self.fsdp...]
    ppermute x87 -> x86, starting transfers between devices: 96.6 us -> 75.8 us  [permute(): self.arrived.append(lax.ppermute(v, axis, along(axis, size, flip)))]
    convert_element_type x10 -> x20, other arithmetic: 30.8 us -> 47.4 us  [low_sum(): return sum((v.astype(F32) for v in terms)).astype(BF16)]
    broadcast_in_dim x15 -> x0, local copies, waits for them, and re-layouts: 15.2 us -> none  [the longest x5 6.14 us: backward_chunk(): masks[:, :, None]]
    unnamed x180 -> x187, local copies, waits for them, and re-layouts: 10.6 us -> 21.5 us
    pallas_call x6 -> x4, Pallas kernels: 22.9 us -> 12.8 us  [combine(): pl.pallas_call(functools.partial(combine_kernel, plan, len(parts), len(to...]
    ppermute x87 -> x86, waiting for transfers between devices: 178 us -> 188 us  [permute(): self.arrived.append(lax.ppermute(v, axis, along(axis, size, flip)))]
    pallas_call x3 -> x4, Pallas kernels: 14.6 us -> 17 us  [place_grads(): pl.pallas_call(functools.partial(place_kernel, n_pieces), grid_spec=pltpu...]
  transfers between devices with their start and end apart: 92 -> 91, of which waited for: 36 -> 40; matrix products, arithmetic and copies ran while one was open for 11% -> 13% of each run, Pallas kernels for 30% -> 24%
where the time goes in v3:
time: 684 us; the launch traced here: 674 us
  Pallas kernels  273 us (40%)
  waiting for transfers between devices  193 us (28%)
  starting transfers between devices  81.3 us (12%)
  other arithmetic  79 us (12%)
  local copies, waits for them, and re-layouts  32.8 us (5%)
  between operations  15.5 us (2%)
    ppermute x86, waiting for transfers between devices, permute(): self.arrived.append(lax.ppermute(v, axis, along(axis, size, flip)))  188 us
    pallas_call x4, Pallas kernels, backward_chunk(): pl.pallas_call(functools.partial(backward_kernel, n, first, len(arrays),...  124 us
    ppermute x86, starting transfers between devices, permute(): self.arrived.append(lax.ppermute(v, axis, along(axis, size, flip)))  75.8 us
    pallas_call x3, Pallas kernels, forward_chunk(): pl.pallas_call(functools.partial(forward_kernel, n, first, len(arrays), l...  72.4 us
    convert_element_type x20, other arithmetic, low_sum(): return sum((v.astype(F32) for v in terms)).astype(BF16)  47.4 us
    unnamed x187, local copies, waits for them, and re-layouts  21.5 us
    pallas_call x4, Pallas kernels, place_grads(): pl.pallas_call(functools.partial(place_kernel, n_pieces), grid_spec=pltpu...  17 us
  transfers between devices with their start and end apart: 91, of which 40 were waited for; matrix products, arithmetic and copies ran while one was open for 13% of the time, Pallas kernels for 24%

profile of v3, /device:TPU:0, one launch (start us, length us, event | category | flops | bytes accessed | tf_op | source)
XLA Modules:
  0.0 674.2 jit_solution(591737131584416637)
XLA Ops:
  7.2 2.5 pack.3.refs_0_
  9.7 4.0 collective-permute-start
  13.7 13.5 %collective-permute-done.refs_2_ = bf16[1,3,32,1536]{3,2,1,0:T(8,128)(2,1)S(1)} collective-permute-done((bf16[1,3,32,1536]{3,2,1,0:T(8,128)(2,1)}, bf16[1,3,32,1536]{3,2,1,0:T(8,128)(2,1)S(1)}, u32[]{:S(2)}, u32[]{:S(2)}) %collective-permute-start) | collective-permute-done | bytes 294944 | tf_op jit(solution)/shard_map/ppermute | solution.py:543
  31.1 3.8 local_stats.2.refs_3_.refs_0_
  35.0 8.0 %collective-permute-done.1.refs_1_ = bf16[2,3,32,1536]{3,2,1,0:T(8,128)(2,1)S(1)} collective-permute-done((bf16[2,3,32,1536]{3,2,1,0:T(8,128)(2,1)S(1)}, bf16[2,3,32,1536]{3,2,1,0:T(8,128)(2,1)S(1)}, u32[]{:S(2)}, u32[]{:S(2)}) %collective-permute-start.1) | collective-permute-done | bytes 589856 | tf_op jit(solution)/shard_map/ppermute | solution.py:543
  43.8 3.2 combine.4.refs_0_.refs_5_.refs_11_
  49.8 2.4 pack.4.refs_0_
  52.3 3.3 collective-permute-start.2
  55.5 12.6 %collective-permute-done.2.refs_3_.refs_2_ = bf16[1,3,32,1536]{3,2,1,0:T(8,128)(2,1)S(1)} collective-permute-done((bf16[1,3,32,1536]{3,2,1,0:T(8,128)(2,1)}, bf16[1,3,32,1536]{3,2,1,0:T(8,128)(2,1)S(1)}, u32[]{:S(2)}, u32[]{:S(2)}) %collective-permute-start.2) | collective-permute-done | bytes 294944 | tf_op jit(solution)/shard_map/ppermute | solution.py:543
  70.1 13.5 %collective-permute-done.3.refs_2_.refs_1_ = bf16[2,3,32,1536]{3,2,1,0:T(8,128)(2,1)S(1)} collective-permute-done((bf16[2,3,32,1536]{3,2,1,0:T(8,128)(2,1)S(1)}, bf16[2,3,32,1536]{3,2,1,0:T(8,128)(2,1)S(1)}, u32[]{:S(2)}, u32[]{:S(2)}) %collective-permute-start.3) | collective-permute-done | bytes 589856 | tf_op jit(solution)/shard_map/ppermute | solution.py:543
  85.9 3.2 combine.5
  89.1 3.9 pack.5
  93.1 3.2 combine.6.refs_1_.refs_5_.refs_11_
  106.4 4.4 collective-permute-start.12
  114.0 2.5 collective-permute-done.11
  122.4 3.6 norm_rows.2
  126.0 29.6 %collective-permute-done.14.refs_9_.refs_15_ = bf16[2,3,32,1536]{3,2,1,0:T(8,128)(2,1)} collective-permute-done((bf16[2,3,32,1536]{3,2,1,0:T(8,128)(2,1)}, bf16[2,3,32,1536]{3,2,1,0:T(8,128)(2,1)}, u32[]{:S(2)}, u32[]{:S(2)}) %collective-permute-start.14) | collective-permute-done | bytes 589856 | tf_op jit(solution)/shard_map/ppermute | solution.py:543
  155.5 8.5 %collective-permute-done.13.refs_8_.refs_14_ = bf16[2,3,32,1536]{3,2,1,0:T(8,128)(2,1)S(1)} collective-permute-done((bf16[2,3,32,1536]{3,2,1,0:T(8,128)(2,1)S(1)}, bf16[2,3,32,1536]{3,2,1,0:T(8,128)(2,1)S(1)}, u32[]{:S(2)}, u32[]{:S(2)}) %collective-permute-start.13) | collective-permute-done | bytes 589856 | tf_op jit(solution)/shard_map/ppermute | solution.py:543
  164.6 3.2 combine.7
  170.5 21.2 %forward_sections.3 = (f32[768,512]{1,0:T(8,128)}, f32[3,768,512]{2,1,0:T(8,128)}, f32[3,768,512]{2,1,0:T(8,128)}, f32[3,768,512]{2,1,0:T(8,128)}, f32[3,768,512...) custom-call(s32[32]{0:T(128)} %stack.116.table, ...), custom_call_target="tpu_custom_call" | custom-call | flops 20000000000 | bytes 1 | tf_op jit(solution)/shard_map/forward_sections/pallas_call | solution.py:116
  196.9 19.4 %forward_sections.4 = (f32[768,512]{1,0:T(8,128)}, f32[3,768,512]{2,1,0:T(8,128)}, f32[3,768,512]{2,1,0:T(8,128)}, f32[3,768,512]{2,1,0:T(8,128)}, f32[3,768,512...) custom-call(s32[32]{0:T(128)} %stack.116.table, ...), custom_call_target="tpu_custom_call" | custom-call | flops 20000000000 | bytes 1 | tf_op jit(solution)/shard_map/forward_sections/pallas_call | solution.py:116
  216.3 4.4 local_stats.3
  230.3 4.0 collective-permute-start.35
  237.2 4.0 collective-permute-done.34
  241.8 4.0 norm_rows.3
  245.8 31.9 %forward_sections.5 = (bf16[768,512]{1,0:T(8,128)(2,1)}, f32[6,768,512]{2,1,0:T(8,128)}, f32[6,768,512]{2,1,0:T(8,128)}, f32[6,768,512]{2,1,0:T(8,128)}, f32[6,7...) custom-call(s32[32]{0:T(128)} %constant.45.clone.table, ...), custom_call_target="tpu_custom_call" | custom-call | flops 20000000000 | bytes 1 | tf_op jit(solution)/shard_map/forward_sections/pallas_call | solution.py:116
  277.7 31.1 %backward_sections.4 = (f32[768,512]{1,0:T(8,128)}, f32[768,512]{1,0:T(8,128)}, f32[3,1,2048]{2,1,0:T(1,128)}, bf16[4,3,32,1536]{3,2,1,0:T(8,128)(2,1)}, bf16[4,...) custom-call(s32[64]{0:T(128)} %concatenate.91.table, ...), custom_call_target="tpu_custom_call" | custom-call | flops 20000000000 | bytes 1 | tf_op jit(solution)/shard_map/backward_sections/pallas_call | solution.py:249
  308.9 8.1 %collective-permute-done.36 = bf16[16,3,32,1536]{3,2,1,0:T(8,128)(2,1)S(1)} collective-permute-done((bf16[16,3,32,1536]{3,2,1,0:T(8,128)(2,1)}, bf16[16,3,32,1536]{3,2,1,0:T(8,128)(2,1)S(1)}, u32[]{:S(2)}, u32[]{:S(2)}) %collective-permute-start.36) | collective-permute-done | bytes 4718624 | tf_op jit(solution)/shard_map/ppermute | solution.py:543
  317.0 2.2 copy-done.11
  319.3 2.6 add_convert_fusion.22
  321.9 31.1 %backward_sections.5 = (f32[768,512]{1,0:T(8,128)}, f32[768,512]{1,0:T(8,128)}, f32[3,1,2048]{2,1,0:T(1,128)}, bf16[4,3,32,1536]{3,2,1,0:T(8,128)(2,1)}, bf16[4,...) custom-call(s32[64]{0:T(128)} %concatenate.91.table, ...), custom_call_target="tpu_custom_call" | custom-call | flops 20000000000 | bytes 1 | tf_op jit(solution)/shard_map/backward_sections/pallas_call | solution.py:249
  354.8 6.0 pool_grads.2
  370.9 2.5 collective-permute-done.40
  374.7 3.0 collective-permute-done.38
  378.4 2.9 add_convert_fusion.19
  385.1 2.9 collective-permute-start.43
  396.5 2.8 add_convert_fusion.16
  400.8 5.3 carry_grads.2.refs_0_.carried_ref
  406.2 30.8 %backward_sections.6 = (f32[768,512]{1,0:T(8,128)}, f32[768,512]{1,0:T(8,128)}, f32[3,1,2048]{2,1,0:T(1,128)}, bf16[4,3,32,1536]{3,2,1,0:T(8,128)(2,1)}, bf16[4,...) custom-call(s32[64]{0:T(128)} %concatenate.90.table, ...), custom_call_target="tpu_custom_call" | custom-call | flops 20000000000 | bytes 1 | tf_op jit(solution)/shard_map/backward_sections/pallas_call | solution.py:249
  443.5 2.6 add_convert_fusion.11
  452.1 2.8 add_convert_fusion.14
  456.5 30.9 %backward_sections.7 = (f32[768,512]{1,0:T(8,128)}, f32[768,512]{1,0:T(8,128)}, f32[3,1,2048]{2,1,0:T(1,128)}, bf16[4,3,32,1536]{3,2,1,0:T(8,128)(2,1)}, bf16[4,...) custom-call(s32[64]{0:T(128)} %concatenate.90.table, ...), custom_call_target="tpu_custom_call" | custom-call | flops 20000000000 | bytes 1 | tf_op jit(solution)/shard_map/backward_sections/pallas_call | solution.py:249
  487.4 4.2 collective-permute-done.53.refs_4_
  499.8 2.8 add_convert_fusion.7
  508.4 5.8 pool_grads.3
  514.3 2.6 add_convert_fusion.4
  519.6 4.4 collective-permute-done.64
  523.9 2.2 add_convert_fusion.36.refs_0_
  526.2 21.2 %collective-permute-done.61 = bf16[2,3,32,1536]{3,2,1,0:T(8,128)(2,1)} collective-permute-done((bf16[2,3,32,1536]{3,2,1,0:T(8,128)(2,1)}, bf16[2,3,32,1536]{3,2,1,0:T(8,128)(2,1)}, u32[]{:S(2)}, u32[]{:S(2)}) %collective-permute-start.61) | collective-permute-done | bytes 589856 | tf_op jit(solution)/shard_map/ppermute | solution.py:543
  547.3 3.3 add_convert_fusion.1
  560.2 7.6 %collective-permute-done.67 = bf16[2,3,32,1536]{3,2,1,0:T(8,128)(2,1)} collective-permute-done((bf16[2,3,32,1536]{3,2,1,0:T(8,128)(2,1)S(1)}, bf16[2,3,32,1536]{3,2,1,0:T(8,128)(2,1)}, u32[]{:S(2)}, u32[]{:S(2)}) %collective-permute-start.67) | collective-permute-done | bytes 589856 | tf_op jit(solution)/shard_map/ppermute | solution.py:543
  570.6 10.5 %collective-permute-done.65 = bf16[4,3,32,1536]{3,2,1,0:T(8,128)(2,1)} collective-permute-done((bf16[4,3,32,1536]{3,2,1,0:T(8,128)(2,1)}, bf16[4,3,32,1536]{3,2,1,0:T(8,128)(2,1)}, u32[]{:S(2)}, u32[]{:S(2)}) %collective-permute-start.65) | collective-permute-done | bytes 1179680 | tf_op jit(solution)/shard_map/ppermute | solution.py:543
  588.3 2.2 add_convert_fusion.38.refs_0_
  590.5 3.7 collective-permute-done.69.refs_2_
  594.1 5.1 collective-permute-done.75
  602.9 4.5 place_grads.4
  619.7 2.3 add_convert_fusion.24.refs_0_
  626.9 5.1 carry_grads.3.refs_1_
  633.3 3.1 collective-permute-done.79
  636.4 2.3 add_convert_fusion.26.refs_0_
  640.1 4.2 place_grads.5
  647.0 5.9 collective-permute-done.85.refs_0_
  657.6 4.2 place_grads.6
  662.6 4.2 place_grads.7
  (456 shorter events, 162.0 us)
Async XLA Ops:
  7.2 238.7 %all-gather.2.cloned.1.call-start = ((), (), s32[]{:S(2)}) async-start(), calls=%async_computation | async-start | bytes 19464192 | tf_op jit(solution)/shard_map/all_gather | solution.py:600
  9.7 17.6 %collective-permute-start = (bf16[1,3,32,1536]{3,2,1,0:T(8,128)(2,1)}, bf16[1,3,32,1536]{3,2,1,0:T(8,128)(2,1)S(1)}, u32[]{:S(2)}, u32[]{:S(2)}) collective-permute-start(bf16[1,3,32,1536]{3,2,1,0:T(8,128)(2,1)} %pack.3.refs_0_), channel_id=1, source_target_pairs={{0,4},{1,5},{2,6},{3,7},{4,0},{5,1},{6,2},{7,3},{8,12},{9,13},{10,... | collective-permute-start | bytes 884744 | tf_op jit(solution)/shard_map/ppermute | solution.py:543
  28.4 14.6 %collective-permute-start.1 = (bf16[2,3,32,1536]{3,2,1,0:T(8,128)(2,1)S(1)}, bf16[2,3,32,1536]{3,2,1,0:T(8,128)(2,1)S(1)}, u32[]{:S(2)}, u32[]{:S(2)}) collective-permute-start(bf16[2,3,32,1536]{3,2,1,0:T(8,128)(2,1)S(1)} %pad_maximum_fusion.8), channel_id=1, source_target_pairs={{0,2},{1,3},{2,0},{3,1},{4,6},{5,7},{6,4},{7,5},{8,10},{9,11},{10,... | collective-permute-start | bytes 1769480 | tf_op jit(solution)/shard_map/ppermute | solution.py:543
  47.0 36.7 %collective-permute-start.5 = (bf16[4,3,32,1536]{3,2,1,0:T(8,128)(2,1)}, bf16[4,3,32,1536]{3,2,1,0:T(8,128)(2,1)S(1)}, u32[]{:S(2)}, u32[]{:S(2)}) collective-permute-start(bf16[4,3,32,1536]{3,2,1,0:T(8,128)(2,1)} %combine.4.refs_0_.refs_5_.refs_11_), channel_id=1, source_target_pairs={{0,16},{8,24},{16,0},{24,8},{1,17},{9,25},{17,1},{25,9},{2,18},{10... | collective-permute-start | bytes 3538952 | tf_op jit(solution)/shard_map/ppermute | solution.py:543
  48.3 35.4 %collective-permute-start.4 = (bf16[4,3,32,1536]{3,2,1,0:T(8,128)(2,1)}, bf16[4,3,32,1536]{3,2,1,0:T(8,128)(2,1)S(1)}, u32[]{:S(2)}, u32[]{:S(2)}) collective-permute-start(bf16[4,3,32,1536]{3,2,1,0:T(8,128)(2,1)} %combine.4.refs_0_.refs_5_.refs_11_), channel_id=1, source_target_pairs={{0,1},{1,0},{2,3},{3,2},{4,5},{5,4},{6,7},{7,6},{8,9},{9,8},{10,11... | collective-permute-start | bytes 3538952 | tf_op jit(solution)/shard_map/ppermute | solution.py:543
  52.3 15.9 %collective-permute-start.2 = (bf16[1,3,32,1536]{3,2,1,0:T(8,128)(2,1)}, bf16[1,3,32,1536]{3,2,1,0:T(8,128)(2,1)S(1)}, u32[]{:S(2)}, u32[]{:S(2)}) collective-permute-start(bf16[1,3,32,1536]{3,2,1,0:T(8,128)(2,1)} %pack.4.refs_0_), channel_id=1, source_target_pairs={{0,4},{1,5},{2,6},{3,7},{4,0},{5,1},{6,2},{7,3},{8,12},{9,13},{10,... | collective-permute-start | bytes 884744 | tf_op jit(solution)/shard_map/ppermute | solution.py:543
  69.3 14.4 %collective-permute-start.3 = (bf16[2,3,32,1536]{3,2,1,0:T(8,128)(2,1)S(1)}, bf16[2,3,32,1536]{3,2,1,0:T(8,128)(2,1)S(1)}, u32[]{:S(2)}, u32[]{:S(2)}) collective-permute-start(bf16[2,3,32,1536]{3,2,1,0:T(8,128)(2,1)S(1)} %pad_maximum_fusion.9), channel_id=1, source_target_pairs={{0,2},{1,3},{2,0},{3,1},{4,6},{5,7},{6,4},{7,5},{8,10},{9,11},{10,... | collective-permute-start | bytes 1769480 | tf_op jit(solution)/shard_map/ppermute | solution.py:543
  103.2 60.8 %collective-permute-start.21 = (bf16[4,3,32,1536]{3,2,1,0:T(8,128)(2,1)}, bf16[4,3,32,1536]{3,2,1,0:T(8,128)(2,1)}, u32[]{:S(2)}, u32[]{:S(2)}) collective-permute-start(bf16[4,3,32,1536]{3,2,1,0:T(8,128)(2,1)} %combine.6.refs_1_.refs_5_.refs_11_), channel_id=1, source_target_pairs={{0,16},{8,24},{16,0},{24,8},{1,17},{9,25},{17,1},{25,9},{2,18},{10... | collective-permute-start | bytes 3538952 | tf_op jit(solution)/shard_map/ppermute | solution.py:543
  103.7 60.8 %collective-permute-start.20 = (bf16[4,3,32,1536]{3,2,1,0:T(8,128)(2,1)}, bf16[4,3,32,1536]{3,2,1,0:T(8,128)(2,1)}, u32[]{:S(2)}, u32[]{:S(2)}) collective-permute-start(bf16[4,3,32,1536]{3,2,1,0:T(8,128)(2,1)} %combine.6.refs_1_.refs_5_.refs_11_), channel_id=1, source_target_pairs={{0,1},{1,0},{2,3},{3,2},{4,5},{5,4},{6,7},{7,6},{8,9},{9,8},{10,11... | collective-permute-start | bytes 3538952 | tf_op jit(solution)/shard_map/ppermute | solution.py:543
  106.4 7.3 %collective-permute-start.12 = (f32[12,512]{1,0:T(8,128)S(1)}, f32[12,512]{1,0:T(8,128)S(1)}, u32[]{:S(2)}, u32[]{:S(2)}) collective-permute-start(f32[12,512]{1,0:T(8,128)S(1)} %pad_maximum_fusion.16), channel_id=1, source_target_pairs={{0,6},{1,7},{2,4},{3,5},{4,2},{5,3},{6,0},{7,1},{8,14},{9,15},{10,... | collective-permute-start | bytes 73736 | tf_op jit(solution)/shard_map/ppermute | solution.py:543
  112.0 52.0 %collective-permute-start.13 = (bf16[2,3,32,1536]{3,2,1,0:T(8,128)(2,1)S(1)}, bf16[2,3,32,1536]{3,2,1,0:T(8,128)(2,1)S(1)}, u32[]{:S(2)}, u32[]{:S(2)}) collective-permute-start(bf16[2,3,32,1536]{3,2,1,0:T(8,128)(2,1)S(1)} %copy-done.39), channel_id=1, source_target_pairs={{0,16},{8,24},{16,0},{24,8},{1,17},{9,25},{17,1},{25,9},{2,18},{10... | collective-permute-start | bytes 1769480 | tf_op jit(solution)/shard_map/ppermute | solution.py:543
  113.7 41.8 %collective-permute-start.14 = (bf16[2,3,32,1536]{3,2,1,0:T(8,128)(2,1)}, bf16[2,3,32,1536]{3,2,1,0:T(8,128)(2,1)}, u32[]{:S(2)}, u32[]{:S(2)}) collective-permute-start(bf16[2,3,32,1536]{3,2,1,0:T(8,128)(2,1)} %get-tuple-element.110), channel_id=1, source_target_pairs={{0,1},{1,0},{2,3},{3,2},{4,5},{5,4},{6,7},{7,6},{8,9},{9,8},{10,11... | collective-permute-start | bytes 1769480 | tf_op jit(solution)/shard_map/ppermute | solution.py:543
  121.7 46.0 %collective-permute-start.15 = (bf16[4,3,32,1536]{3,2,1,0:T(8,128)(2,1)S(1)}, bf16[4,3,32,1536]{3,2,1,0:T(8,128)(2,1)}, u32[]{:S(2)}, u32[]{:S(2)}) collective-permute-start(bf16[4,3,32,1536]{3,2,1,0:T(8,128)(2,1)S(1)} %copy-done.23), channel_id=1, source_target_pairs={{0,8},{8,0},{16,24},{24,16},{1,9},{9,1},{17,25},{25,17},{2,10},{10... | collective-permute-start | bytes 3538952 | tf_op jit(solution)/shard_map/ppermute | solution.py:543
  155.5 12.7 %collective-permute-start.17 = (bf16[4,3,32,1536]{3,2,1,0:T(8,128)(2,1)}, bf16[4,3,32,1536]{3,2,1,0:T(8,128)(2,1)}, u32[]{:S(2)}, u32[]{:S(2)}) collective-permute-start(bf16[4,3,32,1536]{3,2,1,0:T(8,128)(2,1)} %copy-done.82), channel_id=1, source_target_pairs={{0,8},{8,0},{16,24},{24,16},{1,9},{9,1},{17,25},{25,17},{2,10},{10... | collective-permute-start | bytes 3538952 | tf_op jit(solution)/shard_map/ppermute | solution.py:543
  167.7 25.5 %collective-permute-start.24 = (bf16[4,3,32,1536]{3,2,1,0:T(8,128)(2,1)S(1)}, bf16[4,3,32,1536]{3,2,1,0:T(8,128)(2,1)}, u32[]{:S(2)}, u32[]{:S(2)}) collective-permute-start(bf16[4,3,32,1536]{3,2,1,0:T(8,128)(2,1)S(1)} %copy-done.25), channel_id=1, source_target_pairs={{0,8},{8,0},{16,24},{24,16},{1,9},{9,1},{17,25},{25,17},{2,10},{10... | collective-permute-start | bytes 3538952 | tf_op jit(solution)/shard_map/ppermute | solution.py:543
  168.3 23.4 %collective-permute-start.23 = (bf16[2,3,32,1536]{3,2,1,0:T(8,128)(2,1)}, bf16[2,3,32,1536]{3,2,1,0:T(8,128)(2,1)S(1)}, u32[]{:S(2)}, u32[]{:S(2)}) collective-permute-start(bf16[2,3,32,1536]{3,2,1,0:T(8,128)(2,1)} %get-tuple-element.113), channel_id=1, source_target_pairs={{0,1},{1,0},{2,3},{3,2},{4,5},{5,4},{6,7},{7,6},{8,9},{9,8},{10,11... | collective-permute-start | bytes 1769480 | tf_op jit(solution)/shard_map/ppermute | solution.py:543
  169.2 22.5 %collective-permute-start.22 = (bf16[2,3,32,1536]{3,2,1,0:T(8,128)(2,1)}, bf16[2,3,32,1536]{3,2,1,0:T(8,128)(2,1)S(1)}, u32[]{:S(2)}, u32[]{:S(2)}) collective-permute-start(bf16[2,3,32,1536]{3,2,1,0:T(8,128)(2,1)} %get-tuple-element.111.refs_15_), channel_id=1, source_target_pairs={{0,16},{8,24},{16,0},{24,8},{1,17},{9,25},{17,1},{25,9},{2,18},{10... | collective-permute-start | bytes 1769480 | tf_op jit(solution)/shard_map/ppermute | solution.py:543
  170.0 26.1 %collective-permute-start.26 = (bf16[4,3,32,1536]{3,2,1,0:T(8,128)(2,1)}, bf16[4,3,32,1536]{3,2,1,0:T(8,128)(2,1)}, u32[]{:S(2)}, u32[]{:S(2)}) collective-permute-start(bf16[4,3,32,1536]{3,2,1,0:T(8,128)(2,1)} %collective-permute-done.21.refs_1_.refs_7_.refs_13_), channel_id=1, source_target_pairs={{0,8},{8,0},{16,24},{24,16},{1,9},{9,1},{17,25},{25,17},{2,10},{10... | collective-permute-start | bytes 3538952 | tf_op jit(solution)/shard_map/ppermute | solution.py:543
  170.0 26.1 %collective-permute-start.25 = (bf16[4,3,32,1536]{3,2,1,0:T(8,128)(2,1)}, bf16[4,3,32,1536]{3,2,1,0:T(8,128)(2,1)}, u32[]{:S(2)}, u32[]{:S(2)}) collective-permute-start(bf16[4,3,32,1536]{3,2,1,0:T(8,128)(2,1)} %collective-permute-done.20.refs_0_.refs_6_.refs_12_), channel_id=1, source_target_pairs={{0,8},{8,0},{16,24},{24,16},{1,9},{9,1},{17,25},{25,17},{2,10},{10... | collective-permute-start | bytes 3538952 | tf_op jit(solution)/shard_map/ppermute | solution.py:543
  230.3 6.9 %collective-permute-start.35 = (f32[12,512]{1,0:T(8,128)S(1)}, f32[12,512]{1,0:T(8,128)S(1)}, u32[]{:S(2)}, u32[]{:S(2)}) collective-permute-start(f32[12,512]{1,0:T(8,128)S(1)} %pad_maximum_fusion.19), channel_id=1, source_target_pairs={{0,6},{1,7},{2,4},{3,5},{4,2},{5,3},{6,0},{7,1},{8,14},{9,15},{10,... | collective-permute-start | bytes 73736 | tf_op jit(solution)/shard_map/ppermute | solution.py:543
  234.4 6.8 %collective-permute-start.34 = (f32[12,512]{1,0:T(8,128)S(1)}, f32[12,512]{1,0:T(8,128)S(1)}, u32[]{:S(2)}, u32[]{:S(2)}) collective-permute-start(f32[12,512]{1,0:T(8,128)S(1)} %pad_maximum_fusion.19), channel_id=1, source_target_pairs={{0,4},{1,5},{2,6},{3,7},{4,0},{5,1},{6,2},{7,3},{8,12},{9,13},{10,... | collective-permute-start | bytes 73736 | tf_op jit(solution)/shard_map/ppermute | solution.py:543
  234.4 6.8 %collective-permute-start.33 = (f32[12,512]{1,0:T(8,128)S(1)}, f32[12,512]{1,0:T(8,128)S(1)}, u32[]{:S(2)}, u32[]{:S(2)}) collective-permute-start(f32[12,512]{1,0:T(8,128)S(1)} %pad_maximum_fusion.19), channel_id=1, source_target_pairs={{0,2},{1,3},{2,0},{3,1},{4,6},{5,7},{6,4},{7,5},{8,10},{9,11},{10,... | collective-permute-start | bytes 73736 | tf_op jit(solution)/shard_map/ppermute | solution.py:543
  308.9 8.2 %collective-permute-start.36 = (bf16[16,3,32,1536]{3,2,1,0:T(8,128)(2,1)}, bf16[16,3,32,1536]{3,2,1,0:T(8,128)(2,1)S(1)}, u32[]{:S(2)}, u32[]{:S(2)}) collective-permute-start(bf16[16,3,32,1536]{3,2,1,0:T(8,128)(2,1)} %get-tuple-element.132), channel_id=1, source_target_pairs={{0,8},{8,0},{16,24},{24,16},{1,9},{9,1},{17,25},{25,17},{2,10},{10... | collective-permute-start | bytes 14155784 | tf_op jit(solution)/shard_map/ppermute | solution.py:543
  353.0 43.5 %collective-permute-start.46 = (bf16[16,3,32,1536]{3,2,1,0:T(8,128)(2,1)}, bf16[16,3,32,1536]{3,2,1,0:T(8,128)(2,1)}, u32[]{:S(2)}, u32[]{:S(2)}) collective-permute-start(bf16[16,3,32,1536]{3,2,1,0:T(8,128)(2,1)} %get-tuple-element.136.refs_3_), channel_id=1, source_target_pairs={{0,8},{8,0},{16,24},{24,16},{1,9},{9,1},{17,25},{25,17},{2,10},{10... | collective-permute-start | bytes 14155784 | tf_op jit(solution)/shard_map/ppermute | solution.py:543
  353.2 25.2 %collective-permute-start.42 = (bf16[2,3,32,1536]{3,2,1,0:T(8,128)(2,1)S(1)}, bf16[2,3,32,1536]{3,2,1,0:T(8,128)(2,1)}, u32[]{:S(2)}, u32[]{:S(2)}) collective-permute-start(bf16[2,3,32,1536]{3,2,1,0:T(8,128)(2,1)S(1)} %copy-done.22), channel_id=1, source_target_pairs={{0,1},{1,0},{2,3},{3,2},{4,5},{5,4},{6,7},{7,6},{8,9},{9,8},{10,11... | collective-permute-start | bytes 1769480 | tf_op jit(solution)/shard_map/ppermute | solution.py:543
  354.1 24.3 %collective-permute-start.41 = (bf16[2,3,32,1536]{3,2,1,0:T(8,128)(2,1)S(1)}, bf16[2,3,32,1536]{3,2,1,0:T(8,128)(2,1)}, u32[]{:S(2)}, u32[]{:S(2)}) collective-permute-start(bf16[2,3,32,1536]{3,2,1,0:T(8,128)(2,1)S(1)} %copy-done.21), channel_id=1, source_target_pairs={{0,16},{8,24},{16,0},{24,8},{1,17},{9,25},{17,1},{25,9},{2,18},{10... | collective-permute-start | bytes 1769480 | tf_op jit(solution)/shard_map/ppermute | solution.py:543
  393.4 43.5 %collective-permute-start.47 = (bf16[4,3,32,1536]{3,2,1,0:T(8,128)(2,1)}, bf16[4,3,32,1536]{3,2,1,0:T(8,128)(2,1)S(1)}, u32[]{:S(2)}, u32[]{:S(2)}) collective-permute-start(bf16[4,3,32,1536]{3,2,1,0:T(8,128)(2,1)} %get-tuple-element.143.refs_0_), channel_id=1, source_target_pairs={{0,1},{1,0},{2,3},{3,2},{4,5},{5,4},{6,7},{7,6},{8,9},{9,8},{10,11... | collective-permute-start | bytes 3538952 | tf_op jit(solution)/shard_map/ppermute | solution.py:543
  394.7 42.3 %collective-permute-start.48 = (bf16[4,3,32,1536]{3,2,1,0:T(8,128)(2,1)}, bf16[4,3,32,1536]{3,2,1,0:T(8,128)(2,1)S(1)}, u32[]{:S(2)}, u32[]{:S(2)}) collective-permute-start(bf16[4,3,32,1536]{3,2,1,0:T(8,128)(2,1)} %get-tuple-element.144.refs_1_), channel_id=1, source_target_pairs={{0,16},{8,24},{16,0},{24,8},{1,17},{9,25},{17,1},{25,9},{2,18},{10... | collective-permute-start | bytes 3538952 | tf_op jit(solution)/shard_map/ppermute | solution.py:543
  399.2 37.8 %collective-permute-start.49 = (bf16[2,3,32,1536]{3,2,1,0:T(8,128)(2,1)}, bf16[2,3,32,1536]{3,2,1,0:T(8,128)(2,1)S(1)}, u32[]{:S(2)}, u32[]{:S(2)}) collective-permute-start(bf16[2,3,32,1536]{3,2,1,0:T(8,128)(2,1)} %get-tuple-element.147.refs_2_), channel_id=1, source_target_pairs={{0,16},{8,24},{16,0},{24,8},{1,17},{9,25},{17,1},{25,9},{2,18},{10... | collective-permute-start | bytes 1769480 | tf_op jit(solution)/shard_map/ppermute | solution.py:543
  400.1 36.9 %collective-permute-start.50 = (bf16[2,3,32,1536]{3,2,1,0:T(8,128)(2,1)}, bf16[2,3,32,1536]{3,2,1,0:T(8,128)(2,1)S(1)}, u32[]{:S(2)}, u32[]{:S(2)}) collective-permute-start(bf16[2,3,32,1536]{3,2,1,0:T(8,128)(2,1)} %get-tuple-element.148.refs_3_), channel_id=1, source_target_pairs={{0,1},{1,0},{2,3},{3,2},{4,5},{5,4},{6,7},{7,6},{8,9},{9,8},{10,11... | collective-permute-start | bytes 1769480 | tf_op jit(solution)/shard_map/ppermute | solution.py:543
  438.8 13.3 %collective-permute-start.51 = (bf16[16,3,32,1536]{3,2,1,0:T(8,128)(2,1)}, bf16[16,3,32,1536]{3,2,1,0:T(8,128)(2,1)}, u32[]{:S(2)}, u32[]{:S(2)}) collective-permute-start(bf16[16,3,32,1536]{3,2,1,0:T(8,128)(2,1)} %tie.33.refs_1_), channel_id=1, source_target_pairs={{0,8},{8,0},{16,24},{24,16},{1,9},{9,1},{17,25},{25,17},{2,10},{10... | collective-permute-start | bytes 14155784 | tf_op jit(solution)/shard_map/ppermute | solution.py:543
  448.5 38.9 %collective-permute-start.52 = (bf16[2,3,32,1536]{3,2,1,0:T(8,128)(2,1)S(1)}, bf16[2,3,32,1536]{3,2,1,0:T(8,128)(2,1)}, u32[]{:S(2)}, u32[]{:S(2)}) collective-permute-start(bf16[2,3,32,1536]{3,2,1,0:T(8,128)(2,1)S(1)} %copy-done), channel_id=1, source_target_pairs={{0,2},{1,3},{2,0},{3,1},{4,6},{5,7},{6,4},{7,5},{8,10},{9,11},{10,... | collective-permute-start | bytes 1769480 | tf_op jit(solution)/shard_map/ppermute | solution.py:543
  449.7 37.8 %collective-permute-start.55 = (bf16[4,3,32,1536]{3,2,1,0:T(8,128)(2,1)}, bf16[4,3,32,1536]{3,2,1,0:T(8,128)(2,1)S(1)}, u32[]{:S(2)}, u32[]{:S(2)}) collective-permute-start(bf16[4,3,32,1536]{3,2,1,0:T(8,128)(2,1)} %get-tuple-element.172.refs_2_), channel_id=1, source_target_pairs={{0,1},{1,0},{2,3},{3,2},{4,5},{5,4},{6,7},{7,6},{8,9},{9,8},{10,11... | collective-permute-start | bytes 3538952 | tf_op jit(solution)/shard_map/ppermute | solution.py:543
  450.9 36.5 %collective-permute-start.56 = (bf16[4,3,32,1536]{3,2,1,0:T(8,128)(2,1)}, bf16[4,3,32,1536]{3,2,1,0:T(8,128)(2,1)S(1)}, u32[]{:S(2)}, u32[]{:S(2)}) collective-permute-start(bf16[4,3,32,1536]{3,2,1,0:T(8,128)(2,1)} %get-tuple-element.173.refs_3_), channel_id=1, source_target_pairs={{0,16},{8,24},{16,0},{24,8},{1,17},{9,25},{17,1},{25,9},{2,18},{10... | collective-permute-start | bytes 3538952 | tf_op jit(solution)/shard_map/ppermute | solution.py:543
  454.9 36.7 %collective-permute-start.53 = (bf16[2,3,32,1536]{3,2,1,0:T(8,128)(2,1)}, bf16[2,3,32,1536]{3,2,1,0:T(8,128)(2,1)S(1)}, u32[]{:S(2)}, u32[]{:S(2)}) collective-permute-start(bf16[2,3,32,1536]{3,2,1,0:T(8,128)(2,1)} %get-tuple-element.174.refs_21_), channel_id=1, source_target_pairs={{0,16},{8,24},{16,0},{24,8},{1,17},{9,25},{17,1},{25,9},{2,18},{10... | collective-permute-start | bytes 1769480 | tf_op jit(solution)/shard_map/ppermute | solution.py:543
  455.8 35.8 %collective-permute-start.54 = (bf16[2,3,32,1536]{3,2,1,0:T(8,128)(2,1)}, bf16[2,3,32,1536]{3,2,1,0:T(8,128)(2,1)}, u32[]{:S(2)}, u32[]{:S(2)}) collective-permute-start(bf16[2,3,32,1536]{3,2,1,0:T(8,128)(2,1)} %get-tuple-element.175.refs_22_), channel_id=1, source_target_pairs={{0,1},{1,0},{2,3},{3,2},{4,5},{5,4},{6,7},{7,6},{8,9},{9,8},{10,11... | collective-permute-start | bytes 1769480 | tf_op jit(solution)/shard_map/ppermute | solution.py:543
  492.5 21.8 %collective-permute-start.57 = (bf16[16,3,32,1536]{3,2,1,0:T(8,128)(2,1)}, bf16[16,3,32,1536]{3,2,1,0:T(8,128)(2,1)}, u32[]{:S(2)}, u32[]{:S(2)}) collective-permute-start(bf16[16,3,32,1536]{3,2,1,0:T(8,128)(2,1)} %tie.37.refs_2_), channel_id=1, source_target_pairs={{0,8},{8,0},{16,24},{24,16},{1,9},{9,1},{17,25},{25,17},{2,10},{10... | collective-permute-start | bytes 14155784 | tf_op jit(solution)/shard_map/ppermute | solution.py:543
  505.6 50.7 %collective-permute-start.59 = (bf16[4,3,32,1536]{3,2,1,0:T(8,128)(2,1)}, bf16[4,3,32,1536]{3,2,1,0:T(8,128)(2,1)}, u32[]{:S(2)}, u32[]{:S(2)}) collective-permute-start(bf16[4,3,32,1536]{3,2,1,0:T(8,128)(2,1)} %get-tuple-element.181.refs_1_), channel_id=1, source_target_pairs={{0,1},{1,0},{2,3},{3,2},{4,5},{5,4},{6,7},{7,6},{8,9},{9,8},{10,11... | collective-permute-start | bytes 3538952 | tf_op jit(solution)/shard_map/ppermute | solution.py:543
  506.3 50.0 %collective-permute-start.60 = (bf16[4,3,32,1536]{3,2,1,0:T(8,128)(2,1)}, bf16[4,3,32,1536]{3,2,1,0:T(8,128)(2,1)}, u32[]{:S(2)}, u32[]{:S(2)}) collective-permute-start(bf16[4,3,32,1536]{3,2,1,0:T(8,128)(2,1)} %get-tuple-element.182.refs_2_), channel_id=1, source_target_pairs={{0,16},{8,24},{16,0},{24,8},{1,17},{9,25},{17,1},{25,9},{2,18},{10... | collective-permute-start | bytes 3538952 | tf_op jit(solution)/shard_map/ppermute | solution.py:543
  507.5 16.4 %collective-permute-start.64 = (bf16[1,3,32,1536]{3,2,1,0:T(8,128)(2,1)}, bf16[1,3,32,1536]{3,2,1,0:T(8,128)(2,1)}, u32[]{:S(2)}, u32[]{:S(2)}) collective-permute-start(bf16[1,3,32,1536]{3,2,1,0:T(8,128)(2,1)} %tie.39.refs_3_), channel_id=1, source_target_pairs={{0,4},{1,5},{2,6},{3,7},{4,0},{5,1},{6,2},{7,3},{8,12},{9,13},{10,... | collective-permute-start | bytes 884744 | tf_op jit(solution)/shard_map/ppermute | solution.py:543
  516.9 30.5 %collective-permute-start.61 = (bf16[2,3,32,1536]{3,2,1,0:T(8,128)(2,1)}, bf16[2,3,32,1536]{3,2,1,0:T(8,128)(2,1)}, u32[]{:S(2)}, u32[]{:S(2)}) collective-permute-start(bf16[2,3,32,1536]{3,2,1,0:T(8,128)(2,1)} %get-tuple-element.190.refs_1_), channel_id=1, source_target_pairs={{0,16},{8,24},{16,0},{24,8},{1,17},{9,25},{17,1},{25,9},{2,18},{10... | collective-permute-start | bytes 1769480 | tf_op jit(solution)/shard_map/ppermute | solution.py:543
  517.6 29.7 %collective-permute-start.62 = (bf16[2,3,32,1536]{3,2,1,0:T(8,128)(2,1)}, bf16[2,3,32,1536]{3,2,1,0:T(8,128)(2,1)}, u32[]{:S(2)}, u32[]{:S(2)}) collective-permute-start(bf16[2,3,32,1536]{3,2,1,0:T(8,128)(2,1)} %get-tuple-element.191.refs_2_), channel_id=1, source_target_pairs={{0,1},{1,0},{2,3},{3,2},{4,5},{5,4},{6,7},{7,6},{8,9},{9,8},{10,11... | collective-permute-start | bytes 1769480 | tf_op jit(solution)/shard_map/ppermute | solution.py:543
  553.0 14.7 %collective-permute-start.67 = (bf16[2,3,32,1536]{3,2,1,0:T(8,128)(2,1)S(1)}, bf16[2,3,32,1536]{3,2,1,0:T(8,128)(2,1)}, u32[]{:S(2)}, u32[]{:S(2)}) collective-permute-start(bf16[2,3,32,1536]{3,2,1,0:T(8,128)(2,1)S(1)} %copy-done.2), channel_id=1, source_target_pairs={{0,2},{1,3},{2,0},{3,1},{4,6},{5,7},{6,4},{7,5},{8,10},{9,11},{10,... | collective-permute-start | bytes 1769480 | tf_op jit(solution)/shard_map/ppermute | solution.py:543
  553.8 27.3 %collective-permute-start.65 = (bf16[4,3,32,1536]{3,2,1,0:T(8,128)(2,1)}, bf16[4,3,32,1536]{3,2,1,0:T(8,128)(2,1)}, u32[]{:S(2)}, u32[]{:S(2)}) collective-permute-start(bf16[4,3,32,1536]{3,2,1,0:T(8,128)(2,1)} %get-tuple-element.195.refs_1_), channel_id=1, source_target_pairs={{0,1},{1,0},{2,3},{3,2},{4,5},{5,4},{6,7},{7,6},{8,9},{9,8},{10,11... | collective-permute-start | bytes 3538952 | tf_op jit(solution)/shard_map/ppermute | solution.py:543
  555.1 27.0 %collective-permute-start.66 = (bf16[4,3,32,1536]{3,2,1,0:T(8,128)(2,1)}, bf16[4,3,32,1536]{3,2,1,0:T(8,128)(2,1)}, u32[]{:S(2)}, u32[]{:S(2)}) collective-permute-start(bf16[4,3,32,1536]{3,2,1,0:T(8,128)(2,1)} %get-tuple-element.196.refs_2_), channel_id=1, source_target_pairs={{0,16},{8,24},{16,0},{24,8},{1,17},{9,25},{17,1},{25,9},{2,18},{10... | collective-permute-start | bytes 3538952 | tf_op jit(solution)/shard_map/ppermute | solution.py:543
  569.8 18.5 %collective-permute-start.63 = (bf16[2,3,32,1536]{3,2,1,0:T(8,128)(2,1)S(1)}, bf16[2,3,32,1536]{3,2,1,0:T(8,128)(2,1)}, u32[]{:S(2)}, u32[]{:S(2)}) collective-permute-start(bf16[2,3,32,1536]{3,2,1,0:T(8,128)(2,1)S(1)} %copy-done.1), channel_id=1, source_target_pairs={{0,2},{1,3},{2,0},{3,1},{4,6},{5,7},{6,4},{7,5},{8,10},{9,11},{10,... | collective-permute-start | bytes 1769480 | tf_op jit(solution)/shard_map/ppermute | solution.py:543
  585.0 14.3 %collective-permute-start.75 = (bf16[1,3,32,1536]{3,2,1,0:T(8,128)(2,1)S(1)}, bf16[1,3,32,1536]{3,2,1,0:T(8,128)(2,1)}, u32[]{:S(2)}, u32[]{:S(2)}) collective-permute-start(bf16[1,3,32,1536]{3,2,1,0:T(8,128)(2,1)S(1)} %copy-done.14), channel_id=1, source_target_pairs={{0,4},{1,5},{2,6},{3,7},{4,0},{5,1},{6,2},{7,3},{8,12},{9,13},{10,... | collective-permute-start | bytes 884744 | tf_op jit(solution)/shard_map/ppermute | solution.py:543
  585.9 25.1 %collective-permute-start.74 = (bf16[2,3,32,1536]{3,2,1,0:T(8,128)(2,1)}, bf16[2,3,32,1536]{3,2,1,0:T(8,128)(2,1)}, u32[]{:S(2)}, u32[]{:S(2)}) collective-permute-start(bf16[2,3,32,1536]{3,2,1,0:T(8,128)(2,1)} %tie.46.refs_1_), channel_id=1, source_target_pairs={{0,2},{1,3},{2,0},{3,1},{4,6},{5,7},{6,4},{7,5},{8,10},{9,11},{10,... | collective-permute-start | bytes 1769480 | tf_op jit(solution)/shard_map/ppermute | solution.py:543
  587.1 7.0 %collective-permute-start.69 = (bf16[1,3,32,1536]{3,2,1,0:T(8,128)(2,1)}, bf16[1,3,32,1536]{3,2,1,0:T(8,128)(2,1)}, u32[]{:S(2)}, u32[]{:S(2)}) collective-permute-start(bf16[1,3,32,1536]{3,2,1,0:T(8,128)(2,1)} %tie.47.refs_1_.refs_0_), channel_id=1, source_target_pairs={{0,16},{8,24},{16,0},{24,8},{1,17},{9,25},{17,1},{25,9},{2,18},{10... | collective-permute-start | bytes 884744 | tf_op jit(solution)/shard_map/ppermute | solution.py:543
  590.5 11.0 %collective-permute-start.68 = (bf16[1,3,32,1536]{3,2,1,0:T(8,128)(2,1)S(1)}, bf16[1,3,32,1536]{3,2,1,0:T(8,128)(2,1)S(1)}, u32[]{:S(2)}, u32[]{:S(2)}) collective-permute-start(bf16[1,3,32,1536]{3,2,1,0:T(8,128)(2,1)S(1)} %copy-done.12), channel_id=1, source_target_pairs={{0,8},{8,0},{16,24},{24,16},{1,9},{9,1},{17,25},{25,17},{2,10},{10... | collective-permute-start | bytes 884744 | tf_op jit(solution)/shard_map/ppermute | solution.py:543
  594.1 7.3 %collective-permute-start.70 = (bf16[1,3,32,1536]{3,2,1,0:T(8,128)(2,1)}, bf16[1,3,32,1536]{3,2,1,0:T(8,128)(2,1)S(1)}, u32[]{:S(2)}, u32[]{:S(2)}) collective-permute-start(bf16[1,3,32,1536]{3,2,1,0:T(8,128)(2,1)} %collective-permute-done.69.refs_2_), channel_id=1, source_target_pairs={{0,8},{8,0},{16,24},{24,16},{1,9},{9,1},{17,25},{25,17},{2,10},{10... | collective-permute-start | bytes 884744 | tf_op jit(solution)/shard_map/ppermute | solution.py:543
  601.4 18.3 %collective-permute-start.80 = (bf16[1,3,32,1536]{3,2,1,0:T(8,128)(2,1)}, bf16[1,3,32,1536]{3,2,1,0:T(8,128)(2,1)S(1)}, u32[]{:S(2)}, u32[]{:S(2)}) collective-permute-start(bf16[1,3,32,1536]{3,2,1,0:T(8,128)(2,1)} %tie.48.refs_1_), channel_id=1, source_target_pairs={{0,4},{1,5},{2,6},{3,7},{4,0},{5,1},{6,2},{7,3},{8,12},{9,13},{10,... | collective-permute-start | bytes 884744 | tf_op jit(solution)/shard_map/ppermute | solution.py:543
  615.2 9.6 %collective-permute-start.78 = (f32[32,512]{1,0:T(8,128)}, f32[32,512]{1,0:T(8,128)S(1)}, u32[]{:S(2)}, u32[]{:S(2)}) collective-permute-start(f32[32,512]{1,0:T(8,128)} %tie.52.refs_1_), channel_id=1, source_target_pairs={{0,6},{1,7},{2,4},{3,5},{4,2},{5,3},{6,0},{7,1},{8,14},{9,15},{10,... | collective-permute-start | bytes 196616 | tf_op jit(solution)/shard_map/ppermute | solution.py:543
  616.8 8.0 %collective-permute-start.77 = (f32[32,512]{1,0:T(8,128)}, f32[32,512]{1,0:T(8,128)S(1)}, u32[]{:S(2)}, u32[]{:S(2)}) collective-permute-start(f32[32,512]{1,0:T(8,128)} %tie.52.refs_1_), channel_id=1, source_target_pairs={{0,4},{1,5},{2,6},{3,7},{4,0},{5,1},{6,2},{7,3},{8,12},{9,13},{10,... | collective-permute-start | bytes 196616 | tf_op jit(solution)/shard_map/ppermute | solution.py:543
  618.8 7.2 %collective-permute-start.76 = (f32[32,512]{1,0:T(8,128)}, f32[32,512]{1,0:T(8,128)S(1)}, u32[]{:S(2)}, u32[]{:S(2)}) collective-permute-start(f32[32,512]{1,0:T(8,128)} %tie.52.refs_1_), channel_id=1, source_target_pairs={{0,2},{1,3},{2,0},{3,1},{4,6},{5,7},{6,4},{7,5},{8,10},{9,11},{10,... | collective-permute-start | bytes 196616 | tf_op jit(solution)/shard_map/ppermute | solution.py:543
  622.0 14.4 %collective-permute-start.79 = (bf16[1,3,32,1536]{3,2,1,0:T(8,128)(2,1)S(1)}, bf16[1,3,32,1536]{3,2,1,0:T(8,128)(2,1)}, u32[]{:S(2)}, u32[]{:S(2)}) collective-permute-start(bf16[1,3,32,1536]{3,2,1,0:T(8,128)(2,1)S(1)} %copy-done.13), channel_id=1, source_target_pairs={{0,4},{1,5},{2,6},{3,7},{4,0},{5,1},{6,2},{7,3},{8,12},{9,13},{10,... | collective-permute-start | bytes 884744 | tf_op jit(solution)/shard_map/ppermute | solution.py:543
  624.0 9.3 %collective-permute-start.82 = (bf16[1,3,32,1536]{3,2,1,0:T(8,128)(2,1)S(1)}, bf16[1,3,32,1536]{3,2,1,0:T(8,128)(2,1)S(1)}, u32[]{:S(2)}, u32[]{:S(2)}) collective-permute-start(bf16[1,3,32,1536]{3,2,1,0:T(8,128)(2,1)S(1)} %copy-done.10), channel_id=1, source_target_pairs={{0,16},{8,24},{16,0},{24,8},{1,17},{9,25},{17,1},{25,9},{2,18},{10... | collective-permute-start | bytes 884744 | tf_op jit(solution)/shard_map/ppermute | solution.py:543
  624.9 13.8 %collective-permute-start.81 = (bf16[1,3,32,1536]{3,2,1,0:T(8,128)(2,1)S(1)}, bf16[1,3,32,1536]{3,2,1,0:T(8,128)(2,1)S(1)}, u32[]{:S(2)}, u32[]{:S(2)}) collective-permute-start(bf16[1,3,32,1536]{3,2,1,0:T(8,128)(2,1)S(1)} %copy-done.10), channel_id=1, source_target_pairs={{0,8},{8,0},{16,24},{24,16},{1,9},{9,1},{17,25},{25,17},{2,10},{10... | collective-permute-start | bytes 884744 | tf_op jit(solution)/shard_map/ppermute | solution.py:543
  624.9 21.6 %collective-permute-start.88 = (bf16[1,3,32,1536]{3,2,1,0:T(8,128)(2,1)}, bf16[1,3,32,1536]{3,2,1,0:T(8,128)(2,1)S(1)}, u32[]{:S(2)}, u32[]{:S(2)}) collective-permute-start(bf16[1,3,32,1536]{3,2,1,0:T(8,128)(2,1)} %tie.53.refs_1_.refs_0_), channel_id=1, source_target_pairs={{0,16},{8,24},{16,0},{24,8},{1,17},{9,25},{17,1},{25,9},{2,18},{10... | collective-permute-start | bytes 884744 | tf_op jit(solution)/shard_map/ppermute | solution.py:543
  626.1 30.1 %collective-permute-start.87 = (bf16[1,3,32,1536]{3,2,1,0:T(8,128)(2,1)}, bf16[1,3,32,1536]{3,2,1,0:T(8,128)(2,1)S(1)}, u32[]{:S(2)}, u32[]{:S(2)}) collective-permute-start(bf16[1,3,32,1536]{3,2,1,0:T(8,128)(2,1)} %tie.53.refs_1_.refs_0_), channel_id=1, source_target_pairs={{0,8},{8,0},{16,24},{24,16},{1,9},{9,1},{17,25},{25,17},{2,10},{10... | collective-permute-start | bytes 884744 | tf_op jit(solution)/shard_map/ppermute | solution.py:543
  644.3 8.6 %collective-permute-start.85 = (bf16[1,3,32,1536]{3,2,1,0:T(8,128)(2,1)}, bf16[1,3,32,1536]{3,2,1,0:T(8,128)(2,1)S(1)}, u32[]{:S(2)}, u32[]{:S(2)}) collective-permute-start(bf16[1,3,32,1536]{3,2,1,0:T(8,128)(2,1)} %tie.54.refs_0_), channel_id=1, source_target_pairs={{0,16},{8,24},{16,0},{24,8},{1,17},{9,25},{17,1},{25,9},{2,18},{10... | collective-permute-start | bytes 884744 | tf_op jit(solution)/shard_map/ppermute | solution.py:543
  646.5 9.7 %collective-permute-start.89 = (bf16[1,3,32,1536]{3,2,1,0:T(8,128)(2,1)S(1)}, bf16[1,3,32,1536]{3,2,1,0:T(8,128)(2,1)S(1)}, u32[]{:S(2)}, u32[]{:S(2)}) collective-permute-start(bf16[1,3,32,1536]{3,2,1,0:T(8,128)(2,1)S(1)} %collective-permute-done.88.refs_2_), channel_id=1, source_target_pairs={{0,8},{8,0},{16,24},{24,16},{1,9},{9,1},{17,25},{25,17},{2,10},{10... | collective-permute-start | bytes 884744 | tf_op jit(solution)/shard_map/ppermute | solution.py:543
  646.5 15.3 %collective-permute-start.84 = (bf16[1,3,32,1536]{3,2,1,0:T(8,128)(2,1)}, bf16[1,3,32,1536]{3,2,1,0:T(8,128)(2,1)S(1)}, u32[]{:S(2)}, u32[]{:S(2)}) collective-permute-start(bf16[1,3,32,1536]{3,2,1,0:T(8,128)(2,1)} %tie.54.refs_0_), channel_id=1, source_target_pairs={{0,8},{8,0},{16,24},{24,16},{1,9},{9,1},{17,25},{25,17},{2,10},{10... | collective-permute-start | bytes 884744 | tf_op jit(solution)/shard_map/ppermute | solution.py:543
  653.6 8.3 %collective-permute-start.86 = (bf16[1,3,32,1536]{3,2,1,0:T(8,128)(2,1)}, bf16[1,3,32,1536]{3,2,1,0:T(8,128)(2,1)S(1)}, u32[]{:S(2)}, u32[]{:S(2)}) collective-permute-start(bf16[1,3,32,1536]{3,2,1,0:T(8,128)(2,1)} %tie.55.refs_2_), channel_id=1, source_target_pairs={{0,8},{8,0},{16,24},{24,16},{1,9},{9,1},{17,25},{25,17},{2,10},{10... | collective-permute-start | bytes 884744 | tf_op jit(solution)/shard_map/ppermute | solution.py:543
  (118 other events, 771.6 us)
Sparse Core Ops, SparseCore 0:
  93.1 151.9 all-gather.1

commit v4 on v3

--- a/solution.py
+++ b/solution.py
@@ -603,12 +603,10 @@
     def begin(self, gate_in, gate_out, lo, hi, tokens=()):
         place = lax.axis_index("dp").astype(jnp.int32)[None]
         own = pack(place, gate_in, gate_out, lo, hi, gate_in.shape[1] // self.dp_size, tokens)
-        by_2 = self.z(own, 2)
-        by_1 = self.z(jnp.concatenate([own, by_2]), 1)
-        return [own, by_1, by_2]
+        return [own] + [self.z(own, j) for j in (1, 2, 3)]
 
     def spread(self, pieces, tokens=()):
-        (held,) = combine([[[(0, 0)], [(1, 0)], [(2, 0)], [(1, 1)]]], pieces, tokens)
+        (held,) = combine([[[(k, 0)] for k in range(4)]], pieces, tokens)
         return held, self.y(held), self.x(held)
 
     def relay(self, arrays, tokens=()):
@@ -702,9 +700,10 @@
     wide = g_in.shape[-1]
     for j, piece in enumerate(pieces):
         row = pl.multiple_of(table[j], pr)
-        value = piece[0, 0].astype(F32)
-        g_in[0, pl.ds(row, pr), :] = value[:, :wide]
-        g_out[0, pl.ds(row, pr), :] = value[:, wide:]
+        for section in range(g_in.shape[0]):
+            value = piece[0, section].astype(F32)
+            g_in[section, pl.ds(row, pr), :] = value[:, :wide]
+            g_out[section, pl.ds(row, pr), :] = value[:, wide:]
 
 
 def place_grads(table, pieces, start, shard_rows, previous):
@@ -714,15 +713,15 @@
         jax.ShapeDtypeStruct((LAYERS * SECTIONS, shard_rows, wide), F32),
         jax.ShapeDtypeStruct((LAYERS * SECTIONS, shard_rows, width - wide), F32),
     ]
-    block = lambda w: pl.BlockSpec((1, shard_rows, w), lambda i, *_: (start + i, 0, 0))
+    block = lambda w: pl.BlockSpec((n, shard_rows, w), lambda i, *_: (start // n, 0, 0))
     n_pieces = len(pieces)
     extra = [] if previous is None else list(previous)
     return pl.pallas_call(
         functools.partial(place_kernel, n_pieces),
         grid_spec=pltpu.PrefetchScalarGridSpec(
             num_scalar_prefetch=1,
-            grid=(n,),
-            in_specs=[pl.BlockSpec((1, 1, pr, width), lambda i, *_: (0, i, 0, 0))] * n_pieces
+            grid=(1,),
+            in_specs=[pl.BlockSpec((1, n, pr, width), lambda i, *_: (0, 0, 0, 0))] * n_pieces
             + [pl.BlockSpec(memory_space=pl.ANY)] * len(extra),
             out_specs=[block(wide), block(width - wide)],
         ),
@@ -837,11 +836,9 @@
     tokens = sums_2.send(())
     current, stats, _, _ = records[1]
     total, pooled = pool_grads(current, micro, stats, [gn_3, gn_2, gh], tokens)
-    vectors = jnp.concatenate([vectors_2, vectors_3])
-    both_1 = moves.all_reduce(jnp.concatenate([pooled, vectors.reshape(-1, columns)]), add, sums_3.ready or ())
-    moves.take_arrived()
+    both_1 = moves.all_reduce(pooled, add, sums_3.ready or ())
     tokens = sums_3.send((both_1,)) + sums_2.send((both_1,))
-    carried = carry_grads(current, micro, valid, stats, gains[1], total, both_1[: 2 * MB], carried, tokens)
+    carried = carry_grads(current, micro, valid, stats, gains[1], total, both_1, carried, tokens)
     gh, gn_1, vectors_1, out_1 = backward(1, carried, ())
     sums_1 = Sending(moves.sums(out_1))
     tokens = sums_1.send(moves.take_arrived())
@@ -856,7 +853,7 @@
     tokens = sums_3.send(tokens)
     current, stats, _, _ = records[0]
     total, pooled = pool_grads(current, micro, stats, [gn_1, gn_0, gh], tokens)
-    vectors = jnp.concatenate([vectors_0, vectors_1])
+    vectors = jnp.concatenate([vectors_0, vectors_1, vectors_2, vectors_3])
     both_0 = Sending(moves.all_reduce_steps(jnp.concatenate([pooled, vectors.reshape(-1, columns)]), add))
     tokens = sums_0.send((total,))
     tokens = sums_2.send(tokens)
@@ -880,9 +877,8 @@
     tokens = sums_0.send([*tokens, *grads])
     grads = place_grads(pieces_table, sums_1.result, 3, shard_rows, grads)
     grads = place_grads(pieces_table, sums_0.result, 0, shard_rows, grads)
-    results = [both_0, both_1]
-    pooled = jnp.stack([both[: 2 * MB] for both in results])
-    stacked = jnp.stack([both[2 * MB :].reshape(SECTIONS, 4 * columns) for both in results])
+    pooled = jnp.stack([both_0[: 2 * MB], both_1])
+    stacked = both_0[2 * MB :].reshape(LAYERS, SECTIONS, 4 * columns)
     _, mask_pull = jax.vjp(jax.vmap(jax.vmap(feature_mask)), mask_logits, thresholds)
     grad_logits, grad_thresholds = mask_pull(stacked[..., :columns])
     unflat = lambda v: v.reshape((LAYERS, SECTIONS) + v.shape[1:])

time: 684 us -> 676 us (0.988)
    ppermute x86 -> x88, starting transfers between devices: 75.8 us -> 71.9 us  [permute(): self.arrived.append(lax.ppermute(v, axis, along(axis, size, flip)))]
    ppermute x86 -> x88, waiting for transfers between devices: 188 us -> 190 us  [permute(): self.arrived.append(lax.ppermute(v, axis, along(axis, size, flip)))]
    unnamed x187 -> x203, local copies, waits for them, and re-layouts: 21.5 us -> 21.9 us
  transfers between devices with their start and end apart: 91 -> 93, of which waited for: 40 -> 41; matrix products, arithmetic and copies ran while one was open for 13% -> 12% of each run, Pallas kernels for 24% -> 24%
where the time goes in v4:
time: 676 us; the launch traced here: 666 us
  Pallas kernels  269 us (40%)
  waiting for transfers between devices  198 us (29%)
  starting transfers between devices  78.6 us (12%)
  other arithmetic  75.5 us (11%)
  local copies, waits for them, and re-layouts  29.8 us (4%)
  between operations  15.5 us (2%)
    ppermute x88, waiting for transfers between devices, permute(): self.arrived.append(lax.ppermute(v, axis, along(axis, size, flip)))  190 us
    pallas_call x4, Pallas kernels, backward_chunk(): pl.pallas_call(functools.partial(backward_kernel, n, first, len(arrays),...  124 us
    ppermute x88, starting transfers between devices, permute(): self.arrived.append(lax.ppermute(v, axis, along(axis, size, flip)))  71.9 us
    pallas_call x3, Pallas kernels, forward_chunk(): pl.pallas_call(functools.partial(forward_kernel, n, first, len(arrays), l...  71 us
    convert_element_type x20, other arithmetic, low_sum(): return sum((v.astype(F32) for v in terms)).astype(BF16)  47.1 us
    unnamed x203, local copies, waits for them, and re-layouts  21.9 us
    pallas_call x4, Pallas kernels, place_grads(): pl.pallas_call(functools.partial(place_kernel, n_pieces), grid_spec=pltpu...  13.8 us
  transfers between devices with their start and end apart: 93, of which 41 were waited for; matrix products, arithmetic and copies ran while one was open for 12% of the time, Pallas kernels for 24%

profile of v4, /device:TPU:0, one launch (start us, length us, event | category | flops | bytes accessed | tf_op | source)
XLA Modules:
  0.0 666.3 jit_solution(6060269356076349666)
XLA Ops:
  7.2 2.5 pack.3.refs_0_
  9.7 5.0 collective-permute-start.2
  17.2 3.8 local_stats.2.refs_4_.refs_0_
  22.9 17.1 %collective-permute-done.1.refs_2_ = bf16[1,3,32,1536]{3,2,1,0:T(8,128)(2,1)S(1)} collective-permute-done((bf16[1,3,32,1536]{3,2,1,0:T(8,128)(2,1)}, bf16[1,3,32,1536]{3,2,1,0:T(8,128)(2,1)S(1)}, u32[]{:S(2)}, u32[]{:S(2)}) %collective-permute-start.1) | collective-permute-done | bytes 294944 | tf_op jit(solution)/shard_map/ppermute | solution.py:543
  41.5 3.2 combine.4.refs_0_.refs_5_.refs_11_
  47.7 2.4 pack.4.refs_0_
  50.2 2.5 collective-permute-start.5
  54.6 7.7 %collective-permute-done.5.refs_4_.refs_3_ = bf16[1,3,32,1536]{3,2,1,0:T(8,128)(2,1)S(1)} collective-permute-done((bf16[1,3,32,1536]{3,2,1,0:T(8,128)(2,1)}, bf16[1,3,32,1536]{3,2,1,0:T(8,128)(2,1)S(1)}, u32[]{:S(2)}, u32[]{:S(2)}) %collective-permute-start.5) | collective-permute-done | bytes 294944 | tf_op jit(solution)/shard_map/ppermute | solution.py:543
  62.2 13.6 %collective-permute-done.4.refs_3_.refs_2_ = bf16[1,3,32,1536]{3,2,1,0:T(8,128)(2,1)S(1)} collective-permute-done((bf16[1,3,32,1536]{3,2,1,0:T(8,128)(2,1)}, bf16[1,3,32,1536]{3,2,1,0:T(8,128)(2,1)S(1)}, u32[]{:S(2)}, u32[]{:S(2)}) %collective-permute-start.4) | collective-permute-done | bytes 294944 | tf_op jit(solution)/shard_map/ppermute | solution.py:543
  78.1 3.2 combine.5
  81.3 3.9 pack.5
  85.3 3.2 combine.6.refs_1_.refs_5_.refs_11_
  111.8 3.6 norm_rows.2
  115.4 30.9 %collective-permute-done.16.refs_9_.refs_15_ = bf16[2,3,32,1536]{3,2,1,0:T(8,128)(2,1)} collective-permute-done((bf16[2,3,32,1536]{3,2,1,0:T(8,128)(2,1)}, bf16[2,3,32,1536]{3,2,1,0:T(8,128)(2,1)}, u32[]{:S(2)}, u32[]{:S(2)}) %collective-permute-start.16) | collective-permute-done | bytes 589856 | tf_op jit(solution)/shard_map/ppermute | solution.py:543
  146.3 8.1 %collective-permute-done.15.refs_8_.refs_14_ = bf16[2,3,32,1536]{3,2,1,0:T(8,128)(2,1)S(1)} collective-permute-done((bf16[2,3,32,1536]{3,2,1,0:T(8,128)(2,1)S(1)}, bf16[2,3,32,1536]{3,2,1,0:T(8,128)(2,1)S(1)}, u32[]{:S(2)}, u32[]{:S(2)}) %collective-permute-start.15) | collective-permute-done | bytes 589856 | tf_op jit(solution)/shard_map/ppermute | solution.py:543
  155.0 3.2 combine.7
  161.5 20.1 %forward_sections.3 = (f32[768,512]{1,0:T(8,128)}, f32[3,768,512]{2,1,0:T(8,128)}, f32[3,768,512]{2,1,0:T(8,128)}, f32[3,768,512]{2,1,0:T(8,128)}, f32[3,768,512...) custom-call(s32[32]{0:T(128)} %stack.114.table, ...), custom_call_target="tpu_custom_call" | custom-call | flops 20000000000 | bytes 1 | tf_op jit(solution)/shard_map/forward_sections/pallas_call | solution.py:116
  186.6 19.3 %forward_sections.4 = (f32[768,512]{1,0:T(8,128)}, f32[3,768,512]{2,1,0:T(8,128)}, f32[3,768,512]{2,1,0:T(8,128)}, f32[3,768,512]{2,1,0:T(8,128)}, f32[3,768,512...) custom-call(s32[32]{0:T(128)} %stack.114.table, ...), custom_call_target="tpu_custom_call" | custom-call | flops 20000000000 | bytes 1 | tf_op jit(solution)/shard_map/forward_sections/pallas_call | solution.py:116
  205.9 4.4 local_stats.3
  213.4 2.5 collective-permute-start.34
  221.0 2.8 collective-permute-start.37
  227.6 3.1 collective-permute-done.36
  231.3 4.0 norm_rows.3
  235.4 31.6 %forward_sections.5 = (bf16[768,512]{1,0:T(8,128)(2,1)}, f32[6,768,512]{2,1,0:T(8,128)}, f32[6,768,512]{2,1,0:T(8,128)}, f32[6,768,512]{2,1,0:T(8,128)}, f32[6,7...) custom-call(s32[32]{0:T(128)} %constant.45.clone.table, ...), custom_call_target="tpu_custom_call" | custom-call | flops 20000000000 | bytes 1 | tf_op jit(solution)/shard_map/forward_sections/pallas_call | solution.py:116
  267.0 31.1 %backward_sections.4 = (f32[768,512]{1,0:T(8,128)}, f32[768,512]{1,0:T(8,128)}, f32[3,1,2048]{2,1,0:T(1,128)}, bf16[4,3,32,1536]{3,2,1,0:T(8,128)(2,1)}, bf16[4,...) custom-call(s32[64]{0:T(128)} %concatenate.77.table, ...), custom_call_target="tpu_custom_call" | custom-call | flops 20000000000 | bytes 1 | tf_op jit(solution)/shard_map/backward_sections/pallas_call | solution.py:249
  298.1 8.1 %collective-permute-done.38 = bf16[16,3,32,1536]{3,2,1,0:T(8,128)(2,1)S(1)} collective-permute-done((bf16[16,3,32,1536]{3,2,1,0:T(8,128)(2,1)}, bf16[16,3,32,1536]{3,2,1,0:T(8,128)(2,1)S(1)}, u32[]{:S(2)}, u32[]{:S(2)}) %collective-permute-start.38) | collective-permute-done | bytes 4718624 | tf_op jit(solution)/shard_map/ppermute | solution.py:543
  306.3 2.2 copy-done.11
  308.5 2.6 add_convert_fusion.22
  311.1 31.2 %backward_sections.5 = (f32[768,512]{1,0:T(8,128)}, f32[768,512]{1,0:T(8,128)}, f32[3,1,2048]{2,1,0:T(1,128)}, bf16[4,3,32,1536]{3,2,1,0:T(8,128)(2,1)}, bf16[4,...) custom-call(s32[64]{0:T(128)} %concatenate.77.table, ...), custom_call_target="tpu_custom_call" | custom-call | flops 20000000000 | bytes 1 | tf_op jit(solution)/shard_map/backward_sections/pallas_call | solution.py:249
  343.9 6.0 pool_grads.2
  355.0 4.7 collective-permute-done.42
  360.7 2.7 collective-permute-done.40.refs_3_
  364.1 2.9 add_convert_fusion.19
  371.3 2.2 collective-permute-start.45
  381.0 2.6 add_convert_fusion.16
  386.1 5.3 carry_grads.2.refs_0_.carried_ref
  391.4 30.8 %backward_sections.6 = (f32[768,512]{1,0:T(8,128)}, f32[768,512]{1,0:T(8,128)}, f32[3,1,2048]{2,1,0:T(1,128)}, bf16[4,3,32,1536]{3,2,1,0:T(8,128)(2,1)}, bf16[4,...) custom-call(s32[64]{0:T(128)} %concatenate.76.table, ...), custom_call_target="tpu_custom_call" | custom-call | flops 20000000000 | bytes 1 | tf_op jit(solution)/shard_map/backward_sections/pallas_call | solution.py:249
  428.8 2.6 add_convert_fusion.11
  435.9 2.8 add_convert_fusion.14
  441.4 30.8 %backward_sections.7 = (f32[768,512]{1,0:T(8,128)}, f32[768,512]{1,0:T(8,128)}, f32[3,1,2048]{2,1,0:T(1,128)}, bf16[4,3,32,1536]{3,2,1,0:T(8,128)(2,1)}, bf16[4,...) custom-call(s32[64]{0:T(128)} %concatenate.76.table, ...), custom_call_target="tpu_custom_call" | custom-call | flops 20000000000 | bytes 1 | tf_op jit(solution)/shard_map/backward_sections/pallas_call | solution.py:249
  472.2 3.7 collective-permute-done.55.refs_4_
  483.4 2.8 add_convert_fusion.7
  493.0 5.8 pool_grads.3
  498.8 2.6 add_convert_fusion.4
  503.8 3.6 collective-permute-done.66
  507.4 2.2 add_convert_fusion.36.refs_0_
  509.6 21.4 %collective-permute-done.63 = bf16[2,3,32,1536]{3,2,1,0:T(8,128)(2,1)} collective-permute-done((bf16[2,3,32,1536]{3,2,1,0:T(8,128)(2,1)}, bf16[2,3,32,1536]{3,2,1,0:T(8,128)(2,1)}, u32[]{:S(2)}, u32[]{:S(2)}) %collective-permute-start.63) | collective-permute-done | bytes 589856 | tf_op jit(solution)/shard_map/ppermute | solution.py:543
  531.0 3.3 add_convert_fusion.1
  543.5 7.3 %collective-permute-done.69 = bf16[2,3,32,1536]{3,2,1,0:T(8,128)(2,1)} collective-permute-done((bf16[2,3,32,1536]{3,2,1,0:T(8,128)(2,1)S(1)}, bf16[2,3,32,1536]{3,2,1,0:T(8,128)(2,1)}, u32[]{:S(2)}, u32[]{:S(2)}) %collective-permute-start.69) | collective-permute-done | bytes 589856 | tf_op jit(solution)/shard_map/ppermute | solution.py:543
  554.1 10.5 %collective-permute-done.67 = bf16[4,3,32,1536]{3,2,1,0:T(8,128)(2,1)} collective-permute-done((bf16[4,3,32,1536]{3,2,1,0:T(8,128)(2,1)}, bf16[4,3,32,1536]{3,2,1,0:T(8,128)(2,1)}, u32[]{:S(2)}, u32[]{:S(2)}) %collective-permute-start.67) | collective-permute-done | bytes 1179680 | tf_op jit(solution)/shard_map/ppermute | solution.py:543
  571.1 2.2 add_convert_fusion.38.refs_0_
  573.4 3.9 collective-permute-done.71.refs_2_
  577.3 4.4 collective-permute-done.77
  585.3 3.4 place_grads.4
  599.0 3.2 collective-permute-start.78
  602.3 10.5 %collective-permute-done.82 = bf16[1,3,32,1536]{3,2,1,0:T(8,128)(2,1)S(1)} collective-permute-done((bf16[1,3,32,1536]{3,2,1,0:T(8,128)(2,1)S(1)}, bf16[1,3,32,1536]{3,2,1,0:T(8,128)(2,1)S(1)}, u32[]{:S(2)}, u32[]{:S(2)}) %collective-permute-start.82) | collective-permute-done | bytes 294944 | tf_op jit(solution)/shard_map/ppermute | solution.py:543
  612.8 2.3 add_convert_fusion.24.refs_0_
  620.7 5.1 carry_grads.3.refs_1_
  626.4 4.4 collective-permute-done.81
  630.8 2.3 add_convert_fusion.26.refs_0_
  633.8 3.4 place_grads.5
  639.9 6.6 collective-permute-done.87.refs_0_
  651.3 3.4 place_grads.6
  655.6 3.4 place_grads.7
  (466 shorter events, 158.2 us)
Async XLA Ops:
  7.2 228.2 %all-gather.2.cloned.1.call-start = ((), (), s32[]{:S(2)}) async-start(), calls=%async_computation | async-start | bytes 19464192 | tf_op jit(solution)/shard_map/all_gather | solution.py:600
  9.7 13.2 %collective-permute-start.2 = (bf16[1,3,32,1536]{3,2,1,0:T(8,128)(2,1)}, bf16[1,3,32,1536]{3,2,1,0:T(8,128)(2,1)S(1)}, u32[]{:S(2)}, u32[]{:S(2)}) collective-permute-start(bf16[1,3,32,1536]{3,2,1,0:T(8,128)(2,1)} %pack.3.refs_0_), channel_id=1, source_target_pairs={{0,6},{1,7},{2,4},{3,5},{4,2},{5,3},{6,0},{7,1},{8,14},{9,15},{10,... | collective-permute-start | bytes 884744 | tf_op jit(solution)/shard_map/ppermute | solution.py:543
  14.8 25.3 %collective-permute-start.1 = (bf16[1,3,32,1536]{3,2,1,0:T(8,128)(2,1)}, bf16[1,3,32,1536]{3,2,1,0:T(8,128)(2,1)S(1)}, u32[]{:S(2)}, u32[]{:S(2)}) collective-permute-start(bf16[1,3,32,1536]{3,2,1,0:T(8,128)(2,1)} %pack.3.refs_0_), channel_id=1, source_target_pairs={{0,4},{1,5},{2,6},{3,7},{4,0},{5,1},{6,2},{7,3},{8,12},{9,13},{10,... | collective-permute-start | bytes 884744 | tf_op jit(solution)/shard_map/ppermute | solution.py:543
  14.8 25.3 %collective-permute-start = (bf16[1,3,32,1536]{3,2,1,0:T(8,128)(2,1)}, bf16[1,3,32,1536]{3,2,1,0:T(8,128)(2,1)S(1)}, u32[]{:S(2)}, u32[]{:S(2)}) collective-permute-start(bf16[1,3,32,1536]{3,2,1,0:T(8,128)(2,1)} %pack.3.refs_0_), channel_id=1, source_target_pairs={{0,2},{1,3},{2,0},{3,1},{4,6},{5,7},{6,4},{7,5},{8,10},{9,11},{10,... | collective-permute-start | bytes 884744 | tf_op jit(solution)/shard_map/ppermute | solution.py:543
  44.7 31.1 %collective-permute-start.7 = (bf16[4,3,32,1536]{3,2,1,0:T(8,128)(2,1)}, bf16[4,3,32,1536]{3,2,1,0:T(8,128)(2,1)S(1)}, u32[]{:S(2)}, u32[]{:S(2)}) collective-permute-start(bf16[4,3,32,1536]{3,2,1,0:T(8,128)(2,1)} %combine.4.refs_0_.refs_5_.refs_11_), channel_id=1, source_target_pairs={{0,16},{8,24},{16,0},{24,8},{1,17},{9,25},{17,1},{25,9},{2,18},{10... | collective-permute-start | bytes 3538952 | tf_op jit(solution)/shard_map/ppermute | solution.py:543
  46.2 29.7 %collective-permute-start.6 = (bf16[4,3,32,1536]{3,2,1,0:T(8,128)(2,1)}, bf16[4,3,32,1536]{3,2,1,0:T(8,128)(2,1)S(1)}, u32[]{:S(2)}, u32[]{:S(2)}) collective-permute-start(bf16[4,3,32,1536]{3,2,1,0:T(8,128)(2,1)} %combine.4.refs_0_.refs_5_.refs_11_), channel_id=1, source_target_pairs={{0,1},{1,0},{2,3},{3,2},{4,5},{5,4},{6,7},{7,6},{8,9},{9,8},{10,11... | collective-permute-start | bytes 3538952 | tf_op jit(solution)/shard_map/ppermute | solution.py:543
  50.2 12.1 %collective-permute-start.5 = (bf16[1,3,32,1536]{3,2,1,0:T(8,128)(2,1)}, bf16[1,3,32,1536]{3,2,1,0:T(8,128)(2,1)S(1)}, u32[]{:S(2)}, u32[]{:S(2)}) collective-permute-start(bf16[1,3,32,1536]{3,2,1,0:T(8,128)(2,1)} %pack.4.refs_0_), channel_id=1, source_target_pairs={{0,6},{1,7},{2,4},{3,5},{4,2},{5,3},{6,0},{7,1},{8,14},{9,15},{10,... | collective-permute-start | bytes 884744 | tf_op jit(solution)/shard_map/ppermute | solution.py:543
  52.7 23.2 %collective-permute-start.4 = (bf16[1,3,32,1536]{3,2,1,0:T(8,128)(2,1)}, bf16[1,3,32,1536]{3,2,1,0:T(8,128)(2,1)S(1)}, u32[]{:S(2)}, u32[]{:S(2)}) collective-permute-start(bf16[1,3,32,1536]{3,2,1,0:T(8,128)(2,1)} %pack.4.refs_0_), channel_id=1, source_target_pairs={{0,4},{1,5},{2,6},{3,7},{4,0},{5,1},{6,2},{7,3},{8,12},{9,13},{10,... | collective-permute-start | bytes 884744 | tf_op jit(solution)/shard_map/ppermute | solution.py:543
  52.7 23.2 %collective-permute-start.3 = (bf16[1,3,32,1536]{3,2,1,0:T(8,128)(2,1)}, bf16[1,3,32,1536]{3,2,1,0:T(8,128)(2,1)S(1)}, u32[]{:S(2)}, u32[]{:S(2)}) collective-permute-start(bf16[1,3,32,1536]{3,2,1,0:T(8,128)(2,1)} %pack.4.refs_0_), channel_id=1, source_target_pairs={{0,2},{1,3},{2,0},{3,1},{4,6},{5,7},{6,4},{7,5},{8,10},{9,11},{10,... | collective-permute-start | bytes 884744 | tf_op jit(solution)/shard_map/ppermute | solution.py:543
  95.4 59.0 %collective-permute-start.23 = (bf16[4,3,32,1536]{3,2,1,0:T(8,128)(2,1)}, bf16[4,3,32,1536]{3,2,1,0:T(8,128)(2,1)}, u32[]{:S(2)}, u32[]{:S(2)}) collective-permute-start(bf16[4,3,32,1536]{3,2,1,0:T(8,128)(2,1)} %combine.6.refs_1_.refs_5_.refs_11_), channel_id=1, source_target_pairs={{0,16},{8,24},{16,0},{24,8},{1,17},{9,25},{17,1},{25,9},{2,18},{10... | collective-permute-start | bytes 3538952 | tf_op jit(solution)/shard_map/ppermute | solution.py:543
  96.0 59.0 %collective-permute-start.22 = (bf16[4,3,32,1536]{3,2,1,0:T(8,128)(2,1)}, bf16[4,3,32,1536]{3,2,1,0:T(8,128)(2,1)}, u32[]{:S(2)}, u32[]{:S(2)}) collective-permute-start(bf16[4,3,32,1536]{3,2,1,0:T(8,128)(2,1)} %combine.6.refs_1_.refs_5_.refs_11_), channel_id=1, source_target_pairs={{0,1},{1,0},{2,3},{3,2},{4,5},{5,4},{6,7},{7,6},{8,9},{9,8},{10,11... | collective-permute-start | bytes 3538952 | tf_op jit(solution)/shard_map/ppermute | solution.py:543
  101.4 53.0 %collective-permute-start.15 = (bf16[2,3,32,1536]{3,2,1,0:T(8,128)(2,1)S(1)}, bf16[2,3,32,1536]{3,2,1,0:T(8,128)(2,1)S(1)}, u32[]{:S(2)}, u32[]{:S(2)}) collective-permute-start(bf16[2,3,32,1536]{3,2,1,0:T(8,128)(2,1)S(1)} %copy-done.39), channel_id=1, source_target_pairs={{0,16},{8,24},{16,0},{24,8},{1,17},{9,25},{17,1},{25,9},{2,18},{10... | collective-permute-start | bytes 1769480 | tf_op jit(solution)/shard_map/ppermute | solution.py:543
  105.0 41.3 %collective-permute-start.16 = (bf16[2,3,32,1536]{3,2,1,0:T(8,128)(2,1)}, bf16[2,3,32,1536]{3,2,1,0:T(8,128)(2,1)}, u32[]{:S(2)}, u32[]{:S(2)}) collective-permute-start(bf16[2,3,32,1536]{3,2,1,0:T(8,128)(2,1)} %get-tuple-element.110), channel_id=1, source_target_pairs={{0,1},{1,0},{2,3},{3,2},{4,5},{5,4},{6,7},{7,6},{8,9},{9,8},{10,11... | collective-permute-start | bytes 1769480 | tf_op jit(solution)/shard_map/ppermute | solution.py:543
  111.2 47.0 %collective-permute-start.17 = (bf16[4,3,32,1536]{3,2,1,0:T(8,128)(2,1)S(1)}, bf16[4,3,32,1536]{3,2,1,0:T(8,128)(2,1)}, u32[]{:S(2)}, u32[]{:S(2)}) collective-permute-start(bf16[4,3,32,1536]{3,2,1,0:T(8,128)(2,1)S(1)} %copy-done.27), channel_id=1, source_target_pairs={{0,8},{8,0},{16,24},{24,16},{1,9},{9,1},{17,25},{25,17},{2,10},{10... | collective-permute-start | bytes 3538952 | tf_op jit(solution)/shard_map/ppermute | solution.py:543
  146.3 12.4 %collective-permute-start.19 = (bf16[4,3,32,1536]{3,2,1,0:T(8,128)(2,1)}, bf16[4,3,32,1536]{3,2,1,0:T(8,128)(2,1)}, u32[]{:S(2)}, u32[]{:S(2)}) collective-permute-start(bf16[4,3,32,1536]{3,2,1,0:T(8,128)(2,1)} %copy-done.87), channel_id=1, source_target_pairs={{0,8},{8,0},{16,24},{24,16},{1,9},{9,1},{17,25},{25,17},{2,10},{10... | collective-permute-start | bytes 3538952 | tf_op jit(solution)/shard_map/ppermute | solution.py:543
  158.2 25.1 %collective-permute-start.26 = (bf16[4,3,32,1536]{3,2,1,0:T(8,128)(2,1)S(1)}, bf16[4,3,32,1536]{3,2,1,0:T(8,128)(2,1)}, u32[]{:S(2)}, u32[]{:S(2)}) collective-permute-start(bf16[4,3,32,1536]{3,2,1,0:T(8,128)(2,1)S(1)} %copy-done.29), channel_id=1, source_target_pairs={{0,8},{8,0},{16,24},{24,16},{1,9},{9,1},{17,25},{25,17},{2,10},{10... | collective-permute-start | bytes 3538952 | tf_op jit(solution)/shard_map/ppermute | solution.py:543
  158.7 23.0 %collective-permute-start.25 = (bf16[2,3,32,1536]{3,2,1,0:T(8,128)(2,1)}, bf16[2,3,32,1536]{3,2,1,0:T(8,128)(2,1)S(1)}, u32[]{:S(2)}, u32[]{:S(2)}) collective-permute-start(bf16[2,3,32,1536]{3,2,1,0:T(8,128)(2,1)} %get-tuple-element.113), channel_id=1, source_target_pairs={{0,1},{1,0},{2,3},{3,2},{4,5},{5,4},{6,7},{7,6},{8,9},{9,8},{10,11... | collective-permute-start | bytes 1769480 | tf_op jit(solution)/shard_map/ppermute | solution.py:543
  160.2 21.5 %collective-permute-start.24 = (bf16[2,3,32,1536]{3,2,1,0:T(8,128)(2,1)}, bf16[2,3,32,1536]{3,2,1,0:T(8,128)(2,1)S(1)}, u32[]{:S(2)}, u32[]{:S(2)}) collective-permute-start(bf16[2,3,32,1536]{3,2,1,0:T(8,128)(2,1)} %get-tuple-element.111.refs_15_), channel_id=1, source_target_pairs={{0,16},{8,24},{16,0},{24,8},{1,17},{9,25},{17,1},{25,9},{2,18},{10... | collective-permute-start | bytes 1769480 | tf_op jit(solution)/shard_map/ppermute | solution.py:543
  160.7 25.1 %collective-permute-start.28 = (bf16[4,3,32,1536]{3,2,1,0:T(8,128)(2,1)}, bf16[4,3,32,1536]{3,2,1,0:T(8,128)(2,1)}, u32[]{:S(2)}, u32[]{:S(2)}) collective-permute-start(bf16[4,3,32,1536]{3,2,1,0:T(8,128)(2,1)} %collective-permute-done.23.refs_1_.refs_7_.refs_13_), channel_id=1, source_target_pairs={{0,8},{8,0},{16,24},{24,16},{1,9},{9,1},{17,25},{25,17},{2,10},{10... | collective-permute-start | bytes 3538952 | tf_op jit(solution)/shard_map/ppermute | solution.py:543
  160.8 25.0 %collective-permute-start.27 = (bf16[4,3,32,1536]{3,2,1,0:T(8,128)(2,1)}, bf16[4,3,32,1536]{3,2,1,0:T(8,128)(2,1)}, u32[]{:S(2)}, u32[]{:S(2)}) collective-permute-start(bf16[4,3,32,1536]{3,2,1,0:T(8,128)(2,1)} %collective-permute-done.22.refs_0_.refs_6_.refs_12_), channel_id=1, source_target_pairs={{0,8},{8,0},{16,24},{24,16},{1,9},{9,1},{17,25},{25,17},{2,10},{10... | collective-permute-start | bytes 3538952 | tf_op jit(solution)/shard_map/ppermute | solution.py:543
  298.1 8.2 %collective-permute-start.38 = (bf16[16,3,32,1536]{3,2,1,0:T(8,128)(2,1)}, bf16[16,3,32,1536]{3,2,1,0:T(8,128)(2,1)S(1)}, u32[]{:S(2)}, u32[]{:S(2)}) collective-permute-start(bf16[16,3,32,1536]{3,2,1,0:T(8,128)(2,1)} %get-tuple-element.132), channel_id=1, source_target_pairs={{0,8},{8,0},{16,24},{24,16},{1,9},{9,1},{17,25},{25,17},{2,10},{10... | collective-permute-start | bytes 14155784 | tf_op jit(solution)/shard_map/ppermute | solution.py:543
  342.3 38.6 %collective-permute-start.48 = (bf16[16,3,32,1536]{3,2,1,0:T(8,128)(2,1)}, bf16[16,3,32,1536]{3,2,1,0:T(8,128)(2,1)}, u32[]{:S(2)}, u32[]{:S(2)}) collective-permute-start(bf16[16,3,32,1536]{3,2,1,0:T(8,128)(2,1)} %get-tuple-element.136.refs_3_), channel_id=1, source_target_pairs={{0,8},{8,0},{16,24},{24,16},{1,9},{9,1},{17,25},{25,17},{2,10},{10... | collective-permute-start | bytes 14155784 | tf_op jit(solution)/shard_map/ppermute | solution.py:543
  342.5 21.5 %collective-permute-start.44 = (bf16[2,3,32,1536]{3,2,1,0:T(8,128)(2,1)S(1)}, bf16[2,3,32,1536]{3,2,1,0:T(8,128)(2,1)S(1)}, u32[]{:S(2)}, u32[]{:S(2)}) collective-permute-start(bf16[2,3,32,1536]{3,2,1,0:T(8,128)(2,1)S(1)} %copy-done.23), channel_id=1, source_target_pairs={{0,1},{1,0},{2,3},{3,2},{4,5},{5,4},{6,7},{7,6},{8,9},{9,8},{10,11... | collective-permute-start | bytes 1769480 | tf_op jit(solution)/shard_map/ppermute | solution.py:543
  343.3 20.8 %collective-permute-start.43 = (bf16[2,3,32,1536]{3,2,1,0:T(8,128)(2,1)S(1)}, bf16[2,3,32,1536]{3,2,1,0:T(8,128)(2,1)}, u32[]{:S(2)}, u32[]{:S(2)}) collective-permute-start(bf16[2,3,32,1536]{3,2,1,0:T(8,128)(2,1)S(1)} %copy-done.22), channel_id=1, source_target_pairs={{0,16},{8,24},{16,0},{24,8},{1,17},{9,25},{17,1},{25,9},{2,18},{10... | collective-permute-start | bytes 1769480 | tf_op jit(solution)/shard_map/ppermute | solution.py:543
  352.1 7.6 %collective-permute-start.42 = (f32[8,512]{1,0:T(8,128)S(1)}, f32[8,512]{1,0:T(8,128)S(1)}, u32[]{:S(2)}, u32[]{:S(2)}) collective-permute-start(f32[8,512]{1,0:T(8,128)S(1)} %add.853), channel_id=1, source_target_pairs={{0,17},{1,16},{2,19},{3,18},{4,21},{5,20},{6,23},{7,22},{8,25},{9,... | collective-permute-start | bytes 49160 | tf_op jit(solution)/shard_map/ppermute | solution.py:564
  379.4 42.9 %collective-permute-start.49 = (bf16[4,3,32,1536]{3,2,1,0:T(8,128)(2,1)}, bf16[4,3,32,1536]{3,2,1,0:T(8,128)(2,1)S(1)}, u32[]{:S(2)}, u32[]{:S(2)}) collective-permute-start(bf16[4,3,32,1536]{3,2,1,0:T(8,128)(2,1)} %get-tuple-element.141.refs_0_), channel_id=1, source_target_pairs={{0,1},{1,0},{2,3},{3,2},{4,5},{5,4},{6,7},{7,6},{8,9},{9,8},{10,11... | collective-permute-start | bytes 3538952 | tf_op jit(solution)/shard_map/ppermute | solution.py:543
  379.8 42.5 %collective-permute-start.50 = (bf16[4,3,32,1536]{3,2,1,0:T(8,128)(2,1)}, bf16[4,3,32,1536]{3,2,1,0:T(8,128)(2,1)S(1)}, u32[]{:S(2)}, u32[]{:S(2)}) collective-permute-start(bf16[4,3,32,1536]{3,2,1,0:T(8,128)(2,1)} %get-tuple-element.142.refs_1_), channel_id=1, source_target_pairs={{0,16},{8,24},{16,0},{24,8},{1,17},{9,25},{17,1},{25,9},{2,18},{10... | collective-permute-start | bytes 3538952 | tf_op jit(solution)/shard_map/ppermute | solution.py:543
  383.6 38.7 %collective-permute-start.51 = (bf16[2,3,32,1536]{3,2,1,0:T(8,128)(2,1)}, bf16[2,3,32,1536]{3,2,1,0:T(8,128)(2,1)S(1)}, u32[]{:S(2)}, u32[]{:S(2)}) collective-permute-start(bf16[2,3,32,1536]{3,2,1,0:T(8,128)(2,1)} %get-tuple-element.145.refs_2_), channel_id=1, source_target_pairs={{0,16},{8,24},{16,0},{24,8},{1,17},{9,25},{17,1},{25,9},{2,18},{10... | collective-permute-start | bytes 1769480 | tf_op jit(solution)/shard_map/ppermute | solution.py:543
  384.4 37.9 %collective-permute-start.52 = (bf16[2,3,32,1536]{3,2,1,0:T(8,128)(2,1)}, bf16[2,3,32,1536]{3,2,1,0:T(8,128)(2,1)S(1)}, u32[]{:S(2)}, u32[]{:S(2)}) collective-permute-start(bf16[2,3,32,1536]{3,2,1,0:T(8,128)(2,1)} %get-tuple-element.146.refs_3_), channel_id=1, source_target_pairs={{0,1},{1,0},{2,3},{3,2},{4,5},{5,4},{6,7},{7,6},{8,9},{9,8},{10,11... | collective-permute-start | bytes 1769480 | tf_op jit(solution)/shard_map/ppermute | solution.py:543
  424.1 11.9 %collective-permute-start.53 = (bf16[16,3,32,1536]{3,2,1,0:T(8,128)(2,1)}, bf16[16,3,32,1536]{3,2,1,0:T(8,128)(2,1)}, u32[]{:S(2)}, u32[]{:S(2)}) collective-permute-start(bf16[16,3,32,1536]{3,2,1,0:T(8,128)(2,1)} %tie.33.refs_1_), channel_id=1, source_target_pairs={{0,8},{8,0},{16,24},{24,16},{1,9},{9,1},{17,25},{25,17},{2,10},{10... | collective-permute-start | bytes 14155784 | tf_op jit(solution)/shard_map/ppermute | solution.py:543
  433.8 38.4 %collective-permute-start.54 = (bf16[2,3,32,1536]{3,2,1,0:T(8,128)(2,1)S(1)}, bf16[2,3,32,1536]{3,2,1,0:T(8,128)(2,1)}, u32[]{:S(2)}, u32[]{:S(2)}) collective-permute-start(bf16[2,3,32,1536]{3,2,1,0:T(8,128)(2,1)S(1)} %copy-done), channel_id=1, source_target_pairs={{0,2},{1,3},{2,0},{3,1},{4,6},{5,7},{6,4},{7,5},{8,10},{9,11},{10,... | collective-permute-start | bytes 1769480 | tf_op jit(solution)/shard_map/ppermute | solution.py:543
  434.5 37.7 %collective-permute-start.57 = (bf16[4,3,32,1536]{3,2,1,0:T(8,128)(2,1)}, bf16[4,3,32,1536]{3,2,1,0:T(8,128)(2,1)S(1)}, u32[]{:S(2)}, u32[]{:S(2)}) collective-permute-start(bf16[4,3,32,1536]{3,2,1,0:T(8,128)(2,1)} %get-tuple-element.170.refs_2_), channel_id=1, source_target_pairs={{0,1},{1,0},{2,3},{3,2},{4,5},{5,4},{6,7},{7,6},{8,9},{9,8},{10,11... | collective-permute-start | bytes 3538952 | tf_op jit(solution)/shard_map/ppermute | solution.py:543
  435.3 37.0 %collective-permute-start.58 = (bf16[4,3,32,1536]{3,2,1,0:T(8,128)(2,1)}, bf16[4,3,32,1536]{3,2,1,0:T(8,128)(2,1)S(1)}, u32[]{:S(2)}, u32[]{:S(2)}) collective-permute-start(bf16[4,3,32,1536]{3,2,1,0:T(8,128)(2,1)} %get-tuple-element.171.refs_3_), channel_id=1, source_target_pairs={{0,16},{8,24},{16,0},{24,8},{1,17},{9,25},{17,1},{25,9},{2,18},{10... | collective-permute-start | bytes 3538952 | tf_op jit(solution)/shard_map/ppermute | solution.py:543
  438.7 37.2 %collective-permute-start.55 = (bf16[2,3,32,1536]{3,2,1,0:T(8,128)(2,1)}, bf16[2,3,32,1536]{3,2,1,0:T(8,128)(2,1)S(1)}, u32[]{:S(2)}, u32[]{:S(2)}) collective-permute-start(bf16[2,3,32,1536]{3,2,1,0:T(8,128)(2,1)} %get-tuple-element.172.refs_21_), channel_id=1, source_target_pairs={{0,16},{8,24},{16,0},{24,8},{1,17},{9,25},{17,1},{25,9},{2,18},{10... | collective-permute-start | bytes 1769480 | tf_op jit(solution)/shard_map/ppermute | solution.py:543
  440.1 35.8 %collective-permute-start.56 = (bf16[2,3,32,1536]{3,2,1,0:T(8,128)(2,1)}, bf16[2,3,32,1536]{3,2,1,0:T(8,128)(2,1)}, u32[]{:S(2)}, u32[]{:S(2)}) collective-permute-start(bf16[2,3,32,1536]{3,2,1,0:T(8,128)(2,1)} %get-tuple-element.173.refs_22_), channel_id=1, source_target_pairs={{0,1},{1,0},{2,3},{3,2},{4,5},{5,4},{6,7},{7,6},{8,9},{9,8},{10,11... | collective-permute-start | bytes 1769480 | tf_op jit(solution)/shard_map/ppermute | solution.py:543
  476.8 22.1 %collective-permute-start.59 = (bf16[16,3,32,1536]{3,2,1,0:T(8,128)(2,1)}, bf16[16,3,32,1536]{3,2,1,0:T(8,128)(2,1)}, u32[]{:S(2)}, u32[]{:S(2)}) collective-permute-start(bf16[16,3,32,1536]{3,2,1,0:T(8,128)(2,1)} %tie.37.refs_2_), channel_id=1, source_target_pairs={{0,8},{8,0},{16,24},{24,16},{1,9},{9,1},{17,25},{25,17},{2,10},{10... | collective-permute-start | bytes 14155784 | tf_op jit(solution)/shard_map/ppermute | solution.py:543
  489.2 50.3 %collective-permute-start.61 = (bf16[4,3,32,1536]{3,2,1,0:T(8,128)(2,1)}, bf16[4,3,32,1536]{3,2,1,0:T(8,128)(2,1)}, u32[]{:S(2)}, u32[]{:S(2)}) collective-permute-start(bf16[4,3,32,1536]{3,2,1,0:T(8,128)(2,1)} %get-tuple-element.179.refs_1_), channel_id=1, source_target_pairs={{0,1},{1,0},{2,3},{3,2},{4,5},{5,4},{6,7},{7,6},{8,9},{9,8},{10,11... | collective-permute-start | bytes 3538952 | tf_op jit(solution)/shard_map/ppermute | solution.py:543
  490.5 49.0 %collective-permute-start.62 = (bf16[4,3,32,1536]{3,2,1,0:T(8,128)(2,1)}, bf16[4,3,32,1536]{3,2,1,0:T(8,128)(2,1)}, u32[]{:S(2)}, u32[]{:S(2)}) collective-permute-start(bf16[4,3,32,1536]{3,2,1,0:T(8,128)(2,1)} %get-tuple-element.180.refs_2_), channel_id=1, source_target_pairs={{0,16},{8,24},{16,0},{24,8},{1,17},{9,25},{17,1},{25,9},{2,18},{10... | collective-permute-start | bytes 3538952 | tf_op jit(solution)/shard_map/ppermute | solution.py:543
  491.5 15.9 %collective-permute-start.66 = (bf16[1,3,32,1536]{3,2,1,0:T(8,128)(2,1)}, bf16[1,3,32,1536]{3,2,1,0:T(8,128)(2,1)}, u32[]{:S(2)}, u32[]{:S(2)}) collective-permute-start(bf16[1,3,32,1536]{3,2,1,0:T(8,128)(2,1)} %tie.39.refs_3_), channel_id=1, source_target_pairs={{0,4},{1,5},{2,6},{3,7},{4,0},{5,1},{6,2},{7,3},{8,12},{9,13},{10,... | collective-permute-start | bytes 884744 | tf_op jit(solution)/shard_map/ppermute | solution.py:543
  501.4 29.6 %collective-permute-start.63 = (bf16[2,3,32,1536]{3,2,1,0:T(8,128)(2,1)}, bf16[2,3,32,1536]{3,2,1,0:T(8,128)(2,1)}, u32[]{:S(2)}, u32[]{:S(2)}) collective-permute-start(bf16[2,3,32,1536]{3,2,1,0:T(8,128)(2,1)} %get-tuple-element.190.refs_1_), channel_id=1, source_target_pairs={{0,16},{8,24},{16,0},{24,8},{1,17},{9,25},{17,1},{25,9},{2,18},{10... | collective-permute-start | bytes 1769480 | tf_op jit(solution)/shard_map/ppermute | solution.py:543
  502.4 28.6 %collective-permute-start.64 = (bf16[2,3,32,1536]{3,2,1,0:T(8,128)(2,1)}, bf16[2,3,32,1536]{3,2,1,0:T(8,128)(2,1)}, u32[]{:S(2)}, u32[]{:S(2)}) collective-permute-start(bf16[2,3,32,1536]{3,2,1,0:T(8,128)(2,1)} %get-tuple-element.191.refs_2_), channel_id=1, source_target_pairs={{0,1},{1,0},{2,3},{3,2},{4,5},{5,4},{6,7},{7,6},{8,9},{9,8},{10,11... | collective-permute-start | bytes 1769480 | tf_op jit(solution)/shard_map/ppermute | solution.py:543
  536.6 14.2 %collective-permute-start.69 = (bf16[2,3,32,1536]{3,2,1,0:T(8,128)(2,1)S(1)}, bf16[2,3,32,1536]{3,2,1,0:T(8,128)(2,1)}, u32[]{:S(2)}, u32[]{:S(2)}) collective-permute-start(bf16[2,3,32,1536]{3,2,1,0:T(8,128)(2,1)S(1)} %copy-done.2), channel_id=1, source_target_pairs={{0,2},{1,3},{2,0},{3,1},{4,6},{5,7},{6,4},{7,5},{8,10},{9,11},{10,... | collective-permute-start | bytes 1769480 | tf_op jit(solution)/shard_map/ppermute | solution.py:543
  537.9 26.7 %collective-permute-start.67 = (bf16[4,3,32,1536]{3,2,1,0:T(8,128)(2,1)}, bf16[4,3,32,1536]{3,2,1,0:T(8,128)(2,1)}, u32[]{:S(2)}, u32[]{:S(2)}) collective-permute-start(bf16[4,3,32,1536]{3,2,1,0:T(8,128)(2,1)} %get-tuple-element.195.refs_1_), channel_id=1, source_target_pairs={{0,1},{1,0},{2,3},{3,2},{4,5},{5,4},{6,7},{7,6},{8,9},{9,8},{10,11... | collective-permute-start | bytes 3538952 | tf_op jit(solution)/shard_map/ppermute | solution.py:543
  538.3 26.7 %collective-permute-start.68 = (bf16[4,3,32,1536]{3,2,1,0:T(8,128)(2,1)}, bf16[4,3,32,1536]{3,2,1,0:T(8,128)(2,1)}, u32[]{:S(2)}, u32[]{:S(2)}) collective-permute-start(bf16[4,3,32,1536]{3,2,1,0:T(8,128)(2,1)} %get-tuple-element.196.refs_2_), channel_id=1, source_target_pairs={{0,16},{8,24},{16,0},{24,8},{1,17},{9,25},{17,1},{25,9},{2,18},{10... | collective-permute-start | bytes 3538952 | tf_op jit(solution)/shard_map/ppermute | solution.py:543
  552.8 18.3 %collective-permute-start.65 = (bf16[2,3,32,1536]{3,2,1,0:T(8,128)(2,1)S(1)}, bf16[2,3,32,1536]{3,2,1,0:T(8,128)(2,1)}, u32[]{:S(2)}, u32[]{:S(2)}) collective-permute-start(bf16[2,3,32,1536]{3,2,1,0:T(8,128)(2,1)S(1)} %copy-done.1), channel_id=1, source_target_pairs={{0,2},{1,3},{2,0},{3,1},{4,6},{5,7},{6,4},{7,5},{8,10},{9,11},{10,... | collective-permute-start | bytes 1769480 | tf_op jit(solution)/shard_map/ppermute | solution.py:543
  567.8 13.9 %collective-permute-start.77 = (bf16[1,3,32,1536]{3,2,1,0:T(8,128)(2,1)S(1)}, bf16[1,3,32,1536]{3,2,1,0:T(8,128)(2,1)}, u32[]{:S(2)}, u32[]{:S(2)}) collective-permute-start(bf16[1,3,32,1536]{3,2,1,0:T(8,128)(2,1)S(1)} %copy-done.15), channel_id=1, source_target_pairs={{0,4},{1,5},{2,6},{3,7},{4,0},{5,1},{6,2},{7,3},{8,12},{9,13},{10,... | collective-permute-start | bytes 884744 | tf_op jit(solution)/shard_map/ppermute | solution.py:543
  569.3 23.0 %collective-permute-start.76 = (bf16[2,3,32,1536]{3,2,1,0:T(8,128)(2,1)}, bf16[2,3,32,1536]{3,2,1,0:T(8,128)(2,1)}, u32[]{:S(2)}, u32[]{:S(2)}) collective-permute-start(bf16[2,3,32,1536]{3,2,1,0:T(8,128)(2,1)} %tie.46.refs_1_), channel_id=1, source_target_pairs={{0,2},{1,3},{2,0},{3,1},{4,6},{5,7},{6,4},{7,5},{8,10},{9,11},{10,... | collective-permute-start | bytes 1769480 | tf_op jit(solution)/shard_map/ppermute | solution.py:543
  570.2 7.0 %collective-permute-start.71 = (bf16[1,3,32,1536]{3,2,1,0:T(8,128)(2,1)}, bf16[1,3,32,1536]{3,2,1,0:T(8,128)(2,1)}, u32[]{:S(2)}, u32[]{:S(2)}) collective-permute-start(bf16[1,3,32,1536]{3,2,1,0:T(8,128)(2,1)} %tie.47.refs_1_.refs_0_), channel_id=1, source_target_pairs={{0,16},{8,24},{16,0},{24,8},{1,17},{9,25},{17,1},{25,9},{2,18},{10... | collective-permute-start | bytes 884744 | tf_op jit(solution)/shard_map/ppermute | solution.py:543
  573.4 10.5 %collective-permute-start.70 = (bf16[1,3,32,1536]{3,2,1,0:T(8,128)(2,1)S(1)}, bf16[1,3,32,1536]{3,2,1,0:T(8,128)(2,1)S(1)}, u32[]{:S(2)}, u32[]{:S(2)}) collective-permute-start(bf16[1,3,32,1536]{3,2,1,0:T(8,128)(2,1)S(1)} %copy-done.12), channel_id=1, source_target_pairs={{0,8},{8,0},{16,24},{24,16},{1,9},{9,1},{17,25},{25,17},{2,10},{10... | collective-permute-start | bytes 884744 | tf_op jit(solution)/shard_map/ppermute | solution.py:543
  588.8 7.1 %collective-permute-start.75 = (f32[56,512]{1,0:T(8,128)}, f32[56,512]{1,0:T(8,128)S(1)}, u32[]{:S(2)}, u32[]{:S(2)}) collective-permute-start(f32[56,512]{1,0:T(8,128)} %tie.49.refs_1_), channel_id=1, source_target_pairs={{0,17},{1,16},{2,19},{3,18},{4,21},{5,20},{6,23},{7,22},{8,25},{9,... | collective-permute-start | bytes 344072 | tf_op jit(solution)/shard_map/ppermute | solution.py:564
  594.4 18.4 %collective-permute-start.82 = (bf16[1,3,32,1536]{3,2,1,0:T(8,128)(2,1)S(1)}, bf16[1,3,32,1536]{3,2,1,0:T(8,128)(2,1)S(1)}, u32[]{:S(2)}, u32[]{:S(2)}) collective-permute-start(bf16[1,3,32,1536]{3,2,1,0:T(8,128)(2,1)S(1)} %copy-done.13), channel_id=1, source_target_pairs={{0,4},{1,5},{2,6},{3,7},{4,0},{5,1},{6,2},{7,3},{8,12},{9,13},{10,... | collective-permute-start | bytes 884744 | tf_op jit(solution)/shard_map/ppermute | solution.py:543
  597.8 18.7 %collective-permute-start.80 = (f32[56,512]{1,0:T(8,128)}, f32[56,512]{1,0:T(8,128)S(1)}, u32[]{:S(2)}, u32[]{:S(2)}) collective-permute-start(f32[56,512]{1,0:T(8,128)} %tie.52.refs_1_), channel_id=1, source_target_pairs={{0,6},{1,7},{2,4},{3,5},{4,2},{5,3},{6,0},{7,1},{8,14},{9,15},{10,... | collective-permute-start | bytes 344072 | tf_op jit(solution)/shard_map/ppermute | solution.py:543
  599.0 18.6 %collective-permute-start.79 = (f32[56,512]{1,0:T(8,128)}, f32[56,512]{1,0:T(8,128)S(1)}, u32[]{:S(2)}, u32[]{:S(2)}) collective-permute-start(f32[56,512]{1,0:T(8,128)} %tie.52.refs_1_), channel_id=1, source_target_pairs={{0,4},{1,5},{2,6},{3,7},{4,0},{5,1},{6,2},{7,3},{8,12},{9,13},{10,... | collective-permute-start | bytes 344072 | tf_op jit(solution)/shard_map/ppermute | solution.py:543
  599.0 20.0 %collective-permute-start.78 = (f32[56,512]{1,0:T(8,128)}, f32[56,512]{1,0:T(8,128)}, u32[]{:S(2)}, u32[]{:S(2)}) collective-permute-start(f32[56,512]{1,0:T(8,128)} %tie.52.refs_1_), channel_id=1, source_target_pairs={{0,2},{1,3},{2,0},{3,1},{4,6},{5,7},{6,4},{7,5},{8,10},{9,11},{10,... | collective-permute-start | bytes 344072 | tf_op jit(solution)/shard_map/ppermute | solution.py:543
  615.0 15.8 %collective-permute-start.81 = (bf16[1,3,32,1536]{3,2,1,0:T(8,128)(2,1)S(1)}, bf16[1,3,32,1536]{3,2,1,0:T(8,128)(2,1)}, u32[]{:S(2)}, u32[]{:S(2)}) collective-permute-start(bf16[1,3,32,1536]{3,2,1,0:T(8,128)(2,1)S(1)} %copy-done.14), channel_id=1, source_target_pairs={{0,4},{1,5},{2,6},{3,7},{4,0},{5,1},{6,2},{7,3},{8,12},{9,13},{10,... | collective-permute-start | bytes 884744 | tf_op jit(solution)/shard_map/ppermute | solution.py:543
  615.0 10.8 %collective-permute-start.84 = (bf16[1,3,32,1536]{3,2,1,0:T(8,128)(2,1)S(1)}, bf16[1,3,32,1536]{3,2,1,0:T(8,128)(2,1)S(1)}, u32[]{:S(2)}, u32[]{:S(2)}) collective-permute-start(bf16[1,3,32,1536]{3,2,1,0:T(8,128)(2,1)S(1)} %copy-done.10), channel_id=1, source_target_pairs={{0,16},{8,24},{16,0},{24,8},{1,17},{9,25},{17,1},{25,9},{2,18},{10... | collective-permute-start | bytes 884744 | tf_op jit(solution)/shard_map/ppermute | solution.py:543
  616.6 16.5 %collective-permute-start.83 = (bf16[1,3,32,1536]{3,2,1,0:T(8,128)(2,1)S(1)}, bf16[1,3,32,1536]{3,2,1,0:T(8,128)(2,1)S(1)}, u32[]{:S(2)}, u32[]{:S(2)}) collective-permute-start(bf16[1,3,32,1536]{3,2,1,0:T(8,128)(2,1)S(1)} %copy-done.10), channel_id=1, source_target_pairs={{0,8},{8,0},{16,24},{24,16},{1,9},{9,1},{17,25},{25,17},{2,10},{10... | collective-permute-start | bytes 884744 | tf_op jit(solution)/shard_map/ppermute | solution.py:543
  617.6 21.7 %collective-permute-start.90 = (bf16[1,3,32,1536]{3,2,1,0:T(8,128)(2,1)}, bf16[1,3,32,1536]{3,2,1,0:T(8,128)(2,1)S(1)}, u32[]{:S(2)}, u32[]{:S(2)}) collective-permute-start(bf16[1,3,32,1536]{3,2,1,0:T(8,128)(2,1)} %tie.53.refs_1_.refs_0_), channel_id=1, source_target_pairs={{0,16},{8,24},{16,0},{24,8},{1,17},{9,25},{17,1},{25,9},{2,18},{10... | collective-permute-start | bytes 884744 | tf_op jit(solution)/shard_map/ppermute | solution.py:543
  619.0 30.8 %collective-permute-start.89 = (bf16[1,3,32,1536]{3,2,1,0:T(8,128)(2,1)}, bf16[1,3,32,1536]{3,2,1,0:T(8,128)(2,1)S(1)}, u32[]{:S(2)}, u32[]{:S(2)}) collective-permute-start(bf16[1,3,32,1536]{3,2,1,0:T(8,128)(2,1)} %tie.53.refs_1_.refs_0_), channel_id=1, source_target_pairs={{0,8},{8,0},{16,24},{24,16},{1,9},{9,1},{17,25},{25,17},{2,10},{10... | collective-permute-start | bytes 884744 | tf_op jit(solution)/shard_map/ppermute | solution.py:543
  625.9 7.2 %collective-permute-start.85 = (bf16[1,3,32,1536]{3,2,1,0:T(8,128)(2,1)S(1)}, bf16[1,3,32,1536]{3,2,1,0:T(8,128)(2,1)}, u32[]{:S(2)}, u32[]{:S(2)}) collective-permute-start(bf16[1,3,32,1536]{3,2,1,0:T(8,128)(2,1)S(1)} %collective-permute-done.84.refs_2_), channel_id=1, source_target_pairs={{0,8},{8,0},{16,24},{24,16},{1,9},{9,1},{17,25},{25,17},{2,10},{10... | collective-permute-start | bytes 884744 | tf_op jit(solution)/shard_map/ppermute | solution.py:543
  637.3 9.2 %collective-permute-start.87 = (bf16[1,3,32,1536]{3,2,1,0:T(8,128)(2,1)}, bf16[1,3,32,1536]{3,2,1,0:T(8,128)(2,1)S(1)}, u32[]{:S(2)}, u32[]{:S(2)}) collective-permute-start(bf16[1,3,32,1536]{3,2,1,0:T(8,128)(2,1)} %tie.54.refs_0_), channel_id=1, source_target_pairs={{0,16},{8,24},{16,0},{24,8},{1,17},{9,25},{17,1},{25,9},{2,18},{10... | collective-permute-start | bytes 884744 | tf_op jit(solution)/shard_map/ppermute | solution.py:543
  639.3 10.5 %collective-permute-start.91 = (bf16[1,3,32,1536]{3,2,1,0:T(8,128)(2,1)S(1)}, bf16[1,3,32,1536]{3,2,1,0:T(8,128)(2,1)S(1)}, u32[]{:S(2)}, u32[]{:S(2)}) collective-permute-start(bf16[1,3,32,1536]{3,2,1,0:T(8,128)(2,1)S(1)} %collective-permute-done.90.refs_2_), channel_id=1, source_target_pairs={{0,8},{8,0},{16,24},{24,16},{1,9},{9,1},{17,25},{25,17},{2,10},{10... | collective-permute-start | bytes 884744 | tf_op jit(solution)/shard_map/ppermute | solution.py:543
  639.4 15.3 %collective-permute-start.86 = (bf16[1,3,32,1536]{3,2,1,0:T(8,128)(2,1)}, bf16[1,3,32,1536]{3,2,1,0:T(8,128)(2,1)S(1)}, u32[]{:S(2)}, u32[]{:S(2)}) collective-permute-start(bf16[1,3,32,1536]{3,2,1,0:T(8,128)(2,1)} %tie.54.refs_0_), channel_id=1, source_target_pairs={{0,8},{8,0},{16,24},{24,16},{1,9},{9,1},{17,25},{25,17},{2,10},{10... | collective-permute-start | bytes 884744 | tf_op jit(solution)/shard_map/ppermute | solution.py:543
  647.2 7.5 %collective-permute-start.88 = (bf16[1,3,32,1536]{3,2,1,0:T(8,128)(2,1)}, bf16[1,3,32,1536]{3,2,1,0:T(8,128)(2,1)S(1)}, u32[]{:S(2)}, u32[]{:S(2)}) collective-permute-start(bf16[1,3,32,1536]{3,2,1,0:T(8,128)(2,1)} %tie.55.refs_2_), channel_id=1, source_target_pairs={{0,8},{8,0},{16,24},{24,16},{1,9},{9,1},{17,25},{25,17},{2,10},{10... | collective-permute-start | bytes 884744 | tf_op jit(solution)/shard_map/ppermute | solution.py:543
  (128 other events, 803.0 us)
Sparse Core Ops, SparseCore 0:
  85.4 148.7 all-gather.1

commit v5 on v4

--- a/solution.py
+++ b/solution.py
@@ -873,9 +873,10 @@
     grads = place_grads(pieces_table, sums_2.result, 6, shard_rows, grads)
     both_0 = both_0.result
     carried = carry_grads(current, micro, valid, stats, gains[0], total, both_0[: 2 * MB], carried)
-    moves.before_core = [carried]
-    tokens = sums_0.send([*tokens, *grads])
+    after = [*tokens, *grads]
     grads = place_grads(pieces_table, sums_1.result, 3, shard_rows, grads)
+    moves.before_core = [carried, *grads]
+    sums_0.send(after)
     grads = place_grads(pieces_table, sums_0.result, 0, shard_rows, grads)
     pooled = jnp.stack([both_0[: 2 * MB], both_1])
     stacked = both_0[2 * MB :].reshape(LAYERS, SECTIONS, 4 * columns)

time: 676 us -> 673 us (level)
  no operation moved by 1% of the time
where the time goes in v5:
time: 673 us; the launch traced here: 663 us
  Pallas kernels  269 us (40%)
  waiting for transfers between devices  194 us (29%)
  starting transfers between devices  78.2 us (12%)
  other arithmetic  75.5 us (11%)
  local copies, waits for them, and re-layouts  31.1 us (5%)
  between operations  15.5 us (2%)
    ppermute x88, waiting for transfers between devices, permute(): self.arrived.append(lax.ppermute(v, axis, along(axis, size, flip)))  186 us
    pallas_call x4, Pallas kernels, backward_chunk(): pl.pallas_call(functools.partial(backward_kernel, n, first, len(arrays),...  124 us
    ppermute x88, starting transfers between devices, permute(): self.arrived.append(lax.ppermute(v, axis, along(axis, size, flip)))  71.5 us
    pallas_call x3, Pallas kernels, forward_chunk(): pl.pallas_call(functools.partial(forward_kernel, n, first, len(arrays), l...  71 us
    convert_element_type x20, other arithmetic, low_sum(): return sum((v.astype(F32) for v in terms)).astype(BF16)  47.1 us
    unnamed x203, local copies, waits for them, and re-layouts  23.2 us
    pallas_call x4, Pallas kernels, place_grads(): pl.pallas_call(functools.partial(place_kernel, n_pieces), grid_spec=pltpu...  13.8 us
  transfers between devices with their start and end apart: 93, of which 41 were waited for; matrix products, arithmetic and copies ran while one was open for 12% of the time, Pallas kernels for 24%

profile of v5, /device:TPU:0, one launch (start us, length us, event | category | flops | bytes accessed | tf_op | source)
XLA Modules:
  0.0 663.2 jit_solution(8972448123453542577)
XLA Ops:
  7.2 2.5 pack.3.refs_0_
  9.7 5.0 collective-permute-start.2
  17.2 3.8 local_stats.2.refs_4_.refs_0_
  22.9 17.1 %collective-permute-done.1.refs_2_ = bf16[1,3,32,1536]{3,2,1,0:T(8,128)(2,1)S(1)} collective-permute-done((bf16[1,3,32,1536]{3,2,1,0:T(8,128)(2,1)}, bf16[1,3,32,1536]{3,2,1,0:T(8,128)(2,1)S(1)}, u32[]{:S(2)}, u32[]{:S(2)}) %collective-permute-start.1) | collective-permute-done | bytes 294944 | tf_op jit(solution)/shard_map/ppermute | solution.py:543
  41.5 3.2 combine.4.refs_0_.refs_5_.refs_11_
  47.7 2.4 pack.4.refs_0_
  50.2 2.5 collective-permute-start.5
  54.6 7.7 %collective-permute-done.5.refs_4_.refs_3_ = bf16[1,3,32,1536]{3,2,1,0:T(8,128)(2,1)S(1)} collective-permute-done((bf16[1,3,32,1536]{3,2,1,0:T(8,128)(2,1)}, bf16[1,3,32,1536]{3,2,1,0:T(8,128)(2,1)S(1)}, u32[]{:S(2)}, u32[]{:S(2)}) %collective-permute-start.5) | collective-permute-done | bytes 294944 | tf_op jit(solution)/shard_map/ppermute | solution.py:543
  62.2 13.6 %collective-permute-done.4.refs_3_.refs_2_ = bf16[1,3,32,1536]{3,2,1,0:T(8,128)(2,1)S(1)} collective-permute-done((bf16[1,3,32,1536]{3,2,1,0:T(8,128)(2,1)}, bf16[1,3,32,1536]{3,2,1,0:T(8,128)(2,1)S(1)}, u32[]{:S(2)}, u32[]{:S(2)}) %collective-permute-start.4) | collective-permute-done | bytes 294944 | tf_op jit(solution)/shard_map/ppermute | solution.py:543
  78.1 3.2 combine.5
  81.3 3.9 pack.5
  85.3 3.2 combine.6.refs_1_.refs_5_.refs_11_
  111.8 3.6 norm_rows.2
  115.4 30.9 %collective-permute-done.16.refs_9_.refs_15_ = bf16[2,3,32,1536]{3,2,1,0:T(8,128)(2,1)} collective-permute-done((bf16[2,3,32,1536]{3,2,1,0:T(8,128)(2,1)}, bf16[2,3,32,1536]{3,2,1,0:T(8,128)(2,1)}, u32[]{:S(2)}, u32[]{:S(2)}) %collective-permute-start.16) | collective-permute-done | bytes 589856 | tf_op jit(solution)/shard_map/ppermute | solution.py:543
  146.3 8.1 %collective-permute-done.15.refs_8_.refs_14_ = bf16[2,3,32,1536]{3,2,1,0:T(8,128)(2,1)S(1)} collective-permute-done((bf16[2,3,32,1536]{3,2,1,0:T(8,128)(2,1)S(1)}, bf16[2,3,32,1536]{3,2,1,0:T(8,128)(2,1)S(1)}, u32[]{:S(2)}, u32[]{:S(2)}) %collective-permute-start.15) | collective-permute-done | bytes 589856 | tf_op jit(solution)/shard_map/ppermute | solution.py:543
  155.0 3.2 combine.7
  161.5 20.1 %forward_sections.3 = (f32[768,512]{1,0:T(8,128)}, f32[3,768,512]{2,1,0:T(8,128)}, f32[3,768,512]{2,1,0:T(8,128)}, f32[3,768,512]{2,1,0:T(8,128)}, f32[3,768,512...) custom-call(s32[32]{0:T(128)} %stack.114.table, ...), custom_call_target="tpu_custom_call" | custom-call | flops 20000000000 | bytes 1 | tf_op jit(solution)/shard_map/forward_sections/pallas_call | solution.py:116
  186.6 19.3 %forward_sections.4 = (f32[768,512]{1,0:T(8,128)}, f32[3,768,512]{2,1,0:T(8,128)}, f32[3,768,512]{2,1,0:T(8,128)}, f32[3,768,512]{2,1,0:T(8,128)}, f32[3,768,512...) custom-call(s32[32]{0:T(128)} %stack.114.table, ...), custom_call_target="tpu_custom_call" | custom-call | flops 20000000000 | bytes 1 | tf_op jit(solution)/shard_map/forward_sections/pallas_call | solution.py:116
  205.9 4.4 local_stats.3
  213.4 2.5 collective-permute-start.34
  221.0 2.8 collective-permute-start.37
  227.6 3.1 collective-permute-done.36
  231.3 4.0 norm_rows.3
  235.4 31.6 %forward_sections.5 = (bf16[768,512]{1,0:T(8,128)(2,1)}, f32[6,768,512]{2,1,0:T(8,128)}, f32[6,768,512]{2,1,0:T(8,128)}, f32[6,768,512]{2,1,0:T(8,128)}, f32[6,7...) custom-call(s32[32]{0:T(128)} %constant.45.clone.table, ...), custom_call_target="tpu_custom_call" | custom-call | flops 20000000000 | bytes 1 | tf_op jit(solution)/shard_map/forward_sections/pallas_call | solution.py:116
  267.0 31.1 %backward_sections.4 = (f32[768,512]{1,0:T(8,128)}, f32[768,512]{1,0:T(8,128)}, f32[3,1,2048]{2,1,0:T(1,128)}, bf16[4,3,32,1536]{3,2,1,0:T(8,128)(2,1)}, bf16[4,...) custom-call(s32[64]{0:T(128)} %concatenate.77.table, ...), custom_call_target="tpu_custom_call" | custom-call | flops 20000000000 | bytes 1 | tf_op jit(solution)/shard_map/backward_sections/pallas_call | solution.py:249
  298.1 8.1 %collective-permute-done.38 = bf16[16,3,32,1536]{3,2,1,0:T(8,128)(2,1)S(1)} collective-permute-done((bf16[16,3,32,1536]{3,2,1,0:T(8,128)(2,1)}, bf16[16,3,32,1536]{3,2,1,0:T(8,128)(2,1)S(1)}, u32[]{:S(2)}, u32[]{:S(2)}) %collective-permute-start.38) | collective-permute-done | bytes 4718624 | tf_op jit(solution)/shard_map/ppermute | solution.py:543
  306.3 2.2 copy-done.11
  308.5 2.6 add_convert_fusion.22
  311.1 31.2 %backward_sections.5 = (f32[768,512]{1,0:T(8,128)}, f32[768,512]{1,0:T(8,128)}, f32[3,1,2048]{2,1,0:T(1,128)}, bf16[4,3,32,1536]{3,2,1,0:T(8,128)(2,1)}, bf16[4,...) custom-call(s32[64]{0:T(128)} %concatenate.77.table, ...), custom_call_target="tpu_custom_call" | custom-call | flops 20000000000 | bytes 1 | tf_op jit(solution)/shard_map/backward_sections/pallas_call | solution.py:249
  343.9 6.0 pool_grads.2
  355.0 4.7 collective-permute-done.42
  360.7 2.7 collective-permute-done.40.refs_3_
  364.1 2.9 add_convert_fusion.19
  371.3 2.2 collective-permute-start.45
  381.0 2.6 add_convert_fusion.16
  386.1 5.3 carry_grads.2.refs_0_.carried_ref
  391.4 30.8 %backward_sections.6 = (f32[768,512]{1,0:T(8,128)}, f32[768,512]{1,0:T(8,128)}, f32[3,1,2048]{2,1,0:T(1,128)}, bf16[4,3,32,1536]{3,2,1,0:T(8,128)(2,1)}, bf16[4,...) custom-call(s32[64]{0:T(128)} %concatenate.76.table, ...), custom_call_target="tpu_custom_call" | custom-call | flops 20000000000 | bytes 1 | tf_op jit(solution)/shard_map/backward_sections/pallas_call | solution.py:249
  428.8 2.6 add_convert_fusion.11
  435.9 2.8 add_convert_fusion.14
  441.4 30.8 %backward_sections.7 = (f32[768,512]{1,0:T(8,128)}, f32[768,512]{1,0:T(8,128)}, f32[3,1,2048]{2,1,0:T(1,128)}, bf16[4,3,32,1536]{3,2,1,0:T(8,128)(2,1)}, bf16[4,...) custom-call(s32[64]{0:T(128)} %concatenate.76.table, ...), custom_call_target="tpu_custom_call" | custom-call | flops 20000000000 | bytes 1 | tf_op jit(solution)/shard_map/backward_sections/pallas_call | solution.py:249
  472.2 3.7 collective-permute-done.55.refs_4_
  483.4 2.8 add_convert_fusion.7
  493.0 5.8 pool_grads.3
  498.8 2.6 add_convert_fusion.4
  503.8 3.6 collective-permute-done.66
  507.4 2.2 add_convert_fusion.36.refs_0_
  509.6 21.4 %collective-permute-done.63 = bf16[2,3,32,1536]{3,2,1,0:T(8,128)(2,1)} collective-permute-done((bf16[2,3,32,1536]{3,2,1,0:T(8,128)(2,1)}, bf16[2,3,32,1536]{3,2,1,0:T(8,128)(2,1)}, u32[]{:S(2)}, u32[]{:S(2)}) %collective-permute-start.63) | collective-permute-done | bytes 589856 | tf_op jit(solution)/shard_map/ppermute | solution.py:543
  531.0 3.3 add_convert_fusion.1
  543.5 7.3 %collective-permute-done.69 = bf16[2,3,32,1536]{3,2,1,0:T(8,128)(2,1)} collective-permute-done((bf16[2,3,32,1536]{3,2,1,0:T(8,128)(2,1)S(1)}, bf16[2,3,32,1536]{3,2,1,0:T(8,128)(2,1)}, u32[]{:S(2)}, u32[]{:S(2)}) %collective-permute-start.69) | collective-permute-done | bytes 589856 | tf_op jit(solution)/shard_map/ppermute | solution.py:543
  554.1 10.5 %collective-permute-done.67 = bf16[4,3,32,1536]{3,2,1,0:T(8,128)(2,1)} collective-permute-done((bf16[4,3,32,1536]{3,2,1,0:T(8,128)(2,1)}, bf16[4,3,32,1536]{3,2,1,0:T(8,128)(2,1)}, u32[]{:S(2)}, u32[]{:S(2)}) %collective-permute-start.67) | collective-permute-done | bytes 1179680 | tf_op jit(solution)/shard_map/ppermute | solution.py:543
  571.1 2.2 add_convert_fusion.38.refs_0_
  573.4 3.9 collective-permute-done.71.refs_2_
  577.3 4.4 collective-permute-done.77
  585.3 3.4 place_grads.4
  599.0 3.2 collective-permute-start.78
  602.3 10.5 %collective-permute-done.82 = bf16[1,3,32,1536]{3,2,1,0:T(8,128)(2,1)S(1)} collective-permute-done((bf16[1,3,32,1536]{3,2,1,0:T(8,128)(2,1)S(1)}, bf16[1,3,32,1536]{3,2,1,0:T(8,128)(2,1)S(1)}, u32[]{:S(2)}, u32[]{:S(2)}) %collective-permute-start.82) | collective-permute-done | bytes 294944 | tf_op jit(solution)/shard_map/ppermute | solution.py:543
  612.8 2.3 add_convert_fusion.24.refs_0_
  620.7 5.1 carry_grads.3.refs_1_
  626.4 4.4 collective-permute-done.81
  630.8 2.3 add_convert_fusion.26.refs_0_
  633.9 3.4 place_grads.5
  641.0 3.4 place_grads.6
  644.4 2.5 collective-permute-done.87.refs_0_
  652.4 3.4 place_grads.7
  (466 shorter events, 159.1 us)
Async XLA Ops:
  7.2 228.2 %all-gather.2.cloned.1.call-start = ((), (), s32[]{:S(2)}) async-start(), calls=%async_computation | async-start | bytes 19464192 | tf_op jit(solution)/shard_map/all_gather | solution.py:600
  9.7 13.2 %collective-permute-start.2 = (bf16[1,3,32,1536]{3,2,1,0:T(8,128)(2,1)}, bf16[1,3,32,1536]{3,2,1,0:T(8,128)(2,1)S(1)}, u32[]{:S(2)}, u32[]{:S(2)}) collective-permute-start(bf16[1,3,32,1536]{3,2,1,0:T(8,128)(2,1)} %pack.3.refs_0_), channel_id=1, source_target_pairs={{0,6},{1,7},{2,4},{3,5},{4,2},{5,3},{6,0},{7,1},{8,14},{9,15},{10,... | collective-permute-start | bytes 884744 | tf_op jit(solution)/shard_map/ppermute | solution.py:543
  14.8 25.3 %collective-permute-start.1 = (bf16[1,3,32,1536]{3,2,1,0:T(8,128)(2,1)}, bf16[1,3,32,1536]{3,2,1,0:T(8,128)(2,1)S(1)}, u32[]{:S(2)}, u32[]{:S(2)}) collective-permute-start(bf16[1,3,32,1536]{3,2,1,0:T(8,128)(2,1)} %pack.3.refs_0_), channel_id=1, source_target_pairs={{0,4},{1,5},{2,6},{3,7},{4,0},{5,1},{6,2},{7,3},{8,12},{9,13},{10,... | collective-permute-start | bytes 884744 | tf_op jit(solution)/shard_map/ppermute | solution.py:543
  14.8 25.3 %collective-permute-start = (bf16[1,3,32,1536]{3,2,1,0:T(8,128)(2,1)}, bf16[1,3,32,1536]{3,2,1,0:T(8,128)(2,1)S(1)}, u32[]{:S(2)}, u32[]{:S(2)}) collective-permute-start(bf16[1,3,32,1536]{3,2,1,0:T(8,128)(2,1)} %pack.3.refs_0_), channel_id=1, source_target_pairs={{0,2},{1,3},{2,0},{3,1},{4,6},{5,7},{6,4},{7,5},{8,10},{9,11},{10,... | collective-permute-start | bytes 884744 | tf_op jit(solution)/shard_map/ppermute | solution.py:543
  44.7 31.1 %collective-permute-start.7 = (bf16[4,3,32,1536]{3,2,1,0:T(8,128)(2,1)}, bf16[4,3,32,1536]{3,2,1,0:T(8,128)(2,1)S(1)}, u32[]{:S(2)}, u32[]{:S(2)}) collective-permute-start(bf16[4,3,32,1536]{3,2,1,0:T(8,128)(2,1)} %combine.4.refs_0_.refs_5_.refs_11_), channel_id=1, source_target_pairs={{0,16},{8,24},{16,0},{24,8},{1,17},{9,25},{17,1},{25,9},{2,18},{10... | collective-permute-start | bytes 3538952 | tf_op jit(solution)/shard_map/ppermute | solution.py:543
  46.2 29.7 %collective-permute-start.6 = (bf16[4,3,32,1536]{3,2,1,0:T(8,128)(2,1)}, bf16[4,3,32,1536]{3,2,1,0:T(8,128)(2,1)S(1)}, u32[]{:S(2)}, u32[]{:S(2)}) collective-permute-start(bf16[4,3,32,1536]{3,2,1,0:T(8,128)(2,1)} %combine.4.refs_0_.refs_5_.refs_11_), channel_id=1, source_target_pairs={{0,1},{1,0},{2,3},{3,2},{4,5},{5,4},{6,7},{7,6},{8,9},{9,8},{10,11... | collective-permute-start | bytes 3538952 | tf_op jit(solution)/shard_map/ppermute | solution.py:543
  50.2 12.1 %collective-permute-start.5 = (bf16[1,3,32,1536]{3,2,1,0:T(8,128)(2,1)}, bf16[1,3,32,1536]{3,2,1,0:T(8,128)(2,1)S(1)}, u32[]{:S(2)}, u32[]{:S(2)}) collective-permute-start(bf16[1,3,32,1536]{3,2,1,0:T(8,128)(2,1)} %pack.4.refs_0_), channel_id=1, source_target_pairs={{0,6},{1,7},{2,4},{3,5},{4,2},{5,3},{6,0},{7,1},{8,14},{9,15},{10,... | collective-permute-start | bytes 884744 | tf_op jit(solution)/shard_map/ppermute | solution.py:543
  52.7 23.2 %collective-permute-start.4 = (bf16[1,3,32,1536]{3,2,1,0:T(8,128)(2,1)}, bf16[1,3,32,1536]{3,2,1,0:T(8,128)(2,1)S(1)}, u32[]{:S(2)}, u32[]{:S(2)}) collective-permute-start(bf16[1,3,32,1536]{3,2,1,0:T(8,128)(2,1)} %pack.4.refs_0_), channel_id=1, source_target_pairs={{0,4},{1,5},{2,6},{3,7},{4,0},{5,1},{6,2},{7,3},{8,12},{9,13},{10,... | collective-permute-start | bytes 884744 | tf_op jit(solution)/shard_map/ppermute | solution.py:543
  52.7 23.2 %collective-permute-start.3 = (bf16[1,3,32,1536]{3,2,1,0:T(8,128)(2,1)}, bf16[1,3,32,1536]{3,2,1,0:T(8,128)(2,1)S(1)}, u32[]{:S(2)}, u32[]{:S(2)}) collective-permute-start(bf16[1,3,32,1536]{3,2,1,0:T(8,128)(2,1)} %pack.4.refs_0_), channel_id=1, source_target_pairs={{0,2},{1,3},{2,0},{3,1},{4,6},{5,7},{6,4},{7,5},{8,10},{9,11},{10,... | collective-permute-start | bytes 884744 | tf_op jit(solution)/shard_map/ppermute | solution.py:543
  95.4 59.0 %collective-permute-start.23 = (bf16[4,3,32,1536]{3,2,1,0:T(8,128)(2,1)}, bf16[4,3,32,1536]{3,2,1,0:T(8,128)(2,1)}, u32[]{:S(2)}, u32[]{:S(2)}) collective-permute-start(bf16[4,3,32,1536]{3,2,1,0:T(8,128)(2,1)} %combine.6.refs_1_.refs_5_.refs_11_), channel_id=1, source_target_pairs={{0,16},{8,24},{16,0},{24,8},{1,17},{9,25},{17,1},{25,9},{2,18},{10... | collective-permute-start | bytes 3538952 | tf_op jit(solution)/shard_map/ppermute | solution.py:543
  96.0 59.0 %collective-permute-start.22 = (bf16[4,3,32,1536]{3,2,1,0:T(8,128)(2,1)}, bf16[4,3,32,1536]{3,2,1,0:T(8,128)(2,1)}, u32[]{:S(2)}, u32[]{:S(2)}) collective-permute-start(bf16[4,3,32,1536]{3,2,1,0:T(8,128)(2,1)} %combine.6.refs_1_.refs_5_.refs_11_), channel_id=1, source_target_pairs={{0,1},{1,0},{2,3},{3,2},{4,5},{5,4},{6,7},{7,6},{8,9},{9,8},{10,11... | collective-permute-start | bytes 3538952 | tf_op jit(solution)/shard_map/ppermute | solution.py:543
  101.4 53.0 %collective-permute-start.15 = (bf16[2,3,32,1536]{3,2,1,0:T(8,128)(2,1)S(1)}, bf16[2,3,32,1536]{3,2,1,0:T(8,128)(2,1)S(1)}, u32[]{:S(2)}, u32[]{:S(2)}) collective-permute-start(bf16[2,3,32,1536]{3,2,1,0:T(8,128)(2,1)S(1)} %copy-done.39), channel_id=1, source_target_pairs={{0,16},{8,24},{16,0},{24,8},{1,17},{9,25},{17,1},{25,9},{2,18},{10... | collective-permute-start | bytes 1769480 | tf_op jit(solution)/shard_map/ppermute | solution.py:543
  105.0 41.3 %collective-permute-start.16 = (bf16[2,3,32,1536]{3,2,1,0:T(8,128)(2,1)}, bf16[2,3,32,1536]{3,2,1,0:T(8,128)(2,1)}, u32[]{:S(2)}, u32[]{:S(2)}) collective-permute-start(bf16[2,3,32,1536]{3,2,1,0:T(8,128)(2,1)} %get-tuple-element.110), channel_id=1, source_target_pairs={{0,1},{1,0},{2,3},{3,2},{4,5},{5,4},{6,7},{7,6},{8,9},{9,8},{10,11... | collective-permute-start | bytes 1769480 | tf_op jit(solution)/shard_map/ppermute | solution.py:543
  111.2 47.0 %collective-permute-start.17 = (bf16[4,3,32,1536]{3,2,1,0:T(8,128)(2,1)S(1)}, bf16[4,3,32,1536]{3,2,1,0:T(8,128)(2,1)}, u32[]{:S(2)}, u32[]{:S(2)}) collective-permute-start(bf16[4,3,32,1536]{3,2,1,0:T(8,128)(2,1)S(1)} %copy-done.28), channel_id=1, source_target_pairs={{0,8},{8,0},{16,24},{24,16},{1,9},{9,1},{17,25},{25,17},{2,10},{10... | collective-permute-start | bytes 3538952 | tf_op jit(solution)/shard_map/ppermute | solution.py:543
  146.3 12.4 %collective-permute-start.19 = (bf16[4,3,32,1536]{3,2,1,0:T(8,128)(2,1)}, bf16[4,3,32,1536]{3,2,1,0:T(8,128)(2,1)}, u32[]{:S(2)}, u32[]{:S(2)}) collective-permute-start(bf16[4,3,32,1536]{3,2,1,0:T(8,128)(2,1)} %copy-done.87), channel_id=1, source_target_pairs={{0,8},{8,0},{16,24},{24,16},{1,9},{9,1},{17,25},{25,17},{2,10},{10... | collective-permute-start | bytes 3538952 | tf_op jit(solution)/shard_map/ppermute | solution.py:543
  158.2 25.1 %collective-permute-start.26 = (bf16[4,3,32,1536]{3,2,1,0:T(8,128)(2,1)S(1)}, bf16[4,3,32,1536]{3,2,1,0:T(8,128)(2,1)}, u32[]{:S(2)}, u32[]{:S(2)}) collective-permute-start(bf16[4,3,32,1536]{3,2,1,0:T(8,128)(2,1)S(1)} %copy-done.29), channel_id=1, source_target_pairs={{0,8},{8,0},{16,24},{24,16},{1,9},{9,1},{17,25},{25,17},{2,10},{10... | collective-permute-start | bytes 3538952 | tf_op jit(solution)/shard_map/ppermute | solution.py:543
  158.7 23.0 %collective-permute-start.25 = (bf16[2,3,32,1536]{3,2,1,0:T(8,128)(2,1)}, bf16[2,3,32,1536]{3,2,1,0:T(8,128)(2,1)S(1)}, u32[]{:S(2)}, u32[]{:S(2)}) collective-permute-start(bf16[2,3,32,1536]{3,2,1,0:T(8,128)(2,1)} %get-tuple-element.113), channel_id=1, source_target_pairs={{0,1},{1,0},{2,3},{3,2},{4,5},{5,4},{6,7},{7,6},{8,9},{9,8},{10,11... | collective-permute-start | bytes 1769480 | tf_op jit(solution)/shard_map/ppermute | solution.py:543
  160.2 21.5 %collective-permute-start.24 = (bf16[2,3,32,1536]{3,2,1,0:T(8,128)(2,1)}, bf16[2,3,32,1536]{3,2,1,0:T(8,128)(2,1)S(1)}, u32[]{:S(2)}, u32[]{:S(2)}) collective-permute-start(bf16[2,3,32,1536]{3,2,1,0:T(8,128)(2,1)} %get-tuple-element.111.refs_15_), channel_id=1, source_target_pairs={{0,16},{8,24},{16,0},{24,8},{1,17},{9,25},{17,1},{25,9},{2,18},{10... | collective-permute-start | bytes 1769480 | tf_op jit(solution)/shard_map/ppermute | solution.py:543
  160.7 25.1 %collective-permute-start.28 = (bf16[4,3,32,1536]{3,2,1,0:T(8,128)(2,1)}, bf16[4,3,32,1536]{3,2,1,0:T(8,128)(2,1)}, u32[]{:S(2)}, u32[]{:S(2)}) collective-permute-start(bf16[4,3,32,1536]{3,2,1,0:T(8,128)(2,1)} %collective-permute-done.23.refs_1_.refs_7_.refs_13_), channel_id=1, source_target_pairs={{0,8},{8,0},{16,24},{24,16},{1,9},{9,1},{17,25},{25,17},{2,10},{10... | collective-permute-start | bytes 3538952 | tf_op jit(solution)/shard_map/ppermute | solution.py:543
  160.8 25.0 %collective-permute-start.27 = (bf16[4,3,32,1536]{3,2,1,0:T(8,128)(2,1)}, bf16[4,3,32,1536]{3,2,1,0:T(8,128)(2,1)}, u32[]{:S(2)}, u32[]{:S(2)}) collective-permute-start(bf16[4,3,32,1536]{3,2,1,0:T(8,128)(2,1)} %collective-permute-done.22.refs_0_.refs_6_.refs_12_), channel_id=1, source_target_pairs={{0,8},{8,0},{16,24},{24,16},{1,9},{9,1},{17,25},{25,17},{2,10},{10... | collective-permute-start | bytes 3538952 | tf_op jit(solution)/shard_map/ppermute | solution.py:543
  223.8 6.8 %collective-permute-start.36 = (f32[12,512]{1,0:T(8,128)S(1)}, f32[12,512]{1,0:T(8,128)S(1)}, u32[]{:S(2)}, u32[]{:S(2)}) collective-permute-start(f32[12,512]{1,0:T(8,128)S(1)} %pad_maximum_fusion.17), channel_id=1, source_target_pairs={{0,4},{1,5},{2,6},{3,7},{4,0},{5,1},{6,2},{7,3},{8,12},{9,13},{10,... | collective-permute-start | bytes 73736 | tf_op jit(solution)/shard_map/ppermute | solution.py:543
  298.1 8.2 %collective-permute-start.38 = (bf16[16,3,32,1536]{3,2,1,0:T(8,128)(2,1)}, bf16[16,3,32,1536]{3,2,1,0:T(8,128)(2,1)S(1)}, u32[]{:S(2)}, u32[]{:S(2)}) collective-permute-start(bf16[16,3,32,1536]{3,2,1,0:T(8,128)(2,1)} %get-tuple-element.132), channel_id=1, source_target_pairs={{0,8},{8,0},{16,24},{24,16},{1,9},{9,1},{17,25},{25,17},{2,10},{10... | collective-permute-start | bytes 14155784 | tf_op jit(solution)/shard_map/ppermute | solution.py:543
  342.3 38.6 %collective-permute-start.48 = (bf16[16,3,32,1536]{3,2,1,0:T(8,128)(2,1)}, bf16[16,3,32,1536]{3,2,1,0:T(8,128)(2,1)}, u32[]{:S(2)}, u32[]{:S(2)}) collective-permute-start(bf16[16,3,32,1536]{3,2,1,0:T(8,128)(2,1)} %get-tuple-element.136.refs_3_), channel_id=1, source_target_pairs={{0,8},{8,0},{16,24},{24,16},{1,9},{9,1},{17,25},{25,17},{2,10},{10... | collective-permute-start | bytes 14155784 | tf_op jit(solution)/shard_map/ppermute | solution.py:543
  342.5 21.5 %collective-permute-start.44 = (bf16[2,3,32,1536]{3,2,1,0:T(8,128)(2,1)S(1)}, bf16[2,3,32,1536]{3,2,1,0:T(8,128)(2,1)S(1)}, u32[]{:S(2)}, u32[]{:S(2)}) collective-permute-start(bf16[2,3,32,1536]{3,2,1,0:T(8,128)(2,1)S(1)} %copy-done.23), channel_id=1, source_target_pairs={{0,1},{1,0},{2,3},{3,2},{4,5},{5,4},{6,7},{7,6},{8,9},{9,8},{10,11... | collective-permute-start | bytes 1769480 | tf_op jit(solution)/shard_map/ppermute | solution.py:543
  343.3 20.8 %collective-permute-start.43 = (bf16[2,3,32,1536]{3,2,1,0:T(8,128)(2,1)S(1)}, bf16[2,3,32,1536]{3,2,1,0:T(8,128)(2,1)}, u32[]{:S(2)}, u32[]{:S(2)}) collective-permute-start(bf16[2,3,32,1536]{3,2,1,0:T(8,128)(2,1)S(1)} %copy-done.22), channel_id=1, source_target_pairs={{0,16},{8,24},{16,0},{24,8},{1,17},{9,25},{17,1},{25,9},{2,18},{10... | collective-permute-start | bytes 1769480 | tf_op jit(solution)/shard_map/ppermute | solution.py:543
  352.1 7.6 %collective-permute-start.42 = (f32[8,512]{1,0:T(8,128)S(1)}, f32[8,512]{1,0:T(8,128)S(1)}, u32[]{:S(2)}, u32[]{:S(2)}) collective-permute-start(f32[8,512]{1,0:T(8,128)S(1)} %add.853), channel_id=1, source_target_pairs={{0,17},{1,16},{2,19},{3,18},{4,21},{5,20},{6,23},{7,22},{8,25},{9,... | collective-permute-start | bytes 49160 | tf_op jit(solution)/shard_map/ppermute | solution.py:564
  379.4 42.9 %collective-permute-start.49 = (bf16[4,3,32,1536]{3,2,1,0:T(8,128)(2,1)}, bf16[4,3,32,1536]{3,2,1,0:T(8,128)(2,1)S(1)}, u32[]{:S(2)}, u32[]{:S(2)}) collective-permute-start(bf16[4,3,32,1536]{3,2,1,0:T(8,128)(2,1)} %get-tuple-element.141.refs_0_), channel_id=1, source_target_pairs={{0,1},{1,0},{2,3},{3,2},{4,5},{5,4},{6,7},{7,6},{8,9},{9,8},{10,11... | collective-permute-start | bytes 3538952 | tf_op jit(solution)/shard_map/ppermute | solution.py:543
  379.8 42.5 %collective-permute-start.50 = (bf16[4,3,32,1536]{3,2,1,0:T(8,128)(2,1)}, bf16[4,3,32,1536]{3,2,1,0:T(8,128)(2,1)S(1)}, u32[]{:S(2)}, u32[]{:S(2)}) collective-permute-start(bf16[4,3,32,1536]{3,2,1,0:T(8,128)(2,1)} %get-tuple-element.142.refs_1_), channel_id=1, source_target_pairs={{0,16},{8,24},{16,0},{24,8},{1,17},{9,25},{17,1},{25,9},{2,18},{10... | collective-permute-start | bytes 3538952 | tf_op jit(solution)/shard_map/ppermute | solution.py:543
  383.6 38.7 %collective-permute-start.51 = (bf16[2,3,32,1536]{3,2,1,0:T(8,128)(2,1)}, bf16[2,3,32,1536]{3,2,1,0:T(8,128)(2,1)S(1)}, u32[]{:S(2)}, u32[]{:S(2)}) collective-permute-start(bf16[2,3,32,1536]{3,2,1,0:T(8,128)(2,1)} %get-tuple-element.145.refs_2_), channel_id=1, source_target_pairs={{0,16},{8,24},{16,0},{24,8},{1,17},{9,25},{17,1},{25,9},{2,18},{10... | collective-permute-start | bytes 1769480 | tf_op jit(solution)/shard_map/ppermute | solution.py:543
  384.4 37.9 %collective-permute-start.52 = (bf16[2,3,32,1536]{3,2,1,0:T(8,128)(2,1)}, bf16[2,3,32,1536]{3,2,1,0:T(8,128)(2,1)S(1)}, u32[]{:S(2)}, u32[]{:S(2)}) collective-permute-start(bf16[2,3,32,1536]{3,2,1,0:T(8,128)(2,1)} %get-tuple-element.146.refs_3_), channel_id=1, source_target_pairs={{0,1},{1,0},{2,3},{3,2},{4,5},{5,4},{6,7},{7,6},{8,9},{9,8},{10,11... | collective-permute-start | bytes 1769480 | tf_op jit(solution)/shard_map/ppermute | solution.py:543
  424.1 11.9 %collective-permute-start.53 = (bf16[16,3,32,1536]{3,2,1,0:T(8,128)(2,1)}, bf16[16,3,32,1536]{3,2,1,0:T(8,128)(2,1)}, u32[]{:S(2)}, u32[]{:S(2)}) collective-permute-start(bf16[16,3,32,1536]{3,2,1,0:T(8,128)(2,1)} %tie.33.refs_1_), channel_id=1, source_target_pairs={{0,8},{8,0},{16,24},{24,16},{1,9},{9,1},{17,25},{25,17},{2,10},{10... | collective-permute-start | bytes 14155784 | tf_op jit(solution)/shard_map/ppermute | solution.py:543
  433.8 38.4 %collective-permute-start.54 = (bf16[2,3,32,1536]{3,2,1,0:T(8,128)(2,1)S(1)}, bf16[2,3,32,1536]{3,2,1,0:T(8,128)(2,1)}, u32[]{:S(2)}, u32[]{:S(2)}) collective-permute-start(bf16[2,3,32,1536]{3,2,1,0:T(8,128)(2,1)S(1)} %copy-done), channel_id=1, source_target_pairs={{0,2},{1,3},{2,0},{3,1},{4,6},{5,7},{6,4},{7,5},{8,10},{9,11},{10,... | collective-permute-start | bytes 1769480 | tf_op jit(solution)/shard_map/ppermute | solution.py:543
  434.5 37.7 %collective-permute-start.57 = (bf16[4,3,32,1536]{3,2,1,0:T(8,128)(2,1)}, bf16[4,3,32,1536]{3,2,1,0:T(8,128)(2,1)S(1)}, u32[]{:S(2)}, u32[]{:S(2)}) collective-permute-start(bf16[4,3,32,1536]{3,2,1,0:T(8,128)(2,1)} %get-tuple-element.170.refs_2_), channel_id=1, source_target_pairs={{0,1},{1,0},{2,3},{3,2},{4,5},{5,4},{6,7},{7,6},{8,9},{9,8},{10,11... | collective-permute-start | bytes 3538952 | tf_op jit(solution)/shard_map/ppermute | solution.py:543
  435.3 37.0 %collective-permute-start.58 = (bf16[4,3,32,1536]{3,2,1,0:T(8,128)(2,1)}, bf16[4,3,32,1536]{3,2,1,0:T(8,128)(2,1)S(1)}, u32[]{:S(2)}, u32[]{:S(2)}) collective-permute-start(bf16[4,3,32,1536]{3,2,1,0:T(8,128)(2,1)} %get-tuple-element.171.refs_3_), channel_id=1, source_target_pairs={{0,16},{8,24},{16,0},{24,8},{1,17},{9,25},{17,1},{25,9},{2,18},{10... | collective-permute-start | bytes 3538952 | tf_op jit(solution)/shard_map/ppermute | solution.py:543
  438.7 37.2 %collective-permute-start.55 = (bf16[2,3,32,1536]{3,2,1,0:T(8,128)(2,1)}, bf16[2,3,32,1536]{3,2,1,0:T(8,128)(2,1)S(1)}, u32[]{:S(2)}, u32[]{:S(2)}) collective-permute-start(bf16[2,3,32,1536]{3,2,1,0:T(8,128)(2,1)} %get-tuple-element.172.refs_21_), channel_id=1, source_target_pairs={{0,16},{8,24},{16,0},{24,8},{1,17},{9,25},{17,1},{25,9},{2,18},{10... | collective-permute-start | bytes 1769480 | tf_op jit(solution)/shard_map/ppermute | solution.py:543
  440.1 35.8 %collective-permute-start.56 = (bf16[2,3,32,1536]{3,2,1,0:T(8,128)(2,1)}, bf16[2,3,32,1536]{3,2,1,0:T(8,128)(2,1)}, u32[]{:S(2)}, u32[]{:S(2)}) collective-permute-start(bf16[2,3,32,1536]{3,2,1,0:T(8,128)(2,1)} %get-tuple-element.173.refs_22_), channel_id=1, source_target_pairs={{0,1},{1,0},{2,3},{3,2},{4,5},{5,4},{6,7},{7,6},{8,9},{9,8},{10,11... | collective-permute-start | bytes 1769480 | tf_op jit(solution)/shard_map/ppermute | solution.py:543
  476.8 22.1 %collective-permute-start.59 = (bf16[16,3,32,1536]{3,2,1,0:T(8,128)(2,1)}, bf16[16,3,32,1536]{3,2,1,0:T(8,128)(2,1)}, u32[]{:S(2)}, u32[]{:S(2)}) collective-permute-start(bf16[16,3,32,1536]{3,2,1,0:T(8,128)(2,1)} %tie.37.refs_2_), channel_id=1, source_target_pairs={{0,8},{8,0},{16,24},{24,16},{1,9},{9,1},{17,25},{25,17},{2,10},{10... | collective-permute-start | bytes 14155784 | tf_op jit(solution)/shard_map/ppermute | solution.py:543
  489.2 50.3 %collective-permute-start.61 = (bf16[4,3,32,1536]{3,2,1,0:T(8,128)(2,1)}, bf16[4,3,32,1536]{3,2,1,0:T(8,128)(2,1)}, u32[]{:S(2)}, u32[]{:S(2)}) collective-permute-start(bf16[4,3,32,1536]{3,2,1,0:T(8,128)(2,1)} %get-tuple-element.179.refs_1_), channel_id=1, source_target_pairs={{0,1},{1,0},{2,3},{3,2},{4,5},{5,4},{6,7},{7,6},{8,9},{9,8},{10,11... | collective-permute-start | bytes 3538952 | tf_op jit(solution)/shard_map/ppermute | solution.py:543
  490.5 49.0 %collective-permute-start.62 = (bf16[4,3,32,1536]{3,2,1,0:T(8,128)(2,1)}, bf16[4,3,32,1536]{3,2,1,0:T(8,128)(2,1)}, u32[]{:S(2)}, u32[]{:S(2)}) collective-permute-start(bf16[4,3,32,1536]{3,2,1,0:T(8,128)(2,1)} %get-tuple-element.180.refs_2_), channel_id=1, source_target_pairs={{0,16},{8,24},{16,0},{24,8},{1,17},{9,25},{17,1},{25,9},{2,18},{10... | collective-permute-start | bytes 3538952 | tf_op jit(solution)/shard_map/ppermute | solution.py:543
  491.5 15.9 %collective-permute-start.66 = (bf16[1,3,32,1536]{3,2,1,0:T(8,128)(2,1)}, bf16[1,3,32,1536]{3,2,1,0:T(8,128)(2,1)}, u32[]{:S(2)}, u32[]{:S(2)}) collective-permute-start(bf16[1,3,32,1536]{3,2,1,0:T(8,128)(2,1)} %tie.39.refs_3_), channel_id=1, source_target_pairs={{0,4},{1,5},{2,6},{3,7},{4,0},{5,1},{6,2},{7,3},{8,12},{9,13},{10,... | collective-permute-start | bytes 884744 | tf_op jit(solution)/shard_map/ppermute | solution.py:543
  501.4 29.6 %collective-permute-start.63 = (bf16[2,3,32,1536]{3,2,1,0:T(8,128)(2,1)}, bf16[2,3,32,1536]{3,2,1,0:T(8,128)(2,1)}, u32[]{:S(2)}, u32[]{:S(2)}) collective-permute-start(bf16[2,3,32,1536]{3,2,1,0:T(8,128)(2,1)} %get-tuple-element.190.refs_1_), channel_id=1, source_target_pairs={{0,16},{8,24},{16,0},{24,8},{1,17},{9,25},{17,1},{25,9},{2,18},{10... | collective-permute-start | bytes 1769480 | tf_op jit(solution)/shard_map/ppermute | solution.py:543
  502.4 28.6 %collective-permute-start.64 = (bf16[2,3,32,1536]{3,2,1,0:T(8,128)(2,1)}, bf16[2,3,32,1536]{3,2,1,0:T(8,128)(2,1)}, u32[]{:S(2)}, u32[]{:S(2)}) collective-permute-start(bf16[2,3,32,1536]{3,2,1,0:T(8,128)(2,1)} %get-tuple-element.191.refs_2_), channel_id=1, source_target_pairs={{0,1},{1,0},{2,3},{3,2},{4,5},{5,4},{6,7},{7,6},{8,9},{9,8},{10,11... | collective-permute-start | bytes 1769480 | tf_op jit(solution)/shard_map/ppermute | solution.py:543
  536.6 14.2 %collective-permute-start.69 = (bf16[2,3,32,1536]{3,2,1,0:T(8,128)(2,1)S(1)}, bf16[2,3,32,1536]{3,2,1,0:T(8,128)(2,1)}, u32[]{:S(2)}, u32[]{:S(2)}) collective-permute-start(bf16[2,3,32,1536]{3,2,1,0:T(8,128)(2,1)S(1)} %copy-done.2), channel_id=1, source_target_pairs={{0,2},{1,3},{2,0},{3,1},{4,6},{5,7},{6,4},{7,5},{8,10},{9,11},{10,... | collective-permute-start | bytes 1769480 | tf_op jit(solution)/shard_map/ppermute | solution.py:543
  537.9 26.7 %collective-permute-start.67 = (bf16[4,3,32,1536]{3,2,1,0:T(8,128)(2,1)}, bf16[4,3,32,1536]{3,2,1,0:T(8,128)(2,1)}, u32[]{:S(2)}, u32[]{:S(2)}) collective-permute-start(bf16[4,3,32,1536]{3,2,1,0:T(8,128)(2,1)} %get-tuple-element.195.refs_1_), channel_id=1, source_target_pairs={{0,1},{1,0},{2,3},{3,2},{4,5},{5,4},{6,7},{7,6},{8,9},{9,8},{10,11... | collective-permute-start | bytes 3538952 | tf_op jit(solution)/shard_map/ppermute | solution.py:543
  538.3 26.7 %collective-permute-start.68 = (bf16[4,3,32,1536]{3,2,1,0:T(8,128)(2,1)}, bf16[4,3,32,1536]{3,2,1,0:T(8,128)(2,1)}, u32[]{:S(2)}, u32[]{:S(2)}) collective-permute-start(bf16[4,3,32,1536]{3,2,1,0:T(8,128)(2,1)} %get-tuple-element.196.refs_2_), channel_id=1, source_target_pairs={{0,16},{8,24},{16,0},{24,8},{1,17},{9,25},{17,1},{25,9},{2,18},{10... | collective-permute-start | bytes 3538952 | tf_op jit(solution)/shard_map/ppermute | solution.py:543
  552.8 18.3 %collective-permute-start.65 = (bf16[2,3,32,1536]{3,2,1,0:T(8,128)(2,1)S(1)}, bf16[2,3,32,1536]{3,2,1,0:T(8,128)(2,1)}, u32[]{:S(2)}, u32[]{:S(2)}) collective-permute-start(bf16[2,3,32,1536]{3,2,1,0:T(8,128)(2,1)S(1)} %copy-done.1), channel_id=1, source_target_pairs={{0,2},{1,3},{2,0},{3,1},{4,6},{5,7},{6,4},{7,5},{8,10},{9,11},{10,... | collective-permute-start | bytes 1769480 | tf_op jit(solution)/shard_map/ppermute | solution.py:543
  567.8 13.9 %collective-permute-start.77 = (bf16[1,3,32,1536]{3,2,1,0:T(8,128)(2,1)S(1)}, bf16[1,3,32,1536]{3,2,1,0:T(8,128)(2,1)}, u32[]{:S(2)}, u32[]{:S(2)}) collective-permute-start(bf16[1,3,32,1536]{3,2,1,0:T(8,128)(2,1)S(1)} %copy-done.15), channel_id=1, source_target_pairs={{0,4},{1,5},{2,6},{3,7},{4,0},{5,1},{6,2},{7,3},{8,12},{9,13},{10,... | collective-permute-start | bytes 884744 | tf_op jit(solution)/shard_map/ppermute | solution.py:543
  569.3 23.0 %collective-permute-start.76 = (bf16[2,3,32,1536]{3,2,1,0:T(8,128)(2,1)}, bf16[2,3,32,1536]{3,2,1,0:T(8,128)(2,1)}, u32[]{:S(2)}, u32[]{:S(2)}) collective-permute-start(bf16[2,3,32,1536]{3,2,1,0:T(8,128)(2,1)} %tie.46.refs_1_), channel_id=1, source_target_pairs={{0,2},{1,3},{2,0},{3,1},{4,6},{5,7},{6,4},{7,5},{8,10},{9,11},{10,... | collective-permute-start | bytes 1769480 | tf_op jit(solution)/shard_map/ppermute | solution.py:543
  570.2 7.0 %collective-permute-start.71 = (bf16[1,3,32,1536]{3,2,1,0:T(8,128)(2,1)}, bf16[1,3,32,1536]{3,2,1,0:T(8,128)(2,1)}, u32[]{:S(2)}, u32[]{:S(2)}) collective-permute-start(bf16[1,3,32,1536]{3,2,1,0:T(8,128)(2,1)} %tie.47.refs_1_.refs_0_), channel_id=1, source_target_pairs={{0,16},{8,24},{16,0},{24,8},{1,17},{9,25},{17,1},{25,9},{2,18},{10... | collective-permute-start | bytes 884744 | tf_op jit(solution)/shard_map/ppermute | solution.py:543
  573.4 10.5 %collective-permute-start.70 = (bf16[1,3,32,1536]{3,2,1,0:T(8,128)(2,1)S(1)}, bf16[1,3,32,1536]{3,2,1,0:T(8,128)(2,1)S(1)}, u32[]{:S(2)}, u32[]{:S(2)}) collective-permute-start(bf16[1,3,32,1536]{3,2,1,0:T(8,128)(2,1)S(1)} %copy-done.12), channel_id=1, source_target_pairs={{0,8},{8,0},{16,24},{24,16},{1,9},{9,1},{17,25},{25,17},{2,10},{10... | collective-permute-start | bytes 884744 | tf_op jit(solution)/shard_map/ppermute | solution.py:543
  588.8 7.1 %collective-permute-start.75 = (f32[56,512]{1,0:T(8,128)}, f32[56,512]{1,0:T(8,128)S(1)}, u32[]{:S(2)}, u32[]{:S(2)}) collective-permute-start(f32[56,512]{1,0:T(8,128)} %tie.49.refs_1_), channel_id=1, source_target_pairs={{0,17},{1,16},{2,19},{3,18},{4,21},{5,20},{6,23},{7,22},{8,25},{9,... | collective-permute-start | bytes 344072 | tf_op jit(solution)/shard_map/ppermute | solution.py:564
  590.2 6.9 %collective-permute-start.74 = (f32[56,512]{1,0:T(8,128)}, f32[56,512]{1,0:T(8,128)S(1)}, u32[]{:S(2)}, u32[]{:S(2)}) collective-permute-start(f32[56,512]{1,0:T(8,128)} %tie.49.refs_1_), channel_id=1, source_target_pairs={{0,1},{1,0},{2,3},{3,2},{4,5},{5,4},{6,7},{7,6},{8,9},{9,8},{10,11... | collective-permute-start | bytes 344072 | tf_op jit(solution)/shard_map/ppermute | solution.py:543
  594.4 18.4 %collective-permute-start.82 = (bf16[1,3,32,1536]{3,2,1,0:T(8,128)(2,1)S(1)}, bf16[1,3,32,1536]{3,2,1,0:T(8,128)(2,1)S(1)}, u32[]{:S(2)}, u32[]{:S(2)}) collective-permute-start(bf16[1,3,32,1536]{3,2,1,0:T(8,128)(2,1)S(1)} %copy-done.13), channel_id=1, source_target_pairs={{0,4},{1,5},{2,6},{3,7},{4,0},{5,1},{6,2},{7,3},{8,12},{9,13},{10,... | collective-permute-start | bytes 884744 | tf_op jit(solution)/shard_map/ppermute | solution.py:543
  597.8 18.7 %collective-permute-start.80 = (f32[56,512]{1,0:T(8,128)}, f32[56,512]{1,0:T(8,128)S(1)}, u32[]{:S(2)}, u32[]{:S(2)}) collective-permute-start(f32[56,512]{1,0:T(8,128)} %tie.52.refs_1_), channel_id=1, source_target_pairs={{0,6},{1,7},{2,4},{3,5},{4,2},{5,3},{6,0},{7,1},{8,14},{9,15},{10,... | collective-permute-start | bytes 344072 | tf_op jit(solution)/shard_map/ppermute | solution.py:543
  599.0 18.6 %collective-permute-start.79 = (f32[56,512]{1,0:T(8,128)}, f32[56,512]{1,0:T(8,128)S(1)}, u32[]{:S(2)}, u32[]{:S(2)}) collective-permute-start(f32[56,512]{1,0:T(8,128)} %tie.52.refs_1_), channel_id=1, source_target_pairs={{0,4},{1,5},{2,6},{3,7},{4,0},{5,1},{6,2},{7,3},{8,12},{9,13},{10,... | collective-permute-start | bytes 344072 | tf_op jit(solution)/shard_map/ppermute | solution.py:543
  599.0 20.0 %collective-permute-start.78 = (f32[56,512]{1,0:T(8,128)}, f32[56,512]{1,0:T(8,128)}, u32[]{:S(2)}, u32[]{:S(2)}) collective-permute-start(f32[56,512]{1,0:T(8,128)} %tie.52.refs_1_), channel_id=1, source_target_pairs={{0,2},{1,3},{2,0},{3,1},{4,6},{5,7},{6,4},{7,5},{8,10},{9,11},{10,... | collective-permute-start | bytes 344072 | tf_op jit(solution)/shard_map/ppermute | solution.py:543
  615.0 15.8 %collective-permute-start.81 = (bf16[1,3,32,1536]{3,2,1,0:T(8,128)(2,1)S(1)}, bf16[1,3,32,1536]{3,2,1,0:T(8,128)(2,1)}, u32[]{:S(2)}, u32[]{:S(2)}) collective-permute-start(bf16[1,3,32,1536]{3,2,1,0:T(8,128)(2,1)S(1)} %copy-done.14), channel_id=1, source_target_pairs={{0,4},{1,5},{2,6},{3,7},{4,0},{5,1},{6,2},{7,3},{8,12},{9,13},{10,... | collective-permute-start | bytes 884744 | tf_op jit(solution)/shard_map/ppermute | solution.py:543
  615.0 10.8 %collective-permute-start.84 = (bf16[1,3,32,1536]{3,2,1,0:T(8,128)(2,1)S(1)}, bf16[1,3,32,1536]{3,2,1,0:T(8,128)(2,1)S(1)}, u32[]{:S(2)}, u32[]{:S(2)}) collective-permute-start(bf16[1,3,32,1536]{3,2,1,0:T(8,128)(2,1)S(1)} %copy-done.10), channel_id=1, source_target_pairs={{0,16},{8,24},{16,0},{24,8},{1,17},{9,25},{17,1},{25,9},{2,18},{10... | collective-permute-start | bytes 884744 | tf_op jit(solution)/shard_map/ppermute | solution.py:543
  616.6 16.6 %collective-permute-start.83 = (bf16[1,3,32,1536]{3,2,1,0:T(8,128)(2,1)S(1)}, bf16[1,3,32,1536]{3,2,1,0:T(8,128)(2,1)S(1)}, u32[]{:S(2)}, u32[]{:S(2)}) collective-permute-start(bf16[1,3,32,1536]{3,2,1,0:T(8,128)(2,1)S(1)} %copy-done.10), channel_id=1, source_target_pairs={{0,8},{8,0},{16,24},{24,16},{1,9},{9,1},{17,25},{25,17},{2,10},{10... | collective-permute-start | bytes 884744 | tf_op jit(solution)/shard_map/ppermute | solution.py:543
  617.6 15.5 %collective-permute-start.89 = (bf16[1,3,32,1536]{3,2,1,0:T(8,128)(2,1)}, bf16[1,3,32,1536]{3,2,1,0:T(8,128)(2,1)S(1)}, u32[]{:S(2)}, u32[]{:S(2)}) collective-permute-start(bf16[1,3,32,1536]{3,2,1,0:T(8,128)(2,1)} %tie.53.refs_1_.refs_0_), channel_id=1, source_target_pairs={{0,16},{8,24},{16,0},{24,8},{1,17},{9,25},{17,1},{25,9},{2,18},{10... | collective-permute-start | bytes 884744 | tf_op jit(solution)/shard_map/ppermute | solution.py:543
  619.0 20.5 %collective-permute-start.88 = (bf16[1,3,32,1536]{3,2,1,0:T(8,128)(2,1)}, bf16[1,3,32,1536]{3,2,1,0:T(8,128)(2,1)S(1)}, u32[]{:S(2)}, u32[]{:S(2)}) collective-permute-start(bf16[1,3,32,1536]{3,2,1,0:T(8,128)(2,1)} %tie.53.refs_1_.refs_0_), channel_id=1, source_target_pairs={{0,8},{8,0},{16,24},{24,16},{1,9},{9,1},{17,25},{25,17},{2,10},{10... | collective-permute-start | bytes 884744 | tf_op jit(solution)/shard_map/ppermute | solution.py:543
  625.9 7.3 %collective-permute-start.85 = (bf16[1,3,32,1536]{3,2,1,0:T(8,128)(2,1)S(1)}, bf16[1,3,32,1536]{3,2,1,0:T(8,128)(2,1)}, u32[]{:S(2)}, u32[]{:S(2)}) collective-permute-start(bf16[1,3,32,1536]{3,2,1,0:T(8,128)(2,1)S(1)} %collective-permute-done.84.refs_2_), channel_id=1, source_target_pairs={{0,8},{8,0},{16,24},{24,16},{1,9},{9,1},{17,25},{25,17},{2,10},{10... | collective-permute-start | bytes 884744 | tf_op jit(solution)/shard_map/ppermute | solution.py:543
  637.4 9.6 %collective-permute-start.87 = (bf16[1,3,32,1536]{3,2,1,0:T(8,128)(2,1)}, bf16[1,3,32,1536]{3,2,1,0:T(8,128)(2,1)S(1)}, u32[]{:S(2)}, u32[]{:S(2)}) collective-permute-start(bf16[1,3,32,1536]{3,2,1,0:T(8,128)(2,1)} %tie.54.refs_0_), channel_id=1, source_target_pairs={{0,16},{8,24},{16,0},{24,8},{1,17},{9,25},{17,1},{25,9},{2,18},{10... | collective-permute-start | bytes 884744 | tf_op jit(solution)/shard_map/ppermute | solution.py:543
  639.4 11.6 %collective-permute-start.86 = (bf16[1,3,32,1536]{3,2,1,0:T(8,128)(2,1)}, bf16[1,3,32,1536]{3,2,1,0:T(8,128)(2,1)S(1)}, u32[]{:S(2)}, u32[]{:S(2)}) collective-permute-start(bf16[1,3,32,1536]{3,2,1,0:T(8,128)(2,1)} %tie.54.refs_0_), channel_id=1, source_target_pairs={{0,8},{8,0},{16,24},{24,16},{1,9},{9,1},{17,25},{25,17},{2,10},{10... | collective-permute-start | bytes 884744 | tf_op jit(solution)/shard_map/ppermute | solution.py:543
  (128 other events, 770.3 us)
Sparse Core Ops, SparseCore 0:
  85.4 148.7 all-gather.1
